TPU v7x, 32 devices: a whole 2x2x4 slice. The times are simulated.
32 devices in a mesh: layer: 8 (over z, x), box: 4 (over y, core).
Axes of the slice: x: 2, y: 2, z: 4, core: 2. Of those that a mesh axis runs over, the one named last changes fastest.
Arguments:
- box_maps: bfloat16 [8, 4096, 1024], P('layer', 'box'), may hold values from -0.1875 to 0.1875
- block_pattern: int32 [8, 32, 8], P('layer', 'box'), may hold values 0 or 1
- face_inverses: float32 [8, 3, 256, 256], P('layer'), may hold values from -0.375 to 0.375
- index_map: int32 [8, 1024], P('layer'), may hold values from 0 to 1023, each once within a row
- sources: float32 [8, 16, 1024], P('layer', 'box'), may hold values from -2.5 to 2.5
Outputs:
- merged: bfloat16 [8, 1024, 1024], P('layer')
- sweep_trace: float32 [8, 16, 1024], P('layer', 'box')
Inputs may be any that keep to these rules, and one draw needn't show every extreme that they name: Each row of index_map is a permutation of 0 to 1023.
All inputs are finite; a program needn't handle non-finite values. No bound on the sum of `block_pattern` on one device may be relied on, other than what follows from the above.
Results may differ from a plain program's by a relative error of at most 0.025.
Values may be sent and summed in bfloat16 or wider, within the bound.
No kernel may reach another device: no remote copies, remote signals or barrier semaphores. Data moves between devices by JAX's collectives and lax.ppermute only.
A program may use at most 64 MiB of HBM per device.

v0:
```python
import jax
import jax.numpy as jnp
from jax import lax
from jax.sharding import PartitionSpec as P


def partner_2(value, axis, distance):
    mask = 2**distance
    pairs = [(source, source ^ mask) for source in range(lax.axis_size(axis))]
    return lax.ppermute(value, axis, pairs)


def shifted(block, axis, distance):
    devices = range(lax.axis_size(axis))
    route = [(i - distance, i) for i in devices if i - distance in devices]
    return lax.ppermute(block, axis, route)


def mask_map(one_map, one_pattern):
    blocks_count = one_pattern.shape[0]
    width = one_map.shape[0]
    tiles = one_map.reshape(
        blocks_count, width // blocks_count, blocks_count, width // blocks_count
    )
    kept = one_pattern.astype(jnp.bfloat16)[:, None, :, None]
    return (tiles * kept).reshape(width, width)


def combine(first, second, inverse, level):
    face_size = inverse.shape[0]
    joined = 0.5 * (first.astype(jnp.float32) + second.astype(jnp.float32))
    left_cols = joined[:, level * face_size : (level + 1) * face_size]
    right_rows = joined[level * face_size : (level + 1) * face_size, :]
    product = jnp.dot(left_cols, inverse, precision=lax.Precision.HIGHEST)
    return (joined - jnp.dot(product, right_rows, precision=lax.Precision.HIGHEST)).astype(
        jnp.bfloat16
    )


def on_device(box_maps, block_pattern, face_inverses, index_map, sources):
    boxes = lax.axis_size("box")
    layers = lax.axis_size("layer")
    coupling = float(boxes) ** 0.5
    levels = boxes.bit_length() - 1
    leaf = mask_map(box_maps[0], block_pattern[0])
    inverses = face_inverses[0]
    current = leaf
    position = lax.axis_index("box")
    for level in range(levels):
        partner = partner_2(current, "box", level)
        tree_node = (boxes >> level + 1) - 1 + (position >> level + 1)
        chosen = lax.dynamic_index_in_dim(inverses, tree_node, 0, keepdims=False)
        current = combine(current, partner, chosen, level)
    merged = current
    source_rows = sources[0]
    order_map = index_map[0]
    initial = jnp.zeros(source_rows.shape, jnp.float32)

    def down_step(step, state):
        received = shifted(state, "layer", 1)
        gathered = received[:, order_map].astype(jnp.bfloat16)
        return source_rows + coupling * jnp.dot(
            gathered, merged.T, preferred_element_type=jnp.float32
        )

    downward = lax.fori_loop(0, layers, down_step, initial)

    def up_step(step, state):
        received = shifted(state, "layer", -1)
        return downward + coupling * jnp.dot(
            received.astype(jnp.bfloat16), merged, preferred_element_type=jnp.float32
        )

    upward = lax.fori_loop(0, layers, up_step, initial)
    return (merged[None], upward[None])


def solution(mesh):
    return jax.shard_map(
        on_device,
        mesh=mesh,
        in_specs=(
            P("layer", "box", None),
            P("layer", "box", None),
            P("layer", None, None, None),
            P("layer", None),
            P("layer", "box", None),
        ),
        out_specs=(P("layer", None, None), P("layer", "box", None)),
        check_vma=False,
    )
```

profile of v0, /device:TPU:0, one launch (start us, length us, event | category | flops | bytes accessed | tf_op | source)
XLA Modules:
  0.0 209.4 jit_solution(6074131437407517057)
XLA Ops:
  0.6 0.8 convert_bitcast_fusion
  1.8 1.9 bitcast_multiply_fusion
  3.6 0.5 collective-permute-start.2
  4.1 3.9 %collective-permute-done.2 = bf16[1024,1024]{1,0:T(8,128)(2,1)} collective-permute-done((bf16[1024,1024]{1,0:T(8,128)(2,1)S(1)}, bf16[1024,1024]{1,0:T(8,128)(2,1)}, u32[]{:S(2)}, u32[]{:S(2)}) %collective-permute-start.2) | collective-permute-done | bytes 2097184 | tf_op jit(solution)/shard_map/ppermute | solution.py:10
  8.1 2.5 %add_multiply_fusion.1 = f32[1024,1024]{1,0:T(8,128)S(1)} fusion(bf16[1024,1024]{1,0:T(8,128)(2,1)} %collective-permute-done.2, bf16[1024,1024]{1,0:T(8,128)(2,1)S(1)} %bitcast_multiply_fusion), kind=kLoop, calls=%fused_computation.14 | loop fusion | flops 4194304 | bytes 8388608 | tf_op jit(solution)/shard_map/mul | solution.py:31
  10.6 1.0 fusion.8
  11.6 3.7 %subtract_convert_fusion.1 = bf16[1024,1024]{1,0:T(8,128)(2,1)S(1)} fusion(f32[1024,1024]{1,0:T(8,128)S(1)} %add_multiply_fusion.1, f32[1024,256]{1,0:T(8,128)S(1)} %fusion.8), kind=kOutput, calls=%fused_computation.13 | convolution fusion | flops 3223322624 | bytes 8388608 | tf_op jit(solution)/shard_map/dot_general | solution.py:35
  15.3 3.0 %collective-permute-start.3 = (bf16[1024,1024]{1,0:T(8,128)(2,1)S(1)}, bf16[1024,1024]{1,0:T(8,128)(2,1)}, u32[]{:S(2)}, u32[]{:S(2)}) collective-permute-start(bf16[1024,1024]{1,0:T(8,128)(2,1)S(1)} %subtract_convert_fusion.1), channel_id=1, source_target_pairs={{0,2},{1,3},{2,0},{3,1},{4,6},{5,7},{6,4},{7,5},{8,10},{9,11},{10,... | collective-permute-start | bytes 6291464 | tf_op jit(solution)/shard_map/ppermute | solution.py:10
  18.3 46.0 %collective-permute-done.3 = bf16[1024,1024]{1,0:T(8,128)(2,1)} collective-permute-done((bf16[1024,1024]{1,0:T(8,128)(2,1)S(1)}, bf16[1024,1024]{1,0:T(8,128)(2,1)}, u32[]{:S(2)}, u32[]{:S(2)}) %collective-permute-start.3) | collective-permute-done | bytes 2097184 | tf_op jit(solution)/shard_map/ppermute | solution.py:10
  64.3 2.5 %add_multiply_fusion = f32[1024,1024]{1,0:T(8,128)S(1)} fusion(bf16[1024,1024]{1,0:T(8,128)(2,1)} %collective-permute-done.3, bf16[1024,1024]{1,0:T(8,128)(2,1)S(1)} %subtract_convert_fusion.1), kind=kLoop, calls=%fused_computation.12 | loop fusion | flops 4194304 | bytes 8388608 | tf_op jit(solution)/shard_map/mul | solution.py:31
  66.9 1.0 fusion.5
  67.9 3.7 %subtract_convert_fusion = bf16[1024,1024]{1,0:T(8,128)(2,1)S(1)} fusion(f32[1024,1024]{1,0:T(8,128)S(1)} %add_multiply_fusion, f32[1024,256]{1,0:T(8,128)S(1)} %fusion.5), kind=kOutput, calls=%fused_computation.11 | convolution fusion | flops 3223322624 | bytes 8388608 | tf_op jit(solution)/shard_map/dot_general | solution.py:35
  71.6 81.2 %while.22 = (s32[]{:T(128)}, f32[4,1024]{1,0:T(4,128)S(1)}, s32[1024]{0:T(1024)S(1)}, bf16[1024,1024]{1,0:T(8,128)(2,1)S(1)}, f32[4,1024]{1,0:T(4,128)S(1)}, /*index=5*/s32[]{:T(128)}, s32[]{:T(128)}) while((s32[]{:T(128)}, f32[4,1024]{1,0:T(4,128)S(1)}, s32[1024]{0:T(1024)S(1)}, bf16[1024,1024]{1,0:T(8,128)(2,1)S(1)}, ...), condition=%wide.region_1.2_spmd.clone, body=%wide.region_0.1_spmd.clone.sunk | while | flops 8404995 | bytes 2248831 | solution.py:66
  71.6 3.6 %collective-permute-start = (bf16[4,1024]{1,0:T(4,128)(2,1)S(1)}, bf16[4,1024]{1,0:T(4,128)(2,1)S(1)}, u32[]{:S(2)}, u32[]{:S(2)}) collective-permute-start(bf16[4,1024]{1,0:T(4,128)(2,1)S(1)} %broadcast_select_fusion.4), channel_id=1, source_target_pairs={{0,4},{4,8},{8,12},{12,16},{16,20},{20,24},{24,28},{1,5},{5,9},{9,... | collective-permute-start | bytes 24584 | tf_op jit(solution)/shard_map/while/body/eval_jaxpr/ppermute | solution.py:16
  75.3 1.3 collective-permute-done
  76.8 3.2 %gather_fusion = bf16[1024,4]{1,0:T(8,128)(2,1)S(1)} fusion(bf16[4,1024]{0,1:T(8,128)(2,1)S(1)} %copy.17, s32[1024]{0:T(1024)S(1)} %broadcast_clamp_fusion.2), kind=kCustom, calls=%fused_computation.clone.clone.1 | custom fusion | bytes 20480 | tf_op jit(solution)/shard_map/while/body/eval_jaxpr/gather | solution.py:61
  80.0 0.6 fusion.30
  80.7 4.2 %collective-permute-start = (bf16[4,1024]{1,0:T(4,128)(2,1)S(1)}, bf16[4,1024]{1,0:T(4,128)(2,1)S(1)}, u32[]{:S(2)}, u32[]{:S(2)}) collective-permute-start(bf16[4,1024]{1,0:T(4,128)(2,1)S(1)} %broadcast_select_fusion.4), channel_id=1, source_target_pairs={{0,4},{4,8},{8,12},{12,16},{16,20},{20,24},{24,28},{1,5},{5,9},{9,... | collective-permute-start | bytes 24584 | tf_op jit(solution)/shard_map/while/body/eval_jaxpr/ppermute | solution.py:16
  84.9 1.3 collective-permute-done
  86.5 3.2 %gather_fusion = bf16[1024,4]{1,0:T(8,128)(2,1)S(1)} fusion(bf16[4,1024]{0,1:T(8,128)(2,1)S(1)} %copy.17, s32[1024]{0:T(1024)S(1)} %broadcast_clamp_fusion.2), kind=kCustom, calls=%fused_computation.clone.clone.1 | custom fusion | bytes 20480 | tf_op jit(solution)/shard_map/while/body/eval_jaxpr/gather | solution.py:61
  89.7 0.6 fusion.30
  90.4 4.4 %collective-permute-start = (bf16[4,1024]{1,0:T(4,128)(2,1)S(1)}, bf16[4,1024]{1,0:T(4,128)(2,1)S(1)}, u32[]{:S(2)}, u32[]{:S(2)}) collective-permute-start(bf16[4,1024]{1,0:T(4,128)(2,1)S(1)} %broadcast_select_fusion.4), channel_id=1, source_target_pairs={{0,4},{4,8},{8,12},{12,16},{16,20},{20,24},{24,28},{1,5},{5,9},{9,... | collective-permute-start | bytes 24584 | tf_op jit(solution)/shard_map/while/body/eval_jaxpr/ppermute | solution.py:16
  94.7 1.3 collective-permute-done
  96.3 3.2 %gather_fusion = bf16[1024,4]{1,0:T(8,128)(2,1)S(1)} fusion(bf16[4,1024]{0,1:T(8,128)(2,1)S(1)} %copy.17, s32[1024]{0:T(1024)S(1)} %broadcast_clamp_fusion.2), kind=kCustom, calls=%fused_computation.clone.clone.1 | custom fusion | bytes 20480 | tf_op jit(solution)/shard_map/while/body/eval_jaxpr/gather | solution.py:61
  99.5 0.6 fusion.30
  100.2 5.1 %collective-permute-start = (bf16[4,1024]{1,0:T(4,128)(2,1)S(1)}, bf16[4,1024]{1,0:T(4,128)(2,1)S(1)}, u32[]{:S(2)}, u32[]{:S(2)}) collective-permute-start(bf16[4,1024]{1,0:T(4,128)(2,1)S(1)} %broadcast_select_fusion.4), channel_id=1, source_target_pairs={{0,4},{4,8},{8,12},{12,16},{16,20},{20,24},{24,28},{1,5},{5,9},{9,... | collective-permute-start | bytes 24584 | tf_op jit(solution)/shard_map/while/body/eval_jaxpr/ppermute | solution.py:16
  105.3 1.3 collective-permute-done
  106.8 3.2 %gather_fusion = bf16[1024,4]{1,0:T(8,128)(2,1)S(1)} fusion(bf16[4,1024]{0,1:T(8,128)(2,1)S(1)} %copy.17, s32[1024]{0:T(1024)S(1)} %broadcast_clamp_fusion.2), kind=kCustom, calls=%fused_computation.clone.clone.1 | custom fusion | bytes 20480 | tf_op jit(solution)/shard_map/while/body/eval_jaxpr/gather | solution.py:61
  110.0 0.6 fusion.30
  110.7 5.1 %collective-permute-start = (bf16[4,1024]{1,0:T(4,128)(2,1)S(1)}, bf16[4,1024]{1,0:T(4,128)(2,1)S(1)}, u32[]{:S(2)}, u32[]{:S(2)}) collective-permute-start(bf16[4,1024]{1,0:T(4,128)(2,1)S(1)} %broadcast_select_fusion.4), channel_id=1, source_target_pairs={{0,4},{4,8},{8,12},{12,16},{16,20},{20,24},{24,28},{1,5},{5,9},{9,... | collective-permute-start | bytes 24584 | tf_op jit(solution)/shard_map/while/body/eval_jaxpr/ppermute | solution.py:16
  115.8 1.3 collective-permute-done
  117.3 3.2 %gather_fusion = bf16[1024,4]{1,0:T(8,128)(2,1)S(1)} fusion(bf16[4,1024]{0,1:T(8,128)(2,1)S(1)} %copy.17, s32[1024]{0:T(1024)S(1)} %broadcast_clamp_fusion.2), kind=kCustom, calls=%fused_computation.clone.clone.1 | custom fusion | bytes 20480 | tf_op jit(solution)/shard_map/while/body/eval_jaxpr/gather | solution.py:61
  120.6 0.6 fusion.30
  121.2 5.1 %collective-permute-start = (bf16[4,1024]{1,0:T(4,128)(2,1)S(1)}, bf16[4,1024]{1,0:T(4,128)(2,1)S(1)}, u32[]{:S(2)}, u32[]{:S(2)}) collective-permute-start(bf16[4,1024]{1,0:T(4,128)(2,1)S(1)} %broadcast_select_fusion.4), channel_id=1, source_target_pairs={{0,4},{4,8},{8,12},{12,16},{16,20},{20,24},{24,28},{1,5},{5,9},{9,... | collective-permute-start | bytes 24584 | tf_op jit(solution)/shard_map/while/body/eval_jaxpr/ppermute | solution.py:16
  126.4 1.3 collective-permute-done
  127.9 3.2 %gather_fusion = bf16[1024,4]{1,0:T(8,128)(2,1)S(1)} fusion(bf16[4,1024]{0,1:T(8,128)(2,1)S(1)} %copy.17, s32[1024]{0:T(1024)S(1)} %broadcast_clamp_fusion.2), kind=kCustom, calls=%fused_computation.clone.clone.1 | custom fusion | bytes 20480 | tf_op jit(solution)/shard_map/while/body/eval_jaxpr/gather | solution.py:61
  131.1 0.6 fusion.30
  131.8 5.1 %collective-permute-start = (bf16[4,1024]{1,0:T(4,128)(2,1)S(1)}, bf16[4,1024]{1,0:T(4,128)(2,1)S(1)}, u32[]{:S(2)}, u32[]{:S(2)}) collective-permute-start(bf16[4,1024]{1,0:T(4,128)(2,1)S(1)} %broadcast_select_fusion.4), channel_id=1, source_target_pairs={{0,4},{4,8},{8,12},{12,16},{16,20},{20,24},{24,28},{1,5},{5,9},{9,... | collective-permute-start | bytes 24584 | tf_op jit(solution)/shard_map/while/body/eval_jaxpr/ppermute | solution.py:16
  136.9 1.3 collective-permute-done
  138.4 3.2 %gather_fusion = bf16[1024,4]{1,0:T(8,128)(2,1)S(1)} fusion(bf16[4,1024]{0,1:T(8,128)(2,1)S(1)} %copy.17, s32[1024]{0:T(1024)S(1)} %broadcast_clamp_fusion.2), kind=kCustom, calls=%fused_computation.clone.clone.1 | custom fusion | bytes 20480 | tf_op jit(solution)/shard_map/while/body/eval_jaxpr/gather | solution.py:61
  141.6 0.6 fusion.30
  142.3 5.1 %collective-permute-start = (bf16[4,1024]{1,0:T(4,128)(2,1)S(1)}, bf16[4,1024]{1,0:T(4,128)(2,1)S(1)}, u32[]{:S(2)}, u32[]{:S(2)}) collective-permute-start(bf16[4,1024]{1,0:T(4,128)(2,1)S(1)} %broadcast_select_fusion.4), channel_id=1, source_target_pairs={{0,4},{4,8},{8,12},{12,16},{16,20},{20,24},{24,28},{1,5},{5,9},{9,... | collective-permute-start | bytes 24584 | tf_op jit(solution)/shard_map/while/body/eval_jaxpr/ppermute | solution.py:16
  147.4 1.3 collective-permute-done
  149.0 3.2 %gather_fusion = bf16[1024,4]{1,0:T(8,128)(2,1)S(1)} fusion(bf16[4,1024]{0,1:T(8,128)(2,1)S(1)} %copy.17, s32[1024]{0:T(1024)S(1)} %broadcast_clamp_fusion.2), kind=kCustom, calls=%fused_computation.clone.clone.1 | custom fusion | bytes 20480 | tf_op jit(solution)/shard_map/while/body/eval_jaxpr/gather | solution.py:61
  152.2 0.6 fusion.30
  152.8 55.3 %while.23 = (s32[]{:T(128)}, f32[4,1024]{1,0:T(4,128)S(1)}, bf16[1024,1024]{1,0:T(8,128)(2,1)S(1)}, f32[4,1024]{1,0:T(4,128)S(1)}, s32[]{:T(128)}, /*index=5*/s32[]{:T(128)}) while((s32[]{:T(128)}, f32[4,1024]{1,0:T(4,128)S(1)}, bf16[1024,1024]{1,0:T(8,128)(2,1)S(1)}, f32[4,1024]{1,0:T(4,128)S(1)}, s32[]{:T(128)}, ...), condition=%wide.region_3.4_spmd.clone, body=%wide.region_2.3_spmd.clone.sunk | while | flops 8400899 | bytes 2195575 | solution.py:74
  152.8 1.3 collective-permute-start.1
  154.1 5.4 %collective-permute-done.1 = bf16[4,1024]{1,0:T(4,128)(2,1)S(1)} collective-permute-done((bf16[4,1024]{1,0:T(4,128)(2,1)S(1)}, bf16[4,1024]{1,0:T(4,128)(2,1)S(1)}, u32[]{:S(2)}, u32[]{:S(2)}) %collective-permute-start.1) | collective-permute-done | bytes 8224 | tf_op jit(solution)/shard_map/while/body/eval_jaxpr/ppermute | solution.py:16
  160.0 1.3 collective-permute-start.1
  161.3 5.4 %collective-permute-done.1 = bf16[4,1024]{1,0:T(4,128)(2,1)S(1)} collective-permute-done((bf16[4,1024]{1,0:T(4,128)(2,1)S(1)}, bf16[4,1024]{1,0:T(4,128)(2,1)S(1)}, u32[]{:S(2)}, u32[]{:S(2)}) %collective-permute-start.1) | collective-permute-done | bytes 8224 | tf_op jit(solution)/shard_map/while/body/eval_jaxpr/ppermute | solution.py:16
  166.7 0.4 fusion.33
  167.1 1.3 collective-permute-start.1
  168.4 5.1 %collective-permute-done.1 = bf16[4,1024]{1,0:T(4,128)(2,1)S(1)} collective-permute-done((bf16[4,1024]{1,0:T(4,128)(2,1)S(1)}, bf16[4,1024]{1,0:T(4,128)(2,1)S(1)}, u32[]{:S(2)}, u32[]{:S(2)}) %collective-permute-start.1) | collective-permute-done | bytes 8224 | tf_op jit(solution)/shard_map/while/body/eval_jaxpr/ppermute | solution.py:16
  173.9 1.3 collective-permute-start.1
  175.2 5.1 %collective-permute-done.1 = bf16[4,1024]{1,0:T(4,128)(2,1)S(1)} collective-permute-done((bf16[4,1024]{1,0:T(4,128)(2,1)S(1)}, bf16[4,1024]{1,0:T(4,128)(2,1)S(1)}, u32[]{:S(2)}, u32[]{:S(2)}) %collective-permute-start.1) | collective-permute-done | bytes 8224 | tf_op jit(solution)/shard_map/while/body/eval_jaxpr/ppermute | solution.py:16
  180.8 1.3 collective-permute-start.1
  182.1 5.1 %collective-permute-done.1 = bf16[4,1024]{1,0:T(4,128)(2,1)S(1)} collective-permute-done((bf16[4,1024]{1,0:T(4,128)(2,1)S(1)}, bf16[4,1024]{1,0:T(4,128)(2,1)S(1)}, u32[]{:S(2)}, u32[]{:S(2)}) %collective-permute-start.1) | collective-permute-done | bytes 8224 | tf_op jit(solution)/shard_map/while/body/eval_jaxpr/ppermute | solution.py:16
  187.6 1.3 collective-permute-start.1
  188.9 5.1 %collective-permute-done.1 = bf16[4,1024]{1,0:T(4,128)(2,1)S(1)} collective-permute-done((bf16[4,1024]{1,0:T(4,128)(2,1)S(1)}, bf16[4,1024]{1,0:T(4,128)(2,1)S(1)}, u32[]{:S(2)}, u32[]{:S(2)}) %collective-permute-start.1) | collective-permute-done | bytes 8224 | tf_op jit(solution)/shard_map/while/body/eval_jaxpr/ppermute | solution.py:16
  194.4 1.3 collective-permute-start.1
  195.8 5.1 %collective-permute-done.1 = bf16[4,1024]{1,0:T(4,128)(2,1)S(1)} collective-permute-done((bf16[4,1024]{1,0:T(4,128)(2,1)S(1)}, bf16[4,1024]{1,0:T(4,128)(2,1)S(1)}, u32[]{:S(2)}, u32[]{:S(2)}) %collective-permute-start.1) | collective-permute-done | bytes 8224 | tf_op jit(solution)/shard_map/while/body/eval_jaxpr/ppermute | solution.py:16
  201.3 1.3 collective-permute-start.1
  202.6 5.1 %collective-permute-done.1 = bf16[4,1024]{1,0:T(4,128)(2,1)S(1)} collective-permute-done((bf16[4,1024]{1,0:T(4,128)(2,1)S(1)}, bf16[4,1024]{1,0:T(4,128)(2,1)S(1)}, u32[]{:S(2)}, u32[]{:S(2)}) %collective-permute-start.1) | collective-permute-done | bytes 8224 | tf_op jit(solution)/shard_map/while/body/eval_jaxpr/ppermute | solution.py:16
  208.1 1.3 copy-done.1
  (59 shorter events, 5.1 us)
Async XLA Ops:
  0.6 10.0 %copy-start = (f32[1,3,256,256]{3,2,1,0:T(8,128)S(1)}, f32[1,3,256,256]{3,2,1,0:T(8,128)}, u32[]{:S(2)}) copy-start(f32[1,3,256,256]{3,2,1,0:T(8,128)} %param.11) | copy-start | bytes 2359300
  3.6 4.4 %collective-permute-start.2 = (bf16[1024,1024]{1,0:T(8,128)(2,1)S(1)}, bf16[1024,1024]{1,0:T(8,128)(2,1)}, u32[]{:S(2)}, u32[]{:S(2)}) collective-permute-start(bf16[1024,1024]{1,0:T(8,128)(2,1)S(1)} %bitcast_multiply_fusion), channel_id=1, source_target_pairs={{0,1},{1,0},{2,3},{3,2},{4,5},{5,4},{6,7},{7,6},{8,9},{9,8},{10,11... | collective-permute-start | bytes 6291464 | tf_op jit(solution)/shard_map/ppermute | solution.py:10
  15.3 49.0 %collective-permute-start.3 = (bf16[1024,1024]{1,0:T(8,128)(2,1)S(1)}, bf16[1024,1024]{1,0:T(8,128)(2,1)}, u32[]{:S(2)}, u32[]{:S(2)}) collective-permute-start(bf16[1024,1024]{1,0:T(8,128)(2,1)S(1)} %subtract_convert_fusion.1), channel_id=1, source_target_pairs={{0,2},{1,3},{2,0},{3,1},{4,6},{5,7},{6,4},{7,5},{8,10},{9,11},{10,... | collective-permute-start | bytes 6291464 | tf_op jit(solution)/shard_map/ppermute | solution.py:10
  66.8 4.8 %copy-start.2 = (f32[1,4,1024]{2,1,0:T(4,128)S(1)}, f32[1,4,1024]{2,1,0:T(4,128)}, u32[]{:S(2)}) copy-start(f32[1,4,1024]{2,1,0:T(4,128)} %param.13) | copy-start | bytes 49156
  66.9 4.8 %copy-start.4 = (s32[1,1024]{1,0:T(1,128)S(1)}, s32[1,1024]{1,0:T(1,128)}, u32[]{:S(2)}) copy-start(s32[1,1024]{1,0:T(1,128)} %param.12) | copy-start | bytes 12292
  71.6 5.0 %collective-permute-start = (bf16[4,1024]{1,0:T(4,128)(2,1)S(1)}, bf16[4,1024]{1,0:T(4,128)(2,1)S(1)}, u32[]{:S(2)}, u32[]{:S(2)}) collective-permute-start(bf16[4,1024]{1,0:T(4,128)(2,1)S(1)} %broadcast_select_fusion.4), channel_id=1, source_target_pairs={{0,4},{4,8},{8,12},{12,16},{16,20},{20,24},{24,28},{1,5},{5,9},{9,... | collective-permute-start | bytes 24584 | tf_op jit(solution)/shard_map/while/body/eval_jaxpr/ppermute | solution.py:16
  80.7 5.5 %collective-permute-start = (bf16[4,1024]{1,0:T(4,128)(2,1)S(1)}, bf16[4,1024]{1,0:T(4,128)(2,1)S(1)}, u32[]{:S(2)}, u32[]{:S(2)}) collective-permute-start(bf16[4,1024]{1,0:T(4,128)(2,1)S(1)} %broadcast_select_fusion.4), channel_id=1, source_target_pairs={{0,4},{4,8},{8,12},{12,16},{16,20},{20,24},{24,28},{1,5},{5,9},{9,... | collective-permute-start | bytes 24584 | tf_op jit(solution)/shard_map/while/body/eval_jaxpr/ppermute | solution.py:16
  90.4 5.7 %collective-permute-start = (bf16[4,1024]{1,0:T(4,128)(2,1)S(1)}, bf16[4,1024]{1,0:T(4,128)(2,1)S(1)}, u32[]{:S(2)}, u32[]{:S(2)}) collective-permute-start(bf16[4,1024]{1,0:T(4,128)(2,1)S(1)} %broadcast_select_fusion.4), channel_id=1, source_target_pairs={{0,4},{4,8},{8,12},{12,16},{16,20},{20,24},{24,28},{1,5},{5,9},{9,... | collective-permute-start | bytes 24584 | tf_op jit(solution)/shard_map/while/body/eval_jaxpr/ppermute | solution.py:16
  100.2 6.4 %collective-permute-start = (bf16[4,1024]{1,0:T(4,128)(2,1)S(1)}, bf16[4,1024]{1,0:T(4,128)(2,1)S(1)}, u32[]{:S(2)}, u32[]{:S(2)}) collective-permute-start(bf16[4,1024]{1,0:T(4,128)(2,1)S(1)} %broadcast_select_fusion.4), channel_id=1, source_target_pairs={{0,4},{4,8},{8,12},{12,16},{16,20},{20,24},{24,28},{1,5},{5,9},{9,... | collective-permute-start | bytes 24584 | tf_op jit(solution)/shard_map/while/body/eval_jaxpr/ppermute | solution.py:16
  110.7 6.4 %collective-permute-start = (bf16[4,1024]{1,0:T(4,128)(2,1)S(1)}, bf16[4,1024]{1,0:T(4,128)(2,1)S(1)}, u32[]{:S(2)}, u32[]{:S(2)}) collective-permute-start(bf16[4,1024]{1,0:T(4,128)(2,1)S(1)} %broadcast_select_fusion.4), channel_id=1, source_target_pairs={{0,4},{4,8},{8,12},{12,16},{16,20},{20,24},{24,28},{1,5},{5,9},{9,... | collective-permute-start | bytes 24584 | tf_op jit(solution)/shard_map/while/body/eval_jaxpr/ppermute | solution.py:16
  121.2 6.4 %collective-permute-start = (bf16[4,1024]{1,0:T(4,128)(2,1)S(1)}, bf16[4,1024]{1,0:T(4,128)(2,1)S(1)}, u32[]{:S(2)}, u32[]{:S(2)}) collective-permute-start(bf16[4,1024]{1,0:T(4,128)(2,1)S(1)} %broadcast_select_fusion.4), channel_id=1, source_target_pairs={{0,4},{4,8},{8,12},{12,16},{16,20},{20,24},{24,28},{1,5},{5,9},{9,... | collective-permute-start | bytes 24584 | tf_op jit(solution)/shard_map/while/body/eval_jaxpr/ppermute | solution.py:16
  131.8 6.4 %collective-permute-start = (bf16[4,1024]{1,0:T(4,128)(2,1)S(1)}, bf16[4,1024]{1,0:T(4,128)(2,1)S(1)}, u32[]{:S(2)}, u32[]{:S(2)}) collective-permute-start(bf16[4,1024]{1,0:T(4,128)(2,1)S(1)} %broadcast_select_fusion.4), channel_id=1, source_target_pairs={{0,4},{4,8},{8,12},{12,16},{16,20},{20,24},{24,28},{1,5},{5,9},{9,... | collective-permute-start | bytes 24584 | tf_op jit(solution)/shard_map/while/body/eval_jaxpr/ppermute | solution.py:16
  142.3 6.4 %collective-permute-start = (bf16[4,1024]{1,0:T(4,128)(2,1)S(1)}, bf16[4,1024]{1,0:T(4,128)(2,1)S(1)}, u32[]{:S(2)}, u32[]{:S(2)}) collective-permute-start(bf16[4,1024]{1,0:T(4,128)(2,1)S(1)} %broadcast_select_fusion.4), channel_id=1, source_target_pairs={{0,4},{4,8},{8,12},{12,16},{16,20},{20,24},{24,28},{1,5},{5,9},{9,... | collective-permute-start | bytes 24584 | tf_op jit(solution)/shard_map/while/body/eval_jaxpr/ppermute | solution.py:16
  152.8 6.7 %collective-permute-start.1 = (bf16[4,1024]{1,0:T(4,128)(2,1)S(1)}, bf16[4,1024]{1,0:T(4,128)(2,1)S(1)}, u32[]{:S(2)}, u32[]{:S(2)}) collective-permute-start(bf16[4,1024]{1,0:T(4,128)(2,1)S(1)} %broadcast_select_fusion.5), channel_id=1, source_target_pairs={{4,0},{8,4},{12,8},{16,12},{20,16},{24,20},{28,24},{5,1},{9,5},{13... | collective-permute-start | bytes 24584 | tf_op jit(solution)/shard_map/while/body/eval_jaxpr/ppermute | solution.py:16
  160.0 6.7 %collective-permute-start.1 = (bf16[4,1024]{1,0:T(4,128)(2,1)S(1)}, bf16[4,1024]{1,0:T(4,128)(2,1)S(1)}, u32[]{:S(2)}, u32[]{:S(2)}) collective-permute-start(bf16[4,1024]{1,0:T(4,128)(2,1)S(1)} %broadcast_select_fusion.5), channel_id=1, source_target_pairs={{4,0},{8,4},{12,8},{16,12},{20,16},{24,20},{28,24},{5,1},{9,5},{13... | collective-permute-start | bytes 24584 | tf_op jit(solution)/shard_map/while/body/eval_jaxpr/ppermute | solution.py:16
  167.1 6.4 %collective-permute-start.1 = (bf16[4,1024]{1,0:T(4,128)(2,1)S(1)}, bf16[4,1024]{1,0:T(4,128)(2,1)S(1)}, u32[]{:S(2)}, u32[]{:S(2)}) collective-permute-start(bf16[4,1024]{1,0:T(4,128)(2,1)S(1)} %broadcast_select_fusion.5), channel_id=1, source_target_pairs={{4,0},{8,4},{12,8},{16,12},{20,16},{24,20},{28,24},{5,1},{9,5},{13... | collective-permute-start | bytes 24584 | tf_op jit(solution)/shard_map/while/body/eval_jaxpr/ppermute | solution.py:16
  173.9 6.4 %collective-permute-start.1 = (bf16[4,1024]{1,0:T(4,128)(2,1)S(1)}, bf16[4,1024]{1,0:T(4,128)(2,1)S(1)}, u32[]{:S(2)}, u32[]{:S(2)}) collective-permute-start(bf16[4,1024]{1,0:T(4,128)(2,1)S(1)} %broadcast_select_fusion.5), channel_id=1, source_target_pairs={{4,0},{8,4},{12,8},{16,12},{20,16},{24,20},{28,24},{5,1},{9,5},{13... | collective-permute-start | bytes 24584 | tf_op jit(solution)/shard_map/while/body/eval_jaxpr/ppermute | solution.py:16
  180.8 6.4 %collective-permute-start.1 = (bf16[4,1024]{1,0:T(4,128)(2,1)S(1)}, bf16[4,1024]{1,0:T(4,128)(2,1)S(1)}, u32[]{:S(2)}, u32[]{:S(2)}) collective-permute-start(bf16[4,1024]{1,0:T(4,128)(2,1)S(1)} %broadcast_select_fusion.5), channel_id=1, source_target_pairs={{4,0},{8,4},{12,8},{16,12},{20,16},{24,20},{28,24},{5,1},{9,5},{13... | collective-permute-start | bytes 24584 | tf_op jit(solution)/shard_map/while/body/eval_jaxpr/ppermute | solution.py:16
  187.6 6.4 %collective-permute-start.1 = (bf16[4,1024]{1,0:T(4,128)(2,1)S(1)}, bf16[4,1024]{1,0:T(4,128)(2,1)S(1)}, u32[]{:S(2)}, u32[]{:S(2)}) collective-permute-start(bf16[4,1024]{1,0:T(4,128)(2,1)S(1)} %broadcast_select_fusion.5), channel_id=1, source_target_pairs={{4,0},{8,4},{12,8},{16,12},{20,16},{24,20},{28,24},{5,1},{9,5},{13... | collective-permute-start | bytes 24584 | tf_op jit(solution)/shard_map/while/body/eval_jaxpr/ppermute | solution.py:16
  194.4 6.4 %collective-permute-start.1 = (bf16[4,1024]{1,0:T(4,128)(2,1)S(1)}, bf16[4,1024]{1,0:T(4,128)(2,1)S(1)}, u32[]{:S(2)}, u32[]{:S(2)}) collective-permute-start(bf16[4,1024]{1,0:T(4,128)(2,1)S(1)} %broadcast_select_fusion.5), channel_id=1, source_target_pairs={{4,0},{8,4},{12,8},{16,12},{20,16},{24,20},{28,24},{5,1},{9,5},{13... | collective-permute-start | bytes 24584 | tf_op jit(solution)/shard_map/while/body/eval_jaxpr/ppermute | solution.py:16
  201.3 6.4 %collective-permute-start.1 = (bf16[4,1024]{1,0:T(4,128)(2,1)S(1)}, bf16[4,1024]{1,0:T(4,128)(2,1)S(1)}, u32[]{:S(2)}, u32[]{:S(2)}) collective-permute-start(bf16[4,1024]{1,0:T(4,128)(2,1)S(1)} %broadcast_select_fusion.5), channel_id=1, source_target_pairs={{4,0},{8,4},{12,8},{16,12},{20,16},{24,20},{28,24},{5,1},{9,5},{13... | collective-permute-start | bytes 24584 | tf_op jit(solution)/shard_map/while/body/eval_jaxpr/ppermute | solution.py:16
  208.1 1.3 copy-start.1
  208.1 1.3 copy-start.3
where the time goes:
time: 210 us; the launch traced here: 209 us
  waiting for transfers between devices  102 us (49%)
  starting transfers between devices  51.4 us (24%)
  local copies, waits for them, and re-layouts  29 us (14%)
  matrix products  17.6 us (8%)
  other arithmetic  8.08 us (4%)
    ppermute x16, waiting for transfers between devices, shifted(): return lax.ppermute(block, axis, route)  52.3 us
    ppermute x2, waiting for transfers between devices, partner_2(): return lax.ppermute(value, axis, pairs)  49.9 us
    ppermute x16, starting transfers between devices, shifted(): return lax.ppermute(block, axis, route)  47.9 us
    gather x8, local copies, waits for them, and re-layouts, down_step(): gathered = received[:, order_map].astype(jnp.bfloat16)  25.7 us
    dot_general x2, matrix products, combine(): jnp.dot(product, right_rows, precision=lax.Precision.HIGHEST)  7.42 us
    dot_general x8, matrix products, down_step(): jnp.dot(gathered, merged.T, preferred_element_type=jnp.float32)  5.07 us
    mul x2, other arithmetic, combine(): joined = 0.5 * (first.astype(jnp.float32) + second.astype(jnp.float32))  5.04 us
  transfers between devices with their start and end apart: 18, of which 18 were waited for; matrix products, arithmetic and copies ran while one was open for 0% of the time, Pallas kernels for 0%

commit v1 on v0

v1 whole, which is shorter than its diff:
```python
import functools

import jax
import jax.numpy as jnp
from jax import lax
from jax.experimental import pallas as pl
from jax.experimental.pallas import tpu as pltpu
from jax.sharding import PartitionSpec as P

AXES = ("layer", "box")


def combine_kernel(face_at, row_at, masked, is_face, *refs):
    refs = list(refs)
    if masked:
        own_pattern, other_pattern = refs.pop(0), refs.pop(0)
    own, other, inverse = refs.pop(0), refs.pop(0), refs.pop(0)
    face_rows = None if is_face else refs.pop(0)
    out = refs.pop(0)
    rows, width = own.shape
    face = inverse.shape[0]
    if masked:
        block = width // own_pattern.shape[1]
        strips = []
        for r in range(rows // block):
            tiles = []
            at = slice(r * block, (r + 1) * block)
            for c in range(width // block):
                cols = slice(c * block, (c + 1) * block)
                keep_own = 0.5 * own_pattern[row_at // block + r, c].astype(jnp.float32)
                keep_other = 0.5 * other_pattern[row_at // block + r, c].astype(jnp.float32)
                tiles.append(
                    own[at, cols].astype(jnp.float32) * keep_own
                    + other[at, cols].astype(jnp.float32) * keep_other
                )
            strips.append(jnp.concatenate(tiles, axis=1))
        joined = jnp.concatenate(strips, axis=0)
    else:
        joined = 0.5 * (own[...].astype(jnp.float32) + other[...].astype(jnp.float32))
    left = joined[:, face_at : face_at + face].astype(jnp.bfloat16)
    product = jnp.dot(left, inverse[...], preferred_element_type=jnp.float32)
    if is_face:
        right = joined.astype(jnp.bfloat16)
        refs.pop(0)[...] = right
    else:
        right = face_rows[...]
    out[...] = (
        joined
        - jnp.dot(product.astype(jnp.bfloat16), right, preferred_element_type=jnp.float32)
    ).astype(jnp.bfloat16)


def combine(own, other, inverse, face_rows, face_at, row_at, patterns):
    is_face = face_rows is None
    masked = patterns is not None
    rows, width = own.shape
    operands, specs = [], []
    if masked:
        operands += list(patterns)
        specs += [pl.BlockSpec(memory_space=pltpu.SMEM)] * 2
    operands += [own, other, inverse] + ([] if is_face else [face_rows])
    specs += [pl.BlockSpec(memory_space=pltpu.VMEM)] * (3 if is_face else 4)
    count = 2 if is_face else 1
    shape = jax.ShapeDtypeStruct((rows, width), jnp.bfloat16)
    result = pl.pallas_call(
        functools.partial(combine_kernel, face_at, row_at, masked, is_face),
        out_shape=[shape] * count,
        in_specs=specs,
        out_specs=[pl.BlockSpec(memory_space=pltpu.VMEM)] * count,
        compiler_params=pltpu.CompilerParams(vmem_limit_bytes=16 * 1024 * 1024),
        cost_estimate=pl.CostEstimate(
            flops=2 * rows * inverse.shape[0] * (width + inverse.shape[0]),
            bytes_accessed=2 * rows * width * 3,
            transcendentals=0,
        ),
    )(*operands)
    return result if is_face else (result[0], face_rows)


def row_times(rows, one_map):
    return jnp.dot(rows, one_map, preferred_element_type=jnp.float32)


def row_times_t(rows, one_map):
    return lax.dot_general(
        rows, one_map, (((1,), (1,)), ((), ())), preferred_element_type=jnp.float32
    )


def on_device(box_maps, block_pattern, face_inverses, index_map, sources):
    boxes = lax.axis_size("box")
    layers = lax.axis_size("layer")
    coupling = float(boxes) ** 0.5
    levels = boxes.bit_length() - 1
    face = face_inverses.shape[2]
    width = box_maps.shape[2]
    position = lax.axis_index("box")
    layer = lax.axis_index("layer")
    odd = layer % 2 == 1
    group = layer // 2
    groups = layers // 2
    leads = range(0, boxes, 2)

    def flat(at_layer, at_box):
        return at_layer * boxes + at_box

    def send(value, route):
        return lax.ppermute(value, AXES, route)

    to_lead = [(flat(i, b + 1), flat(i, b)) for i in range(layers) for b in leads]
    from_lead = [(target, source) for source, target in to_lead]
    to_pair = [(flat(i, b), flat(i ^ 1, b)) for i in range(layers) for b in leads]

    def to_box(level):
        return [(flat(i, b), flat(i, b ^ (1 << level))) for i in range(layers) for b in leads]

    def to_group(here, there):
        return [
            (flat(2 * here + side, b), flat(2 * there + side, b)) for side in (0, 1) for b in leads
        ]

    coarse = [(at, face) for at in range(0, width, face)]
    fine = coarse[:-1] + [(width - face, face // 2), (width - face // 2, face // 2)]

    inverses = face_inverses[0].astype(jnp.bfloat16)

    def inverse_of(level):
        node = (boxes >> (level + 1)) - 1 + (position >> (level + 1))
        return lax.dynamic_index_in_dim(inverses, node, 0, keepdims=False)

    raw = box_maps[0]
    patterns = (block_pattern[0], send(block_pattern[0], to_lead))
    raw_other = {at: send(raw[at : at + size], to_lead) for at, size in coarse}
    face_rows = None
    current = {}
    inverse = inverse_of(0)
    for at, size in coarse:
        current[at], face_rows = combine(
            raw[at : at + size], raw_other[at], inverse, face_rows, 0, at, patterns
        )

    pieces = coarse
    arrays = {}
    for level in range(1, levels):
        last = level == levels - 1
        wanted = fine if last else coarse
        first = [piece for piece in wanted if piece[0] == level * face and piece[1] == face]
        order = first + [piece for piece in wanted if piece not in first]
        held = {}
        for at, size in order:
            base = at // face * face
            held[at] = current[base][at - base : at - base + size]
        inverse = inverse_of(level)
        received = {at: send(held[at], to_box(level)) for at, size in order}
        face_rows = None
        current = {}
        for at, size in order:
            current[at], face_rows = combine(
                held[at], received[at], inverse, face_rows, level * face, 0, None
            )
        pieces = order

    rows_here = sources.shape[1]
    own_sources = lax.all_gather(sources[0], "box", axis=0, tiled=True)
    pair_sources = send(own_sources, to_pair)
    own_index = index_map[0]
    pair_index = send(index_map, to_pair)[0]
    place = lax.broadcasted_iota(jnp.int32, (width, width), 0)
    one_hot = []
    for side in (0, 1):
        index = jnp.where(odd == (side == 1), own_index, pair_index)
        one_hot.append((place == index[None, :]).astype(jnp.bfloat16))

    empty = jnp.zeros((width, width), jnp.bfloat16)
    maps = [empty, empty]
    permuted = [empty, empty]
    merged = empty
    for at, size in pieces:
        own = current[at]
        other = send(own, to_pair)
        merged = lax.dynamic_update_slice(merged, own, (at, 0))
        for side in (0, 1):
            piece = jnp.where(odd == (side == 1), own, other)
            maps[side] = lax.dynamic_update_slice(maps[side], piece, (at, 0))
            moved = row_times_t(piece, one_hot[side]).astype(jnp.bfloat16)
            permuted[side] = lax.dynamic_update_slice(permuted[side], moved, (at, 0))

    even_sources = jnp.where(odd, pair_sources, own_sources)
    odd_sources = jnp.where(odd, own_sources, pair_sources)

    arrived = None
    down_even = jnp.zeros(own_sources.shape, jnp.float32)
    down_odd = down_even
    for step in range(groups):
        here = group == step
        now_even = even_sources
        if arrived is not None:
            now_even = even_sources + coupling * row_times_t(arrived, permuted[0])
        now_odd = odd_sources + coupling * row_times_t(
            now_even.astype(jnp.bfloat16), permuted[1]
        )
        if step < groups - 1:
            arrived = send(now_odd.astype(jnp.bfloat16), to_group(step, step + 1))
        down_even = jnp.where(here, now_even, down_even)
        down_odd = jnp.where(here, now_odd, down_odd)

    arrived = None
    up_even = jnp.zeros(own_sources.shape, jnp.float32)
    up_odd = up_even
    for step in reversed(range(groups)):
        here = group == step
        now_odd = down_odd
        if arrived is not None:
            now_odd = down_odd + coupling * row_times(arrived, maps[1])
        now_even = down_even + coupling * row_times(now_odd.astype(jnp.bfloat16), maps[0])
        if step > 0:
            arrived = send(now_even.astype(jnp.bfloat16), to_group(step, step - 1))
        up_even = jnp.where(here, now_even, up_even)
        up_odd = jnp.where(here, now_odd, up_odd)

    up_own = jnp.where(odd, up_odd, up_even)
    lead_at = position // 2 * 2 * rows_here
    lead_rows = lax.dynamic_slice_in_dim(up_own, lead_at, rows_here, 0)
    next_rows = send(
        lax.dynamic_slice_in_dim(up_own, lead_at + rows_here, rows_here, 0), from_lead
    )
    is_lead = position % 2 == 0
    upward = jnp.where(is_lead, lead_rows, next_rows)
    merged = jnp.where(is_lead, merged, send(merged, from_lead))
    return (merged[None], upward[None])


def solution(mesh):
    return jax.shard_map(
        on_device,
        mesh=mesh,
        in_specs=(
            P("layer", "box", None),
            P("layer", "box", None),
            P("layer", None, None, None),
            P("layer", None),
            P("layer", "box", None),
        ),
        out_specs=(P("layer", None, None), P("layer", "box", None)),
        check_vma=False,
    )
```

time: 210 us -> 123 us (0.59)
  waiting for transfers between devices: 102 us -> 17 us
  local copies, waits for them, and re-layouts: 29 us -> 6.24 us
  Pallas kernels: 0 us -> 8.27 us
  blocking collectives: 0 us -> 5.25 us
  starting transfers between devices: 51.4 us -> 55.7 us
    ppermute x18 -> x25, waiting for transfers between devices: 102 us -> 17 us  [send(): return lax.ppermute(value, AXES, route)]
    gather x8 -> x0, local copies, waits for them, and re-layouts: 25.7 us -> none  [down_step(): gathered = received[:, order_map].astype(jnp.bfloat16)]
    pallas_call x0 -> x9, Pallas kernels: none -> 8.27 us  [combine(): pl.pallas_call(functools.partial(combine_kernel, face_at, row_at, masked,...]
    mul x3 -> x0, other arithmetic: 6.91 us -> none  [the longest x2 5.04 us: combine(): joined = 0.5 * (first.astype(jnp.float32) + second.astype(jnp.float32))]
    all_gather x0 -> x1, blocking collectives: none -> 5.25 us  [on_device(): own_sources = lax.all_gather(sources[0], 'box', axis=0, tiled=True)]
    ppermute x18 -> x25, starting transfers between devices: 51.4 us -> 55.7 us  [send(): return lax.ppermute(value, AXES, route)]
    broadcast_in_dim x0 -> x2, other arithmetic: none -> 3.74 us  [on_device(): return (merged[None], upward[None])]
    dynamic_update_slice x0 -> x4, other arithmetic: none -> 3.71 us  [on_device(): maps[side] = lax.dynamic_update_slice(maps[side], piece, (at, 0))]
  transfers between devices with their start and end apart: 18 -> 25, of which waited for: 18 -> 4; matrix products, arithmetic and copies ran while one was open for 0% -> 18% of each run, Pallas kernels for 0% -> 7%
where the time goes in v1:
time: 123 us; the launch traced here: 122 us
  starting transfers between devices  55.7 us (45%)
  matrix products  19.2 us (16%)
  waiting for transfers between devices  17 us (14%)
  other arithmetic  9.58 us (8%)
  Pallas kernels  8.27 us (7%)
  local copies, waits for them, and re-layouts  6.24 us (5%)
  blocking collectives  5.25 us (4%)
  between operations  1.32 us (1%)
    ppermute x25, starting transfers between devices, send(): return lax.ppermute(value, AXES, route)  55.7 us
    ppermute x25, waiting for transfers between devices, send(): return lax.ppermute(value, AXES, route)  17 us
    dot_general x17, matrix products, row_times_t(): lax.dot_general(rows, one_map, (((1,), (1,)), ((), ())), preferred_elemen...  14.8 us
    pallas_call x9, Pallas kernels, combine(): pl.pallas_call(functools.partial(combine_kernel, face_at, row_at, masked,...  8.27 us
    all_gather x1, blocking collectives, on_device(): own_sources = lax.all_gather(sources[0], 'box', axis=0, tiled=True)  5.25 us
    dot_general x7, matrix products, row_times(): return jnp.dot(rows, one_map, preferred_element_type=jnp.float32)  4.33 us
    broadcast_in_dim x2, other arithmetic, on_device(): return (merged[None], upward[None])  3.74 us
    dynamic_update_slice x4, other arithmetic, on_device(): maps[side] = lax.dynamic_update_slice(maps[side], piece, (at, 0))  3.71 us
  transfers between devices with their start and end apart: 25, of which 4 were waited for; matrix products, arithmetic and copies ran while one was open for 18% of the time, Pallas kernels for 7%

profile of v1, /device:TPU:0, one launch (start us, length us, event | category | flops | bytes accessed | tf_op | source)
XLA Modules:
  0.0 122.5 jit_solution(7266309046933039149)
XLA Ops:
  0.6 1.7 %slice_bitcast_fusion = (bf16[256,1024]{1,0:T(8,128)(2,1)S(1)}, bf16[256,1024]{1,0:T(8,128)(2,1)S(1)}, bf16[256,1024]{1,0:T(8,128)(2,1)S(1)}, bf16[256,1024]{1,0:T(8,128)(2,1)S(1)}) fusion(bf16[1,1024,1024]{2,1,0:T(8,128)(2,1)} %param.5), kind=kLoop, calls=%fused_computation.71 | loop fusion | bytes 4194304 | tf_op jit(solution)/shard_map/slice | solution.py:139
  2.3 1.3 %collective-permute-start.2 = (bf16[256,1024]{1,0:T(8,128)(2,1)S(1)}, bf16[256,1024]{1,0:T(8,128)(2,1)S(1)}, u32[]{:S(2)}, u32[]{:S(2)}) collective-permute-start(bf16[256,1024]{1,0:T(8,128)(2,1)S(1)} %get-tuple-element.11.refs_2_), channel_id=1, source_target_pairs={{1,0},{3,2},{5,4},{7,6},{9,8},{11,10},{13,12},{15,14},{17,16},{19,... | collective-permute-start | bytes 1572872 | tf_op jit(solution)/shard_map/ppermute | solution.py:108
  3.6 1.3 %collective-permute-start.1 = (bf16[256,1024]{1,0:T(8,128)(2,1)S(1)}, bf16[256,1024]{1,0:T(8,128)(2,1)}, u32[]{:S(2)}, u32[]{:S(2)}) collective-permute-start(bf16[256,1024]{1,0:T(8,128)(2,1)S(1)} %get-tuple-element.12.refs_2_), channel_id=1, source_target_pairs={{1,0},{3,2},{5,4},{7,6},{9,8},{11,10},{13,12},{15,14},{17,16},{19,... | collective-permute-start | bytes 1572872 | tf_op jit(solution)/shard_map/ppermute | solution.py:108
  4.9 1.3 %collective-permute-start.5 = (bf16[256,1024]{1,0:T(8,128)(2,1)S(1)}, bf16[256,1024]{1,0:T(8,128)(2,1)}, u32[]{:S(2)}, u32[]{:S(2)}) collective-permute-start(bf16[256,1024]{1,0:T(8,128)(2,1)S(1)} %get-tuple-element.13.refs_2_), channel_id=1, source_target_pairs={{1,0},{3,2},{5,4},{7,6},{9,8},{11,10},{13,12},{15,14},{17,16},{19,... | collective-permute-start | bytes 1572872 | tf_op jit(solution)/shard_map/ppermute | solution.py:108
  6.3 1.3 %collective-permute-start = (s32[8,8]{1,0:T(8,128)S(1)}, s32[8,8]{1,0:T(8,128)S(1)}, u32[]{:S(2)}, u32[]{:S(2)}) collective-permute-start(s32[8,8]{1,0:T(8,128)S(1)} %bitcast.49), channel_id=1, source_target_pairs={{1,0},{3,2},{5,4},{7,6},{9,8},{11,10},{13,12},{15,14},{17,16},{19,... | collective-permute-start | bytes 776 | tf_op jit(solution)/shard_map/ppermute | solution.py:108
  7.6 1.2 convert_element_type.78
  8.8 2.1 %collective-permute-done.refs_1_ = s32[8,8]{1,0:T(8,128)S(1)} collective-permute-done((s32[8,8]{1,0:T(8,128)S(1)}, s32[8,8]{1,0:T(8,128)S(1)}, u32[]{:S(2)}, u32[]{:S(2)}) %collective-permute-start) | collective-permute-done | bytes 288 | tf_op jit(solution)/shard_map/ppermute | solution.py:108
  10.9 0.8 copy-done
  11.7 1.0 copy-done.1
  12.8 1.1 shard_map.68
  13.9 1.5 %shard_map.69.refs_0_ = bf16[256,1024]{1,0:T(8,128)(2,1)S(1)} custom-call(s32[8,8]{1,0:T(8,128)S(1)} %bitcast.51, s32[8,8]{1,0:T(8,128)S(1)} %collective-permute-done.refs_1_, bf16[256,1024]{1,0:T(8,128)(2,1)S(1)} %get-tuple-element.12.refs_2_, bf16[256,1024]{1,0:T(8,128)(2,1)} %collective-permute-done.1.refs_3_, ...), custom_call_target="tpu_custom_call" | custom-call | flops 167772160 | bytes 1572864 | tf_op jit(solution)/shard_map/pallas_call | solution.py:65
  15.4 4.9 %collective-permute-start.3 = (bf16[256,1024]{1,0:T(8,128)(2,1)S(1)}, bf16[256,1024]{1,0:T(8,128)(2,1)}, u32[]{:S(2)}, u32[]{:S(2)}) collective-permute-start(bf16[256,1024]{1,0:T(8,128)(2,1)S(1)} %shard_map.69.refs_0_), channel_id=1, source_target_pairs={{0,2},{2,0},{4,6},{6,4},{8,10},{10,8},{12,14},{14,12},{16,18},{18,... | collective-permute-start | bytes 1572872 | tf_op jit(solution)/shard_map/ppermute | solution.py:108
  20.3 1.3 %collective-permute-start.7 = (bf16[256,1024]{1,0:T(8,128)(2,1)S(1)}, bf16[256,1024]{1,0:T(8,128)(2,1)S(1)}, u32[]{:S(2)}, u32[]{:S(2)}) collective-permute-start(bf16[256,1024]{1,0:T(8,128)(2,1)S(1)} %get-tuple-element.10.refs_2_), channel_id=1, source_target_pairs={{1,0},{3,2},{5,4},{7,6},{9,8},{11,10},{13,12},{15,14},{17,16},{19,... | collective-permute-start | bytes 1572872 | tf_op jit(solution)/shard_map/ppermute | solution.py:108
  21.6 3.4 %collective-permute-start.13 = (s32[1,1024]{1,0:T(1,128)S(1)}, s32[1,1024]{1,0:T(1,128)S(1)}, u32[]{:S(2)}, u32[]{:S(2)}) collective-permute-start(s32[1,1024]{1,0:T(1,128)S(1)} %copy-done.5), channel_id=1, source_target_pairs={{0,4},{2,6},{4,0},{6,2},{8,12},{10,14},{12,8},{14,10},{16,20},{18,... | collective-permute-start | bytes 12296 | tf_op jit(solution)/shard_map/ppermute | solution.py:108
  25.0 5.2 %all-gather = f32[1,16,1024]{2,0,1:T(1,128)S(1)} all-gather(f32[1,4,1024]{2,0,1:T(1,128)S(1)} %copy.7), channel_id=2, replica_groups=mesh['layer'=8,'box'=4] {'box'}, dimensions={1}, use_global_device_ids=true | all-gather | bytes 81920 | tf_op jit(solution)/shard_map/all_gather | solution.py:164
  30.3 2.4 %collective-permute-start.11 = (f32[16,1024]{1,0:T(8,128)S(1)}, f32[16,1024]{1,0:T(8,128)}, u32[]{:S(2)}, u32[]{:S(2)}) collective-permute-start(f32[16,1024]{1,0:T(8,128)S(1)} %bitcast.54), channel_id=1, source_target_pairs={{0,4},{2,6},{4,0},{6,2},{8,12},{10,14},{12,8},{14,10},{16,20},{18,... | collective-permute-start | bytes 196616 | tf_op jit(solution)/shard_map/ppermute | solution.py:108
  32.8 3.2 %collective-permute-start.4 = (bf16[256,1024]{1,0:T(8,128)(2,1)S(1)}, bf16[256,1024]{1,0:T(8,128)(2,1)S(1)}, u32[]{:S(2)}, u32[]{:S(2)}) collective-permute-start(bf16[256,1024]{1,0:T(8,128)(2,1)S(1)} %get-tuple-element.8.refs_0_), channel_id=1, source_target_pairs={{0,2},{2,0},{4,6},{6,4},{8,10},{10,8},{12,14},{14,12},{16,18},{18,... | collective-permute-start | bytes 1572872 | tf_op jit(solution)/shard_map/ppermute | solution.py:108
  36.0 1.5 %shard_map.72.refs_0_ = bf16[256,1024]{1,0:T(8,128)(2,1)S(1)} custom-call(s32[8,8]{1,0:T(8,128)S(1)} %bitcast.52, s32[8,8]{1,0:T(8,128)S(1)} %collective-permute-done.refs_1_, bf16[256,1024]{1,0:T(8,128)(2,1)S(1)} %get-tuple-element.13.refs_2_, bf16[256,1024]{1,0:T(8,128)(2,1)} %collective-permute-done.5.refs_3_, ...), custom_call_target="tpu_custom_call" | custom-call | flops 167772160 | bytes 1572864 | tf_op jit(solution)/shard_map/pallas_call | solution.py:65
  37.5 2.6 %collective-permute-start.6 = (bf16[256,1024]{1,0:T(8,128)(2,1)S(1)}, bf16[256,1024]{1,0:T(8,128)(2,1)S(1)}, u32[]{:S(2)}, u32[]{:S(2)}) collective-permute-start(bf16[256,1024]{1,0:T(8,128)(2,1)S(1)} %shard_map.72.refs_0_), channel_id=1, source_target_pairs={{0,2},{2,0},{4,6},{6,4},{8,10},{10,8},{12,14},{14,12},{16,18},{18,... | collective-permute-start | bytes 1572872 | tf_op jit(solution)/shard_map/ppermute | solution.py:108
  40.2 1.5 %shard_map.70 = (bf16[256,1024]{1,0:T(8,128)(2,1)S(1)}, bf16[256,1024]{1,0:T(8,128)(2,1)S(1)}) custom-call(bf16[256,1024]{1,0:T(8,128)(2,1)S(1)} %shard_map.69.refs_0_, bf16[256,1024]{1,0:T(8,128)(2,1)} %collective-permute-done.3.refs_1_, bf16[256,256]{1,0:T(8,128)(2,1)S(1)} %get-tuple-element.28.refs_2_), custom_call_target="tpu_custom_call" | custom-call | flops 167772160 | bytes 1572864 | tf_op jit(solution)/shard_map/pallas_call | solution.py:65
  41.7 3.4 %collective-permute-start.12 = (bf16[256,1024]{1,0:T(8,128)(2,1)S(1)}, bf16[256,1024]{1,0:T(8,128)(2,1)S(1)}, u32[]{:S(2)}, u32[]{:S(2)}) collective-permute-start(bf16[256,1024]{1,0:T(8,128)(2,1)S(1)} %get-tuple-element.7), channel_id=1, source_target_pairs={{0,4},{2,6},{4,0},{6,2},{8,12},{10,14},{12,8},{14,10},{16,20},{18,... | collective-permute-start | bytes 1572872 | tf_op jit(solution)/shard_map/ppermute | solution.py:108
  45.1 1.1 shard_map.74
  46.2 2.4 %collective-permute-start.8 = (bf16[128,1024]{1,0:T(8,128)(2,1)S(1)}, bf16[128,1024]{1,0:T(8,128)(2,1)S(1)}, u32[]{:S(2)}, u32[]{:S(2)}) collective-permute-start(bf16[128,1024]{1,0:T(8,128)(2,1)S(1)} %get-tuple-element.27.refs_0_), channel_id=1, source_target_pairs={{0,2},{2,0},{4,6},{6,4},{8,10},{10,8},{12,14},{14,12},{16,18},{18,... | collective-permute-start | bytes 786440 | tf_op jit(solution)/shard_map/ppermute | solution.py:108
  48.7 3.4 %collective-permute-start.9 = (bf16[128,1024]{1,0:T(8,128)(2,1)S(1)}, bf16[128,1024]{1,0:T(8,128)(2,1)S(1)}, u32[]{:S(2)}, u32[]{:S(2)}) collective-permute-start(bf16[128,1024]{1,0:T(8,128)(2,1)S(1)} %get-tuple-element.26.refs_0_), channel_id=1, source_target_pairs={{0,2},{2,0},{4,6},{6,4},{8,10},{10,8},{12,14},{14,12},{16,18},{18,... | collective-permute-start | bytes 786440 | tf_op jit(solution)/shard_map/ppermute | solution.py:108
  52.1 0.9 broadcast_select_fusion.18
  53.4 2.4 %collective-permute-start.14 = (bf16[256,1024]{1,0:T(8,128)(2,1)S(1)}, bf16[256,1024]{1,0:T(8,128)(2,1)S(1)}, u32[]{:S(2)}, u32[]{:S(2)}) collective-permute-start(bf16[256,1024]{1,0:T(8,128)(2,1)S(1)} %shard_map.71), channel_id=1, source_target_pairs={{0,4},{2,6},{4,0},{6,2},{8,12},{10,14},{12,8},{14,10},{16,20},{18,... | collective-permute-start | bytes 1572872 | tf_op jit(solution)/shard_map/ppermute | solution.py:108
  56.3 3.4 %collective-permute-start.15 = (bf16[256,1024]{1,0:T(8,128)(2,1)S(1)}, bf16[256,1024]{1,0:T(8,128)(2,1)S(1)}, u32[]{:S(2)}, u32[]{:S(2)}) collective-permute-start(bf16[256,1024]{1,0:T(8,128)(2,1)S(1)} %shard_map.73), channel_id=1, source_target_pairs={{0,4},{2,6},{4,0},{6,2},{8,12},{10,14},{12,8},{14,10},{16,20},{18,... | collective-permute-start | bytes 1572872 | tf_op jit(solution)/shard_map/ppermute | solution.py:108
  60.1 2.4 %collective-permute-start.16 = (bf16[128,1024]{1,0:T(8,128)(2,1)S(1)}, bf16[128,1024]{1,0:T(8,128)(2,1)S(1)}, u32[]{:S(2)}, u32[]{:S(2)}) collective-permute-start(bf16[128,1024]{1,0:T(8,128)(2,1)S(1)} %shard_map.75), channel_id=1, source_target_pairs={{0,4},{2,6},{4,0},{6,2},{8,12},{10,14},{12,8},{14,10},{16,20},{18,... | collective-permute-start | bytes 786440 | tf_op jit(solution)/shard_map/ppermute | solution.py:108
  63.0 3.6 %collective-permute-start.17 = (bf16[128,1024]{1,0:T(8,128)(2,1)S(1)}, bf16[128,1024]{1,0:T(8,128)(2,1)S(1)}, u32[]{:S(2)}, u32[]{:S(2)}) collective-permute-start(bf16[128,1024]{1,0:T(8,128)(2,1)S(1)} %shard_map.76), channel_id=1, source_target_pairs={{0,4},{2,6},{4,0},{6,2},{8,12},{10,14},{12,8},{14,10},{16,20},{18,... | collective-permute-start | bytes 786440 | tf_op jit(solution)/shard_map/ppermute | solution.py:108
  66.6 1.6 %dynamic_update_slice.75 = bf16[1024,1024]{1,0:T(8,128)(2,1)} pad(bf16[256,1024]{1,0:T(8,128)(2,1)S(1)} %get-tuple-element.7, bf16[]{:T(256)} %constant.67.clone.1), padding=256_512x0_0 | pad | bytes 2621442 | tf_op jit(solution)/shard_map/dynamic_update_slice | solution.py:181
  68.2 1.0 fusion.20
  69.5 1.0 fusion.29
  70.6 1.0 fusion.28
  71.6 1.0 fusion.23
  73.4 1.0 fusion.31
  74.5 1.3 %collective-permute-done.17 = bf16[128,1024]{1,0:T(8,128)(2,1)S(1)} collective-permute-done((bf16[128,1024]{1,0:T(8,128)(2,1)S(1)}, bf16[128,1024]{1,0:T(8,128)(2,1)S(1)}, u32[]{:S(2)}, u32[]{:S(2)}) %collective-permute-start.17) | collective-permute-done | bytes 262176 | tf_op jit(solution)/shard_map/ppermute | solution.py:108
  75.7 1.0 fusion.33
  76.8 0.6 fusion.73
  77.4 3.5 %collective-permute-start.18 = (bf16[16,1024]{1,0:T(8,128)(2,1)S(1)}, bf16[16,1024]{1,0:T(8,128)(2,1)S(1)}, u32[]{:S(2)}, u32[]{:S(2)}) collective-permute-start(bf16[16,1024]{1,0:T(8,128)(2,1)S(1)} %get-tuple-element.36), channel_id=1, source_target_pairs={{0,8},{2,10},{4,12},{6,14}} | collective-permute-start | bytes 98312 | tf_op jit(solution)/shard_map/ppermute | solution.py:108
  80.9 1.0 fusion.27
  82.0 1.0 fusion.26
  83.0 1.0 fusion.35
  84.0 1.1 fusion.54
  85.1 1.0 fusion.55
  86.1 1.0 fusion.37
  87.2 0.6 fusion.50
  87.8 0.7 fusion.74
  88.5 0.9 collective-permute-start.19
  89.4 0.8 fusion.58
  90.2 0.6 fusion.48
  90.8 0.7 fusion.75
  91.5 0.7 collective-permute-start.20
  92.2 0.8 fusion.59
  93.0 0.7 select_select_fusion.1
  93.6 0.7 fusion.52
  94.7 0.7 collective-permute-start.21
  95.4 2.6 %collective-permute-start.10 = (bf16[1024,1024]{1,0:T(8,128)(2,1)}, bf16[1024,1024]{1,0:T(8,128)(2,1)}, u32[]{:S(2)}, u32[]{:S(2)}) collective-permute-start(bf16[1024,1024]{1,0:T(8,128)(2,1)} %get-tuple-element.30), channel_id=1, source_target_pairs={{0,1},{2,3},{4,5},{6,7},{8,9},{10,11},{12,13},{14,15},{16,17},{18,... | collective-permute-start | bytes 6291464 | tf_op jit(solution)/shard_map/ppermute | solution.py:108
  98.8 0.7 collective-permute-start.22
  100.2 1.3 %collective-permute-start.23 = (bf16[16,1024]{1,0:T(8,128)(2,1)S(1)}, bf16[16,1024]{1,0:T(8,128)(2,1)S(1)}, u32[]{:S(2)}, u32[]{:S(2)}) collective-permute-start(bf16[16,1024]{1,0:T(8,128)(2,1)S(1)} %get-tuple-element.48), channel_id=1, source_target_pairs={{8,0},{10,2},{12,4},{14,6}} | collective-permute-start | bytes 98312 | tf_op jit(solution)/shard_map/ppermute | solution.py:108
  101.5 12.7 %collective-permute-done.23 = bf16[16,1024]{1,0:T(8,128)(2,1)S(1)} collective-permute-done((bf16[16,1024]{1,0:T(8,128)(2,1)S(1)}, bf16[16,1024]{1,0:T(8,128)(2,1)S(1)}, u32[]{:S(2)}, u32[]{:S(2)}) %collective-permute-start.23) | collective-permute-done | bytes 32800 | tf_op jit(solution)/shard_map/ppermute | solution.py:108
  114.2 2.0 %fusion.39 = f32[16,1024]{1,0:T(8,128)S(1)} fusion(f32[16,1024]{1,0:T(8,128)S(1)} %fusion.52, bf16[16,1024]{1,0:T(8,128)(2,1)S(1)} %collective-permute-done.23, bf16[1024,1024]{1,0:T(8,128)(2,1)} %copy-done.3), kind=kOutput, calls=%fused_computation.44 | convolution fusion | flops 33587200 | bytes 2260992 | tf_op jit(solution)/shard_map/dot_general | solution.py:81
  116.6 1.3 %collective-permute-start.24 = (f32[4,1024]{1,0:T(4,128)S(1)}, f32[4,1024]{1,0:T(4,128)S(1)}, u32[]{:S(2)}, u32[]{:S(2)}) collective-permute-start(f32[4,1024]{1,0:T(4,128)S(1)} %constant_dynamic-slice_fusion), channel_id=1, source_target_pairs={{0,1},{2,3},{4,5},{6,7},{8,9},{10,11},{12,13},{14,15},{16,17},{18,... | collective-permute-start | bytes 49160 | tf_op jit(solution)/shard_map/ppermute | solution.py:108
  117.9 0.8 collective-permute-done.24
  119.3 3.1 %select_bitcast_fusion = bf16[1,1024,1024]{2,1,0:T(8,128)(2,1)} fusion(bf16[1024,1024]{1,0:T(8,128)(2,1)} %get-tuple-element.30, bf16[1024,1024]{1,0:T(8,128)(2,1)} %collective-permute-done.10, pred[]{:T(512)S(6)} %eq.53), kind=kLoop, calls=%fused_computation.22 | loop fusion | flops 1048576 | bytes 6291457 | tf_op jit(solution)/shard_map/broadcast_in_dim | solution.py:230
  (53 shorter events, 5.9 us)
Async XLA Ops:
  0.6 5.6 %copy-start.2 = (s32[1,8,8]{2,1,0:T(8,128)S(1)}, s32[1,8,8]{2,1,0:T(8,128)}, u32[]{:S(2)}) copy-start(s32[1,8,8]{2,1,0:T(8,128)} %param.6) | copy-start | bytes 772
  2.3 8.6 %collective-permute-start.2 = (bf16[256,1024]{1,0:T(8,128)(2,1)S(1)}, bf16[256,1024]{1,0:T(8,128)(2,1)S(1)}, u32[]{:S(2)}, u32[]{:S(2)}) collective-permute-start(bf16[256,1024]{1,0:T(8,128)(2,1)S(1)} %get-tuple-element.11.refs_2_), channel_id=1, source_target_pairs={{1,0},{3,2},{5,4},{7,6},{9,8},{11,10},{13,12},{15,14},{17,16},{19,... | collective-permute-start | bytes 1572872 | tf_op jit(solution)/shard_map/ppermute | solution.py:108
  3.6 10.3 %collective-permute-start.1 = (bf16[256,1024]{1,0:T(8,128)(2,1)S(1)}, bf16[256,1024]{1,0:T(8,128)(2,1)}, u32[]{:S(2)}, u32[]{:S(2)}) collective-permute-start(bf16[256,1024]{1,0:T(8,128)(2,1)S(1)} %get-tuple-element.12.refs_2_), channel_id=1, source_target_pairs={{1,0},{3,2},{5,4},{7,6},{9,8},{11,10},{13,12},{15,14},{17,16},{19,... | collective-permute-start | bytes 1572872 | tf_op jit(solution)/shard_map/ppermute | solution.py:108
  4.9 27.8 %collective-permute-start.5 = (bf16[256,1024]{1,0:T(8,128)(2,1)S(1)}, bf16[256,1024]{1,0:T(8,128)(2,1)}, u32[]{:S(2)}, u32[]{:S(2)}) collective-permute-start(bf16[256,1024]{1,0:T(8,128)(2,1)S(1)} %get-tuple-element.13.refs_2_), channel_id=1, source_target_pairs={{1,0},{3,2},{5,4},{7,6},{9,8},{11,10},{13,12},{15,14},{17,16},{19,... | collective-permute-start | bytes 1572872 | tf_op jit(solution)/shard_map/ppermute | solution.py:108
  6.3 4.7 %collective-permute-start = (s32[8,8]{1,0:T(8,128)S(1)}, s32[8,8]{1,0:T(8,128)S(1)}, u32[]{:S(2)}, u32[]{:S(2)}) collective-permute-start(s32[8,8]{1,0:T(8,128)S(1)} %bitcast.49), channel_id=1, source_target_pairs={{1,0},{3,2},{5,4},{7,6},{9,8},{11,10},{13,12},{15,14},{17,16},{19,... | collective-permute-start | bytes 776 | tf_op jit(solution)/shard_map/ppermute | solution.py:108
  8.7 12.8 %copy-start.5 = (s32[1,1024]{1,0:T(1,128)S(1)}, s32[1,1024]{1,0:T(1,128)}, u32[]{:S(2)}) copy-start(s32[1,1024]{1,0:T(1,128)} %param.8) | copy-start | bytes 12292
  8.8 16.2 %copy-start.4 = (f32[1,4,1024]{2,1,0:T(4,128)S(1)}, f32[1,4,1024]{2,1,0:T(4,128)}, u32[]{:S(2)}) copy-start(f32[1,4,1024]{2,1,0:T(4,128)} %param.9) | copy-start | bytes 49156
  10.9 0.8 copy-start
  11.7 1.0 copy-start.1
  15.4 24.8 %collective-permute-start.3 = (bf16[256,1024]{1,0:T(8,128)(2,1)S(1)}, bf16[256,1024]{1,0:T(8,128)(2,1)}, u32[]{:S(2)}, u32[]{:S(2)}) collective-permute-start(bf16[256,1024]{1,0:T(8,128)(2,1)S(1)} %shard_map.69.refs_0_), channel_id=1, source_target_pairs={{0,2},{2,0},{4,6},{6,4},{8,10},{10,8},{12,14},{14,12},{16,18},{18,... | collective-permute-start | bytes 1572872 | tf_op jit(solution)/shard_map/ppermute | solution.py:108
  20.3 24.8 %collective-permute-start.7 = (bf16[256,1024]{1,0:T(8,128)(2,1)S(1)}, bf16[256,1024]{1,0:T(8,128)(2,1)S(1)}, u32[]{:S(2)}, u32[]{:S(2)}) collective-permute-start(bf16[256,1024]{1,0:T(8,128)(2,1)S(1)} %get-tuple-element.10.refs_2_), channel_id=1, source_target_pairs={{1,0},{3,2},{5,4},{7,6},{9,8},{11,10},{13,12},{15,14},{17,16},{19,... | collective-permute-start | bytes 1572872 | tf_op jit(solution)/shard_map/ppermute | solution.py:108
  21.6 15.9 %collective-permute-start.13 = (s32[1,1024]{1,0:T(1,128)S(1)}, s32[1,1024]{1,0:T(1,128)S(1)}, u32[]{:S(2)}, u32[]{:S(2)}) collective-permute-start(s32[1,1024]{1,0:T(1,128)S(1)} %copy-done.5), channel_id=1, source_target_pairs={{0,4},{2,6},{4,0},{6,2},{8,12},{10,14},{12,8},{14,10},{16,20},{18,... | collective-permute-start | bytes 12296 | tf_op jit(solution)/shard_map/ppermute | solution.py:108
  30.3 18.4 %collective-permute-start.11 = (f32[16,1024]{1,0:T(8,128)S(1)}, f32[16,1024]{1,0:T(8,128)}, u32[]{:S(2)}, u32[]{:S(2)}) collective-permute-start(f32[16,1024]{1,0:T(8,128)S(1)} %bitcast.54), channel_id=1, source_target_pairs={{0,4},{2,6},{4,0},{6,2},{8,12},{10,14},{12,8},{14,10},{16,20},{18,... | collective-permute-start | bytes 196616 | tf_op jit(solution)/shard_map/ppermute | solution.py:108
  32.8 20.2 %collective-permute-start.4 = (bf16[256,1024]{1,0:T(8,128)(2,1)S(1)}, bf16[256,1024]{1,0:T(8,128)(2,1)S(1)}, u32[]{:S(2)}, u32[]{:S(2)}) collective-permute-start(bf16[256,1024]{1,0:T(8,128)(2,1)S(1)} %get-tuple-element.8.refs_0_), channel_id=1, source_target_pairs={{0,2},{2,0},{4,6},{6,4},{8,10},{10,8},{12,14},{14,12},{16,18},{18,... | collective-permute-start | bytes 1572872 | tf_op jit(solution)/shard_map/ppermute | solution.py:108
  37.5 18.4 %collective-permute-start.6 = (bf16[256,1024]{1,0:T(8,128)(2,1)S(1)}, bf16[256,1024]{1,0:T(8,128)(2,1)S(1)}, u32[]{:S(2)}, u32[]{:S(2)}) collective-permute-start(bf16[256,1024]{1,0:T(8,128)(2,1)S(1)} %shard_map.72.refs_0_), channel_id=1, source_target_pairs={{0,2},{2,0},{4,6},{6,4},{8,10},{10,8},{12,14},{14,12},{16,18},{18,... | collective-permute-start | bytes 1572872 | tf_op jit(solution)/shard_map/ppermute | solution.py:108
  41.7 26.5 %collective-permute-start.12 = (bf16[256,1024]{1,0:T(8,128)(2,1)S(1)}, bf16[256,1024]{1,0:T(8,128)(2,1)S(1)}, u32[]{:S(2)}, u32[]{:S(2)}) collective-permute-start(bf16[256,1024]{1,0:T(8,128)(2,1)S(1)} %get-tuple-element.7), channel_id=1, source_target_pairs={{0,4},{2,6},{4,0},{6,2},{8,12},{10,14},{12,8},{14,10},{16,20},{18,... | collective-permute-start | bytes 1572872 | tf_op jit(solution)/shard_map/ppermute | solution.py:108
  46.2 13.5 %collective-permute-start.8 = (bf16[128,1024]{1,0:T(8,128)(2,1)S(1)}, bf16[128,1024]{1,0:T(8,128)(2,1)S(1)}, u32[]{:S(2)}, u32[]{:S(2)}) collective-permute-start(bf16[128,1024]{1,0:T(8,128)(2,1)S(1)} %get-tuple-element.27.refs_0_), channel_id=1, source_target_pairs={{0,2},{2,0},{4,6},{6,4},{8,10},{10,8},{12,14},{14,12},{16,18},{18,... | collective-permute-start | bytes 786440 | tf_op jit(solution)/shard_map/ppermute | solution.py:108
  48.7 13.9 %collective-permute-start.9 = (bf16[128,1024]{1,0:T(8,128)(2,1)S(1)}, bf16[128,1024]{1,0:T(8,128)(2,1)S(1)}, u32[]{:S(2)}, u32[]{:S(2)}) collective-permute-start(bf16[128,1024]{1,0:T(8,128)(2,1)S(1)} %get-tuple-element.26.refs_0_), channel_id=1, source_target_pairs={{0,2},{2,0},{4,6},{6,4},{8,10},{10,8},{12,14},{14,12},{16,18},{18,... | collective-permute-start | bytes 786440 | tf_op jit(solution)/shard_map/ppermute | solution.py:108
  53.4 16.1 %collective-permute-start.14 = (bf16[256,1024]{1,0:T(8,128)(2,1)S(1)}, bf16[256,1024]{1,0:T(8,128)(2,1)S(1)}, u32[]{:S(2)}, u32[]{:S(2)}) collective-permute-start(bf16[256,1024]{1,0:T(8,128)(2,1)S(1)} %shard_map.71), channel_id=1, source_target_pairs={{0,4},{2,6},{4,0},{6,2},{8,12},{10,14},{12,8},{14,10},{16,20},{18,... | collective-permute-start | bytes 1572872 | tf_op jit(solution)/shard_map/ppermute | solution.py:108
  56.3 14.2 %collective-permute-start.15 = (bf16[256,1024]{1,0:T(8,128)(2,1)S(1)}, bf16[256,1024]{1,0:T(8,128)(2,1)S(1)}, u32[]{:S(2)}, u32[]{:S(2)}) collective-permute-start(bf16[256,1024]{1,0:T(8,128)(2,1)S(1)} %shard_map.73), channel_id=1, source_target_pairs={{0,4},{2,6},{4,0},{6,2},{8,12},{10,14},{12,8},{14,10},{16,20},{18,... | collective-permute-start | bytes 1572872 | tf_op jit(solution)/shard_map/ppermute | solution.py:108
  60.1 13.3 %collective-permute-start.16 = (bf16[128,1024]{1,0:T(8,128)(2,1)S(1)}, bf16[128,1024]{1,0:T(8,128)(2,1)S(1)}, u32[]{:S(2)}, u32[]{:S(2)}) collective-permute-start(bf16[128,1024]{1,0:T(8,128)(2,1)S(1)} %shard_map.75), channel_id=1, source_target_pairs={{0,4},{2,6},{4,0},{6,2},{8,12},{10,14},{12,8},{14,10},{16,20},{18,... | collective-permute-start | bytes 786440 | tf_op jit(solution)/shard_map/ppermute | solution.py:108
  63.0 12.8 %collective-permute-start.17 = (bf16[128,1024]{1,0:T(8,128)(2,1)S(1)}, bf16[128,1024]{1,0:T(8,128)(2,1)S(1)}, u32[]{:S(2)}, u32[]{:S(2)}) collective-permute-start(bf16[128,1024]{1,0:T(8,128)(2,1)S(1)} %shard_map.76), channel_id=1, source_target_pairs={{0,4},{2,6},{4,0},{6,2},{8,12},{10,14},{12,8},{14,10},{16,20},{18,... | collective-permute-start | bytes 786440 | tf_op jit(solution)/shard_map/ppermute | solution.py:108
  77.4 9.7 %collective-permute-start.18 = (bf16[16,1024]{1,0:T(8,128)(2,1)S(1)}, bf16[16,1024]{1,0:T(8,128)(2,1)S(1)}, u32[]{:S(2)}, u32[]{:S(2)}) collective-permute-start(bf16[16,1024]{1,0:T(8,128)(2,1)S(1)} %get-tuple-element.36), channel_id=1, source_target_pairs={{0,8},{2,10},{4,12},{6,14}} | collective-permute-start | bytes 98312 | tf_op jit(solution)/shard_map/ppermute | solution.py:108
  88.5 1.7 %collective-permute-start.19 = (bf16[16,1024]{1,0:T(8,128)(2,1)S(1)}, bf16[16,1024]{1,0:T(8,128)(2,1)S(1)}, u32[]{:S(2)}, u32[]{:S(2)}) collective-permute-start(bf16[16,1024]{1,0:T(8,128)(2,1)S(1)} %get-tuple-element.38), channel_id=1, source_target_pairs={{8,16},{10,18},{12,20},{14,22}} | collective-permute-start | bytes 98312 | tf_op jit(solution)/shard_map/ppermute | solution.py:108
  91.5 1.5 %collective-permute-start.20 = (bf16[16,1024]{1,0:T(8,128)(2,1)S(1)}, bf16[16,1024]{1,0:T(8,128)(2,1)S(1)}, u32[]{:S(2)}, u32[]{:S(2)}) collective-permute-start(bf16[16,1024]{1,0:T(8,128)(2,1)S(1)} %get-tuple-element.40), channel_id=1, source_target_pairs={{16,24},{18,26},{20,28},{22,30}} | collective-permute-start | bytes 98312 | tf_op jit(solution)/shard_map/ppermute | solution.py:108
  93.0 6.5 %copy-start.3 = (bf16[1024,1024]{1,0:T(8,128)(2,1)}, bf16[1024,1024]{1,0:T(8,128)(2,1)S(1)}, u32[]{:S(2)}) copy-start(bf16[1024,1024]{1,0:T(8,128)(2,1)S(1)} %get-tuple-element.20) | copy-start | bytes 6291460
  94.7 3.3 %collective-permute-start.21 = (bf16[16,1024]{1,0:T(8,128)(2,1)S(1)}, bf16[16,1024]{1,0:T(8,128)(2,1)S(1)}, u32[]{:S(2)}, u32[]{:S(2)}) collective-permute-start(bf16[16,1024]{1,0:T(8,128)(2,1)S(1)} %get-tuple-element.44), channel_id=1, source_target_pairs={{24,16},{26,18},{28,20},{30,22}} | collective-permute-start | bytes 98312 | tf_op jit(solution)/shard_map/ppermute | solution.py:108
  95.4 24.0 %collective-permute-start.10 = (bf16[1024,1024]{1,0:T(8,128)(2,1)}, bf16[1024,1024]{1,0:T(8,128)(2,1)}, u32[]{:S(2)}, u32[]{:S(2)}) collective-permute-start(bf16[1024,1024]{1,0:T(8,128)(2,1)} %get-tuple-element.30), channel_id=1, source_target_pairs={{0,1},{2,3},{4,5},{6,7},{8,9},{10,11},{12,13},{14,15},{16,17},{18,... | collective-permute-start | bytes 6291464 | tf_op jit(solution)/shard_map/ppermute | solution.py:108
  98.8 0.7 collective-permute-start.22
  100.2 14.0 %collective-permute-start.23 = (bf16[16,1024]{1,0:T(8,128)(2,1)S(1)}, bf16[16,1024]{1,0:T(8,128)(2,1)S(1)}, u32[]{:S(2)}, u32[]{:S(2)}) collective-permute-start(bf16[16,1024]{1,0:T(8,128)(2,1)S(1)} %get-tuple-element.48), channel_id=1, source_target_pairs={{8,0},{10,2},{12,4},{14,6}} | collective-permute-start | bytes 98312 | tf_op jit(solution)/shard_map/ppermute | solution.py:108
  116.6 2.1 %collective-permute-start.24 = (f32[4,1024]{1,0:T(4,128)S(1)}, f32[4,1024]{1,0:T(4,128)S(1)}, u32[]{:S(2)}, u32[]{:S(2)}) collective-permute-start(f32[4,1024]{1,0:T(4,128)S(1)} %constant_dynamic-slice_fusion), channel_id=1, source_target_pairs={{0,1},{2,3},{4,5},{6,7},{8,9},{10,11},{12,13},{14,15},{16,17},{18,... | collective-permute-start | bytes 49160 | tf_op jit(solution)/shard_map/ppermute | solution.py:108

commit v2 on v0

v2 whole, which is shorter than its diff:
```python
import functools

import jax
import jax.numpy as jnp
from jax import lax
from jax.experimental import pallas as pl
from jax.experimental.pallas import tpu as pltpu
from jax.sharding import PartitionSpec as P

AXES = ("layer", "box")
VMEM = pl.BlockSpec(memory_space=pltpu.VMEM)
SMEM = pl.BlockSpec(memory_space=pltpu.SMEM)
PARAMS = pltpu.CompilerParams(vmem_limit_bytes=24 * 1024 * 1024)
OWN, PAIR, EXTRA = 0, 1, 2


def cost(flops, moved):
    return pl.CostEstimate(flops=flops, bytes_accessed=moved, transcendentals=0)


def dot32(a, b):
    return jnp.dot(a, b, preferred_element_type=jnp.float32)


def dot32_t(a, b):
    return lax.dot_general(a, b, (((1,), (1,)), ((), ())), preferred_element_type=jnp.float32)


def minus_face(joined, face_at, inverse, right):
    face = inverse.shape[0]
    left = joined[:, face_at : face_at + face].astype(jnp.bfloat16)
    product = dot32(left, inverse).astype(jnp.bfloat16)
    return (joined - dot32(product, right)).astype(jnp.bfloat16)


def masked_mean(own, other, own_pattern, other_pattern, row_at, row_count, block_at):
    width = own.shape[1]
    block = width // own_pattern.shape[1]
    strips = []
    for r in range(row_count // block):
        tiles = []
        at = slice(row_at + r * block, row_at + (r + 1) * block)
        for c in range(width // block):
            cols = slice(c * block, (c + 1) * block)
            keep_own = 0.5 * own_pattern[block_at + r, c].astype(jnp.float32)
            keep_other = 0.5 * other_pattern[block_at + r, c].astype(jnp.float32)
            tiles.append(
                own[at, cols].astype(jnp.float32) * keep_own
                + other[at, cols].astype(jnp.float32) * keep_other
            )
        strips.append(jnp.concatenate(tiles, axis=1))
    return jnp.concatenate(strips, axis=0)


def leaf_kernel(first_row, is_face, own_pattern, other_pattern, own, other, inverse, *refs):
    refs = list(refs)
    face = inverse.shape[0]
    right = None if is_face else refs.pop(0)[...]
    block = own.shape[1] // own_pattern.shape[1]
    for i in range(own.shape[0] // face):
        joined = masked_mean(
            own, other, own_pattern, other_pattern, i * face, face, (first_row + i * face) // block
        )
        if right is None:
            right = joined.astype(jnp.bfloat16)
            refs[-1][...] = right
        refs[i][...] = minus_face(joined, 0, inverse[...], right)


def leaf_combine(own_pattern, other_pattern, own, other, inverse, face_rows, half):
    is_face = face_rows is None
    width = own.shape[1]
    rows = own.shape[0] // 2
    face = inverse.shape[0]
    count = rows // face
    piece = jax.ShapeDtypeStruct((face, width), jnp.bfloat16)
    map_spec = pl.BlockSpec((rows, width), lambda i: (half, 0))
    extra = [] if is_face else [face_rows]
    results = pl.pallas_call(
        functools.partial(leaf_kernel, half * rows, is_face),
        grid=(1,),
        out_shape=[piece] * (count + (1 if is_face else 0)),
        in_specs=[SMEM, SMEM, map_spec, map_spec, VMEM] + [VMEM] * len(extra),
        out_specs=[VMEM] * (count + (1 if is_face else 0)),
        compiler_params=PARAMS,
        cost_estimate=cost(2 * rows * face * (width + face), 6 * rows * width),
    )(own_pattern, other_pattern, own, other, inverse, *extra)
    return results


def combine_kernel(face_at, is_face, own, other, inverse, *refs):
    joined = 0.5 * (own[...].astype(jnp.float32) + other[...].astype(jnp.float32))
    if is_face:
        right = joined.astype(jnp.bfloat16)
        refs[1][...] = right
        refs[0][...] = minus_face(joined, face_at, inverse[...], right)
    else:
        refs[1][...] = minus_face(joined, face_at, inverse[...], refs[0][...])


def combine(own, other, inverse, face_rows, face_at):
    is_face = face_rows is None
    rows, width = own.shape
    extra = [] if is_face else [face_rows]
    shape = jax.ShapeDtypeStruct((rows, width), jnp.bfloat16)
    result = pl.pallas_call(
        functools.partial(combine_kernel, face_at, is_face),
        out_shape=[shape] * (2 if is_face else 1),
        in_specs=[VMEM] * (3 + len(extra)),
        out_specs=[VMEM] * (2 if is_face else 1),
        compiler_params=PARAMS,
        cost_estimate=cost(2 * rows * inverse.shape[0] * (width + inverse.shape[0]), 6 * rows * width),
    )(own, other, inverse, *extra)
    return (result[0], result[1]) if is_face else (result[0], face_rows)


def spread(pieces, rows):
    return jnp.concatenate([dot32_t(rows, piece[...]) for piece in pieces], axis=1)


def gather_sum(pieces, rows):
    at, total = 0, None
    for piece in pieces:
        size = piece.shape[0]
        term = dot32(rows[:, at : at + size], piece[...])
        total = term if total is None else total + term
        at += size
    return total


def segment_kernel(coupling, pieces_each, down_steps, up_steps, *refs):
    refs = list(refs)
    state = refs.pop(0)[...]
    maps, downs = {}, {}
    operands = []
    for slot in down_steps:
        operands.append((refs.pop(0), refs.pop(0)))
        maps[slot] = [refs.pop(0) for _ in range(pieces_each)]
    for slot in up_steps:
        if slot not in down_steps:
            downs[slot] = refs.pop(0)[...]
            maps[slot] = [refs.pop(0) for _ in range(pieces_each)]
    for slot, (source, one_hot) in zip(down_steps, operands):
        moved = dot32(state, one_hot[...]).astype(jnp.bfloat16)
        downs[slot] = source[...] + coupling * spread(maps[slot], moved)
        state = downs[slot].astype(jnp.bfloat16)
        refs.pop(0)[...] = downs[slot]
    for slot in up_steps:
        value = downs[slot] + coupling * gather_sum(maps[slot], state)
        state = value.astype(jnp.bfloat16)
        refs.pop(0)[...] = value
    refs.pop(0)[...] = state


def segment(coupling, arrived, sources, one_hots, downs, maps, down_steps, up_steps):
    operands = [arrived]
    for slot in down_steps:
        operands += [sources[slot], one_hots[slot], *maps[slot]]
    for slot in up_steps:
        if slot not in down_steps:
            operands += [downs[slot], *maps[slot]]
    rows = jax.ShapeDtypeStruct(arrived.shape, jnp.float32)
    steps = len(down_steps) + len(up_steps)
    results = pl.pallas_call(
        functools.partial(segment_kernel, coupling, len(maps[OWN]), down_steps, up_steps),
        out_shape=[rows] * steps + [jax.ShapeDtypeStruct(arrived.shape, jnp.bfloat16)],
        in_specs=[VMEM] * len(operands),
        out_specs=[VMEM] * (steps + 1),
        compiler_params=PARAMS,
        cost_estimate=cost(steps * 2 * 256 * 1024 * 1024, steps * 2 * 1024 * 1024),
    )(*operands)
    return results[:-1], results[-1]


def last_kernel(coupling, count, odd, from_pair, from_own, source, down_odd, *refs):
    own, pair, out = refs[:count], refs[count : 2 * count], refs[2 * count]
    total = gather_sum(pair, from_pair[...]) + gather_sum(own, from_own[...])
    up_odd = down_odd[...] + coupling * total
    up_even = source[...] + coupling * gather_sum(own, up_odd.astype(jnp.bfloat16))
    out[...] = jnp.where(odd[0] == 1, up_odd, up_even)


def on_device(box_maps, block_pattern, face_inverses, index_map, sources):
    boxes = lax.axis_size("box")
    layers = lax.axis_size("layer")
    coupling = float(boxes) ** 0.5
    levels = boxes.bit_length() - 1
    face = face_inverses.shape[2]
    width = box_maps.shape[2]
    rows_here = sources.shape[1]
    position = lax.axis_index("box")
    layer = lax.axis_index("layer")
    is_lead = position % 2 == 0
    pairs = layers // 2
    leads = range(0, boxes, 2)

    chain = []
    for p in range(1, pairs, 3):
        chain.append((2 * p, (OWN, PAIR, EXTRA)))
        chain.append((2 * (p + 2) + 1, (EXTRA, PAIR, OWN)))

    def route(moves, source_core=0, target_core=0):
        return [
            (a * boxes + b + source_core, z * boxes + b + target_core)
            for a, z in moves
            for b in leads
        ]

    def send(value, pairs_of_devices):
        return lax.ppermute(value, AXES, pairs_of_devices)

    every = [(i, i) for i in range(layers)]
    pair_moves = [(at ^ 1, at) for at, _ in chain]
    extra_moves = [(at + 2 if at % 2 == 0 else at - 2, at) for at, _ in chain]
    everywhere = [
        (i * boxes + b, i * boxes + (b ^ 1)) for i in range(layers) for b in range(boxes)
    ]

    raw = box_maps[0]
    pattern = block_pattern[0]
    raw_other = send(raw, everywhere)
    pattern_other = send(pattern, everywhere)
    next_sources = send(sources[0], route(every, 1, 0))

    def inverse_of(level):
        node = (boxes >> (level + 1)) - 1 + (position >> (level + 1))
        return lax.dynamic_index_in_dim(face_inverses[0], node, 0, keepdims=False).astype(
            jnp.bfloat16
        )

    inverse = inverse_of(0)
    half = width // 2 // face
    top = leaf_combine(pattern, pattern_other, raw, raw_other, inverse, None, 0)
    bottom = leaf_combine(pattern, pattern_other, raw, raw_other, inverse, top[-1], 1)
    current = list(top[:half]) + list(bottom)

    count = width // face
    order = list(range(count))
    for level in range(1, levels):
        mask = 1 << level
        if level == levels - 1:
            moves = [
                (i * boxes + b, i * boxes + (b ^ mask ^ 1)) for i in range(layers) for b in leads
            ]
        else:
            moves = [
                (i * boxes + b, i * boxes + (b ^ mask)) for i in range(layers) for b in range(boxes)
            ]
        inverse = inverse_of(level)
        order = [level] + [j for j in range(count) if j != level]
        received = {j: send(current[j], moves) for j in order}
        face_rows = None
        renewed = [None] * count
        for j in order:
            renewed[j], face_rows = combine(
                current[j], received[j], inverse, face_rows, level * face
            )
        before, current = current, renewed

    packed = jnp.concatenate(
        [sources[0], next_sources, index_map.astype(jnp.float32)], axis=0
    )
    packed, _ = lax.optimization_barrier((packed, before[count - 1]))
    small = [
        packed,
        send(packed, route(pair_moves + [(0, 1)])),
        send(packed, route(extra_moves)),
    ]
    place = lax.broadcasted_iota(jnp.int32, (width, width), 0)
    row_sources = [entry[: 2 * rows_here] for entry in small]
    one_hots = [
        (place == entry[2 * rows_here :].astype(jnp.int32)).astype(jnp.bfloat16)
        for entry in small
    ]

    maps = [[None] * count for _ in range(3)]
    for j in order:
        maps[PAIR][j] = send(current[j], route(pair_moves + [(1, 0)], 1, 0))
        maps[EXTRA][j] = send(current[j], route(extra_moves, 1, 0))
        maps[OWN][j] = send(current[j], route(every, 1, 0))
    merged = jnp.concatenate(
        [jnp.where(is_lead, maps[OWN][j], current[j]) for j in range(count)], axis=0
    )

    first = row_sources[PAIR].astype(jnp.bfloat16)
    (down_odd,), state = segment(
        coupling, first, row_sources, one_hots, {}, maps, (OWN,), ()
    )
    at = 1
    kept = []
    ups = {}
    for k, (target, slots) in enumerate(chain):
        arrived = send(state, route([(at, target)]))
        at = target
        turn = k == len(chain) - 1
        if turn:
            arrived, merged = lax.optimization_barrier((arrived, merged))
        rows, state = segment(
            coupling,
            arrived,
            row_sources,
            one_hots,
            {},
            maps,
            slots,
            tuple(reversed(slots))[1:] if turn else (),
        )
        kept.append(dict(zip(slots, rows)))
        if turn:
            ups[at] = dict(zip(tuple(reversed(slots))[1:], rows[len(slots) :]))
            ups[at][slots[-1]] = rows[len(slots) - 1]
    down_odd_pair = send(down_odd, route([(1, 0)]))
    down_odd = jnp.where(layer == 0, down_odd_pair, down_odd)

    for k in reversed(range(len(chain) - 1)):
        target, slots = chain[k]
        arrived = send(state, route([(at, target)]))
        at = target
        back = tuple(reversed(slots))
        rows, state = segment(
            coupling, arrived, row_sources, one_hots, kept[k], maps, (), back
        )
        ups[at] = dict(zip(back, rows))
    from_pair = send(state, route([(at, 0)]))
    from_own = send(state, route([(at, 1)]))

    mine = [jnp.zeros(row_sources[OWN].shape, jnp.float32)] * 3
    for target, values in ups.items():
        for slot in (OWN, PAIR, EXTRA):
            mine[slot] = jnp.where(layer == target, values[slot], mine[slot])
    settled = (
        mine[OWN]
        + send(mine[PAIR], route([(z, a) for a, z in pair_moves]))
        + send(mine[EXTRA], route([(z, a) for a, z in extra_moves]))
    )

    odd = (layer % 2).astype(jnp.int32)[None]
    last = pl.pallas_call(
        functools.partial(last_kernel, coupling, count),
        out_shape=jax.ShapeDtypeStruct(row_sources[OWN].shape, jnp.float32),
        in_specs=[SMEM] + [VMEM] * (4 + 2 * count),
        out_specs=VMEM,
        compiler_params=PARAMS,
        cost_estimate=cost(6 * 256 * 1024 * 1024, 6 * 1024 * 1024),
    )(odd, from_pair, from_own, row_sources[OWN], down_odd, *maps[OWN], *maps[PAIR])
    upward = jnp.where(layer < 2, last, settled)
    next_rows = send(upward[rows_here:], route(every, 0, 1))
    upward = jnp.where(is_lead, upward[:rows_here], next_rows)
    return (merged[None], upward[None])


def solution(mesh):
    return jax.shard_map(
        on_device,
        mesh=mesh,
        in_specs=(
            P("layer", "box", None),
            P("layer", "box", None),
            P("layer", None, None, None),
            P("layer", None),
            P("layer", "box", None),
        ),
        out_specs=(P("layer", None, None), P("layer", "box", None)),
        check_vma=False,
    )
```

time: 210 us -> 103 us (0.49)
  waiting for transfers between devices: 102 us -> 40.9 us
  local copies, waits for them, and re-layouts: 29 us -> 3.36 us
  matrix products: 17.6 us -> 0 us
  starting transfers between devices: 51.4 us -> 35.8 us
  Pallas kernels: 0 us -> 13.7 us
    ppermute x18 -> x30, waiting for transfers between devices: 102 us -> 40.9 us  [send(): return lax.ppermute(value, AXES, pairs_of_devices)]
    gather x8 -> x0, local copies, waits for them, and re-layouts: 25.7 us -> none  [down_step(): gathered = received[:, order_map].astype(jnp.bfloat16)]
    dot_general x20 -> x0, matrix products: 17.6 us -> none  [the longest x2 7.42 us: combine(): jnp.dot(product, right_rows, precision=lax.Precision.HIGHEST)]
    ppermute x18 -> x30, starting transfers between devices: 51.4 us -> 35.8 us  [send(): return lax.ppermute(value, AXES, pairs_of_devices)]
    pallas_call x0 -> x11, Pallas kernels: none -> 13.7 us  [the longest x4 8.19 us: segment(): pl.pallas_call(functools.partial(segment_kernel, coupling, len(maps[OWN])...]
    mul x3 -> x0, other arithmetic: 6.91 us -> none  [the longest x2 5.04 us: combine(): joined = 0.5 * (first.astype(jnp.float32) + second.astype(jnp.float32))]
    convert_element_type x1 -> x7, other arithmetic: 0.76 us -> 3.36 us  [the longest x3 2.65 us: on_device(): (place == entry[2 * rows_here:].astype(jnp.int32)).astype(jnp.bfloat16)]
    concatenate x0 -> x2, other arithmetic: none -> 2.22 us  [the longest x1 1.49 us: on_device(): jnp.concatenate([jnp.where(is_lead, maps[OWN][j], current[j]) for j in ra...]
  transfers between devices with their start and end apart: 18 -> 30, of which waited for: 18 -> 10; matrix products, arithmetic and copies ran while one was open for 0% -> 7% of each run, Pallas kernels for 0% -> 11%
where the time goes in v2:
time: 103 us; the launch traced here: 102 us
  waiting for transfers between devices  40.9 us (40%)
  starting transfers between devices  35.8 us (35%)
  Pallas kernels  13.7 us (13%)
  other arithmetic  6.48 us (6%)
  local copies, waits for them, and re-layouts  3.36 us (3%)
  between operations  1.23 us (1%)
    ppermute x30, waiting for transfers between devices, send(): return lax.ppermute(value, AXES, pairs_of_devices)  40.9 us
    ppermute x30, starting transfers between devices, send(): return lax.ppermute(value, AXES, pairs_of_devices)  35.8 us
    pallas_call x4, Pallas kernels, segment(): pl.pallas_call(functools.partial(segment_kernel, coupling, len(maps[OWN])...  8.19 us
    pallas_call x2, Pallas kernels, leaf_combine(): pl.pallas_call(functools.partial(leaf_kernel, half * rows, is_face), grid...  2.79 us
    convert_element_type x3, other arithmetic, on_device(): (place == entry[2 * rows_here:].astype(jnp.int32)).astype(jnp.bfloat16)  2.65 us
    unnamed x4, local copies, waits for them, and re-layouts  2.27 us
  transfers between devices with their start and end apart: 30, of which 10 were waited for; matrix products, arithmetic and copies ran while one was open for 7% of the time, Pallas kernels for 11%

profile of v2, /device:TPU:0, one launch (start us, length us, event | category | flops | bytes accessed | tf_op | source)
XLA Modules:
  0.0 101.5 jit_solution(198843784763284819)
XLA Ops:
  0.6 0.5 collective-permute-start.2
  1.1 0.1 collective-permute-start.1
  1.2 1.3 %collective-permute-start = (f32[4,1024]{1,0:T(4,128)}, f32[4,1024]{1,0:T(4,128)S(1)}, u32[]{:S(2)}, u32[]{:S(2)}) collective-permute-start(f32[4,1024]{1,0:T(4,128)} %bitcast.24), channel_id=1, source_target_pairs={{1,0},{3,2},{5,4},{7,6},{9,8},{11,10},{13,12},{15,14},{17,16},{19,... | collective-permute-start | bytes 49160 | tf_op jit(solution)/shard_map/ppermute | solution.py:210
  2.5 1.1 %fusion.4 = (bf16[256,256]{1,0:T(8,128)(2,1)S(1)}, bf16[256,256]{1,0:T(8,128)(2,1)S(1)}) fusion(f32[1,3,256,256]{3,2,1,0:T(8,128)} %param.7, s32[]{:T(128)S(6)} %select_n.89, s32[]{:T(128)S(6)} %select_n.88), kind=kLoop, calls=%fused_computation.14 | loop fusion | bytes 524296 | tf_op jit(solution)/shard_map/convert_element_type | solution.py:227
  3.6 0.7 convert_element_type.34
  4.3 0.8 collective-permute-done
  5.1 0.7 pad_maximum_fusion.1
  5.9 1.6 %copy-done = bf16[1,1024,1024]{2,1,0:T(8,128)(2,1)S(1)} copy-done((bf16[1,1024,1024]{2,1,0:T(8,128)(2,1)S(1)}, bf16[1,1024,1024]{2,1,0:T(8,128)(2,1)}, u32[]{:S(2)}) %copy-start) | copy-done | bytes 2097176
  7.4 0.7 copy-done.1
  8.1 1.4 %shard_map.68 = (bf16[256,1024]{1,0:T(8,128)(2,1)S(1)}, bf16[256,1024]{1,0:T(8,128)(2,1)S(1)}, bf16[256,1024]{1,0:T(8,128)(2,1)S(1)}) custom-call(s32[8,8]{1,0:T(8,128)S(1)} %bitcast.18, s32[8,8]{1,0:T(8,128)S(1)} %collective-permute-done.1.other_pattern, bf16[1024,1024]{1,0:T(8,128)(2,1)S(1)} %bitcast.15, ...), custom_call_target="tpu_custom_call" | custom-call | flops 335544320 | bytes 3145728 | tf_op jit(solution)/shard_map/pallas_call | solution.py:79
  9.5 4.8 %collective-permute-start.5 = (bf16[256,1024]{1,0:T(8,128)(2,1)S(1)}, bf16[256,1024]{1,0:T(8,128)(2,1)S(1)}, u32[]{:S(2)}, u32[]{:S(2)}) collective-permute-start(bf16[256,1024]{1,0:T(8,128)(2,1)S(1)} %get-tuple-element.30.own), channel_id=1, source_target_pairs={{0,3},{2,1},{4,7},{6,5},{8,11},{10,9},{12,15},{14,13},{16,19},{18,... | collective-permute-start | bytes 1572872 | tf_op jit(solution)/shard_map/ppermute | solution.py:210
  14.4 1.4 %shard_map.69 = (bf16[256,1024]{1,0:T(8,128)(2,1)S(1)}, bf16[256,1024]{1,0:T(8,128)(2,1)S(1)}) custom-call(s32[8,8]{1,0:T(8,128)S(1)} %bitcast.19, s32[8,8]{1,0:T(8,128)S(1)} %collective-permute-done.1.other_pattern, bf16[1024,1024]{1,0:T(8,128)(2,1)S(1)} %bitcast.16, bf16[1024,1024]{1,0:T(8,128)(2,1)S(1)} %collective-permute-done.2.other, ...), custom_call_target="tpu_custom_call" | custom-call | flops 335544320 | bytes 3145728 | tf_op jit(solution)/shard_map/pallas_call | solution.py:79
  15.8 1.3 %collective-permute-start.8 = (bf16[256,1024]{1,0:T(8,128)(2,1)S(1)}, bf16[256,1024]{1,0:T(8,128)(2,1)S(1)}, u32[]{:S(2)}, u32[]{:S(2)}) collective-permute-start(bf16[256,1024]{1,0:T(8,128)(2,1)S(1)} %get-tuple-element.33.own), channel_id=1, source_target_pairs={{0,3},{2,1},{4,7},{6,5},{8,11},{10,9},{12,15},{14,13},{16,19},{18,... | collective-permute-start | bytes 1572872 | tf_op jit(solution)/shard_map/ppermute | solution.py:210
  17.1 1.3 %collective-permute-start.10 = (bf16[256,1024]{1,0:T(8,128)(2,1)S(1)}, bf16[256,1024]{1,0:T(8,128)(2,1)S(1)}, u32[]{:S(2)}, u32[]{:S(2)}) collective-permute-start(bf16[256,1024]{1,0:T(8,128)(2,1)S(1)} %get-tuple-element.27.own), channel_id=1, source_target_pairs={{0,3},{2,1},{4,7},{6,5},{8,11},{10,9},{12,15},{14,13},{16,19},{18,... | collective-permute-start | bytes 1572872 | tf_op jit(solution)/shard_map/ppermute | solution.py:210
  18.5 3.4 %collective-permute-start.3 = (f32[9,1024]{1,0:T(8,128)S(1)}, f32[9,1024]{1,0:T(8,128)S(1)}, u32[]{:S(2)}, u32[]{:S(2)}) collective-permute-start(f32[9,1024]{1,0:T(8,128)S(1)} %pad_maximum_fusion.1), channel_id=1, source_target_pairs={{12,8},{14,10},{24,28},{26,30},{0,4},{2,6}} | collective-permute-start | bytes 110600 | tf_op jit(solution)/shard_map/ppermute | solution.py:210
  21.9 1.3 %collective-permute-start.4 = (bf16[256,1024]{1,0:T(8,128)(2,1)S(1)}, bf16[256,1024]{1,0:T(8,128)(2,1)S(1)}, u32[]{:S(2)}, u32[]{:S(2)}) collective-permute-start(bf16[256,1024]{1,0:T(8,128)(2,1)S(1)} %get-tuple-element.29.own), channel_id=1, source_target_pairs={{0,3},{2,1},{4,7},{6,5},{8,11},{10,9},{12,15},{14,13},{16,19},{18,... | collective-permute-start | bytes 1572872 | tf_op jit(solution)/shard_map/ppermute | solution.py:210
  23.2 0.9 fusion.refs_2_.refs_14_
  24.1 0.7 collective-permute-start.17
  24.8 0.4 shard_map.70
  25.3 1.4 %collective-permute-done.8.other = bf16[256,1024]{1,0:T(8,128)(2,1)S(1)} collective-permute-done((bf16[256,1024]{1,0:T(8,128)(2,1)S(1)}, bf16[256,1024]{1,0:T(8,128)(2,1)S(1)}, u32[]{:S(2)}, u32[]{:S(2)}) %collective-permute-start.8) | collective-permute-done | bytes 524320 | tf_op jit(solution)/shard_map/ppermute | solution.py:210
  26.6 0.4 shard_map.72
  27.1 1.3 %collective-permute-start.9 = (bf16[256,1024]{1,0:T(8,128)(2,1)S(1)}, bf16[256,1024]{1,0:T(8,128)(2,1)S(1)}, u32[]{:S(2)}, u32[]{:S(2)}) collective-permute-start(bf16[256,1024]{1,0:T(8,128)(2,1)S(1)} %shard_map.72), channel_id=1, source_target_pairs={{1,0},{3,2},{5,4},{7,6},{9,8},{11,10},{13,12},{15,14},{17,16},{19,... | collective-permute-start | bytes 1572872 | tf_op jit(solution)/shard_map/ppermute | solution.py:210
  28.4 3.9 %collective-permute-done.10.other = bf16[256,1024]{1,0:T(8,128)(2,1)S(1)} collective-permute-done((bf16[256,1024]{1,0:T(8,128)(2,1)S(1)}, bf16[256,1024]{1,0:T(8,128)(2,1)S(1)}, u32[]{:S(2)}, u32[]{:S(2)}) %collective-permute-start.10) | collective-permute-done | bytes 524320 | tf_op jit(solution)/shard_map/ppermute | solution.py:210
  32.2 0.4 shard_map.73
  32.7 1.3 %collective-permute-start.11 = (bf16[256,1024]{1,0:T(8,128)(2,1)S(1)}, bf16[256,1024]{1,0:T(8,128)(2,1)S(1)}, u32[]{:S(2)}, u32[]{:S(2)}) collective-permute-start(bf16[256,1024]{1,0:T(8,128)(2,1)S(1)} %shard_map.73), channel_id=1, source_target_pairs={{1,0},{3,2},{5,4},{7,6},{9,8},{11,10},{13,12},{15,14},{17,16},{19,... | collective-permute-start | bytes 1572872 | tf_op jit(solution)/shard_map/ppermute | solution.py:210
  34.0 3.9 %collective-permute-done.4.other = bf16[256,1024]{1,0:T(8,128)(2,1)S(1)} collective-permute-done((bf16[256,1024]{1,0:T(8,128)(2,1)S(1)}, bf16[256,1024]{1,0:T(8,128)(2,1)S(1)}, u32[]{:S(2)}, u32[]{:S(2)}) %collective-permute-start.4) | collective-permute-done | bytes 524320 | tf_op jit(solution)/shard_map/ppermute | solution.py:210
  37.9 0.5 shard_map.71
  38.3 1.3 %collective-permute-start.6 = (bf16[256,1024]{1,0:T(8,128)(2,1)S(1)}, bf16[256,1024]{1,0:T(8,128)(2,1)S(1)}, u32[]{:S(2)}, u32[]{:S(2)}) collective-permute-start(bf16[256,1024]{1,0:T(8,128)(2,1)S(1)} %shard_map.71), channel_id=1, source_target_pairs={{1,0},{3,2},{5,4},{7,6},{9,8},{11,10},{13,12},{15,14},{17,16},{19,... | collective-permute-start | bytes 1572872 | tf_op jit(solution)/shard_map/ppermute | solution.py:210
  39.6 1.3 %collective-permute-start.7 = (bf16[256,1024]{1,0:T(8,128)(2,1)S(1)}, bf16[256,1024]{1,0:T(8,128)(2,1)S(1)}, u32[]{:S(2)}, u32[]{:S(2)}) collective-permute-start(bf16[256,1024]{1,0:T(8,128)(2,1)S(1)} %get-tuple-element.32), channel_id=1, source_target_pairs={{1,0},{3,2},{5,4},{7,6},{9,8},{11,10},{13,12},{15,14},{17,16},{19,... | collective-permute-start | bytes 1572872 | tf_op jit(solution)/shard_map/ppermute | solution.py:210
  40.9 0.9 fusion.1.refs_8_
  41.9 0.9 fusion.2.refs_14_.refs_2_
  42.8 1.3 %collective-permute-start.16 = (bf16[256,1024]{1,0:T(8,128)(2,1)S(1)}, bf16[256,1024]{1,0:T(8,128)(2,1)S(1)}, u32[]{:S(2)}, u32[]{:S(2)}) collective-permute-start(bf16[256,1024]{1,0:T(8,128)(2,1)S(1)} %shard_map.73), channel_id=1, source_target_pairs={{13,8},{15,10},{25,28},{27,30},{5,0},{7,2}} | collective-permute-start | bytes 1572872 | tf_op jit(solution)/shard_map/ppermute | solution.py:210
  44.1 0.7 collective-permute-start.21
  44.8 1.3 %collective-permute-start.15 = (bf16[256,1024]{1,0:T(8,128)(2,1)S(1)}, bf16[256,1024]{1,0:T(8,128)(2,1)S(1)}, u32[]{:S(2)}, u32[]{:S(2)}) collective-permute-start(bf16[256,1024]{1,0:T(8,128)(2,1)S(1)} %shard_map.72), channel_id=1, source_target_pairs={{13,8},{15,10},{25,28},{27,30},{5,0},{7,2}} | collective-permute-start | bytes 1572872 | tf_op jit(solution)/shard_map/ppermute | solution.py:210
  46.1 0.7 collective-permute-start.20
  46.8 1.3 %collective-permute-start.13 = (bf16[256,1024]{1,0:T(8,128)(2,1)S(1)}, bf16[256,1024]{1,0:T(8,128)(2,1)S(1)}, u32[]{:S(2)}, u32[]{:S(2)}) collective-permute-start(bf16[256,1024]{1,0:T(8,128)(2,1)S(1)} %shard_map.71), channel_id=1, source_target_pairs={{13,8},{15,10},{25,28},{27,30},{5,0},{7,2}} | collective-permute-start | bytes 1572872 | tf_op jit(solution)/shard_map/ppermute | solution.py:210
  48.1 0.9 shard_map.74
  49.0 0.1 broadcast_select_fusion.1
  49.1 0.1 broadcast_select_fusion
  49.2 4.1 %collective-permute-done.16.refs_12_.refs_10_.refs_7_ = bf16[256,1024]{1,0:T(8,128)(2,1)S(1)} collective-permute-done((bf16[256,1024]{1,0:T(8,128)(2,1)S(1)}, bf16[256,1024]{1,0:T(8,128)(2,1)S(1)}, u32[]{:S(2)}, u32[]{:S(2)}) %collective-permute-start.16) | collective-permute-done | bytes 524320 | tf_op jit(solution)/shard_map/ppermute | solution.py:210
  53.3 0.7 collective-permute-start.18
  54.0 1.3 %collective-permute-start.14 = (bf16[256,1024]{1,0:T(8,128)(2,1)S(1)}, bf16[256,1024]{1,0:T(8,128)(2,1)S(1)}, u32[]{:S(2)}, u32[]{:S(2)}) collective-permute-start(bf16[256,1024]{1,0:T(8,128)(2,1)S(1)} %get-tuple-element.32), channel_id=1, source_target_pairs={{13,8},{15,10},{25,28},{27,30},{5,0},{7,2}} | collective-permute-start | bytes 1572872 | tf_op jit(solution)/shard_map/ppermute | solution.py:210
  55.3 3.6 %collective-permute-done.15.refs_11_.refs_9_.refs_6_ = bf16[256,1024]{1,0:T(8,128)(2,1)S(1)} collective-permute-done((bf16[256,1024]{1,0:T(8,128)(2,1)S(1)}, bf16[256,1024]{1,0:T(8,128)(2,1)S(1)}, u32[]{:S(2)}, u32[]{:S(2)}) %collective-permute-start.15) | collective-permute-done | bytes 524320 | tf_op jit(solution)/shard_map/ppermute | solution.py:210
  58.9 0.7 collective-permute-start.19
  59.6 0.1 broadcast_select_fusion.3
  59.6 0.7 collective-permute-start.12
  60.4 4.1 %collective-permute-done.13.refs_9_.refs_7_.refs_4_ = bf16[256,1024]{1,0:T(8,128)(2,1)S(1)} collective-permute-done((bf16[256,1024]{1,0:T(8,128)(2,1)S(1)}, bf16[256,1024]{1,0:T(8,128)(2,1)S(1)}, u32[]{:S(2)}, u32[]{:S(2)}) %collective-permute-start.13) | collective-permute-done | bytes 524320 | tf_op jit(solution)/shard_map/ppermute | solution.py:210
  64.5 1.3 %collective-permute-start.26 = (f32[8,1024]{1,0:T(8,128)S(1)}, f32[8,1024]{1,0:T(8,128)S(1)}, u32[]{:S(2)}, u32[]{:S(2)}) collective-permute-start(f32[8,1024]{1,0:T(8,128)S(1)} %get-tuple-element.43), channel_id=1, source_target_pairs={{4,0},{6,2}} | collective-permute-start | bytes 98312 | tf_op jit(solution)/shard_map/ppermute | solution.py:210
  65.8 4.4 %collective-permute-done.14.refs_10_.refs_8_.refs_5_ = bf16[256,1024]{1,0:T(8,128)(2,1)S(1)} collective-permute-done((bf16[256,1024]{1,0:T(8,128)(2,1)S(1)}, bf16[256,1024]{1,0:T(8,128)(2,1)S(1)}, u32[]{:S(2)}, u32[]{:S(2)}) %collective-permute-start.14) | collective-permute-done | bytes 524320 | tf_op jit(solution)/shard_map/ppermute | solution.py:210
  70.2 2.6 %shard_map.75 = (f32[8,1024]{1,0:T(8,128)S(1)}, f32[8,1024]{1,0:T(8,128)S(1)}, f32[8,1024]{1,0:T(8,128)S(1)}, bf16[8,1024]{1,0:T(8,128)(2,1)S(1)}) custom-call(bf16[8,1024]{1,0:T(8,128)(2,1)S(1)} %collective-permute-done.12.refs_0_, f32[8,1024]{1,0:T(8,128)S(1)} %slice.25.refs_1_.refs_13_.source, bf16[1024,1024]{1,0:T(8,128)(2,1)S(1)} %fusion.refs_2_.refs_14_, ...), custom_call_target="tpu_custom_call" | custom-call | flops 1610612736 | bytes 6291456 | tf_op jit(solution)/shard_map/pallas_call | solution.py:164
  72.8 0.9 collective-permute-start.22
  73.7 1.5 %pad_maximum_fusion = bf16[1024,1024]{1,0:T(8,128)(2,1)} fusion(bf16[256,1024]{1,0:T(8,128)(2,1)S(1)} %broadcast_select_fusion, bf16[256,1024]{1,0:T(8,128)(2,1)S(1)} %broadcast_select_fusion.1, bf16[256,1024]{1,0:T(8,128)(2,1)S(1)} %broadcast_select_fusion.2, bf16[256,1024]{1,0:T(8,128)(2,1)S(1)} %broadcast_select_fusion.3), kind=kLoop, calls=%fused_computation.6 | loop fusion | flops 8388608 | bytes 4194304 | tf_op jit(solution)/shard_map/concatenate | solution.py:281
  75.2 3.7 %shard_map.76 = (f32[8,1024]{1,0:T(8,128)}, f32[8,1024]{1,0:T(8,128)}, f32[8,1024]{1,0:T(8,128)S(1)}, f32[8,1024]{1,0:T(8,128)S(1)}, f32[8,1024]{1,0:T(8,128)S(1)}, /*index=5*/bf16[8,1024]{1,0:T(8,128)(2,1)S(1)}) custom-call(bf16[8,1024]{1,0:T(8,128)(2,1)S(1)} %collective-permute-done.22.refs_0_, f32[8,1024]{1,0:T(8,128)S(1)} %slice.34.refs_13_.refs_1_, ...), custom_call_target="tpu_custom_call" | custom-call | flops 2684354560 | bytes 10485760 | tf_op jit(solution)/shard_map/pallas_call | solution.py:164
  78.8 0.7 collective-permute-start.23
  79.5 1.0 %shard_map.77 = (f32[8,1024]{1,0:T(8,128)S(1)}, f32[8,1024]{1,0:T(8,128)S(1)}, f32[8,1024]{1,0:T(8,128)S(1)}, bf16[8,1024]{1,0:T(8,128)(2,1)S(1)}) custom-call(bf16[8,1024]{1,0:T(8,128)(2,1)S(1)} %collective-permute-done.23.refs_0_, f32[8,1024]{1,0:T(8,128)S(1)} %get-tuple-element.39.refs_1_, ...), custom_call_target="tpu_custom_call" | custom-call | flops 1610612736 | bytes 6291456 | tf_op jit(solution)/shard_map/pallas_call | solution.py:164
  80.5 1.3 %collective-permute-start.24 = (bf16[8,1024]{1,0:T(8,128)(2,1)S(1)}, bf16[8,1024]{1,0:T(8,128)(2,1)S(1)}, u32[]{:S(2)}, u32[]{:S(2)}) collective-permute-start(bf16[8,1024]{1,0:T(8,128)(2,1)S(1)} %get-tuple-element.42), channel_id=1, source_target_pairs={{8,0},{10,2}} | collective-permute-start | bytes 49160 | tf_op jit(solution)/shard_map/ppermute | solution.py:210
  81.8 0.7 collective-permute-start.25
  82.5 0.7 collective-permute-start.27
  83.2 0.7 collective-permute-start.28
  83.9 13.9 %collective-permute-done.24.from_pair = bf16[8,1024]{1,0:T(8,128)(2,1)S(1)} collective-permute-done((bf16[8,1024]{1,0:T(8,128)(2,1)S(1)}, bf16[8,1024]{1,0:T(8,128)(2,1)S(1)}, u32[]{:S(2)}, u32[]{:S(2)}) %collective-permute-start.24) | collective-permute-done | bytes 16416 | tf_op jit(solution)/shard_map/ppermute | solution.py:210
  97.8 1.0 shard_map.78
  98.8 1.3 %collective-permute-start.29 = (f32[4,1024]{1,0:T(4,128)S(1)}, f32[4,1024]{1,0:T(4,128)S(1)}, u32[]{:S(2)}, u32[]{:S(2)}) collective-permute-start(f32[4,1024]{1,0:T(4,128)S(1)} %slice.37), channel_id=1, source_target_pairs={{0,1},{2,3},{4,5},{6,7},{8,9},{10,11},{12,13},{14,15},{16,17},{18,... | collective-permute-start | bytes 49160 | tf_op jit(solution)/shard_map/ppermute | solution.py:210
  100.1 0.8 collective-permute-done.29
  100.9 0.6 fusion.5
  (35 shorter events, 0.2 us)
Async XLA Ops:
  0.6 5.2 %collective-permute-start.2 = (bf16[1024,1024]{1,0:T(8,128)(2,1)}, bf16[1024,1024]{1,0:T(8,128)(2,1)S(1)}, u32[]{:S(2)}, u32[]{:S(2)}) collective-permute-start(bf16[1024,1024]{1,0:T(8,128)(2,1)} %bitcast.14), channel_id=1, source_target_pairs={{0,1},{1,0},{2,3},{3,2},{4,5},{5,4},{6,7},{7,6},{8,9},{9,8},{10,11... | collective-permute-start | bytes 6291464 | tf_op jit(solution)/shard_map/ppermute | solution.py:210
  1.1 4.7 %collective-permute-start.1 = (s32[8,8]{1,0:T(8,128)}, s32[8,8]{1,0:T(8,128)S(1)}, u32[]{:S(2)}, u32[]{:S(2)}) collective-permute-start(s32[8,8]{1,0:T(8,128)} %bitcast.17), channel_id=1, source_target_pairs={{0,1},{1,0},{2,3},{3,2},{4,5},{5,4},{6,7},{7,6},{8,9},{9,8},{10,11... | collective-permute-start | bytes 776 | tf_op jit(solution)/shard_map/ppermute | solution.py:210
  1.2 3.9 %collective-permute-start = (f32[4,1024]{1,0:T(4,128)}, f32[4,1024]{1,0:T(4,128)S(1)}, u32[]{:S(2)}, u32[]{:S(2)}) collective-permute-start(f32[4,1024]{1,0:T(4,128)} %bitcast.24), channel_id=1, source_target_pairs={{1,0},{3,2},{5,4},{7,6},{9,8},{11,10},{13,12},{15,14},{17,16},{19,... | collective-permute-start | bytes 49160 | tf_op jit(solution)/shard_map/ppermute | solution.py:210
  5.9 1.6 %copy-start = (bf16[1,1024,1024]{2,1,0:T(8,128)(2,1)S(1)}, bf16[1,1024,1024]{2,1,0:T(8,128)(2,1)}, u32[]{:S(2)}) copy-start(bf16[1,1024,1024]{2,1,0:T(8,128)(2,1)} %param.5) | copy-start | bytes 6291460
  7.4 0.7 copy-start.1
  9.5 15.3 %collective-permute-start.5 = (bf16[256,1024]{1,0:T(8,128)(2,1)S(1)}, bf16[256,1024]{1,0:T(8,128)(2,1)S(1)}, u32[]{:S(2)}, u32[]{:S(2)}) collective-permute-start(bf16[256,1024]{1,0:T(8,128)(2,1)S(1)} %get-tuple-element.30.own), channel_id=1, source_target_pairs={{0,3},{2,1},{4,7},{6,5},{8,11},{10,9},{12,15},{14,13},{16,19},{18,... | collective-permute-start | bytes 1572872 | tf_op jit(solution)/shard_map/ppermute | solution.py:210
  15.8 10.8 %collective-permute-start.8 = (bf16[256,1024]{1,0:T(8,128)(2,1)S(1)}, bf16[256,1024]{1,0:T(8,128)(2,1)S(1)}, u32[]{:S(2)}, u32[]{:S(2)}) collective-permute-start(bf16[256,1024]{1,0:T(8,128)(2,1)S(1)} %get-tuple-element.33.own), channel_id=1, source_target_pairs={{0,3},{2,1},{4,7},{6,5},{8,11},{10,9},{12,15},{14,13},{16,19},{18,... | collective-permute-start | bytes 1572872 | tf_op jit(solution)/shard_map/ppermute | solution.py:210
  17.1 15.1 %collective-permute-start.10 = (bf16[256,1024]{1,0:T(8,128)(2,1)S(1)}, bf16[256,1024]{1,0:T(8,128)(2,1)S(1)}, u32[]{:S(2)}, u32[]{:S(2)}) collective-permute-start(bf16[256,1024]{1,0:T(8,128)(2,1)S(1)} %get-tuple-element.27.own), channel_id=1, source_target_pairs={{0,3},{2,1},{4,7},{6,5},{8,11},{10,9},{12,15},{14,13},{16,19},{18,... | collective-permute-start | bytes 1572872 | tf_op jit(solution)/shard_map/ppermute | solution.py:210
  18.5 5.6 %collective-permute-start.3 = (f32[9,1024]{1,0:T(8,128)S(1)}, f32[9,1024]{1,0:T(8,128)S(1)}, u32[]{:S(2)}, u32[]{:S(2)}) collective-permute-start(f32[9,1024]{1,0:T(8,128)S(1)} %pad_maximum_fusion.1), channel_id=1, source_target_pairs={{12,8},{14,10},{24,28},{26,30},{0,4},{2,6}} | collective-permute-start | bytes 110600 | tf_op jit(solution)/shard_map/ppermute | solution.py:210
  21.9 16.0 %collective-permute-start.4 = (bf16[256,1024]{1,0:T(8,128)(2,1)S(1)}, bf16[256,1024]{1,0:T(8,128)(2,1)S(1)}, u32[]{:S(2)}, u32[]{:S(2)}) collective-permute-start(bf16[256,1024]{1,0:T(8,128)(2,1)S(1)} %get-tuple-element.29.own), channel_id=1, source_target_pairs={{0,3},{2,1},{4,7},{6,5},{8,11},{10,9},{12,15},{14,13},{16,19},{18,... | collective-permute-start | bytes 1572872 | tf_op jit(solution)/shard_map/ppermute | solution.py:210
  24.1 17.7 %collective-permute-start.17 = (f32[9,1024]{1,0:T(8,128)S(1)}, f32[9,1024]{1,0:T(8,128)S(1)}, u32[]{:S(2)}, u32[]{:S(2)}) collective-permute-start(f32[9,1024]{1,0:T(8,128)S(1)} %pad_maximum_fusion.1), channel_id=1, source_target_pairs={{16,8},{18,10},{20,28},{22,30}} | collective-permute-start | bytes 110600 | tf_op jit(solution)/shard_map/ppermute | solution.py:210
  27.1 17.0 %collective-permute-start.9 = (bf16[256,1024]{1,0:T(8,128)(2,1)S(1)}, bf16[256,1024]{1,0:T(8,128)(2,1)S(1)}, u32[]{:S(2)}, u32[]{:S(2)}) collective-permute-start(bf16[256,1024]{1,0:T(8,128)(2,1)S(1)} %shard_map.72), channel_id=1, source_target_pairs={{1,0},{3,2},{5,4},{7,6},{9,8},{11,10},{13,12},{15,14},{17,16},{19,... | collective-permute-start | bytes 1572872 | tf_op jit(solution)/shard_map/ppermute | solution.py:210
  32.7 12.1 %collective-permute-start.11 = (bf16[256,1024]{1,0:T(8,128)(2,1)S(1)}, bf16[256,1024]{1,0:T(8,128)(2,1)S(1)}, u32[]{:S(2)}, u32[]{:S(2)}) collective-permute-start(bf16[256,1024]{1,0:T(8,128)(2,1)S(1)} %shard_map.73), channel_id=1, source_target_pairs={{1,0},{3,2},{5,4},{7,6},{9,8},{11,10},{13,12},{15,14},{17,16},{19,... | collective-permute-start | bytes 1572872 | tf_op jit(solution)/shard_map/ppermute | solution.py:210
  38.3 7.8 %collective-permute-start.6 = (bf16[256,1024]{1,0:T(8,128)(2,1)S(1)}, bf16[256,1024]{1,0:T(8,128)(2,1)S(1)}, u32[]{:S(2)}, u32[]{:S(2)}) collective-permute-start(bf16[256,1024]{1,0:T(8,128)(2,1)S(1)} %shard_map.71), channel_id=1, source_target_pairs={{1,0},{3,2},{5,4},{7,6},{9,8},{11,10},{13,12},{15,14},{17,16},{19,... | collective-permute-start | bytes 1572872 | tf_op jit(solution)/shard_map/ppermute | solution.py:210
  39.6 7.2 %collective-permute-start.7 = (bf16[256,1024]{1,0:T(8,128)(2,1)S(1)}, bf16[256,1024]{1,0:T(8,128)(2,1)S(1)}, u32[]{:S(2)}, u32[]{:S(2)}) collective-permute-start(bf16[256,1024]{1,0:T(8,128)(2,1)S(1)} %get-tuple-element.32), channel_id=1, source_target_pairs={{1,0},{3,2},{5,4},{7,6},{9,8},{11,10},{13,12},{15,14},{17,16},{19,... | collective-permute-start | bytes 1572872 | tf_op jit(solution)/shard_map/ppermute | solution.py:210
  42.8 10.5 %collective-permute-start.16 = (bf16[256,1024]{1,0:T(8,128)(2,1)S(1)}, bf16[256,1024]{1,0:T(8,128)(2,1)S(1)}, u32[]{:S(2)}, u32[]{:S(2)}) collective-permute-start(bf16[256,1024]{1,0:T(8,128)(2,1)S(1)} %shard_map.73), channel_id=1, source_target_pairs={{13,8},{15,10},{25,28},{27,30},{5,0},{7,2}} | collective-permute-start | bytes 1572872 | tf_op jit(solution)/shard_map/ppermute | solution.py:210
  44.1 9.9 %collective-permute-start.21 = (bf16[256,1024]{1,0:T(8,128)(2,1)S(1)}, bf16[256,1024]{1,0:T(8,128)(2,1)S(1)}, u32[]{:S(2)}, u32[]{:S(2)}) collective-permute-start(bf16[256,1024]{1,0:T(8,128)(2,1)S(1)} %shard_map.73), channel_id=1, source_target_pairs={{17,8},{19,10},{21,28},{23,30}} | collective-permute-start | bytes 1572872 | tf_op jit(solution)/shard_map/ppermute | solution.py:210
  44.8 14.1 %collective-permute-start.15 = (bf16[256,1024]{1,0:T(8,128)(2,1)S(1)}, bf16[256,1024]{1,0:T(8,128)(2,1)S(1)}, u32[]{:S(2)}, u32[]{:S(2)}) collective-permute-start(bf16[256,1024]{1,0:T(8,128)(2,1)S(1)} %shard_map.72), channel_id=1, source_target_pairs={{13,8},{15,10},{25,28},{27,30},{5,0},{7,2}} | collective-permute-start | bytes 1572872 | tf_op jit(solution)/shard_map/ppermute | solution.py:210
  46.1 13.5 %collective-permute-start.20 = (bf16[256,1024]{1,0:T(8,128)(2,1)S(1)}, bf16[256,1024]{1,0:T(8,128)(2,1)S(1)}, u32[]{:S(2)}, u32[]{:S(2)}) collective-permute-start(bf16[256,1024]{1,0:T(8,128)(2,1)S(1)} %shard_map.72), channel_id=1, source_target_pairs={{17,8},{19,10},{21,28},{23,30}} | collective-permute-start | bytes 1572872 | tf_op jit(solution)/shard_map/ppermute | solution.py:210
  46.8 17.7 %collective-permute-start.13 = (bf16[256,1024]{1,0:T(8,128)(2,1)S(1)}, bf16[256,1024]{1,0:T(8,128)(2,1)S(1)}, u32[]{:S(2)}, u32[]{:S(2)}) collective-permute-start(bf16[256,1024]{1,0:T(8,128)(2,1)S(1)} %shard_map.71), channel_id=1, source_target_pairs={{13,8},{15,10},{25,28},{27,30},{5,0},{7,2}} | collective-permute-start | bytes 1572872 | tf_op jit(solution)/shard_map/ppermute | solution.py:210
  53.3 12.5 %collective-permute-start.18 = (bf16[256,1024]{1,0:T(8,128)(2,1)S(1)}, bf16[256,1024]{1,0:T(8,128)(2,1)S(1)}, u32[]{:S(2)}, u32[]{:S(2)}) collective-permute-start(bf16[256,1024]{1,0:T(8,128)(2,1)S(1)} %shard_map.71), channel_id=1, source_target_pairs={{17,8},{19,10},{21,28},{23,30}} | collective-permute-start | bytes 1572872 | tf_op jit(solution)/shard_map/ppermute | solution.py:210
  54.0 16.3 %collective-permute-start.14 = (bf16[256,1024]{1,0:T(8,128)(2,1)S(1)}, bf16[256,1024]{1,0:T(8,128)(2,1)S(1)}, u32[]{:S(2)}, u32[]{:S(2)}) collective-permute-start(bf16[256,1024]{1,0:T(8,128)(2,1)S(1)} %get-tuple-element.32), channel_id=1, source_target_pairs={{13,8},{15,10},{25,28},{27,30},{5,0},{7,2}} | collective-permute-start | bytes 1572872 | tf_op jit(solution)/shard_map/ppermute | solution.py:210
  58.9 11.3 %collective-permute-start.19 = (bf16[256,1024]{1,0:T(8,128)(2,1)S(1)}, bf16[256,1024]{1,0:T(8,128)(2,1)S(1)}, u32[]{:S(2)}, u32[]{:S(2)}) collective-permute-start(bf16[256,1024]{1,0:T(8,128)(2,1)S(1)} %get-tuple-element.32), channel_id=1, source_target_pairs={{17,8},{19,10},{21,28},{23,30}} | collective-permute-start | bytes 1572872 | tf_op jit(solution)/shard_map/ppermute | solution.py:210
  59.6 10.6 %collective-permute-start.12 = (bf16[8,1024]{1,0:T(8,128)(2,1)S(1)}, bf16[8,1024]{1,0:T(8,128)(2,1)S(1)}, u32[]{:S(2)}, u32[]{:S(2)}) collective-permute-start(bf16[8,1024]{1,0:T(8,128)(2,1)S(1)} %get-tuple-element.34), channel_id=1, source_target_pairs={{4,8},{6,10}} | collective-permute-start | bytes 49160 | tf_op jit(solution)/shard_map/ppermute | solution.py:210
  64.5 15.0 %collective-permute-start.26 = (f32[8,1024]{1,0:T(8,128)S(1)}, f32[8,1024]{1,0:T(8,128)S(1)}, u32[]{:S(2)}, u32[]{:S(2)}) collective-permute-start(f32[8,1024]{1,0:T(8,128)S(1)} %get-tuple-element.43), channel_id=1, source_target_pairs={{4,0},{6,2}} | collective-permute-start | bytes 98312 | tf_op jit(solution)/shard_map/ppermute | solution.py:210
  72.8 2.4 %collective-permute-start.22 = (bf16[8,1024]{1,0:T(8,128)(2,1)S(1)}, bf16[8,1024]{1,0:T(8,128)(2,1)S(1)}, u32[]{:S(2)}, u32[]{:S(2)}) collective-permute-start(bf16[8,1024]{1,0:T(8,128)(2,1)S(1)} %get-tuple-element.35), channel_id=1, source_target_pairs={{8,28},{10,30}} | collective-permute-start | bytes 49160 | tf_op jit(solution)/shard_map/ppermute | solution.py:210
  78.8 0.7 collective-permute-start.23
  80.5 17.2 %collective-permute-start.24 = (bf16[8,1024]{1,0:T(8,128)(2,1)S(1)}, bf16[8,1024]{1,0:T(8,128)(2,1)S(1)}, u32[]{:S(2)}, u32[]{:S(2)}) collective-permute-start(bf16[8,1024]{1,0:T(8,128)(2,1)S(1)} %get-tuple-element.42), channel_id=1, source_target_pairs={{8,0},{10,2}} | collective-permute-start | bytes 49160 | tf_op jit(solution)/shard_map/ppermute | solution.py:210
  81.8 15.9 %collective-permute-start.25 = (bf16[8,1024]{1,0:T(8,128)(2,1)S(1)}, bf16[8,1024]{1,0:T(8,128)(2,1)S(1)}, u32[]{:S(2)}, u32[]{:S(2)}) collective-permute-start(bf16[8,1024]{1,0:T(8,128)(2,1)S(1)} %get-tuple-element.42), channel_id=1, source_target_pairs={{8,4},{10,6}} | collective-permute-start | bytes 49160 | tf_op jit(solution)/shard_map/ppermute | solution.py:210
  82.5 16.2 %collective-permute-start.27 = (f32[8,1024]{1,0:T(8,128)S(1)}, f32[8,1024]{1,0:T(8,128)S(1)}, u32[]{:S(2)}, u32[]{:S(2)}) collective-permute-start(f32[8,1024]{1,0:T(8,128)S(1)} %select_select_fusion.1), channel_id=1, source_target_pairs={{8,12},{10,14},{28,24},{30,26}} | collective-permute-start | bytes 98312 | tf_op jit(solution)/shard_map/ppermute | solution.py:210
  83.2 15.6 %collective-permute-start.28 = (f32[8,1024]{1,0:T(8,128)S(1)}, f32[8,1024]{1,0:T(8,128)S(1)}, u32[]{:S(2)}, u32[]{:S(2)}) collective-permute-start(f32[8,1024]{1,0:T(8,128)S(1)} %select_select_fusion), channel_id=1, source_target_pairs={{8,16},{10,18},{28,20},{30,22}} | collective-permute-start | bytes 98312 | tf_op jit(solution)/shard_map/ppermute | solution.py:210
  98.8 2.1 %collective-permute-start.29 = (f32[4,1024]{1,0:T(4,128)S(1)}, f32[4,1024]{1,0:T(4,128)S(1)}, u32[]{:S(2)}, u32[]{:S(2)}) collective-permute-start(f32[4,1024]{1,0:T(4,128)S(1)} %slice.37), channel_id=1, source_target_pairs={{0,1},{2,3},{4,5},{6,7},{8,9},{10,11},{12,13},{14,15},{16,17},{18,... | collective-permute-start | bytes 49160 | tf_op jit(solution)/shard_map/ppermute | solution.py:210

commit v3 on v2

v3 whole, which is shorter than its diff:
```python
import functools

import jax
import jax.numpy as jnp
from jax import lax
from jax.experimental import pallas as pl
from jax.experimental.pallas import tpu as pltpu
from jax.sharding import PartitionSpec as P

AXES = ("layer", "box")
LAST_PIECES = ((0, 256), (256, 256), (512, 256), (768, 128), (896, 128))
Y_TIE = 2
X_TIE = 2
VMEM = pl.BlockSpec(memory_space=pltpu.VMEM)
SMEM = pl.BlockSpec(memory_space=pltpu.SMEM)
PARAMS = pltpu.CompilerParams(vmem_limit_bytes=24 * 1024 * 1024)
OWN, PAIR, EXTRA = 0, 1, 2


def cost(flops, moved):
    return pl.CostEstimate(flops=flops, bytes_accessed=moved, transcendentals=0)


def dot32(a, b):
    return jnp.dot(a, b, preferred_element_type=jnp.float32)


def dot32_t(a, b):
    return lax.dot_general(a, b, (((1,), (1,)), ((), ())), preferred_element_type=jnp.float32)


def minus_face(joined, face_at, inverse, right):
    face = inverse.shape[0]
    left = joined[:, face_at : face_at + face].astype(jnp.bfloat16)
    product = dot32(left, inverse).astype(jnp.bfloat16)
    return (joined - dot32(product, right)).astype(jnp.bfloat16)


def masked(values, pattern, row_at, row_count, block_at):
    width = values.shape[1]
    block = width // pattern.shape[1]
    strips = []
    for r in range(row_count // block):
        at = slice(row_at + r * block, row_at + (r + 1) * block)
        strips.append(
            jnp.concatenate(
                [
                    values[at, c * block : (c + 1) * block].astype(jnp.float32)
                    * (0.5 * pattern[block_at + r, c].astype(jnp.float32))
                    for c in range(width // block)
                ],
                axis=1,
            )
        )
    return jnp.concatenate(strips, axis=0)


def mask_kernel(pattern, values, out):
    block = values.shape[1] // pattern.shape[1]
    for r in range(values.shape[0] // block):
        out[r * block : (r + 1) * block] = masked(values, pattern, r * block, block, r).astype(
            jnp.bfloat16
        )


def leaf_kernel(first_row, is_face, pieces, other_pattern, own, other, inverse, *refs):
    refs = list(refs)
    face = inverse.shape[0]
    right = None if is_face else refs.pop(0)[...]
    block = own.shape[1] // other_pattern.shape[1]
    for i in range(own.shape[0] // face):
        at = first_row + i * face
        joined = own[i * face : (i + 1) * face].astype(jnp.float32) + masked(
            other, other_pattern, i * face, face, at // block
        )
        if right is None:
            right = joined.astype(jnp.bfloat16)
            refs[-1][...] = right
        result = minus_face(joined, 0, inverse[...], right)
        for ref, (start, size) in zip(refs, pieces):
            low, high = max(start, at), min(start + size, at + face)
            if low < high:
                ref[low - start : high - start] = result[low - at : high - at]


def leaf_combine(other_pattern, own, other, inverse, face_rows, half, pieces):
    is_face = face_rows is None
    width = own.shape[1]
    rows = own.shape[0] // 2
    face = inverse.shape[0]
    shapes = [jax.ShapeDtypeStruct((size, width), jnp.bfloat16) for _, size in pieces]
    if is_face:
        shapes.append(jax.ShapeDtypeStruct((face, width), jnp.bfloat16))
    map_spec = pl.BlockSpec((rows, width), lambda i: (half, 0))
    extra = [] if is_face else [face_rows]
    return pl.pallas_call(
        functools.partial(leaf_kernel, half * rows, is_face, pieces),
        grid=(1,),
        out_shape=shapes,
        in_specs=[SMEM, map_spec, map_spec, VMEM] + [VMEM] * len(extra),
        out_specs=[VMEM] * len(shapes),
        compiler_params=PARAMS,
        cost_estimate=cost(2 * rows * face * (width + face), 6 * rows * width),
    )(other_pattern, own, other, inverse, *extra)


def combine_kernel(face_at, is_face, whole_rows, own, other, inverse, *refs):
    refs = list(refs)
    joined = 0.5 * (own[...].astype(jnp.float32) + other[...].astype(jnp.float32))
    if is_face:
        right = joined.astype(jnp.bfloat16)
    else:
        right = refs.pop(0)[...]
        refs.pop(0)
    piece = minus_face(joined, face_at, inverse[...], right)
    refs[0][...] = piece
    refs[1][whole_rows, :] = piece
    if is_face:
        refs[2][...] = right


def combine(own, other, inverse, state, face_at, row_at):
    is_face = state is None
    rows, width = own.shape
    extra = [] if is_face else list(state)
    piece = jax.ShapeDtypeStruct((rows, width), jnp.bfloat16)
    whole = jax.ShapeDtypeStruct((width, width), jnp.bfloat16)
    result = pl.pallas_call(
        functools.partial(combine_kernel, face_at, is_face, slice(row_at, row_at + rows)),
        out_shape=[piece, whole] + ([piece] if is_face else []),
        in_specs=[VMEM] * (3 + len(extra)),
        out_specs=[VMEM] * (3 if is_face else 2),
        input_output_aliases={} if is_face else {4: 1},
        compiler_params=PARAMS,
        cost_estimate=cost(0, 0),
    )(own, other, inverse, *extra)
    return result[0], ((result[2] if is_face else state[0]), result[1])


def spread(pieces, rows):
    return jnp.concatenate([dot32_t(rows, piece[...]) for piece in pieces], axis=1)


def gather_sum(pieces, rows):
    at, total = 0, None
    for piece in pieces:
        size = piece.shape[0]
        term = dot32(rows[:, at : at + size], piece[...])
        total = term if total is None else total + term
        at += size
    return total


def lanes_at(rows, index_row):
    lanes = 128
    count, width = rows.shape
    parts = [rows[:, at : at + lanes] for at in range(0, width, lanes)]
    outs = []
    for at in range(0, width, lanes):
        index = jnp.broadcast_to(index_row[:, at : at + lanes].astype(jnp.int32), (count, lanes))
        lane, part = index % lanes, index // lanes
        total = jnp.zeros((count, lanes), rows.dtype)
        for k, values in enumerate(parts):
            total = jnp.where(part == k, jnp.take_along_axis(values, lane, axis=1), total)
        outs.append(total)
    return jnp.concatenate(outs, axis=1)


def segment_kernel(coupling, pieces_of, down_steps, up_steps, *refs):
    refs = list(refs)
    state = refs.pop(0)[...]
    maps, downs = {}, {}
    operands = []
    for slot in down_steps:
        operands.append(refs.pop(0))
        maps[slot] = [refs.pop(0) for _ in range(pieces_of[slot])]
    for slot in up_steps:
        if slot not in down_steps:
            downs[slot] = refs.pop(0)[...]
            maps[slot] = [refs.pop(0) for _ in range(pieces_of[slot])]
    for slot, packed in zip(down_steps, operands):
        count = state.shape[0]
        moved = lanes_at(state.astype(jnp.float32), packed[count:]).astype(jnp.bfloat16)
        downs[slot] = packed[:count] + coupling * spread(maps[slot], moved)
        state = downs[slot].astype(jnp.bfloat16)
        refs.pop(0)[...] = downs[slot]
    for slot in up_steps:
        value = downs[slot] + coupling * gather_sum(maps[slot], state)
        state = value.astype(jnp.bfloat16)
        refs.pop(0)[...] = value
    refs.pop(0)[...] = state


def segment(coupling, arrived, packed, downs, maps, down_steps, up_steps):
    operands = [arrived]
    for slot in down_steps:
        operands += [packed[slot], *maps[slot]]
    for slot in up_steps:
        if slot not in down_steps:
            operands += [downs[slot], *maps[slot]]
    rows = jax.ShapeDtypeStruct(arrived.shape, jnp.float32)
    steps = len(down_steps) + len(up_steps)
    results = pl.pallas_call(
        functools.partial(
            segment_kernel, coupling, [len(entry) for entry in maps], down_steps, up_steps
        ),
        out_shape=[rows] * steps + [jax.ShapeDtypeStruct(arrived.shape, jnp.bfloat16)],
        in_specs=[VMEM] * len(operands),
        out_specs=[VMEM] * (steps + 1),
        compiler_params=PARAMS,
        cost_estimate=cost(steps * 2 * 256 * 1024 * 1024, steps * 2 * 1024 * 1024),
    )(*operands)
    return results[:-1], results[-1]


def last_kernel(coupling, count, odd, from_pair, from_own, source, down_odd, *refs):
    own, pair, out = refs[:1], refs[1 : 1 + count], refs[1 + count]
    total = gather_sum(pair, from_pair[...]) + gather_sum(own, from_own[...])
    up_odd = down_odd[...] + coupling * total
    up_even = source[...] + coupling * gather_sum(own, up_odd.astype(jnp.bfloat16))
    out[...] = jnp.where(odd[0] == 1, up_odd, up_even)


def on_device(box_maps, block_pattern, face_inverses, index_map, sources):
    boxes = lax.axis_size("box")
    layers = lax.axis_size("layer")
    coupling = float(boxes) ** 0.5
    levels = boxes.bit_length() - 1
    face = face_inverses.shape[2]
    width = box_maps.shape[2]
    rows_here = sources.shape[1]
    position = lax.axis_index("box")
    layer = lax.axis_index("layer")
    is_lead = position % 2 == 1
    pairs = layers // 2

    chain = []
    for p in range(1, pairs, 3):
        chain.append((2 * p, (OWN, PAIR, EXTRA)))
        chain.append((2 * (p + 2) + 1, (EXTRA, PAIR, OWN)))

    def route(moves, source_core=1, target_core=1):
        return [
            (a * boxes + b + source_core, z * boxes + b + target_core)
            for a, z in moves
            for b in range(0, boxes, 2)
        ]

    def send(value, pairs_of_devices):
        return lax.ppermute(value, AXES, pairs_of_devices)

    def after(value, *others):
        return lax.optimization_barrier((value, *others))[0]

    every = [(i, i) for i in range(layers)]
    pair_moves = [(at ^ 1, at) for at, _ in chain]
    extra_moves = [(at + 2 if at % 2 == 0 else at - 2, at) for at, _ in chain]

    def over_box(change, starts):
        return [(i * boxes + b, i * boxes + (b ^ change)) for i in range(layers) for b in starts]

    raw = box_maps[0]
    pattern = block_pattern[0]
    raw_other = send(raw, over_box(1, range(boxes)))
    pattern_other = send(pattern, over_box(1, range(boxes)))
    next_sources = send(sources[0], route(every, 0, 1))
    own_half = pl.pallas_call(
        mask_kernel,
        out_shape=jax.ShapeDtypeStruct(raw.shape, jnp.bfloat16),
        in_specs=[SMEM, VMEM],
        out_specs=VMEM,
        compiler_params=PARAMS,
        cost_estimate=cost(width * width, 4 * width * width),
    )(pattern, raw)

    def inverse_of(level):
        node = (boxes >> (level + 1)) - 1 + (position >> (level + 1))
        return lax.dynamic_index_in_dim(face_inverses[0], node, 0, keepdims=False).astype(
            jnp.bfloat16
        )

    whole_faces = tuple((at, face) for at in range(0, width, face))
    last_face = (levels - 1) * face
    if last_face == face:
        parts = LAST_PIECES
    else:
        parts = whole_faces
    cuts = [tuple(parts)] if levels == 2 else [whole_faces] * (levels - 1)

    inverse = inverse_of(0)
    half = width // 2
    upper = tuple(piece for piece in cuts[0] if piece[0] < half)
    lower = tuple(piece for piece in cuts[0] if piece[0] >= half)
    top = leaf_combine(pattern_other, own_half, raw_other, inverse, None, 0, upper)
    bottom = leaf_combine(pattern_other, own_half, raw_other, inverse, top[-1], 1, lower)
    current = dict(zip(upper + lower, [*top[:-1], *bottom]))

    rows = -(-2 * rows_here // 8) * 8
    packed = jnp.concatenate(
        [
            next_sources,
            sources[0],
            jnp.zeros((rows - 2 * rows_here, width), jnp.float32),
            index_map.astype(jnp.float32),
        ],
        axis=0,
    )
    sendable = after(packed, bottom[0])
    small = [
        packed,
        send(sendable, route(pair_moves + [(0, 1)])),
        send(sendable, route(extra_moves)),
    ]

    maps = [[], [], []]
    for level in range(1, levels):
        final = level == levels - 1
        change = 1 << level
        if final:
            moves = over_box(change ^ 1, range(0, boxes, 2))
        else:
            moves = over_box(change, range(boxes))
        inverse = inverse_of(level)
        order = sorted(current, key=lambda piece: (piece[0] != level * face, piece[0]))
        received = {}
        for k, piece in enumerate(order):
            value = current[piece]
            if k >= Y_TIE:
                value = after(value, received[order[k - Y_TIE]])
            received[piece] = send(value, moves)
        state = None
        sent = {PAIR: {}, EXTRA: {}}
        renewed = {}
        for k, piece in enumerate(order):
            other = received[piece]
            if final and k == 0:
                other = after(other, small[PAIR], small[EXTRA])
            if final and k >= X_TIE:
                before = order[k - X_TIE]
                other = after(other, sent[PAIR][before], sent[EXTRA][before])
            renewed[piece], state = combine(
                current[piece], other, inverse, state, level * face, piece[0]
            )
            if final:
                sent[PAIR][piece] = send(renewed[piece], route(pair_moves + [(1, 0)]))
                sent[EXTRA][piece] = send(renewed[piece], route(extra_moves))
        current = renewed
    merged = state[1]
    inner = sorted(current)
    maps = [[merged]] + [[sent[slot][piece] for piece in inner] for slot in (PAIR, EXTRA)]

    first = small[PAIR][:rows].astype(jnp.bfloat16)
    (down_odd,), state = segment(coupling, first, small, {}, maps, (OWN,), ())
    at = 1
    kept = []
    ups = {}
    for k, (target, slots) in enumerate(chain):
        arrived = send(state, route([(at, target)]))
        at = target
        turn = k == len(chain) - 1
        back = tuple(reversed(slots))
        results, state = segment(
            coupling, arrived, small, {}, maps, slots, back[1:] if turn else ()
        )
        kept.append(dict(zip(slots, results)))
        if k == 0:
            copied = send(after(merged, state), route(every, 1, 0))
        if turn:
            ups[at] = dict(zip(back[1:], results[len(slots) :]))
            ups[at][back[0]] = results[len(slots) - 1]
    down_odd = jnp.where(layer == 0, send(after(down_odd, state), route([(1, 0)])), down_odd)
    merged = jnp.where(is_lead, merged, after(copied, state))

    for k in reversed(range(len(chain) - 1)):
        target, slots = chain[k]
        arrived = send(state, route([(at, target)]))
        if k == len(chain) - 2:
            arrived, merged = lax.optimization_barrier((arrived, merged))
        at = target
        back = tuple(reversed(slots))
        results, state = segment(coupling, arrived, small, kept[k], maps, (), back)
        ups[at] = dict(zip(back, results))
    from_pair = send(state, route([(at, 0)]))
    from_own = send(state, route([(at, 1)]))

    mine = [jnp.zeros((rows, width), jnp.float32)] * 3
    for target, values in ups.items():
        for slot in (OWN, PAIR, EXTRA):
            mine[slot] = jnp.where(layer == target, values[slot], mine[slot])
    settled = (
        mine[OWN]
        + send(mine[PAIR], route([(z, a) for a, z in pair_moves]))
        + send(mine[EXTRA], route([(z, a) for a, z in extra_moves]))
    )

    odd = (layer % 2).astype(jnp.int32)[None]
    last = pl.pallas_call(
        functools.partial(last_kernel, coupling, len(inner)),
        out_shape=jax.ShapeDtypeStruct((rows, width), jnp.float32),
        in_specs=[SMEM] + [VMEM] * (5 + len(inner)),
        out_specs=VMEM,
        compiler_params=PARAMS,
        cost_estimate=cost(6 * 256 * 1024 * 1024, 6 * 1024 * 1024),
    )(odd, from_pair, from_own, packed[:rows], down_odd, *maps[OWN], *maps[PAIR])
    upward = jnp.where(layer < 2, last, settled)
    lead_rows = upward[rows_here : 2 * rows_here]
    upward = jnp.where(is_lead, lead_rows, send(upward[:rows_here], route(every, 1, 0)))
    return (merged[None], upward[None])


def solution(mesh):
    return jax.shard_map(
        on_device,
        mesh=mesh,
        in_specs=(
            P("layer", "box", None),
            P("layer", "box", None),
            P("layer", None, None, None),
            P("layer", None),
            P("layer", "box", None),
        ),
        out_specs=(P("layer", None, None), P("layer", "box", None)),
        check_vma=False,
    )
```

time: 103 us -> 98.3 us (0.954)
  waiting for transfers between devices: 40.9 us -> 25.1 us
  local copies, waits for them, and re-layouts: 3.36 us -> 14.3 us
  other arithmetic: 6.48 us -> 3.95 us
  starting transfers between devices: 35.8 us -> 37.5 us
    ppermute x30, waiting for transfers between devices: 40.9 us -> 25.1 us  [send(): return lax.ppermute(value, AXES, pairs_of_devices)]
    unnamed x4 -> x72, local copies, waits for them, and re-layouts: 2.27 us -> 13.2 us
    select_n x5 -> x2, other arithmetic: 0.25 us -> 3.27 us  [the longest x1 3.27 us: on_device(): merged = jnp.where(is_lead, merged, after(copied, state))]
    convert_element_type x6 -> x0, other arithmetic: 2.67 us -> none  [the longest x3 2.65 us: on_device(): (place == entry[2 * rows_here:].astype(jnp.int32)).astype(jnp.bfloat16)]
    concatenate x2, other arithmetic: 2.22 us -> 0.03 us  [on_device(): jnp.concatenate([next_sources, sources[0], jnp.zeros((rows - 2 * rows_her...]
    ppermute x30, starting transfers between devices: 35.8 us -> 37.5 us  [send(): return lax.ppermute(value, AXES, pairs_of_devices)]
    pallas_call x11 -> x13, Pallas kernels: 13.7 us -> 14.1 us  [the longest x4 7.49 us: segment(): pl.pallas_call(functools.partial(segment_kernel, coupling, [len(entry) fo...]
  transfers between devices with their start and end apart: 30 -> 30, of which waited for: 10 -> 5; matrix products, arithmetic and copies ran while one was open for 7% -> 5% of each run, Pallas kernels for 11% -> 9%
where the time goes in v3:
time: 98.3 us; the launch traced here: 96.4 us
  starting transfers between devices  37.5 us (38%)
  waiting for transfers between devices  25.1 us (26%)
  local copies, waits for them, and re-layouts  14.3 us (15%)
  Pallas kernels  14.1 us (14%)
  other arithmetic  3.95 us (4%)
  between operations  1.47 us (1%)
    ppermute x30, starting transfers between devices, send(): return lax.ppermute(value, AXES, pairs_of_devices)  37.5 us
    ppermute x30, waiting for transfers between devices, send(): return lax.ppermute(value, AXES, pairs_of_devices)  25.1 us
    unnamed x72, local copies, waits for them, and re-layouts  13.2 us
    pallas_call x4, Pallas kernels, segment(): pl.pallas_call(functools.partial(segment_kernel, coupling, [len(entry) fo...  7.49 us
    select_n x1, other arithmetic, on_device(): merged = jnp.where(is_lead, merged, after(copied, state))  3.27 us
    pallas_call x2, Pallas kernels, leaf_combine(): pl.pallas_call(functools.partial(leaf_kernel, half * rows, is_face, piece...  2.66 us
    pallas_call x5, Pallas kernels, combine(): pl.pallas_call(functools.partial(combine_kernel, face_at, is_face, slice(...  2.06 us
  transfers between devices with their start and end apart: 30, of which 5 were waited for; matrix products, arithmetic and copies ran while one was open for 5% of the time, Pallas kernels for 9%

profile of v3, /device:TPU:0, one launch (start us, length us, event | category | flops | bytes accessed | tf_op | source)
XLA Modules:
  0.0 96.4 jit_solution(3193926471822131985)
XLA Ops:
  0.6 0.5 collective-permute-start.2
  1.2 1.1 %fusion.1 = (bf16[256,256]{1,0:T(8,128)(2,1)S(1)}, bf16[256,256]{1,0:T(8,128)(2,1)S(1)}) fusion(f32[1,3,256,256]{3,2,1,0:T(8,128)} %param.7, s32[]{:T(128)S(6)} %select_n.77, s32[]{:T(128)S(6)} %select_n.76), kind=kLoop, calls=%fused_computation.4 | loop fusion | bytes 524296 | tf_op jit(solution)/shard_map/convert_element_type | solution.py:278
  2.3 1.6 %copy-done.11 = bf16[1,1024,1024]{2,1,0:T(8,128)(2,1)S(1)} copy-done((bf16[1,1024,1024]{2,1,0:T(8,128)(2,1)S(1)}, bf16[1,1024,1024]{2,1,0:T(8,128)(2,1)}, u32[]{:S(2)}) %copy-start.11) | copy-done | bytes 2097176
  3.9 0.7 copy-done.30
  4.6 0.9 shard_map.68.own
  5.6 1.3 %shard_map.69 = (bf16[256,1024]{1,0:T(8,128)(2,1)S(1)}, bf16[256,1024]{1,0:T(8,128)(2,1)S(1)}, bf16[256,1024]{1,0:T(8,128)(2,1)S(1)}) custom-call(s32[8,8]{1,0:T(8,128)S(1)} %collective-permute-done.1.other_pattern, bf16[1024,1024]{1,0:T(8,128)(2,1)S(1)} %shard_map.68.own, bf16[1024,1024]{1,0:T(8,128)(2,1)S(1)} %collective-permute-done.2.other, ...), custom_call_target="tpu_custom_call" | custom-call | flops 335544320 | bytes 3145728 | tf_op jit(solution)/shard_map/pallas_call | solution.py:96
  6.9 4.6 %collective-permute-start.4 = (bf16[256,1024]{1,0:T(8,128)(2,1)S(1)}, bf16[256,1024]{1,0:T(8,128)(2,1)S(1)}, u32[]{:S(2)}, u32[]{:S(2)}) collective-permute-start(bf16[256,1024]{1,0:T(8,128)(2,1)S(1)} %get-tuple-element.50.own), channel_id=1, source_target_pairs={{0,3},{2,1},{4,7},{6,5},{8,11},{10,9},{12,15},{14,13},{16,19},{18,... | collective-permute-start | bytes 1572872 | tf_op jit(solution)/shard_map/ppermute | solution.py:250
  11.5 1.3 %collective-permute-start = (f32[4,1024]{1,0:T(4,128)S(1)}, f32[4,1024]{1,0:T(4,128)S(1)}, u32[]{:S(2)}, u32[]{:S(2)}) collective-permute-start(f32[4,1024]{1,0:T(4,128)S(1)} %bitcast.16), channel_id=1, source_target_pairs={{0,1},{2,3},{4,5},{6,7},{8,9},{10,11},{12,13},{14,15},{16,17},{18,... | collective-permute-start | bytes 49160 | tf_op jit(solution)/shard_map/ppermute | solution.py:250
  12.8 0.8 collective-permute-done
  13.6 0.6 copy-done.33
  14.2 1.3 %shard_map.70 = (bf16[256,1024]{1,0:T(8,128)(2,1)S(1)}, bf16[128,1024]{1,0:T(8,128)(2,1)S(1)}, bf16[128,1024]{1,0:T(8,128)(2,1)S(1)}) custom-call(s32[8,8]{1,0:T(8,128)S(1)} %collective-permute-done.1.other_pattern, bf16[1024,1024]{1,0:T(8,128)(2,1)S(1)} %shard_map.68.own, bf16[1024,1024]{1,0:T(8,128)(2,1)S(1)} %collective-permute-done.2.other, ...), custom_call_target="tpu_custom_call" | custom-call | flops 335544320 | bytes 3145728 | tf_op jit(solution)/shard_map/pallas_call | solution.py:96
  15.6 0.7 collective-permute-start.3
  16.2 0.7 collective-permute-start.7
  16.9 4.8 %collective-permute-start.10 = (bf16[256,1024]{1,0:T(8,128)(2,1)S(1)}, bf16[256,1024]{1,0:T(8,128)(2,1)S(1)}, u32[]{:S(2)}, u32[]{:S(2)}) collective-permute-start(bf16[256,1024]{1,0:T(8,128)(2,1)S(1)} %get-tuple-element.57.own), channel_id=1, source_target_pairs={{0,3},{2,1},{4,7},{6,5},{8,11},{10,9},{12,15},{14,13},{16,19},{18,... | collective-permute-start | bytes 1572872 | tf_op jit(solution)/shard_map/ppermute | solution.py:250
  21.8 0.4 shard_map.71
  22.2 0.7 collective-permute-start.8
  22.9 0.7 collective-permute-start.9
  23.7 1.9 %collective-permute-start.5 = (bf16[256,1024]{1,0:T(8,128)(2,1)S(1)}, bf16[256,1024]{1,0:T(8,128)(2,1)S(1)}, u32[]{:S(2)}, u32[]{:S(2)}) collective-permute-start(bf16[256,1024]{1,0:T(8,128)(2,1)S(1)} %get-tuple-element.51.own), channel_id=1, source_target_pairs={{0,3},{2,1},{4,7},{6,5},{8,11},{10,9},{12,15},{14,13},{16,19},{18,... | collective-permute-start | bytes 1572872 | tf_op jit(solution)/shard_map/ppermute | solution.py:250
  25.6 2.9 %collective-permute-done.10.other = bf16[256,1024]{1,0:T(8,128)(2,1)S(1)} collective-permute-done((bf16[256,1024]{1,0:T(8,128)(2,1)S(1)}, bf16[256,1024]{1,0:T(8,128)(2,1)S(1)}, u32[]{:S(2)}, u32[]{:S(2)}) %collective-permute-start.10) | collective-permute-done | bytes 524320 | tf_op jit(solution)/shard_map/ppermute | solution.py:250
  28.4 0.4 shard_map.72
  28.8 0.7 collective-permute-start.14
  29.5 0.7 collective-permute-start.15
  30.3 4.4 %collective-permute-start.13 = (bf16[128,1024]{1,0:T(8,128)(2,1)S(1)}, bf16[128,1024]{1,0:T(8,128)(2,1)S(1)}, u32[]{:S(2)}, u32[]{:S(2)}) collective-permute-start(bf16[128,1024]{1,0:T(8,128)(2,1)S(1)} %get-tuple-element.63.own), channel_id=1, source_target_pairs={{0,3},{2,1},{4,7},{6,5},{8,11},{10,9},{12,15},{14,13},{16,19},{18,... | collective-permute-start | bytes 786440 | tf_op jit(solution)/shard_map/ppermute | solution.py:250
  34.7 0.4 shard_map.73
  35.2 0.7 collective-permute-start.11
  35.9 0.7 collective-permute-start.12
  36.6 2.0 %collective-permute-done.13.other = bf16[128,1024]{1,0:T(8,128)(2,1)S(1)} collective-permute-done((bf16[128,1024]{1,0:T(8,128)(2,1)S(1)}, bf16[128,1024]{1,0:T(8,128)(2,1)S(1)}, u32[]{:S(2)}, u32[]{:S(2)}) %collective-permute-start.13) | collective-permute-done | bytes 262176 | tf_op jit(solution)/shard_map/ppermute | solution.py:250
  38.6 3.8 %collective-permute-start.6 = (bf16[128,1024]{1,0:T(8,128)(2,1)S(1)}, bf16[128,1024]{1,0:T(8,128)(2,1)S(1)}, u32[]{:S(2)}, u32[]{:S(2)}) collective-permute-start(bf16[128,1024]{1,0:T(8,128)(2,1)S(1)} %get-tuple-element.52.own), channel_id=1, source_target_pairs={{0,3},{2,1},{4,7},{6,5},{8,11},{10,9},{12,15},{14,13},{16,19},{18,... | collective-permute-start | bytes 786440 | tf_op jit(solution)/shard_map/ppermute | solution.py:250
  42.8 0.7 collective-permute-start.17
  43.5 0.7 collective-permute-start.19
  44.2 2.1 %collective-permute-done.6.other = bf16[128,1024]{1,0:T(8,128)(2,1)S(1)} collective-permute-done((bf16[128,1024]{1,0:T(8,128)(2,1)S(1)}, bf16[128,1024]{1,0:T(8,128)(2,1)S(1)}, u32[]{:S(2)}, u32[]{:S(2)}) %collective-permute-start.6) | collective-permute-done | bytes 262176 | tf_op jit(solution)/shard_map/ppermute | solution.py:250
  46.2 0.4 shard_map.75
  46.6 0.7 collective-permute-start.18
  47.3 0.7 collective-permute-start.20
  48.0 0.7 shard_map.76
  48.7 0.6 copy-done.28
  49.3 0.7 collective-permute-start.16
  50.1 2.6 %shard_map.77 = (f32[8,1024]{1,0:T(8,128)S(1)}, f32[8,1024]{1,0:T(8,128)S(1)}, f32[8,1024]{1,0:T(8,128)S(1)}, bf16[8,1024]{1,0:T(8,128)(2,1)}) custom-call(bf16[8,1024]{1,0:T(8,128)(2,1)S(1)} %collective-permute-done.16.refs_0_, f32[9,1024]{1,0:T(8,128)S(1)} %pad_maximum_fusion.refs_1_.refs_13_, ...), custom_call_target="tpu_custom_call" | custom-call | flops 1610612736 | bytes 6291456 | tf_op jit(solution)/shard_map/pallas_call | solution.py:203
  52.7 0.6 copy-done.22
  53.3 0.6 copy-done.24
  53.9 0.6 copy-done.26
  54.5 1.3 %collective-permute-start.23 = (bf16[1024,1024]{1,0:T(8,128)(2,1)S(1)}, bf16[1024,1024]{1,0:T(8,128)(2,1)}, u32[]{:S(2)}, u32[]{:S(2)}) collective-permute-start(bf16[1024,1024]{1,0:T(8,128)(2,1)S(1)} %get-tuple-element.74.refs_2_.refs_14_.refs_0_), channel_id=1, source_target_pairs={{1,0},{3,2},{5,4},{7,6},{9,8},{11,10},{13,12},{15,14},{17,16},{19,... | collective-permute-start | bytes 6291464 | tf_op jit(solution)/shard_map/ppermute | solution.py:250
  55.8 0.7 collective-permute-start.21
  56.6 1.0 %copy-done.1 = bf16[256,1024]{1,0:T(8,128)(2,1)S(1)} copy-done((bf16[256,1024]{1,0:T(8,128)(2,1)S(1)}, bf16[256,1024]{1,0:T(8,128)(2,1)}, u32[]{:S(2)}) %copy-start.1) | copy-done | bytes 524312
  57.6 1.0 %copy-done.4 = bf16[256,1024]{1,0:T(8,128)(2,1)S(1)} copy-done((bf16[256,1024]{1,0:T(8,128)(2,1)S(1)}, bf16[256,1024]{1,0:T(8,128)(2,1)}, u32[]{:S(2)}) %copy-start.4) | copy-done | bytes 524312
  58.6 1.0 %copy-done.6 = bf16[256,1024]{1,0:T(8,128)(2,1)S(1)} copy-done((bf16[256,1024]{1,0:T(8,128)(2,1)S(1)}, bf16[256,1024]{1,0:T(8,128)(2,1)}, u32[]{:S(2)}) %copy-start.6) | copy-done | bytes 524312
  59.7 1.0 %copy-done.9 = bf16[256,1024]{1,0:T(8,128)(2,1)S(1)} copy-done((bf16[256,1024]{1,0:T(8,128)(2,1)S(1)}, bf16[256,1024]{1,0:T(8,128)(2,1)}, u32[]{:S(2)}) %copy-start.9) | copy-done | bytes 524312
  60.7 0.9 copy-done.13
  61.7 0.9 copy-done.15
  62.6 0.9 copy-done.18
  63.6 0.8 copy-done.21
  64.4 3.1 %shard_map.78 = (f32[8,1024]{1,0:T(8,128)}, f32[8,1024]{1,0:T(8,128)}, f32[8,1024]{1,0:T(8,128)S(1)}, f32[8,1024]{1,0:T(8,128)S(1)}, f32[8,1024]{1,0:T(8,128)S(1)}, /*index=5*/bf16[8,1024]{1,0:T(8,128)(2,1)S(1)}) custom-call(bf16[8,1024]{1,0:T(8,128)(2,1)S(1)} %collective-permute-done.21.refs_0_, f32[9,1024]{1,0:T(8,128)S(1)} %copy-done.21, ...), custom_call_target="tpu_custom_call" | custom-call | flops 2684354560 | bytes 10485760 | tf_op jit(solution)/shard_map/pallas_call | solution.py:203
  67.5 0.7 collective-permute-start.26
  68.2 0.7 collective-permute-start.22
  69.0 3.3 %broadcast_select_fusion = bf16[1024,1024]{1,0:T(8,128)(2,1)} fusion(bf16[1024,1024]{1,0:T(8,128)(2,1)S(1)} %get-tuple-element.74.refs_2_.refs_14_.refs_0_, bf16[1024,1024]{1,0:T(8,128)(2,1)} %collective-permute-done.23, pred[]{:T(512)S(6)} %eq.19), kind=kLoop, calls=%fused_computation | loop fusion | flops 1048576 | bytes 6291457 | tf_op jit(solution)/shard_map/jit(_where)/select_n | solution.py:372
  72.4 1.1 %shard_map.79 = (f32[8,1024]{1,0:T(8,128)S(1)}, f32[8,1024]{1,0:T(8,128)S(1)}, f32[8,1024]{1,0:T(8,128)S(1)}, bf16[8,1024]{1,0:T(8,128)(2,1)S(1)}) custom-call(bf16[8,1024]{1,0:T(8,128)(2,1)S(1)} %collective-permute-done.22.refs_0_, f32[8,1024]{1,0:T(8,128)S(1)} %copy-done.27, bf16[256,1024]{1,0:T(8,128)(2,1)S(1)} %copy-done.7, ...), custom_call_target="tpu_custom_call" | custom-call | flops 1610612736 | bytes 6291456 | tf_op jit(solution)/shard_map/pallas_call | solution.py:203
  73.4 0.7 collective-permute-start.24
  74.1 0.7 collective-permute-start.25
  74.8 0.7 collective-permute-start.27
  75.5 0.7 collective-permute-start.28
  76.1 0.9 shard_map.80
  77.1 1.3 %collective-permute-start.29 = (f32[4,1024]{1,0:T(4,128)S(1)}, f32[4,1024]{1,0:T(4,128)S(1)}, u32[]{:S(2)}, u32[]{:S(2)}) collective-permute-start(f32[4,1024]{1,0:T(4,128)S(1)} %slice.17), channel_id=1, source_target_pairs={{1,0},{3,2},{5,4},{7,6},{9,8},{11,10},{13,12},{15,14},{17,16},{19,... | collective-permute-start | bytes 49160 | tf_op jit(solution)/shard_map/ppermute | solution.py:250
  78.4 17.4 %collective-permute-done.29 = f32[4,1024]{1,0:T(4,128)S(1)} collective-permute-done((f32[4,1024]{1,0:T(4,128)S(1)}, f32[4,1024]{1,0:T(4,128)S(1)}, u32[]{:S(2)}, u32[]{:S(2)}) %collective-permute-start.29) | collective-permute-done | bytes 16416 | tf_op jit(solution)/shard_map/ppermute | solution.py:250
  95.8 0.6 fusion.2
  (93 shorter events, 0.7 us)
Async XLA Ops:
  0.6 4.9 %collective-permute-start.2 = (bf16[1024,1024]{1,0:T(8,128)(2,1)}, bf16[1024,1024]{1,0:T(8,128)(2,1)S(1)}, u32[]{:S(2)}, u32[]{:S(2)}) collective-permute-start(bf16[1024,1024]{1,0:T(8,128)(2,1)} %bitcast.11), channel_id=1, source_target_pairs={{0,1},{1,0},{2,3},{3,2},{4,5},{5,4},{6,7},{7,6},{8,9},{9,8},{10,11... | collective-permute-start | bytes 6291464 | tf_op jit(solution)/shard_map/ppermute | solution.py:250
  1.1 4.4 %collective-permute-start.1 = (s32[8,8]{1,0:T(8,128)}, s32[8,8]{1,0:T(8,128)S(1)}, u32[]{:S(2)}, u32[]{:S(2)}) collective-permute-start(s32[8,8]{1,0:T(8,128)} %bitcast.13), channel_id=1, source_target_pairs={{0,1},{1,0},{2,3},{3,2},{4,5},{5,4},{6,7},{7,6},{8,9},{9,8},{10,11... | collective-permute-start | bytes 776 | tf_op jit(solution)/shard_map/ppermute | solution.py:250
  2.3 1.6 %copy-start.11 = (bf16[1,1024,1024]{2,1,0:T(8,128)(2,1)S(1)}, bf16[1,1024,1024]{2,1,0:T(8,128)(2,1)}, u32[]{:S(2)}) copy-start(bf16[1,1024,1024]{2,1,0:T(8,128)(2,1)} %param.5) | copy-start | bytes 6291460
  3.9 0.7 copy-start.30
  5.5 5.9 %copy-start.31 = (f32[1,4,1024]{2,1,0:T(4,128)S(1)}, f32[1,4,1024]{2,1,0:T(4,128)}, u32[]{:S(2)}) copy-start(f32[1,4,1024]{2,1,0:T(4,128)} %param.9) | copy-start | bytes 49156
  5.6 7.2 %copy-start.35 = (s32[1,1024]{1,0:T(1,128)S(1)}, s32[1,1024]{1,0:T(1,128)}, u32[]{:S(2)}) copy-start(s32[1,1024]{1,0:T(1,128)} %param.8) | copy-start | bytes 12292
  6.9 14.9 %collective-permute-start.4 = (bf16[256,1024]{1,0:T(8,128)(2,1)S(1)}, bf16[256,1024]{1,0:T(8,128)(2,1)S(1)}, u32[]{:S(2)}, u32[]{:S(2)}) collective-permute-start(bf16[256,1024]{1,0:T(8,128)(2,1)S(1)} %get-tuple-element.50.own), channel_id=1, source_target_pairs={{0,3},{2,1},{4,7},{6,5},{8,11},{10,9},{12,15},{14,13},{16,19},{18,... | collective-permute-start | bytes 1572872 | tf_op jit(solution)/shard_map/ppermute | solution.py:250
  11.5 2.1 %collective-permute-start = (f32[4,1024]{1,0:T(4,128)S(1)}, f32[4,1024]{1,0:T(4,128)S(1)}, u32[]{:S(2)}, u32[]{:S(2)}) collective-permute-start(f32[4,1024]{1,0:T(4,128)S(1)} %bitcast.16), channel_id=1, source_target_pairs={{0,1},{2,3},{4,5},{6,7},{8,9},{10,11},{12,13},{14,15},{16,17},{18,... | collective-permute-start | bytes 49160 | tf_op jit(solution)/shard_map/ppermute | solution.py:250
  13.6 0.6 copy-start.33
  15.6 6.2 %collective-permute-start.3 = (f32[9,1024]{1,0:T(8,128)S(1)}, f32[9,1024]{1,0:T(8,128)S(1)}, u32[]{:S(2)}, u32[]{:S(2)}) collective-permute-start(f32[9,1024]{1,0:T(8,128)S(1)} %pad_maximum_fusion.refs_1_.refs_13_), channel_id=1, source_target_pairs={{13,9},{15,11},{25,29},{27,31},{1,5},{3,7}} | collective-permute-start | bytes 110600 | tf_op jit(solution)/shard_map/ppermute | solution.py:250
  16.2 5.5 %collective-permute-start.7 = (f32[9,1024]{1,0:T(8,128)S(1)}, f32[9,1024]{1,0:T(8,128)S(1)}, u32[]{:S(2)}, u32[]{:S(2)}) collective-permute-start(f32[9,1024]{1,0:T(8,128)S(1)} %pad_maximum_fusion.refs_1_.refs_13_), channel_id=1, source_target_pairs={{17,9},{19,11},{21,29},{23,31}} | collective-permute-start | bytes 110600 | tf_op jit(solution)/shard_map/ppermute | solution.py:250
  16.9 11.5 %collective-permute-start.10 = (bf16[256,1024]{1,0:T(8,128)(2,1)S(1)}, bf16[256,1024]{1,0:T(8,128)(2,1)S(1)}, u32[]{:S(2)}, u32[]{:S(2)}) collective-permute-start(bf16[256,1024]{1,0:T(8,128)(2,1)S(1)} %get-tuple-element.57.own), channel_id=1, source_target_pairs={{0,3},{2,1},{4,7},{6,5},{8,11},{10,9},{12,15},{14,13},{16,19},{18,... | collective-permute-start | bytes 1572872 | tf_op jit(solution)/shard_map/ppermute | solution.py:250
  21.8 28.3 %copy-start.20 = (f32[9,1024]{1,0:T(8,128)}, f32[9,1024]{1,0:T(8,128)S(1)}, u32[]{:S(2)}) copy-start(f32[9,1024]{1,0:T(8,128)S(1)} %collective-permute-done.7.refs_9_.refs_1_) | copy-start | bytes 110596
  22.2 8.0 %collective-permute-start.8 = (bf16[256,1024]{1,0:T(8,128)(2,1)S(1)}, bf16[256,1024]{1,0:T(8,128)(2,1)S(1)}, u32[]{:S(2)}, u32[]{:S(2)}) collective-permute-start(bf16[256,1024]{1,0:T(8,128)(2,1)S(1)} %get-tuple-element.54), channel_id=1, source_target_pairs={{13,9},{15,11},{25,29},{27,31},{5,1},{7,3}} | collective-permute-start | bytes 1572872 | tf_op jit(solution)/shard_map/ppermute | solution.py:250
  22.9 11.7 %collective-permute-start.9 = (bf16[256,1024]{1,0:T(8,128)(2,1)S(1)}, bf16[256,1024]{1,0:T(8,128)(2,1)S(1)}, u32[]{:S(2)}, u32[]{:S(2)}) collective-permute-start(bf16[256,1024]{1,0:T(8,128)(2,1)S(1)} %get-tuple-element.54), channel_id=1, source_target_pairs={{17,9},{19,11},{21,29},{23,31}} | collective-permute-start | bytes 1572872 | tf_op jit(solution)/shard_map/ppermute | solution.py:250
  23.7 11.1 %collective-permute-start.5 = (bf16[256,1024]{1,0:T(8,128)(2,1)S(1)}, bf16[256,1024]{1,0:T(8,128)(2,1)S(1)}, u32[]{:S(2)}, u32[]{:S(2)}) collective-permute-start(bf16[256,1024]{1,0:T(8,128)(2,1)S(1)} %get-tuple-element.51.own), channel_id=1, source_target_pairs={{0,3},{2,1},{4,7},{6,5},{8,11},{10,9},{12,15},{14,13},{16,19},{18,... | collective-permute-start | bytes 1572872 | tf_op jit(solution)/shard_map/ppermute | solution.py:250
  28.8 13.5 %collective-permute-start.14 = (bf16[256,1024]{1,0:T(8,128)(2,1)S(1)}, bf16[256,1024]{1,0:T(8,128)(2,1)S(1)}, u32[]{:S(2)}, u32[]{:S(2)}) collective-permute-start(bf16[256,1024]{1,0:T(8,128)(2,1)S(1)} %get-tuple-element.64), channel_id=1, source_target_pairs={{13,9},{15,11},{25,29},{27,31},{5,1},{7,3}} | collective-permute-start | bytes 1572872 | tf_op jit(solution)/shard_map/ppermute | solution.py:250
  29.5 12.8 %collective-permute-start.15 = (bf16[256,1024]{1,0:T(8,128)(2,1)S(1)}, bf16[256,1024]{1,0:T(8,128)(2,1)S(1)}, u32[]{:S(2)}, u32[]{:S(2)}) collective-permute-start(bf16[256,1024]{1,0:T(8,128)(2,1)S(1)} %get-tuple-element.64), channel_id=1, source_target_pairs={{17,9},{19,11},{21,29},{23,31}} | collective-permute-start | bytes 1572872 | tf_op jit(solution)/shard_map/ppermute | solution.py:250
  30.3 8.3 %collective-permute-start.13 = (bf16[128,1024]{1,0:T(8,128)(2,1)S(1)}, bf16[128,1024]{1,0:T(8,128)(2,1)S(1)}, u32[]{:S(2)}, u32[]{:S(2)}) collective-permute-start(bf16[128,1024]{1,0:T(8,128)(2,1)S(1)} %get-tuple-element.63.own), channel_id=1, source_target_pairs={{0,3},{2,1},{4,7},{6,5},{8,11},{10,9},{12,15},{14,13},{16,19},{18,... | collective-permute-start | bytes 786440 | tf_op jit(solution)/shard_map/ppermute | solution.py:250
  34.7 15.3 %copy-start = (bf16[256,1024]{1,0:T(8,128)(2,1)}, bf16[256,1024]{1,0:T(8,128)(2,1)S(1)}, u32[]{:S(2)}) copy-start(bf16[256,1024]{1,0:T(8,128)(2,1)S(1)} %collective-permute-done.9.refs_11_.refs_3_) | copy-start | bytes 1572868
  35.2 11.1 %collective-permute-start.11 = (bf16[256,1024]{1,0:T(8,128)(2,1)S(1)}, bf16[256,1024]{1,0:T(8,128)(2,1)S(1)}, u32[]{:S(2)}, u32[]{:S(2)}) collective-permute-start(bf16[256,1024]{1,0:T(8,128)(2,1)S(1)} %get-tuple-element.60), channel_id=1, source_target_pairs={{13,9},{15,11},{25,29},{27,31},{5,1},{7,3}} | collective-permute-start | bytes 1572872 | tf_op jit(solution)/shard_map/ppermute | solution.py:250
  35.9 10.4 %collective-permute-start.12 = (bf16[256,1024]{1,0:T(8,128)(2,1)S(1)}, bf16[256,1024]{1,0:T(8,128)(2,1)S(1)}, u32[]{:S(2)}, u32[]{:S(2)}) collective-permute-start(bf16[256,1024]{1,0:T(8,128)(2,1)S(1)} %get-tuple-element.60), channel_id=1, source_target_pairs={{17,9},{19,11},{21,29},{23,31}} | collective-permute-start | bytes 1572872 | tf_op jit(solution)/shard_map/ppermute | solution.py:250
  38.6 7.7 %collective-permute-start.6 = (bf16[128,1024]{1,0:T(8,128)(2,1)S(1)}, bf16[128,1024]{1,0:T(8,128)(2,1)S(1)}, u32[]{:S(2)}, u32[]{:S(2)}) collective-permute-start(bf16[128,1024]{1,0:T(8,128)(2,1)S(1)} %get-tuple-element.52.own), channel_id=1, source_target_pairs={{0,3},{2,1},{4,7},{6,5},{8,11},{10,9},{12,15},{14,13},{16,19},{18,... | collective-permute-start | bytes 786440 | tf_op jit(solution)/shard_map/ppermute | solution.py:250
  42.4 7.7 %copy-start.5 = (bf16[256,1024]{1,0:T(8,128)(2,1)}, bf16[256,1024]{1,0:T(8,128)(2,1)S(1)}, u32[]{:S(2)}) copy-start(bf16[256,1024]{1,0:T(8,128)(2,1)S(1)} %collective-permute-done.15.refs_10_.refs_2_) | copy-start | bytes 1572868
  42.8 7.2 %collective-permute-start.17 = (bf16[128,1024]{1,0:T(8,128)(2,1)S(1)}, bf16[128,1024]{1,0:T(8,128)(2,1)S(1)}, u32[]{:S(2)}, u32[]{:S(2)}) collective-permute-start(bf16[128,1024]{1,0:T(8,128)(2,1)S(1)} %get-tuple-element.70), channel_id=1, source_target_pairs={{13,9},{15,11},{25,29},{27,31},{5,1},{7,3}} | collective-permute-start | bytes 786440 | tf_op jit(solution)/shard_map/ppermute | solution.py:250
  43.5 6.5 %collective-permute-start.19 = (bf16[128,1024]{1,0:T(8,128)(2,1)S(1)}, bf16[128,1024]{1,0:T(8,128)(2,1)S(1)}, u32[]{:S(2)}, u32[]{:S(2)}) collective-permute-start(bf16[128,1024]{1,0:T(8,128)(2,1)S(1)} %get-tuple-element.70), channel_id=1, source_target_pairs={{17,9},{19,11},{21,29},{23,31}} | collective-permute-start | bytes 786440 | tf_op jit(solution)/shard_map/ppermute | solution.py:250
  46.2 3.8 %copy-start.3 = (bf16[256,1024]{1,0:T(8,128)(2,1)}, bf16[256,1024]{1,0:T(8,128)(2,1)S(1)}, u32[]{:S(2)}) copy-start(bf16[256,1024]{1,0:T(8,128)(2,1)S(1)} %collective-permute-done.11.refs_6_.refs_10_.refs_3_) | copy-start | bytes 1572868
  46.2 3.8 %copy-start.8 = (bf16[256,1024]{1,0:T(8,128)(2,1)}, bf16[256,1024]{1,0:T(8,128)(2,1)S(1)}, u32[]{:S(2)}) copy-start(bf16[256,1024]{1,0:T(8,128)(2,1)S(1)} %collective-permute-done.12.refs_12_.refs_4_) | copy-start | bytes 1572868
  46.6 3.4 %collective-permute-start.18 = (bf16[128,1024]{1,0:T(8,128)(2,1)S(1)}, bf16[128,1024]{1,0:T(8,128)(2,1)S(1)}, u32[]{:S(2)}, u32[]{:S(2)}) collective-permute-start(bf16[128,1024]{1,0:T(8,128)(2,1)S(1)} %get-tuple-element.71), channel_id=1, source_target_pairs={{13,9},{15,11},{25,29},{27,31},{5,1},{7,3}} | collective-permute-start | bytes 786440 | tf_op jit(solution)/shard_map/ppermute | solution.py:250
  47.3 2.7 %collective-permute-start.20 = (bf16[128,1024]{1,0:T(8,128)(2,1)S(1)}, bf16[128,1024]{1,0:T(8,128)(2,1)S(1)}, u32[]{:S(2)}, u32[]{:S(2)}) collective-permute-start(bf16[128,1024]{1,0:T(8,128)(2,1)S(1)} %get-tuple-element.71), channel_id=1, source_target_pairs={{17,9},{19,11},{21,29},{23,31}} | collective-permute-start | bytes 786440 | tf_op jit(solution)/shard_map/ppermute | solution.py:250
  48.7 0.6 copy-start.28
  49.3 0.7 collective-permute-start.16
  50.0 2.8 %copy-start.14 = (bf16[128,1024]{1,0:T(8,128)(2,1)}, bf16[128,1024]{1,0:T(8,128)(2,1)S(1)}, u32[]{:S(2)}) copy-start(bf16[128,1024]{1,0:T(8,128)(2,1)S(1)} %collective-permute-done.19.refs_13_.refs_5_) | copy-start | bytes 786436
  50.0 2.7 %copy-start.12 = (bf16[128,1024]{1,0:T(8,128)(2,1)}, bf16[128,1024]{1,0:T(8,128)(2,1)S(1)}, u32[]{:S(2)}) copy-start(bf16[128,1024]{1,0:T(8,128)(2,1)S(1)} %collective-permute-done.18.refs_8_.refs_12_.refs_5_) | copy-start | bytes 786436
  50.1 2.7 %copy-start.17 = (bf16[128,1024]{1,0:T(8,128)(2,1)}, bf16[128,1024]{1,0:T(8,128)(2,1)S(1)}, u32[]{:S(2)}) copy-start(bf16[128,1024]{1,0:T(8,128)(2,1)S(1)} %collective-permute-done.20.refs_14_.refs_6_) | copy-start | bytes 786436
  53.9 0.6 copy-start.26
  54.5 14.5 %collective-permute-start.23 = (bf16[1024,1024]{1,0:T(8,128)(2,1)S(1)}, bf16[1024,1024]{1,0:T(8,128)(2,1)}, u32[]{:S(2)}, u32[]{:S(2)}) collective-permute-start(bf16[1024,1024]{1,0:T(8,128)(2,1)S(1)} %get-tuple-element.74.refs_2_.refs_14_.refs_0_), channel_id=1, source_target_pairs={{1,0},{3,2},{5,4},{7,6},{9,8},{11,10},{13,12},{15,14},{17,16},{19,... | collective-permute-start | bytes 6291464 | tf_op jit(solution)/shard_map/ppermute | solution.py:250
  55.8 0.7 collective-permute-start.21
  56.5 1.0 %copy-start.1 = (bf16[256,1024]{1,0:T(8,128)(2,1)S(1)}, bf16[256,1024]{1,0:T(8,128)(2,1)}, u32[]{:S(2)}) copy-start(bf16[256,1024]{1,0:T(8,128)(2,1)} %copy-done) | copy-start | bytes 1572868
  57.6 1.0 %copy-start.4 = (bf16[256,1024]{1,0:T(8,128)(2,1)S(1)}, bf16[256,1024]{1,0:T(8,128)(2,1)}, u32[]{:S(2)}) copy-start(bf16[256,1024]{1,0:T(8,128)(2,1)} %copy-done.3) | copy-start | bytes 1572868
  58.6 1.0 %copy-start.6 = (bf16[256,1024]{1,0:T(8,128)(2,1)S(1)}, bf16[256,1024]{1,0:T(8,128)(2,1)}, u32[]{:S(2)}) copy-start(bf16[256,1024]{1,0:T(8,128)(2,1)} %copy-done.5) | copy-start | bytes 1572868
  59.7 1.0 %copy-start.9 = (bf16[256,1024]{1,0:T(8,128)(2,1)S(1)}, bf16[256,1024]{1,0:T(8,128)(2,1)}, u32[]{:S(2)}) copy-start(bf16[256,1024]{1,0:T(8,128)(2,1)} %copy-done.8) | copy-start | bytes 1572868
  60.7 0.9 copy-start.13
  61.7 0.9 copy-start.15
  62.6 0.9 copy-start.18
  63.6 0.8 copy-start.21
  64.4 3.1 %copy-start.29 = (f32[8,1024]{1,0:T(8,128)S(1)}, f32[8,1024]{1,0:T(8,128)}, u32[]{:S(2)}) copy-start(f32[8,1024]{1,0:T(8,128)} %copy-done.28) | copy-start | bytes 98308
  64.4 3.8 %copy-start.32 = (f32[1,4,1024]{2,1,0:T(4,128)S(1)}, f32[1,4,1024]{2,1,0:T(4,128)}, u32[]{:S(2)}) copy-start(f32[1,4,1024]{2,1,0:T(4,128)} %param.9) | copy-start | bytes 49156
  64.4 3.8 %copy-start.34 = (f32[4,1024]{1,0:T(4,128)S(1)}, f32[4,1024]{1,0:T(4,128)}, u32[]{:S(2)}) copy-start(f32[4,1024]{1,0:T(4,128)} %copy-done.33) | copy-start | bytes 49156
  67.5 1.4 %collective-permute-start.26 = (f32[8,1024]{1,0:T(8,128)S(1)}, f32[8,1024]{1,0:T(8,128)S(1)}, u32[]{:S(2)}, u32[]{:S(2)}) collective-permute-start(f32[8,1024]{1,0:T(8,128)S(1)} %copy-done.29), channel_id=1, source_target_pairs={{5,1},{7,3}} | collective-permute-start | bytes 98312 | tf_op jit(solution)/shard_map/ppermute | solution.py:250
  68.2 4.1 %collective-permute-start.22 = (bf16[8,1024]{1,0:T(8,128)(2,1)S(1)}, bf16[8,1024]{1,0:T(8,128)(2,1)S(1)}, u32[]{:S(2)}, u32[]{:S(2)}) collective-permute-start(bf16[8,1024]{1,0:T(8,128)(2,1)S(1)} %get-tuple-element.73), channel_id=1, source_target_pairs={{29,9},{31,11}} | collective-permute-start | bytes 49160 | tf_op jit(solution)/shard_map/ppermute | solution.py:250
  68.9 3.4 %copy-start.2 = (bf16[256,1024]{1,0:T(8,128)(2,1)S(1)}, bf16[256,1024]{1,0:T(8,128)(2,1)}, u32[]{:S(2)}) copy-start(bf16[256,1024]{1,0:T(8,128)(2,1)} %copy-done) | copy-start | bytes 1572868
  68.9 3.4 %copy-start.7 = (bf16[256,1024]{1,0:T(8,128)(2,1)S(1)}, bf16[256,1024]{1,0:T(8,128)(2,1)}, u32[]{:S(2)}) copy-start(bf16[256,1024]{1,0:T(8,128)(2,1)} %copy-done.5) | copy-start | bytes 1572868
  68.9 3.4 %copy-start.10 = (bf16[256,1024]{1,0:T(8,128)(2,1)S(1)}, bf16[256,1024]{1,0:T(8,128)(2,1)}, u32[]{:S(2)}) copy-start(bf16[256,1024]{1,0:T(8,128)(2,1)} %copy-done.8) | copy-start | bytes 1572868
  69.0 3.4 %copy-start.16 = (bf16[128,1024]{1,0:T(8,128)(2,1)S(1)}, bf16[128,1024]{1,0:T(8,128)(2,1)}, u32[]{:S(2)}) copy-start(bf16[128,1024]{1,0:T(8,128)(2,1)} %copy-done.14) | copy-start | bytes 786436
  69.0 3.4 %copy-start.19 = (bf16[128,1024]{1,0:T(8,128)(2,1)S(1)}, bf16[128,1024]{1,0:T(8,128)(2,1)}, u32[]{:S(2)}) copy-start(bf16[128,1024]{1,0:T(8,128)(2,1)} %copy-done.17) | copy-start | bytes 786436
  69.0 3.4 %copy-start.23 = (f32[8,1024]{1,0:T(8,128)S(1)}, f32[8,1024]{1,0:T(8,128)}, u32[]{:S(2)}) copy-start(f32[8,1024]{1,0:T(8,128)} %copy-done.22) | copy-start | bytes 98308
  69.0 3.4 %copy-start.25 = (f32[8,1024]{1,0:T(8,128)S(1)}, f32[8,1024]{1,0:T(8,128)}, u32[]{:S(2)}) copy-start(f32[8,1024]{1,0:T(8,128)} %copy-done.24) | copy-start | bytes 98308
  69.0 3.4 %copy-start.27 = (f32[8,1024]{1,0:T(8,128)S(1)}, f32[8,1024]{1,0:T(8,128)}, u32[]{:S(2)}) copy-start(f32[8,1024]{1,0:T(8,128)} %copy-done.26) | copy-start | bytes 98308
  73.4 2.7 %collective-permute-start.24 = (bf16[8,1024]{1,0:T(8,128)(2,1)S(1)}, bf16[8,1024]{1,0:T(8,128)(2,1)S(1)}, u32[]{:S(2)}, u32[]{:S(2)}) collective-permute-start(bf16[8,1024]{1,0:T(8,128)(2,1)S(1)} %get-tuple-element.81), channel_id=1, source_target_pairs={{9,1},{11,3}} | collective-permute-start | bytes 49160 | tf_op jit(solution)/shard_map/ppermute | solution.py:250
  74.1 2.1 %collective-permute-start.25 = (bf16[8,1024]{1,0:T(8,128)(2,1)S(1)}, bf16[8,1024]{1,0:T(8,128)(2,1)S(1)}, u32[]{:S(2)}, u32[]{:S(2)}) collective-permute-start(bf16[8,1024]{1,0:T(8,128)(2,1)S(1)} %get-tuple-element.81), channel_id=1, source_target_pairs={{9,5},{11,7}} | collective-permute-start | bytes 49160 | tf_op jit(solution)/shard_map/ppermute | solution.py:250
  74.8 2.3 %collective-permute-start.27 = (f32[8,1024]{1,0:T(8,128)S(1)}, f32[8,1024]{1,0:T(8,128)S(1)}, u32[]{:S(2)}, u32[]{:S(2)}) collective-permute-start(f32[8,1024]{1,0:T(8,128)S(1)} %select_select_fusion.1), channel_id=1, source_target_pairs={{9,13},{11,15},{29,25},{31,27}} | collective-permute-start | bytes 98312 | tf_op jit(solution)/shard_map/ppermute | solution.py:250
  75.5 1.6 %collective-permute-start.28 = (f32[8,1024]{1,0:T(8,128)S(1)}, f32[8,1024]{1,0:T(8,128)S(1)}, u32[]{:S(2)}, u32[]{:S(2)}) collective-permute-start(f32[8,1024]{1,0:T(8,128)S(1)} %select_select_fusion), channel_id=1, source_target_pairs={{9,17},{11,19},{29,21},{31,23}} | collective-permute-start | bytes 98312 | tf_op jit(solution)/shard_map/ppermute | solution.py:250
  77.1 18.7 %collective-permute-start.29 = (f32[4,1024]{1,0:T(4,128)S(1)}, f32[4,1024]{1,0:T(4,128)S(1)}, u32[]{:S(2)}, u32[]{:S(2)}) collective-permute-start(f32[4,1024]{1,0:T(4,128)S(1)} %slice.17), channel_id=1, source_target_pairs={{1,0},{3,2},{5,4},{7,6},{9,8},{11,10},{13,12},{15,14},{17,16},{19,... | collective-permute-start | bytes 49160 | tf_op jit(solution)/shard_map/ppermute | solution.py:250
  (2 other events, 1.2 us)

commit v4 on v3

--- a/solution.py
+++ b/solution.py
@@ -8,12 +8,11 @@
 from jax.sharding import PartitionSpec as P
 
 AXES = ("layer", "box")
-LAST_PIECES = ((0, 256), (256, 256), (512, 256), (768, 128), (896, 128))
-Y_TIE = 2
-X_TIE = 2
+AHEAD = 2
+SMALL_AT = 0
 VMEM = pl.BlockSpec(memory_space=pltpu.VMEM)
 SMEM = pl.BlockSpec(memory_space=pltpu.SMEM)
-PARAMS = pltpu.CompilerParams(vmem_limit_bytes=24 * 1024 * 1024)
+PARAMS = pltpu.CompilerParams(vmem_limit_bytes=10 * 1024 * 1024)
 OWN, PAIR, EXTRA = 0, 1, 2
 
 
@@ -104,8 +103,9 @@
     )(other_pattern, own, other, inverse, *extra)
 
 
-def combine_kernel(face_at, is_face, whole_rows, own, other, inverse, *refs):
+def combine_kernel(face_at, is_face, with_next, whole_rows, is_second, own, other, inverse, *refs):
     refs = list(refs)
+    following = refs.pop(0) if with_next else None
     joined = 0.5 * (own[...].astype(jnp.float32) + other[...].astype(jnp.float32))
     if is_face:
         right = joined.astype(jnp.bfloat16)
@@ -113,27 +113,40 @@
         right = refs.pop(0)[...]
         refs.pop(0)
     piece = minus_face(joined, face_at, inverse[...], right)
-    refs[0][...] = piece
     refs[1][whole_rows, :] = piece
     if is_face:
         refs[2][...] = right
-
-
-def combine(own, other, inverse, state, face_at, row_at):
+    refs[0][...] = piece
+    if with_next:
+
+        @pl.when(is_second[0] == 0)
+        def _():
+            refs[0][...] = following[...]
+
+
+def combine(is_second, own, other, inverse, following, state, face_at, row_at):
     is_face = state is None
     rows, width = own.shape
-    extra = [] if is_face else list(state)
+    extra = [] if following is None else [following]
+    aliases = {} if is_face else {4 + len(extra) + 1: 1}
+    extra += [] if is_face else list(state)
     piece = jax.ShapeDtypeStruct((rows, width), jnp.bfloat16)
     whole = jax.ShapeDtypeStruct((width, width), jnp.bfloat16)
     result = pl.pallas_call(
-        functools.partial(combine_kernel, face_at, is_face, slice(row_at, row_at + rows)),
+        functools.partial(
+            combine_kernel,
+            face_at,
+            is_face,
+            following is not None,
+            slice(row_at, row_at + rows),
+        ),
         out_shape=[piece, whole] + ([piece] if is_face else []),
-        in_specs=[VMEM] * (3 + len(extra)),
+        in_specs=[SMEM] + [VMEM] * (3 + len(extra)),
         out_specs=[VMEM] * (3 if is_face else 2),
-        input_output_aliases={} if is_face else {4: 1},
+        input_output_aliases=aliases,
         compiler_params=PARAMS,
         cost_estimate=cost(0, 0),
-    )(own, other, inverse, *extra)
+    )(is_second, own, other, inverse, *extra)
     return result[0], ((result[2] if is_face else state[0]), result[1])
 
 
@@ -231,21 +244,22 @@
     rows_here = sources.shape[1]
     position = lax.axis_index("box")
     layer = lax.axis_index("layer")
-    is_lead = position % 2 == 1
-    pairs = layers // 2
-
-    chain = []
-    for p in range(1, pairs, 3):
-        chain.append((2 * p, (OWN, PAIR, EXTRA)))
-        chain.append((2 * (p + 2) + 1, (EXTRA, PAIR, OWN)))
-
-    def route(moves, source_core=1, target_core=1):
+    is_second = position % 2 == 1
+    second_flag = is_second.astype(jnp.int32)[None]
+
+    chain = [(layer_at, (OWN, PAIR)) for layer_at in range(2, layers, 2)]
+    pair_moves = [(layer_at + 1, layer_at) for layer_at in range(0, layers, 2)]
+
+    def route(moves, source_core=0, target_core=0):
         return [
             (a * boxes + b + source_core, z * boxes + b + target_core)
             for a, z in moves
             for b in range(0, boxes, 2)
         ]
 
+    def over_box(change, starts):
+        return [(i * boxes + b, i * boxes + (b ^ change)) for i in range(layers) for b in starts]
+
     def send(value, pairs_of_devices):
         return lax.ppermute(value, AXES, pairs_of_devices)
 
@@ -253,17 +267,12 @@
         return lax.optimization_barrier((value, *others))[0]
 
     every = [(i, i) for i in range(layers)]
-    pair_moves = [(at ^ 1, at) for at, _ in chain]
-    extra_moves = [(at + 2 if at % 2 == 0 else at - 2, at) for at, _ in chain]
-
-    def over_box(change, starts):
-        return [(i * boxes + b, i * boxes + (b ^ change)) for i in range(layers) for b in starts]
 
     raw = box_maps[0]
     pattern = block_pattern[0]
     raw_other = send(raw, over_box(1, range(boxes)))
     pattern_other = send(pattern, over_box(1, range(boxes)))
-    next_sources = send(sources[0], route(every, 0, 1))
+    other_sources = send(sources[0], over_box(1, range(boxes)))
     own_half = pl.pallas_call(
         mask_kernel,
         out_shape=jax.ShapeDtypeStruct(raw.shape, jnp.bfloat16),
@@ -271,7 +280,7 @@
         out_specs=VMEM,
         compiler_params=PARAMS,
         cost_estimate=cost(width * width, 4 * width * width),
-    )(pattern, raw)
+    )(after(pattern, other_sources), raw)
 
     def inverse_of(level):
         node = (boxes >> (level + 1)) - 1 + (position >> (level + 1))
@@ -279,84 +288,93 @@
             jnp.bfloat16
         )
 
-    whole_faces = tuple((at, face) for at in range(0, width, face))
-    last_face = (levels - 1) * face
-    if last_face == face:
-        parts = LAST_PIECES
-    else:
-        parts = whole_faces
-    cuts = [tuple(parts)] if levels == 2 else [whole_faces] * (levels - 1)
-
-    inverse = inverse_of(0)
-    half = width // 2
-    upper = tuple(piece for piece in cuts[0] if piece[0] < half)
-    lower = tuple(piece for piece in cuts[0] if piece[0] >= half)
-    top = leaf_combine(pattern_other, own_half, raw_other, inverse, None, 0, upper)
-    bottom = leaf_combine(pattern_other, own_half, raw_other, inverse, top[-1], 1, lower)
-    current = dict(zip(upper + lower, [*top[:-1], *bottom]))
-
     rows = -(-2 * rows_here // 8) * 8
     packed = jnp.concatenate(
         [
-            next_sources,
-            sources[0],
+            jnp.where(is_second, other_sources, sources[0]),
+            jnp.where(is_second, sources[0], other_sources),
             jnp.zeros((rows - 2 * rows_here, width), jnp.float32),
             index_map.astype(jnp.float32),
         ],
         axis=0,
     )
-    sendable = after(packed, bottom[0])
-    small = [
-        packed,
-        send(sendable, route(pair_moves + [(0, 1)])),
-        send(sendable, route(extra_moves)),
-    ]
-
-    maps = [[], [], []]
+
+    pieces = tuple((at, face) for at in range(0, width, face))
+    upper = tuple(piece for piece in pieces if piece[0] < width // 2)
+    lower = tuple(piece for piece in pieces if piece[0] >= width // 2)
+    inverse = inverse_of(0)
+    top = leaf_combine(pattern_other, own_half, raw_other, inverse, None, 0, upper)
+    bottom = leaf_combine(pattern_other, own_half, raw_other, inverse, top[-1], 1, lower)
+    current = dict(zip(upper + lower, [*top[:-1], *bottom]))
+
     for level in range(1, levels):
         final = level == levels - 1
         change = 1 << level
-        if final:
-            moves = over_box(change ^ 1, range(0, boxes, 2))
-        else:
-            moves = over_box(change, range(boxes))
         inverse = inverse_of(level)
-        order = sorted(current, key=lambda piece: (piece[0] != level * face, piece[0]))
+        order = sorted(pieces, key=lambda piece: (piece[0] != level * face, piece[0]))
         received = {}
+        state = None
+        if not final:
+            for piece in order:
+                received[piece] = send(current[piece], over_box(change, range(boxes)))
+            renewed = {}
+            for piece in order:
+                renewed[piece], state = combine(
+                    second_flag,
+                    current[piece],
+                    received[piece],
+                    inverse,
+                    None,
+                    state,
+                    level * face,
+                    piece[0],
+                )
+            current = renewed
+            continue
+        over = over_box(change ^ 1, range(0, boxes, 2))
+        forward = route(pair_moves, 1, 0)
+        for piece in order[:AHEAD]:
+            received[piece] = send(current[piece], over)
+        pair_pieces = {}
         for k, piece in enumerate(order):
-            value = current[piece]
-            if k >= Y_TIE:
-                value = after(value, received[order[k - Y_TIE]])
-            received[piece] = send(value, moves)
-        state = None
-        sent = {PAIR: {}, EXTRA: {}}
-        renewed = {}
-        for k, piece in enumerate(order):
+            following = order[k + AHEAD] if k + AHEAD < len(order) else None
             other = received[piece]
-            if final and k == 0:
-                other = after(other, small[PAIR], small[EXTRA])
-            if final and k >= X_TIE:
-                before = order[k - X_TIE]
-                other = after(other, sent[PAIR][before], sent[EXTRA][before])
-            renewed[piece], state = combine(
-                current[piece], other, inverse, state, level * face, piece[0]
+            if k == SMALL_AT + 2:
+                other = after(other, pair_packed)
+            if k > AHEAD:
+                other = after(other, pair_pieces[order[k - 1]])
+            payload, state = combine(
+                second_flag,
+                current[piece],
+                other,
+                inverse,
+                None if following is None else current[following],
+                state,
+                level * face,
+                piece[0],
             )
-            if final:
-                sent[PAIR][piece] = send(renewed[piece], route(pair_moves + [(1, 0)]))
-                sent[EXTRA][piece] = send(renewed[piece], route(extra_moves))
-        current = renewed
+            pair_pieces[piece] = send(payload, forward + ([] if following is None else over))
+            if following is not None:
+                received[following] = pair_pieces[piece]
+            if k == SMALL_AT:
+                sendable = after(packed, payload)
+                pair_packed = send(sendable, route(pair_moves[1:]) + route([(0, 1)], 1, 1))
     merged = state[1]
-    inner = sorted(current)
-    maps = [[merged]] + [[sent[slot][piece] for piece in inner] for slot in (PAIR, EXTRA)]
-
-    first = small[PAIR][:rows].astype(jnp.bfloat16)
-    (down_odd,), state = segment(coupling, first, small, {}, maps, (OWN,), ())
-    at = 1
+    small = [packed, pair_packed]
+    pair_maps = [pair_pieces[piece] for piece in pieces]
+
+    first = pair_packed[:rows].astype(jnp.bfloat16)
+    (down_odd,), state = segment(
+        coupling, first, small, {}, [[merged], pair_maps], (OWN,), ()
+    )
+    merged_first = send(after(merged, state), route(every, 1, 0))
+    maps = [[merged_first], pair_maps]
+    at, core = 1, 1
     kept = []
     ups = {}
     for k, (target, slots) in enumerate(chain):
-        arrived = send(state, route([(at, target)]))
-        at = target
+        arrived = send(state, route([(at, target)], core, 0))
+        at, core = target, 0
         turn = k == len(chain) - 1
         back = tuple(reversed(slots))
         results, state = segment(
@@ -364,12 +382,12 @@
         )
         kept.append(dict(zip(slots, results)))
         if k == 0:
-            copied = send(after(merged, state), route(every, 1, 0))
+            down_odd_first = send(after(down_odd, state), route([(1, 0)], 1, 0))
         if turn:
             ups[at] = dict(zip(back[1:], results[len(slots) :]))
             ups[at][back[0]] = results[len(slots) - 1]
-    down_odd = jnp.where(layer == 0, send(after(down_odd, state), route([(1, 0)])), down_odd)
-    merged = jnp.where(is_lead, merged, after(copied, state))
+    merged = jnp.where(is_second, merged, merged_first)
+    down_odd = jnp.where(layer == 0, down_odd_first, down_odd)
 
     for k in reversed(range(len(chain) - 1)):
         target, slots = chain[k]
@@ -380,32 +398,33 @@
         back = tuple(reversed(slots))
         results, state = segment(coupling, arrived, small, kept[k], maps, (), back)
         ups[at] = dict(zip(back, results))
+    from_own = send(state, route([(at, 1)], 0, 1))
     from_pair = send(state, route([(at, 0)]))
-    from_own = send(state, route([(at, 1)]))
-
-    mine = [jnp.zeros((rows, width), jnp.float32)] * 3
+
+    mine = [jnp.zeros((rows, width), jnp.float32)] * 2
     for target, values in ups.items():
-        for slot in (OWN, PAIR, EXTRA):
+        for slot in (OWN, PAIR):
             mine[slot] = jnp.where(layer == target, values[slot], mine[slot])
-    settled = (
-        mine[OWN]
-        + send(mine[PAIR], route([(z, a) for a, z in pair_moves]))
-        + send(mine[EXTRA], route([(z, a) for a, z in extra_moves]))
-    )
+    settled = mine[OWN] + send(mine[PAIR], route([(z, a) for a, z in pair_moves[1:]]))
 
     odd = (layer % 2).astype(jnp.int32)[None]
     last = pl.pallas_call(
-        functools.partial(last_kernel, coupling, len(inner)),
+        functools.partial(last_kernel, coupling, len(pair_maps)),
         out_shape=jax.ShapeDtypeStruct((rows, width), jnp.float32),
-        in_specs=[SMEM] + [VMEM] * (5 + len(inner)),
+        in_specs=[SMEM] + [VMEM] * (5 + len(pair_maps)),
         out_specs=VMEM,
         compiler_params=PARAMS,
         cost_estimate=cost(6 * 256 * 1024 * 1024, 6 * 1024 * 1024),
-    )(odd, from_pair, from_own, packed[:rows], down_odd, *maps[OWN], *maps[PAIR])
+    )(odd, from_pair, from_own, packed[:rows], down_odd, merged, *pair_maps)
     upward = jnp.where(layer < 2, last, settled)
-    lead_rows = upward[rows_here : 2 * rows_here]
-    upward = jnp.where(is_lead, lead_rows, send(upward[:rows_here], route(every, 1, 0)))
-    return (merged[None], upward[None])
+    ends = upward[:rows_here], upward[rows_here : 2 * rows_here]
+    there = send(
+        jnp.where(is_second, ends[0], ends[1]),
+        route([(1, 1)], 1, 0) + route([move for move in every if move[0] != 1], 0, 1),
+    )
+    here = jnp.where(is_second, ends[1], ends[0])
+    runs = jnp.logical_xor(is_second, layer != 1)
+    return (merged[None], jnp.where(runs, here, there)[None])
 
 
 def solution(mesh):

time: 98.3 us -> 96.6 us (0.983); the launches traced: 96.4 us -> 95.8 us
  waiting for transfers between devices: 25.1 us -> 40.8 us
  starting transfers between devices: 37.5 us -> 29.1 us
  local copies, waits for them, and re-layouts: 14.3 us -> 7.43 us
  other arithmetic: 3.95 us -> 0.91 us
  Pallas kernels: 14.1 us -> 16.5 us
    ppermute x30 -> x21, waiting for transfers between devices: 25.1 us -> 40.8 us  [send(): return lax.ppermute(value, AXES, pairs_of_devices)]
    ppermute x30 -> x21, starting transfers between devices: 37.5 us -> 29.1 us  [send(): return lax.ppermute(value, AXES, pairs_of_devices)]
    unnamed x72 -> x30, local copies, waits for them, and re-layouts: 13.2 us -> 6.37 us
    select_n x2 -> x4, other arithmetic: 3.27 us -> 0.24 us  [the longest x1 0.22 us: on_device(): merged = jnp.where(is_second, merged, merged_first)]
    pallas_call x2, Pallas kernels: 2.66 us -> 4.7 us  [leaf_combine(): pl.pallas_call(functools.partial(leaf_kernel, half * rows, is_face, piece...]
    pallas_call x6 -> x5, Pallas kernels: 3.01 us -> 3.98 us  [the longest x4 3.03 us: combine(): pl.pallas_call(functools.partial(combine_kernel, face_at, is_face, follow...]
    pallas_call x4 -> x6, Pallas kernels: 7.49 us -> 6.86 us  [segment(): pl.pallas_call(functools.partial(segment_kernel, coupling, [len(entry) fo...]
  transfers between devices with their start and end apart: 30 -> 21, of which waited for: 5 -> 8; matrix products, arithmetic and copies ran while one was open for 5% -> 1% of each run, Pallas kernels for 9% -> 10%
where the time goes in v4:
time: 96.6 us; the launch traced here: 95.8 us
  waiting for transfers between devices  40.8 us (42%)
  starting transfers between devices  29.1 us (30%)
  Pallas kernels  16.5 us (17%)
  local copies, waits for them, and re-layouts  7.43 us (8%)
  between operations  1.11 us (1%)
    ppermute x21, waiting for transfers between devices, send(): return lax.ppermute(value, AXES, pairs_of_devices)  40.8 us
    ppermute x21, starting transfers between devices, send(): return lax.ppermute(value, AXES, pairs_of_devices)  29.1 us
    pallas_call x6, Pallas kernels, segment(): pl.pallas_call(functools.partial(segment_kernel, coupling, [len(entry) fo...  6.86 us
    unnamed x30, local copies, waits for them, and re-layouts  6.37 us
    pallas_call x2, Pallas kernels, leaf_combine(): pl.pallas_call(functools.partial(leaf_kernel, half * rows, is_face, piece...  4.7 us
    pallas_call x4, Pallas kernels, combine(): pl.pallas_call(functools.partial(combine_kernel, face_at, is_face, follow...  3.03 us
  transfers between devices with their start and end apart: 21, of which 8 were waited for; matrix products, arithmetic and copies ran while one was open for 1% of the time, Pallas kernels for 10%

profile of v4, /device:TPU:0, one launch (start us, length us, event | category | flops | bytes accessed | tf_op | source)
XLA Modules:
  0.0 95.8 jit_solution(8885060740840733369)
XLA Ops:
  0.6 0.5 collective-permute-start.2
  1.1 0.1 collective-permute-start
  1.2 0.4 collective-permute-start.1
  1.7 1.1 %fusion.1 = (bf16[256,256]{1,0:T(8,128)(2,1)S(1)}, bf16[256,256]{1,0:T(8,128)(2,1)S(1)}) fusion(f32[1,3,256,256]{3,2,1,0:T(8,128)} %param.7, s32[]{:T(128)S(6)} %select_n.101, s32[]{:T(128)S(6)} %select_n.100), kind=kLoop, calls=%fused_computation.4 | loop fusion | bytes 524296 | tf_op jit(solution)/shard_map/convert_element_type | solution.py:287
  2.7 2.4 %collective-permute-done = f32[4,1024]{1,0:T(4,128)S(1)} collective-permute-done((f32[4,1024]{1,0:T(4,128)}, f32[4,1024]{1,0:T(4,128)S(1)}, u32[]{:S(2)}, u32[]{:S(2)}) %collective-permute-start) | collective-permute-done | bytes 16416 | tf_op jit(solution)/shard_map/ppermute | solution.py:264
  5.1 1.6 %copy-done.9 = bf16[1,1024,1024]{2,1,0:T(8,128)(2,1)S(1)} copy-done((bf16[1,1024,1024]{2,1,0:T(8,128)(2,1)S(1)}, bf16[1,1024,1024]{2,1,0:T(8,128)(2,1)}, u32[]{:S(2)}) %copy-start.9) | copy-done | bytes 2097176
  6.7 0.7 copy-done.12
  7.4 0.9 shard_map.68.own
  8.3 0.0 collective-permute-done.1.other_pattern
  8.3 0.0 collective-permute-done.2.other
  8.3 2.7 %shard_map.69 = (bf16[256,1024]{1,0:T(8,128)(2,1)S(1)}, bf16[256,1024]{1,0:T(8,128)(2,1)}, bf16[256,1024]{1,0:T(8,128)(2,1)S(1)}) custom-call(s32[8,8]{1,0:T(8,128)S(1)} %collective-permute-done.1.other_pattern, bf16[1024,1024]{1,0:T(8,128)(2,1)S(1)} %shard_map.68.own, bf16[1024,1024]{1,0:T(8,128)(2,1)} %collective-permute-done.2.other, ...), custom_call_target="tpu_custom_call" | custom-call | flops 335544320 | bytes 3145728 | tf_op jit(solution)/shard_map/pallas_call | solution.py:95
  11.1 0.8 copy-done.10
  11.9 5.3 %collective-permute-start.3 = (bf16[256,1024]{1,0:T(8,128)(2,1)}, bf16[256,1024]{1,0:T(8,128)(2,1)}, u32[]{:S(2)}, u32[]{:S(2)}) collective-permute-start(bf16[256,1024]{1,0:T(8,128)(2,1)} %get-tuple-element.42.own), channel_id=1, source_target_pairs={{0,3},{2,1},{4,7},{6,5},{8,11},{10,9},{12,15},{14,13},{16,19},{18,... | collective-permute-start | bytes 1572872 | tf_op jit(solution)/shard_map/ppermute | solution.py:264
  17.2 1.3 %collective-permute-start.5 = (bf16[256,1024]{1,0:T(8,128)(2,1)S(1)}, bf16[256,1024]{1,0:T(8,128)(2,1)S(1)}, u32[]{:S(2)}, u32[]{:S(2)}) collective-permute-start(bf16[256,1024]{1,0:T(8,128)(2,1)S(1)} %get-tuple-element.48.own), channel_id=1, source_target_pairs={{0,3},{2,1},{4,7},{6,5},{8,11},{10,9},{12,15},{14,13},{16,19},{18,... | collective-permute-start | bytes 1572872 | tf_op jit(solution)/shard_map/ppermute | solution.py:264
  18.5 1.0 %copy-done.11 = bf16[256,1024]{1,0:T(8,128)(2,1)S(1)} copy-done((bf16[256,1024]{1,0:T(8,128)(2,1)S(1)}, bf16[256,1024]{1,0:T(8,128)(2,1)}, u32[]{:S(2)}) %copy-start.11) | copy-done | bytes 524312
  19.5 2.0 %shard_map.70 = (bf16[256,1024]{1,0:T(8,128)(2,1)S(1)}, bf16[256,1024]{1,0:T(8,128)(2,1)S(1)}) custom-call(s32[8,8]{1,0:T(8,128)S(1)} %collective-permute-done.1.other_pattern, bf16[1024,1024]{1,0:T(8,128)(2,1)S(1)} %shard_map.68.own, bf16[1024,1024]{1,0:T(8,128)(2,1)} %collective-permute-done.2.other, bf16[256,256]{1,0:T(8,128)(2,1)S(1)} %get-tuple-element.81.inverse, ...), custom_call_target="tpu_custom_call" | custom-call | flops 335544320 | bytes 3145728 | tf_op jit(solution)/shard_map/pallas_call | solution.py:95
  21.5 1.9 %collective-permute-done.3.other = bf16[256,1024]{1,0:T(8,128)(2,1)} collective-permute-done((bf16[256,1024]{1,0:T(8,128)(2,1)}, bf16[256,1024]{1,0:T(8,128)(2,1)}, u32[]{:S(2)}, u32[]{:S(2)}) %collective-permute-start.3) | collective-permute-done | bytes 524320 | tf_op jit(solution)/shard_map/ppermute | solution.py:264
  23.4 1.7 %shard_map.71 = (bf16[256,1024]{1,0:T(8,128)(2,1)S(1)}, bf16[1024,1024]{1,0:T(8,128)(2,1)S(1)}, bf16[256,1024]{1,0:T(8,128)(2,1)S(1)}) custom-call(s32[1]{0:T(128)} %bitcast.1.is_second, bf16[256,1024]{1,0:T(8,128)(2,1)} %get-tuple-element.42.own, bf16[256,1024]{1,0:T(8,128)(2,1)} %collective-permute-done.3.other, ...), custom_call_target="tpu_custom_call" | custom-call | tf_op jit(solution)/shard_map/pallas_call | solution.py:135
  25.0 3.8 %collective-permute-start.7 = (bf16[256,1024]{1,0:T(8,128)(2,1)S(1)}, bf16[256,1024]{1,0:T(8,128)(2,1)S(1)}, u32[]{:S(2)}, u32[]{:S(2)}) collective-permute-start(bf16[256,1024]{1,0:T(8,128)(2,1)S(1)} %get-tuple-element.45), channel_id=1, source_target_pairs={{5,0},{7,2},{13,8},{15,10},{21,16},{23,18},{29,24},{31,26},{0,3},{... | collective-permute-start | bytes 1572872 | tf_op jit(solution)/shard_map/ppermute | solution.py:264
  28.9 0.7 collective-permute-start.4
  29.6 0.0 collective-permute-done.5.other
  29.6 0.5 shard_map.72
  30.1 4.3 %collective-permute-start.6 = (bf16[256,1024]{1,0:T(8,128)(2,1)S(1)}, bf16[256,1024]{1,0:T(8,128)(2,1)S(1)}, u32[]{:S(2)}, u32[]{:S(2)}) collective-permute-start(bf16[256,1024]{1,0:T(8,128)(2,1)S(1)} %get-tuple-element.51), channel_id=1, source_target_pairs={{5,0},{7,2},{13,8},{15,10},{21,16},{23,18},{29,24},{31,26},{0,3},{... | collective-permute-start | bytes 1572872 | tf_op jit(solution)/shard_map/ppermute | solution.py:264
  34.4 1.2 %collective-permute-done.7.other.refs_5_.refs_3_.refs_2_ = bf16[256,1024]{1,0:T(8,128)(2,1)S(1)} collective-permute-done((bf16[256,1024]{1,0:T(8,128)(2,1)S(1)}, bf16[256,1024]{1,0:T(8,128)(2,1)S(1)}, u32[]{:S(2)}, u32[]{:S(2)}) %collective-permute-start.7) | collective-permute-done | bytes 524320 | tf_op jit(solution)/shard_map/ppermute | solution.py:264
  35.6 0.4 shard_map.73
  36.1 1.3 %collective-permute-start.8 = (bf16[256,1024]{1,0:T(8,128)(2,1)S(1)}, bf16[256,1024]{1,0:T(8,128)(2,1)S(1)}, u32[]{:S(2)}, u32[]{:S(2)}) collective-permute-start(bf16[256,1024]{1,0:T(8,128)(2,1)S(1)} %get-tuple-element.54), channel_id=1, source_target_pairs={{5,0},{7,2},{13,8},{15,10},{21,16},{23,18},{29,24},{31,26}} | collective-permute-start | bytes 1572872 | tf_op jit(solution)/shard_map/ppermute | solution.py:264
  37.4 3.9 %collective-permute-done.6.other.refs_4_.refs_2_.refs_1_ = bf16[256,1024]{1,0:T(8,128)(2,1)S(1)} collective-permute-done((bf16[256,1024]{1,0:T(8,128)(2,1)S(1)}, bf16[256,1024]{1,0:T(8,128)(2,1)S(1)}, u32[]{:S(2)}, u32[]{:S(2)}) %collective-permute-start.6) | collective-permute-done | bytes 524320 | tf_op jit(solution)/shard_map/ppermute | solution.py:264
  41.3 5.6 %collective-permute-done.8.refs_6_.refs_4_.refs_3_ = bf16[256,1024]{1,0:T(8,128)(2,1)S(1)} collective-permute-done((bf16[256,1024]{1,0:T(8,128)(2,1)S(1)}, bf16[256,1024]{1,0:T(8,128)(2,1)S(1)}, u32[]{:S(2)}, u32[]{:S(2)}) %collective-permute-start.8) | collective-permute-done | bytes 524320 | tf_op jit(solution)/shard_map/ppermute | solution.py:264
  46.9 0.4 shard_map.74
  47.3 0.0 copy-start
  47.3 0.7 shard_map.75
  48.0 1.3 %collective-permute-start.10 = (bf16[1024,1024]{1,0:T(8,128)(2,1)S(1)}, bf16[1024,1024]{1,0:T(8,128)(2,1)S(1)}, u32[]{:S(2)}, u32[]{:S(2)}) collective-permute-start(bf16[1024,1024]{1,0:T(8,128)(2,1)S(1)} %get-tuple-element.59.refs_2_), channel_id=1, source_target_pairs={{1,0},{3,2},{5,4},{7,6},{9,8},{11,10},{13,12},{15,14},{17,16},{19,... | collective-permute-start | bytes 6291464 | tf_op jit(solution)/shard_map/ppermute | solution.py:264
  49.3 1.3 %collective-permute-start.11 = (bf16[256,1024]{1,0:T(8,128)(2,1)S(1)}, bf16[256,1024]{1,0:T(8,128)(2,1)S(1)}, u32[]{:S(2)}, u32[]{:S(2)}) collective-permute-start(bf16[256,1024]{1,0:T(8,128)(2,1)S(1)} %get-tuple-element.60), channel_id=1, source_target_pairs={{5,0},{7,2},{13,8},{15,10},{21,16},{23,18},{29,24},{31,26}} | collective-permute-start | bytes 1572872 | tf_op jit(solution)/shard_map/ppermute | solution.py:264
  50.6 0.7 collective-permute-start.9
  51.3 0.0 collective-permute-done.9.refs_0_
  51.3 8.5 %collective-permute-done.11.refs_7_.refs_5_.refs_4_ = bf16[256,1024]{1,0:T(8,128)(2,1)S(1)} collective-permute-done((bf16[256,1024]{1,0:T(8,128)(2,1)S(1)}, bf16[256,1024]{1,0:T(8,128)(2,1)S(1)}, u32[]{:S(2)}, u32[]{:S(2)}) %collective-permute-start.11) | collective-permute-done | bytes 524320 | tf_op jit(solution)/shard_map/ppermute | solution.py:264
  59.8 1.3 %shard_map.76 = (f32[8,1024]{1,0:T(8,128)S(1)}, f32[8,1024]{1,0:T(8,128)S(1)}, bf16[8,1024]{1,0:T(8,128)(2,1)S(1)}) custom-call(bf16[8,1024]{1,0:T(8,128)(2,1)S(1)} %collective-permute-done.9.refs_0_, f32[9,1024]{1,0:T(8,128)S(1)} %pad_maximum_fusion.refs_1_, bf16[1024,1024]{1,0:T(8,128)(2,1)S(1)} %collective-permute-done.10.refs_2_.refs_7_, ...), custom_call_target="tpu_custom_call" | custom-call | flops 1073741824 | bytes 4194304 | tf_op jit(solution)/shard_map/pallas_call | solution.py:216
  61.2 0.0 copy-done.5
  61.2 0.7 collective-permute-start.12
  61.9 0.0 collective-permute-done.12.refs_0_
  61.9 1.0 %copy-done.3 = bf16[256,1024]{1,0:T(8,128)(2,1)S(1)} copy-done((bf16[256,1024]{1,0:T(8,128)(2,1)S(1)}, bf16[256,1024]{1,0:T(8,128)(2,1)}, u32[]{:S(2)}) %copy-start.3) | copy-done | bytes 524312
  62.9 1.0 %copy-done.6 = bf16[256,1024]{1,0:T(8,128)(2,1)S(1)} copy-done((bf16[256,1024]{1,0:T(8,128)(2,1)S(1)}, bf16[256,1024]{1,0:T(8,128)(2,1)}, u32[]{:S(2)}) %copy-start.6) | copy-done | bytes 524312
  64.0 1.3 %shard_map.77 = (f32[8,1024]{1,0:T(8,128)S(1)}, f32[8,1024]{1,0:T(8,128)S(1)}, bf16[8,1024]{1,0:T(8,128)(2,1)S(1)}) custom-call(bf16[8,1024]{1,0:T(8,128)(2,1)S(1)} %collective-permute-done.12.refs_0_, f32[9,1024]{1,0:T(8,128)S(1)} %pad_maximum_fusion.refs_1_, bf16[1024,1024]{1,0:T(8,128)(2,1)S(1)} %collective-permute-done.10.refs_2_.refs_7_, ...), custom_call_target="tpu_custom_call" | custom-call | flops 1073741824 | bytes 4194304 | tf_op jit(solution)/shard_map/pallas_call | solution.py:216
  65.3 0.7 collective-permute-start.13
  66.0 0.0 copy-start.1
  66.0 1.4 %collective-permute-start.18 = (f32[8,1024]{1,0:T(8,128)S(1)}, f32[8,1024]{1,0:T(8,128)S(1)}, u32[]{:S(2)}, u32[]{:S(2)}) collective-permute-start(f32[8,1024]{1,0:T(8,128)S(1)} %get-tuple-element.73), channel_id=1, source_target_pairs={{5,0},{7,2}} | collective-permute-start | bytes 98312 | tf_op jit(solution)/shard_map/ppermute | solution.py:264
  67.5 0.0 collective-permute-done.13.refs_0_
  67.5 2.1 %shard_map.78 = (f32[8,1024]{1,0:T(8,128)}, f32[8,1024]{1,0:T(8,128)S(1)}, f32[8,1024]{1,0:T(8,128)S(1)}, bf16[8,1024]{1,0:T(8,128)(2,1)S(1)}) custom-call(bf16[8,1024]{1,0:T(8,128)(2,1)S(1)} %collective-permute-done.13.refs_0_, f32[9,1024]{1,0:T(8,128)S(1)} %pad_maximum_fusion.refs_1_, bf16[1024,1024]{1,0:T(8,128)(2,1)S(1)} %collective-permute-done.10.refs_2_.refs_7_, ...), custom_call_target="tpu_custom_call" | custom-call | flops 1610612736 | bytes 6291456 | tf_op jit(solution)/shard_map/pallas_call | solution.py:216
  69.6 0.8 collective-permute-start.14
  70.4 0.2 broadcast_select_fusion.refs_0_
  70.6 0.0 copy-start.8
  70.6 0.0 collective-permute-done.14.refs_0_
  70.6 0.1 copy-done.7
  70.8 0.7 shard_map.79
  71.5 0.7 collective-permute-start.15
  72.2 0.7 shard_map.80
  72.9 1.3 %collective-permute-start.16 = (bf16[8,1024]{1,0:T(8,128)(2,1)S(1)}, bf16[8,1024]{1,0:T(8,128)(2,1)S(1)}, u32[]{:S(2)}, u32[]{:S(2)}) collective-permute-start(bf16[8,1024]{1,0:T(8,128)(2,1)S(1)} %get-tuple-element.71), channel_id=1, source_target_pairs={{8,0},{10,2}} | collective-permute-start | bytes 49160 | tf_op jit(solution)/shard_map/ppermute | solution.py:264
  74.2 0.7 collective-permute-start.17
  74.9 0.7 collective-permute-start.19
  75.5 16.5 %collective-permute-done.16.from_pair = bf16[8,1024]{1,0:T(8,128)(2,1)S(1)} collective-permute-done((bf16[8,1024]{1,0:T(8,128)(2,1)S(1)}, bf16[8,1024]{1,0:T(8,128)(2,1)S(1)}, u32[]{:S(2)}, u32[]{:S(2)}) %collective-permute-start.16) | collective-permute-done | bytes 16416 | tf_op jit(solution)/shard_map/ppermute | solution.py:264
  92.1 0.9 shard_map.81
  93.1 1.3 %collective-permute-start.20 = (f32[4,1024]{1,0:T(4,128)S(1)}, f32[4,1024]{1,0:T(4,128)S(1)}, u32[]{:S(2)}, u32[]{:S(2)}) collective-permute-start(f32[4,1024]{1,0:T(4,128)S(1)} %slice_select_fusion), channel_id=1, source_target_pairs={{5,4},{7,6},{0,1},{2,3},{8,9},{10,11},{12,13},{14,15},{16,17},{18,... | collective-permute-start | bytes 49160 | tf_op jit(solution)/shard_map/ppermute | solution.py:264
  94.4 0.8 collective-permute-done.20
  95.2 0.6 select_bitcast_fusion
  (34 shorter events, 0.1 us)
Async XLA Ops:
  0.6 7.7 %collective-permute-start.2 = (bf16[1024,1024]{1,0:T(8,128)(2,1)}, bf16[1024,1024]{1,0:T(8,128)(2,1)}, u32[]{:S(2)}, u32[]{:S(2)}) collective-permute-start(bf16[1024,1024]{1,0:T(8,128)(2,1)} %bitcast.15), channel_id=1, source_target_pairs={{0,1},{1,0},{2,3},{3,2},{4,5},{5,4},{6,7},{7,6},{8,9},{9,8},{10,11... | collective-permute-start | bytes 6291464 | tf_op jit(solution)/shard_map/ppermute | solution.py:264
  1.1 3.9 %collective-permute-start = (f32[4,1024]{1,0:T(4,128)}, f32[4,1024]{1,0:T(4,128)S(1)}, u32[]{:S(2)}, u32[]{:S(2)}) collective-permute-start(f32[4,1024]{1,0:T(4,128)} %bitcast.19), channel_id=1, source_target_pairs={{0,1},{1,0},{2,3},{3,2},{4,5},{5,4},{6,7},{7,6},{8,9},{9,8},{10,11... | collective-permute-start | bytes 49160 | tf_op jit(solution)/shard_map/ppermute | solution.py:264
  1.2 7.1 %collective-permute-start.1 = (s32[8,8]{1,0:T(8,128)}, s32[8,8]{1,0:T(8,128)S(1)}, u32[]{:S(2)}, u32[]{:S(2)}) collective-permute-start(s32[8,8]{1,0:T(8,128)} %bitcast.17), channel_id=1, source_target_pairs={{0,1},{1,0},{2,3},{3,2},{4,5},{5,4},{6,7},{7,6},{8,9},{9,8},{10,11... | collective-permute-start | bytes 776 | tf_op jit(solution)/shard_map/ppermute | solution.py:264
  5.1 1.6 %copy-start.9 = (bf16[1,1024,1024]{2,1,0:T(8,128)(2,1)S(1)}, bf16[1,1024,1024]{2,1,0:T(8,128)(2,1)}, u32[]{:S(2)}) copy-start(bf16[1,1024,1024]{2,1,0:T(8,128)(2,1)} %param.5) | copy-start | bytes 6291460
  6.7 0.7 copy-start.12
  11.1 0.8 copy-start.10
  11.9 11.5 %collective-permute-start.3 = (bf16[256,1024]{1,0:T(8,128)(2,1)}, bf16[256,1024]{1,0:T(8,128)(2,1)}, u32[]{:S(2)}, u32[]{:S(2)}) collective-permute-start(bf16[256,1024]{1,0:T(8,128)(2,1)} %get-tuple-element.42.own), channel_id=1, source_target_pairs={{0,3},{2,1},{4,7},{6,5},{8,11},{10,9},{12,15},{14,13},{16,19},{18,... | collective-permute-start | bytes 1572872 | tf_op jit(solution)/shard_map/ppermute | solution.py:264
  17.2 12.4 %collective-permute-start.5 = (bf16[256,1024]{1,0:T(8,128)(2,1)S(1)}, bf16[256,1024]{1,0:T(8,128)(2,1)S(1)}, u32[]{:S(2)}, u32[]{:S(2)}) collective-permute-start(bf16[256,1024]{1,0:T(8,128)(2,1)S(1)} %get-tuple-element.48.own), channel_id=1, source_target_pairs={{0,3},{2,1},{4,7},{6,5},{8,11},{10,9},{12,15},{14,13},{16,19},{18,... | collective-permute-start | bytes 1572872 | tf_op jit(solution)/shard_map/ppermute | solution.py:264
  18.5 1.0 %copy-start.11 = (bf16[256,1024]{1,0:T(8,128)(2,1)S(1)}, bf16[256,1024]{1,0:T(8,128)(2,1)}, u32[]{:S(2)}) copy-start(bf16[256,1024]{1,0:T(8,128)(2,1)} %copy-done.10) | copy-start | bytes 1572868
  19.5 9.3 %copy-start.14 = (s32[1,1024]{1,0:T(1,128)S(1)}, s32[1,1024]{1,0:T(1,128)}, u32[]{:S(2)}) copy-start(s32[1,1024]{1,0:T(1,128)} %param.8) | copy-start | bytes 12292
  19.5 9.3 %copy-start.13 = (f32[1,4,1024]{2,1,0:T(4,128)S(1)}, f32[1,4,1024]{2,1,0:T(4,128)}, u32[]{:S(2)}) copy-start(f32[1,4,1024]{2,1,0:T(4,128)} %param.9) | copy-start | bytes 49156
  25.0 10.6 %collective-permute-start.7 = (bf16[256,1024]{1,0:T(8,128)(2,1)S(1)}, bf16[256,1024]{1,0:T(8,128)(2,1)S(1)}, u32[]{:S(2)}, u32[]{:S(2)}) collective-permute-start(bf16[256,1024]{1,0:T(8,128)(2,1)S(1)} %get-tuple-element.45), channel_id=1, source_target_pairs={{5,0},{7,2},{13,8},{15,10},{21,16},{23,18},{29,24},{31,26},{0,3},{... | collective-permute-start | bytes 1572872 | tf_op jit(solution)/shard_map/ppermute | solution.py:264
  28.9 5.5 %collective-permute-start.4 = (f32[9,1024]{1,0:T(8,128)S(1)}, f32[9,1024]{1,0:T(8,128)S(1)}, u32[]{:S(2)}, u32[]{:S(2)}) collective-permute-start(f32[9,1024]{1,0:T(8,128)S(1)} %pad_maximum_fusion.refs_1_), channel_id=1, source_target_pairs={{12,8},{14,10},{20,16},{22,18},{28,24},{30,26},{1,5},{3,7}} | collective-permute-start | bytes 110600 | tf_op jit(solution)/shard_map/ppermute | solution.py:264
  30.1 11.2 %collective-permute-start.6 = (bf16[256,1024]{1,0:T(8,128)(2,1)S(1)}, bf16[256,1024]{1,0:T(8,128)(2,1)S(1)}, u32[]{:S(2)}, u32[]{:S(2)}) collective-permute-start(bf16[256,1024]{1,0:T(8,128)(2,1)S(1)} %get-tuple-element.51), channel_id=1, source_target_pairs={{5,0},{7,2},{13,8},{15,10},{21,16},{23,18},{29,24},{31,26},{0,3},{... | collective-permute-start | bytes 1572872 | tf_op jit(solution)/shard_map/ppermute | solution.py:264
  36.1 10.8 %collective-permute-start.8 = (bf16[256,1024]{1,0:T(8,128)(2,1)S(1)}, bf16[256,1024]{1,0:T(8,128)(2,1)S(1)}, u32[]{:S(2)}, u32[]{:S(2)}) collective-permute-start(bf16[256,1024]{1,0:T(8,128)(2,1)S(1)} %get-tuple-element.54), channel_id=1, source_target_pairs={{5,0},{7,2},{13,8},{15,10},{21,16},{23,18},{29,24},{31,26}} | collective-permute-start | bytes 1572872 | tf_op jit(solution)/shard_map/ppermute | solution.py:264
  46.9 13.0 %copy-start.2 = (bf16[256,1024]{1,0:T(8,128)(2,1)}, bf16[256,1024]{1,0:T(8,128)(2,1)S(1)}, u32[]{:S(2)}) copy-start(bf16[256,1024]{1,0:T(8,128)(2,1)S(1)} %collective-permute-done.8.refs_6_.refs_4_.refs_3_) | copy-start | bytes 1572868
  47.3 13.8 %copy-start = (bf16[1024,1024]{1,0:T(8,128)(2,1)}, bf16[1024,1024]{1,0:T(8,128)(2,1)S(1)}, u32[]{:S(2)}) copy-start(bf16[1024,1024]{1,0:T(8,128)(2,1)S(1)} %get-tuple-element.59.refs_2_) | copy-start | bytes 6291460
  48.0 11.8 %collective-permute-start.10 = (bf16[1024,1024]{1,0:T(8,128)(2,1)S(1)}, bf16[1024,1024]{1,0:T(8,128)(2,1)S(1)}, u32[]{:S(2)}, u32[]{:S(2)}) collective-permute-start(bf16[1024,1024]{1,0:T(8,128)(2,1)S(1)} %get-tuple-element.59.refs_2_), channel_id=1, source_target_pairs={{1,0},{3,2},{5,4},{7,6},{9,8},{11,10},{13,12},{15,14},{17,16},{19,... | collective-permute-start | bytes 6291464 | tf_op jit(solution)/shard_map/ppermute | solution.py:264
  49.3 10.5 %collective-permute-start.11 = (bf16[256,1024]{1,0:T(8,128)(2,1)S(1)}, bf16[256,1024]{1,0:T(8,128)(2,1)S(1)}, u32[]{:S(2)}, u32[]{:S(2)}) collective-permute-start(bf16[256,1024]{1,0:T(8,128)(2,1)S(1)} %get-tuple-element.60), channel_id=1, source_target_pairs={{5,0},{7,2},{13,8},{15,10},{21,16},{23,18},{29,24},{31,26}} | collective-permute-start | bytes 1572872 | tf_op jit(solution)/shard_map/ppermute | solution.py:264
  50.6 0.7 collective-permute-start.9
  59.8 1.4 %copy-start.5 = (bf16[256,1024]{1,0:T(8,128)(2,1)}, bf16[256,1024]{1,0:T(8,128)(2,1)S(1)}, u32[]{:S(2)}) copy-start(bf16[256,1024]{1,0:T(8,128)(2,1)S(1)} %collective-permute-done.11.refs_7_.refs_5_.refs_4_) | copy-start | bytes 1572868
  61.2 0.7 collective-permute-start.12
  61.9 1.0 %copy-start.3 = (bf16[256,1024]{1,0:T(8,128)(2,1)S(1)}, bf16[256,1024]{1,0:T(8,128)(2,1)}, u32[]{:S(2)}) copy-start(bf16[256,1024]{1,0:T(8,128)(2,1)} %copy-done.2) | copy-start | bytes 1572868
  62.9 1.0 %copy-start.6 = (bf16[256,1024]{1,0:T(8,128)(2,1)S(1)}, bf16[256,1024]{1,0:T(8,128)(2,1)}, u32[]{:S(2)}) copy-start(bf16[256,1024]{1,0:T(8,128)(2,1)} %copy-done.5) | copy-start | bytes 1572868
  65.3 2.1 %collective-permute-start.13 = (bf16[8,1024]{1,0:T(8,128)(2,1)S(1)}, bf16[8,1024]{1,0:T(8,128)(2,1)S(1)}, u32[]{:S(2)}, u32[]{:S(2)}) collective-permute-start(bf16[8,1024]{1,0:T(8,128)(2,1)S(1)} %get-tuple-element.62), channel_id=1, source_target_pairs={{16,24},{18,26}} | collective-permute-start | bytes 49160 | tf_op jit(solution)/shard_map/ppermute | solution.py:264
  66.0 4.4 %copy-start.1 = (bf16[1024,1024]{1,0:T(8,128)(2,1)S(1)}, bf16[1024,1024]{1,0:T(8,128)(2,1)}, u32[]{:S(2)}) copy-start(bf16[1024,1024]{1,0:T(8,128)(2,1)} %copy-done) | copy-start | bytes 6291460
  66.0 6.1 %collective-permute-start.18 = (f32[8,1024]{1,0:T(8,128)S(1)}, f32[8,1024]{1,0:T(8,128)S(1)}, u32[]{:S(2)}, u32[]{:S(2)}) collective-permute-start(f32[8,1024]{1,0:T(8,128)S(1)} %get-tuple-element.73), channel_id=1, source_target_pairs={{5,0},{7,2}} | collective-permute-start | bytes 98312 | tf_op jit(solution)/shard_map/ppermute | solution.py:264
  69.6 1.1 %copy-start.4 = (bf16[256,1024]{1,0:T(8,128)(2,1)S(1)}, bf16[256,1024]{1,0:T(8,128)(2,1)}, u32[]{:S(2)}) copy-start(bf16[256,1024]{1,0:T(8,128)(2,1)} %copy-done.2) | copy-start | bytes 1572868
  69.6 1.2 %copy-start.7 = (bf16[256,1024]{1,0:T(8,128)(2,1)S(1)}, bf16[256,1024]{1,0:T(8,128)(2,1)}, u32[]{:S(2)}) copy-start(bf16[256,1024]{1,0:T(8,128)(2,1)} %copy-done.5) | copy-start | bytes 1572868
  69.6 1.0 %collective-permute-start.14 = (bf16[8,1024]{1,0:T(8,128)(2,1)S(1)}, bf16[8,1024]{1,0:T(8,128)(2,1)S(1)}, u32[]{:S(2)}, u32[]{:S(2)}) collective-permute-start(bf16[8,1024]{1,0:T(8,128)(2,1)S(1)} %get-tuple-element.63), channel_id=1, source_target_pairs={{24,16},{26,18}} | collective-permute-start | bytes 49160 | tf_op jit(solution)/shard_map/ppermute | solution.py:264
  70.6 21.5 %copy-start.8 = (bf16[1024,1024]{1,0:T(8,128)(2,1)}, bf16[1024,1024]{1,0:T(8,128)(2,1)S(1)}, u32[]{:S(2)}) copy-start(bf16[1024,1024]{1,0:T(8,128)(2,1)S(1)} %broadcast_select_fusion.refs_0_) | copy-start | bytes 6291460
  71.5 0.7 collective-permute-start.15
  72.9 19.2 %collective-permute-start.16 = (bf16[8,1024]{1,0:T(8,128)(2,1)S(1)}, bf16[8,1024]{1,0:T(8,128)(2,1)S(1)}, u32[]{:S(2)}, u32[]{:S(2)}) collective-permute-start(bf16[8,1024]{1,0:T(8,128)(2,1)S(1)} %get-tuple-element.71), channel_id=1, source_target_pairs={{8,0},{10,2}} | collective-permute-start | bytes 49160 | tf_op jit(solution)/shard_map/ppermute | solution.py:264
  74.2 17.9 %collective-permute-start.17 = (bf16[8,1024]{1,0:T(8,128)(2,1)S(1)}, bf16[8,1024]{1,0:T(8,128)(2,1)S(1)}, u32[]{:S(2)}, u32[]{:S(2)}) collective-permute-start(bf16[8,1024]{1,0:T(8,128)(2,1)S(1)} %get-tuple-element.71), channel_id=1, source_target_pairs={{8,5},{10,7}} | collective-permute-start | bytes 49160 | tf_op jit(solution)/shard_map/ppermute | solution.py:264
  74.9 18.2 %collective-permute-start.19 = (f32[8,1024]{1,0:T(8,128)S(1)}, f32[8,1024]{1,0:T(8,128)S(1)}, u32[]{:S(2)}, u32[]{:S(2)}) collective-permute-start(f32[8,1024]{1,0:T(8,128)S(1)} %select_select_fusion), channel_id=1, source_target_pairs={{8,12},{10,14},{16,20},{18,22},{24,28},{26,30}} | collective-permute-start | bytes 98312 | tf_op jit(solution)/shard_map/ppermute | solution.py:264
  93.1 2.1 %collective-permute-start.20 = (f32[4,1024]{1,0:T(4,128)S(1)}, f32[4,1024]{1,0:T(4,128)S(1)}, u32[]{:S(2)}, u32[]{:S(2)}) collective-permute-start(f32[4,1024]{1,0:T(4,128)S(1)} %slice_select_fusion), channel_id=1, source_target_pairs={{5,4},{7,6},{0,1},{2,3},{8,9},{10,11},{12,13},{14,15},{16,17},{18,... | collective-permute-start | bytes 49160 | tf_op jit(solution)/shard_map/ppermute | solution.py:264

commit v5 on v4

--- a/solution.py
+++ b/solution.py
@@ -12,8 +12,9 @@
 SMALL_AT = 0
 VMEM = pl.BlockSpec(memory_space=pltpu.VMEM)
 SMEM = pl.BlockSpec(memory_space=pltpu.SMEM)
-PARAMS = pltpu.CompilerParams(vmem_limit_bytes=10 * 1024 * 1024)
-OWN, PAIR, EXTRA = 0, 1, 2
+PARAMS = pltpu.CompilerParams(vmem_limit_bytes=24 * 1024 * 1024)
+SWEEP_PARAMS = pltpu.CompilerParams(vmem_limit_bytes=10 * 1024 * 1024)
+OWN, PAIR = 0, 1
 
 
 def cost(flops, moved):
@@ -220,7 +221,7 @@
         out_shape=[rows] * steps + [jax.ShapeDtypeStruct(arrived.shape, jnp.bfloat16)],
         in_specs=[VMEM] * len(operands),
         out_specs=[VMEM] * (steps + 1),
-        compiler_params=PARAMS,
+        compiler_params=SWEEP_PARAMS,
         cost_estimate=cost(steps * 2 * 256 * 1024 * 1024, steps * 2 * 1024 * 1024),
     )(*operands)
     return results[:-1], results[-1]
@@ -280,7 +281,7 @@
         out_specs=VMEM,
         compiler_params=PARAMS,
         cost_estimate=cost(width * width, 4 * width * width),
-    )(after(pattern, other_sources), raw)
+    )(pattern, raw)
 
     def inverse_of(level):
         node = (boxes >> (level + 1)) - 1 + (position >> (level + 1))
@@ -413,7 +414,7 @@
         out_shape=jax.ShapeDtypeStruct((rows, width), jnp.float32),
         in_specs=[SMEM] + [VMEM] * (5 + len(pair_maps)),
         out_specs=VMEM,
-        compiler_params=PARAMS,
+        compiler_params=SWEEP_PARAMS,
         cost_estimate=cost(6 * 256 * 1024 * 1024, 6 * 1024 * 1024),
     )(odd, from_pair, from_own, packed[:rows], down_odd, merged, *pair_maps)
     upward = jnp.where(layer < 2, last, settled)

time: 96.6 us -> 94.2 us (0.975)
  waiting for transfers between devices: 40.8 us -> 38.5 us
    ppermute x21, waiting for transfers between devices: 40.8 us -> 38.5 us  [send(): return lax.ppermute(value, AXES, pairs_of_devices)]
  transfers between devices with their start and end apart: 21 -> 21, of which waited for: 8 -> 7; matrix products, arithmetic and copies ran while one was open for 1% -> 1% of each run, Pallas kernels for 10% -> 10%
where the time goes in v5:
time: 94.2 us; the launch traced here: 93.5 us
  waiting for transfers between devices  38.5 us (41%)
  starting transfers between devices  29 us (31%)
  Pallas kernels  16.5 us (18%)
  local copies, waits for them, and re-layouts  7.43 us (8%)
  between operations  1.12 us (1%)
    ppermute x21, waiting for transfers between devices, send(): return lax.ppermute(value, AXES, pairs_of_devices)  38.5 us
    ppermute x21, starting transfers between devices, send(): return lax.ppermute(value, AXES, pairs_of_devices)  29 us
    pallas_call x6, Pallas kernels, segment(): pl.pallas_call(functools.partial(segment_kernel, coupling, [len(entry) fo...  6.86 us
    unnamed x30, local copies, waits for them, and re-layouts  6.36 us
    pallas_call x2, Pallas kernels, leaf_combine(): pl.pallas_call(functools.partial(leaf_kernel, half * rows, is_face, piece...  4.71 us
    pallas_call x4, Pallas kernels, combine(): pl.pallas_call(functools.partial(combine_kernel, face_at, is_face, follow...  3.02 us
  transfers between devices with their start and end apart: 21, of which 7 were waited for; matrix products, arithmetic and copies ran while one was open for 1% of the time, Pallas kernels for 10%

profile of v5, /device:TPU:0, one launch (start us, length us, event | category | flops | bytes accessed | tf_op | source)
XLA Modules:
  0.0 93.5 jit_solution(6147293223552477507)
XLA Ops:
  0.6 0.5 collective-permute-start.2
  1.1 0.1 collective-permute-start.1
  1.2 1.1 %fusion.1 = (bf16[256,256]{1,0:T(8,128)(2,1)S(1)}, bf16[256,256]{1,0:T(8,128)(2,1)S(1)}) fusion(f32[1,3,256,256]{3,2,1,0:T(8,128)} %param.7, s32[]{:T(128)S(6)} %select_n.101, s32[]{:T(128)S(6)} %select_n.100), kind=kLoop, calls=%fused_computation.4 | loop fusion | bytes 524296 | tf_op jit(solution)/shard_map/convert_element_type | solution.py:288
  2.3 0.0 copy-start.9
  2.3 1.6 %copy-done.9 = bf16[1,1024,1024]{2,1,0:T(8,128)(2,1)S(1)} copy-done((bf16[1,1024,1024]{2,1,0:T(8,128)(2,1)S(1)}, bf16[1,1024,1024]{2,1,0:T(8,128)(2,1)}, u32[]{:S(2)}) %copy-start.9) | copy-done | bytes 2097176
  3.9 0.7 copy-done.12
  4.6 0.9 %shard_map.68.own = bf16[1024,1024]{1,0:T(8,128)(2,1)S(1)} custom-call(s32[8,8]{1,0:T(8,128)S(1)} %bitcast.18, bf16[1024,1024]{1,0:T(8,128)(2,1)S(1)} %bitcast.16), custom_call_target="tpu_custom_call" | custom-call | flops 1048576 | bytes 4194304 | tf_op jit(solution)/shard_map/pallas_call | solution.py:277
  5.5 0.0 collective-permute-done.1.other_pattern
  5.5 2.7 %shard_map.69 = (bf16[256,1024]{1,0:T(8,128)(2,1)S(1)}, bf16[256,1024]{1,0:T(8,128)(2,1)}, bf16[256,1024]{1,0:T(8,128)(2,1)S(1)}) custom-call(s32[8,8]{1,0:T(8,128)S(1)} %collective-permute-done.1.other_pattern, bf16[1024,1024]{1,0:T(8,128)(2,1)S(1)} %shard_map.68.own, bf16[1024,1024]{1,0:T(8,128)(2,1)} %collective-permute-done.2.other, ...), custom_call_target="tpu_custom_call" | custom-call | flops 335544320 | bytes 3145728 | tf_op jit(solution)/shard_map/pallas_call | solution.py:96
  8.3 0.8 copy-done.10
  9.1 5.3 %collective-permute-start.3 = (bf16[256,1024]{1,0:T(8,128)(2,1)}, bf16[256,1024]{1,0:T(8,128)(2,1)}, u32[]{:S(2)}, u32[]{:S(2)}) collective-permute-start(bf16[256,1024]{1,0:T(8,128)(2,1)} %get-tuple-element.40.own), channel_id=1, source_target_pairs={{0,3},{2,1},{4,7},{6,5},{8,11},{10,9},{12,15},{14,13},{16,19},{18,... | collective-permute-start | bytes 1572872 | tf_op jit(solution)/shard_map/ppermute | solution.py:265
  14.4 1.3 %collective-permute-start.5 = (bf16[256,1024]{1,0:T(8,128)(2,1)S(1)}, bf16[256,1024]{1,0:T(8,128)(2,1)S(1)}, u32[]{:S(2)}, u32[]{:S(2)}) collective-permute-start(bf16[256,1024]{1,0:T(8,128)(2,1)S(1)} %get-tuple-element.46.own), channel_id=1, source_target_pairs={{0,3},{2,1},{4,7},{6,5},{8,11},{10,9},{12,15},{14,13},{16,19},{18,... | collective-permute-start | bytes 1572872 | tf_op jit(solution)/shard_map/ppermute | solution.py:265
  15.7 1.0 %copy-done.11 = bf16[256,1024]{1,0:T(8,128)(2,1)S(1)} copy-done((bf16[256,1024]{1,0:T(8,128)(2,1)S(1)}, bf16[256,1024]{1,0:T(8,128)(2,1)}, u32[]{:S(2)}) %copy-start.11) | copy-done | bytes 524312
  16.8 2.0 %shard_map.70 = (bf16[256,1024]{1,0:T(8,128)(2,1)S(1)}, bf16[256,1024]{1,0:T(8,128)(2,1)S(1)}) custom-call(s32[8,8]{1,0:T(8,128)S(1)} %collective-permute-done.1.other_pattern, bf16[1024,1024]{1,0:T(8,128)(2,1)S(1)} %shard_map.68.own, bf16[1024,1024]{1,0:T(8,128)(2,1)} %collective-permute-done.2.other, bf16[256,256]{1,0:T(8,128)(2,1)S(1)} %get-tuple-element.79.inverse, ...), custom_call_target="tpu_custom_call" | custom-call | flops 335544320 | bytes 3145728 | tf_op jit(solution)/shard_map/pallas_call | solution.py:96
  18.8 1.8 %collective-permute-done.3.other = bf16[256,1024]{1,0:T(8,128)(2,1)} collective-permute-done((bf16[256,1024]{1,0:T(8,128)(2,1)}, bf16[256,1024]{1,0:T(8,128)(2,1)}, u32[]{:S(2)}, u32[]{:S(2)}) %collective-permute-start.3) | collective-permute-done | bytes 524320 | tf_op jit(solution)/shard_map/ppermute | solution.py:265
  20.6 1.7 %shard_map.71 = (bf16[256,1024]{1,0:T(8,128)(2,1)S(1)}, bf16[1024,1024]{1,0:T(8,128)(2,1)S(1)}, bf16[256,1024]{1,0:T(8,128)(2,1)S(1)}) custom-call(s32[1]{0:T(128)} %bitcast.1.is_second, bf16[256,1024]{1,0:T(8,128)(2,1)} %get-tuple-element.40.own, bf16[256,1024]{1,0:T(8,128)(2,1)} %collective-permute-done.3.other, ...), custom_call_target="tpu_custom_call" | custom-call | tf_op jit(solution)/shard_map/pallas_call | solution.py:136
  22.3 3.8 %collective-permute-start.7 = (bf16[256,1024]{1,0:T(8,128)(2,1)S(1)}, bf16[256,1024]{1,0:T(8,128)(2,1)S(1)}, u32[]{:S(2)}, u32[]{:S(2)}) collective-permute-start(bf16[256,1024]{1,0:T(8,128)(2,1)S(1)} %get-tuple-element.43), channel_id=1, source_target_pairs={{5,0},{7,2},{13,8},{15,10},{21,16},{23,18},{29,24},{31,26},{0,3},{... | collective-permute-start | bytes 1572872 | tf_op jit(solution)/shard_map/ppermute | solution.py:265
  26.1 0.1 collective-permute-start
  26.2 1.1 %collective-permute-done = f32[4,1024]{1,0:T(4,128)S(1)} collective-permute-done((f32[4,1024]{1,0:T(4,128)S(1)}, f32[4,1024]{1,0:T(4,128)S(1)}, u32[]{:S(2)}, u32[]{:S(2)}) %collective-permute-start) | collective-permute-done | bytes 16416 | tf_op jit(solution)/shard_map/ppermute | solution.py:265
  27.4 0.7 collective-permute-start.4
  28.0 0.0 collective-permute-done.5.other
  28.0 0.5 shard_map.72
  28.5 4.6 %collective-permute-start.6 = (bf16[256,1024]{1,0:T(8,128)(2,1)S(1)}, bf16[256,1024]{1,0:T(8,128)(2,1)S(1)}, u32[]{:S(2)}, u32[]{:S(2)}) collective-permute-start(bf16[256,1024]{1,0:T(8,128)(2,1)S(1)} %get-tuple-element.49), channel_id=1, source_target_pairs={{5,0},{7,2},{13,8},{15,10},{21,16},{23,18},{29,24},{31,26},{0,3},{... | collective-permute-start | bytes 1572872 | tf_op jit(solution)/shard_map/ppermute | solution.py:265
  33.2 0.0 collective-permute-done.7.other.refs_5_.refs_3_.refs_2_
  33.2 0.4 shard_map.73
  33.6 1.3 %collective-permute-start.8 = (bf16[256,1024]{1,0:T(8,128)(2,1)S(1)}, bf16[256,1024]{1,0:T(8,128)(2,1)S(1)}, u32[]{:S(2)}, u32[]{:S(2)}) collective-permute-start(bf16[256,1024]{1,0:T(8,128)(2,1)S(1)} %get-tuple-element.52), channel_id=1, source_target_pairs={{5,0},{7,2},{13,8},{15,10},{21,16},{23,18},{29,24},{31,26}} | collective-permute-start | bytes 1572872 | tf_op jit(solution)/shard_map/ppermute | solution.py:265
  34.9 4.9 %collective-permute-done.6.other.refs_4_.refs_2_.refs_1_ = bf16[256,1024]{1,0:T(8,128)(2,1)S(1)} collective-permute-done((bf16[256,1024]{1,0:T(8,128)(2,1)S(1)}, bf16[256,1024]{1,0:T(8,128)(2,1)S(1)}, u32[]{:S(2)}, u32[]{:S(2)}) %collective-permute-start.6) | collective-permute-done | bytes 524320 | tf_op jit(solution)/shard_map/ppermute | solution.py:265
  39.8 4.9 %collective-permute-done.8.refs_6_.refs_4_.refs_3_ = bf16[256,1024]{1,0:T(8,128)(2,1)S(1)} collective-permute-done((bf16[256,1024]{1,0:T(8,128)(2,1)S(1)}, bf16[256,1024]{1,0:T(8,128)(2,1)S(1)}, u32[]{:S(2)}, u32[]{:S(2)}) %collective-permute-start.8) | collective-permute-done | bytes 524320 | tf_op jit(solution)/shard_map/ppermute | solution.py:265
  44.8 0.4 shard_map.74
  45.2 0.0 copy-start
  45.3 0.7 shard_map.75
  45.9 1.3 %collective-permute-start.10 = (bf16[1024,1024]{1,0:T(8,128)(2,1)S(1)}, bf16[1024,1024]{1,0:T(8,128)(2,1)S(1)}, u32[]{:S(2)}, u32[]{:S(2)}) collective-permute-start(bf16[1024,1024]{1,0:T(8,128)(2,1)S(1)} %get-tuple-element.57.refs_2_), channel_id=1, source_target_pairs={{1,0},{3,2},{5,4},{7,6},{9,8},{11,10},{13,12},{15,14},{17,16},{19,... | collective-permute-start | bytes 6291464 | tf_op jit(solution)/shard_map/ppermute | solution.py:265
  47.2 1.3 %collective-permute-start.11 = (bf16[256,1024]{1,0:T(8,128)(2,1)S(1)}, bf16[256,1024]{1,0:T(8,128)(2,1)S(1)}, u32[]{:S(2)}, u32[]{:S(2)}) collective-permute-start(bf16[256,1024]{1,0:T(8,128)(2,1)S(1)} %get-tuple-element.58), channel_id=1, source_target_pairs={{5,0},{7,2},{13,8},{15,10},{21,16},{23,18},{29,24},{31,26}} | collective-permute-start | bytes 1572872 | tf_op jit(solution)/shard_map/ppermute | solution.py:265
  48.5 0.7 collective-permute-start.9
  49.2 0.0 collective-permute-done.9.refs_0_
  49.2 8.5 %collective-permute-done.11.refs_7_.refs_5_.refs_4_ = bf16[256,1024]{1,0:T(8,128)(2,1)S(1)} collective-permute-done((bf16[256,1024]{1,0:T(8,128)(2,1)S(1)}, bf16[256,1024]{1,0:T(8,128)(2,1)S(1)}, u32[]{:S(2)}, u32[]{:S(2)}) %collective-permute-start.11) | collective-permute-done | bytes 524320 | tf_op jit(solution)/shard_map/ppermute | solution.py:265
  57.7 1.3 %shard_map.76 = (f32[8,1024]{1,0:T(8,128)S(1)}, f32[8,1024]{1,0:T(8,128)S(1)}, bf16[8,1024]{1,0:T(8,128)(2,1)S(1)}) custom-call(bf16[8,1024]{1,0:T(8,128)(2,1)S(1)} %collective-permute-done.9.refs_0_, f32[9,1024]{1,0:T(8,128)S(1)} %pad_maximum_fusion.refs_1_, bf16[1024,1024]{1,0:T(8,128)(2,1)S(1)} %collective-permute-done.10.refs_2_.refs_7_, ...), custom_call_target="tpu_custom_call" | custom-call | flops 1073741824 | bytes 4194304 | tf_op jit(solution)/shard_map/pallas_call | solution.py:217
  59.1 0.0 copy-done.5
  59.1 0.7 collective-permute-start.12
  59.8 1.0 %copy-done.3 = bf16[256,1024]{1,0:T(8,128)(2,1)S(1)} copy-done((bf16[256,1024]{1,0:T(8,128)(2,1)S(1)}, bf16[256,1024]{1,0:T(8,128)(2,1)}, u32[]{:S(2)}) %copy-start.3) | copy-done | bytes 524312
  60.9 1.0 %copy-done.6 = bf16[256,1024]{1,0:T(8,128)(2,1)S(1)} copy-done((bf16[256,1024]{1,0:T(8,128)(2,1)S(1)}, bf16[256,1024]{1,0:T(8,128)(2,1)}, u32[]{:S(2)}) %copy-start.6) | copy-done | bytes 524312
  61.9 1.3 %shard_map.77 = (f32[8,1024]{1,0:T(8,128)S(1)}, f32[8,1024]{1,0:T(8,128)S(1)}, bf16[8,1024]{1,0:T(8,128)(2,1)S(1)}) custom-call(bf16[8,1024]{1,0:T(8,128)(2,1)S(1)} %collective-permute-done.12.refs_0_, f32[9,1024]{1,0:T(8,128)S(1)} %pad_maximum_fusion.refs_1_, bf16[1024,1024]{1,0:T(8,128)(2,1)S(1)} %collective-permute-done.10.refs_2_.refs_7_, ...), custom_call_target="tpu_custom_call" | custom-call | flops 1073741824 | bytes 4194304 | tf_op jit(solution)/shard_map/pallas_call | solution.py:217
  63.2 0.7 collective-permute-start.13
  63.9 0.0 copy-start.1
  63.9 1.4 %collective-permute-start.18 = (f32[8,1024]{1,0:T(8,128)S(1)}, f32[8,1024]{1,0:T(8,128)S(1)}, u32[]{:S(2)}, u32[]{:S(2)}) collective-permute-start(f32[8,1024]{1,0:T(8,128)S(1)} %get-tuple-element.71), channel_id=1, source_target_pairs={{5,0},{7,2}} | collective-permute-start | bytes 98312 | tf_op jit(solution)/shard_map/ppermute | solution.py:265
  65.4 0.0 collective-permute-done.13.refs_0_
  65.4 2.1 %shard_map.78 = (f32[8,1024]{1,0:T(8,128)}, f32[8,1024]{1,0:T(8,128)S(1)}, f32[8,1024]{1,0:T(8,128)S(1)}, bf16[8,1024]{1,0:T(8,128)(2,1)S(1)}) custom-call(bf16[8,1024]{1,0:T(8,128)(2,1)S(1)} %collective-permute-done.13.refs_0_, f32[9,1024]{1,0:T(8,128)S(1)} %pad_maximum_fusion.refs_1_, bf16[1024,1024]{1,0:T(8,128)(2,1)S(1)} %collective-permute-done.10.refs_2_.refs_7_, ...), custom_call_target="tpu_custom_call" | custom-call | flops 1610612736 | bytes 6291456 | tf_op jit(solution)/shard_map/pallas_call | solution.py:217
  67.5 0.8 collective-permute-start.14
  68.3 0.2 broadcast_select_fusion.refs_0_
  68.5 0.0 copy-start.8
  68.5 0.0 collective-permute-done.14.refs_0_
  68.6 0.1 copy-done.7
  68.7 0.7 shard_map.79
  69.4 0.7 collective-permute-start.15
  70.1 0.0 collective-permute-done.18
  70.1 0.7 shard_map.80
  70.8 1.3 %collective-permute-start.16 = (bf16[8,1024]{1,0:T(8,128)(2,1)S(1)}, bf16[8,1024]{1,0:T(8,128)(2,1)S(1)}, u32[]{:S(2)}, u32[]{:S(2)}) collective-permute-start(bf16[8,1024]{1,0:T(8,128)(2,1)S(1)} %get-tuple-element.69), channel_id=1, source_target_pairs={{8,0},{10,2}} | collective-permute-start | bytes 49160 | tf_op jit(solution)/shard_map/ppermute | solution.py:265
  72.1 0.7 collective-permute-start.17
  72.8 0.7 collective-permute-start.19
  73.5 16.3 %collective-permute-done.16.from_pair = bf16[8,1024]{1,0:T(8,128)(2,1)S(1)} collective-permute-done((bf16[8,1024]{1,0:T(8,128)(2,1)S(1)}, bf16[8,1024]{1,0:T(8,128)(2,1)S(1)}, u32[]{:S(2)}, u32[]{:S(2)}) %collective-permute-start.16) | collective-permute-done | bytes 16416 | tf_op jit(solution)/shard_map/ppermute | solution.py:265
  89.8 0.9 %shard_map.81 = f32[8,1024]{1,0:T(8,128)S(1)} custom-call(s32[1]{0:T(128)} %bitcast.7.odd, bf16[8,1024]{1,0:T(8,128)(2,1)S(1)} %collective-permute-done.16.from_pair, bf16[8,1024]{1,0:T(8,128)(2,1)S(1)} %collective-permute-done.17.from_own, f32[8,1024]{1,0:T(8,128)S(1)} %pad_maximum_fusion.1.source, f32[8,1024]{1,0:T(8,128)S(1)} %broadcast_select_fusion.1.down_odd, ...), custom_call_target="tpu_custom_call" | custom-call | flops 1610612736 | bytes 6291456 | tf_op jit(solution)/shard_map/pallas_call | solution.py:412
  90.8 1.3 %collective-permute-start.20 = (f32[4,1024]{1,0:T(4,128)S(1)}, f32[4,1024]{1,0:T(4,128)S(1)}, u32[]{:S(2)}, u32[]{:S(2)}) collective-permute-start(f32[4,1024]{1,0:T(4,128)S(1)} %slice_select_fusion), channel_id=1, source_target_pairs={{5,4},{7,6},{0,1},{2,3},{8,9},{10,11},{12,13},{14,15},{16,17},{18,... | collective-permute-start | bytes 49160 | tf_op jit(solution)/shard_map/ppermute | solution.py:265
  92.1 0.8 collective-permute-done.20
  92.9 0.6 select_bitcast_fusion
  (34 shorter events, 0.1 us)
Async XLA Ops:
  0.6 4.9 %collective-permute-start.2 = (bf16[1024,1024]{1,0:T(8,128)(2,1)}, bf16[1024,1024]{1,0:T(8,128)(2,1)}, u32[]{:S(2)}, u32[]{:S(2)}) collective-permute-start(bf16[1024,1024]{1,0:T(8,128)(2,1)} %bitcast.15), channel_id=1, source_target_pairs={{0,1},{1,0},{2,3},{3,2},{4,5},{5,4},{6,7},{7,6},{8,9},{9,8},{10,11... | collective-permute-start | bytes 6291464 | tf_op jit(solution)/shard_map/ppermute | solution.py:265
  1.1 4.4 %collective-permute-start.1 = (s32[8,8]{1,0:T(8,128)}, s32[8,8]{1,0:T(8,128)S(1)}, u32[]{:S(2)}, u32[]{:S(2)}) collective-permute-start(s32[8,8]{1,0:T(8,128)} %bitcast.17), channel_id=1, source_target_pairs={{0,1},{1,0},{2,3},{3,2},{4,5},{5,4},{6,7},{7,6},{8,9},{9,8},{10,11... | collective-permute-start | bytes 776 | tf_op jit(solution)/shard_map/ppermute | solution.py:265
  2.3 1.6 %copy-start.9 = (bf16[1,1024,1024]{2,1,0:T(8,128)(2,1)S(1)}, bf16[1,1024,1024]{2,1,0:T(8,128)(2,1)}, u32[]{:S(2)}) copy-start(bf16[1,1024,1024]{2,1,0:T(8,128)(2,1)} %param.5) | copy-start | bytes 6291460
  3.9 0.7 copy-start.12
  8.3 0.8 copy-start.10
  9.1 11.5 %collective-permute-start.3 = (bf16[256,1024]{1,0:T(8,128)(2,1)}, bf16[256,1024]{1,0:T(8,128)(2,1)}, u32[]{:S(2)}, u32[]{:S(2)}) collective-permute-start(bf16[256,1024]{1,0:T(8,128)(2,1)} %get-tuple-element.40.own), channel_id=1, source_target_pairs={{0,3},{2,1},{4,7},{6,5},{8,11},{10,9},{12,15},{14,13},{16,19},{18,... | collective-permute-start | bytes 1572872 | tf_op jit(solution)/shard_map/ppermute | solution.py:265
  14.4 13.6 %collective-permute-start.5 = (bf16[256,1024]{1,0:T(8,128)(2,1)S(1)}, bf16[256,1024]{1,0:T(8,128)(2,1)S(1)}, u32[]{:S(2)}, u32[]{:S(2)}) collective-permute-start(bf16[256,1024]{1,0:T(8,128)(2,1)S(1)} %get-tuple-element.46.own), channel_id=1, source_target_pairs={{0,3},{2,1},{4,7},{6,5},{8,11},{10,9},{12,15},{14,13},{16,19},{18,... | collective-permute-start | bytes 1572872 | tf_op jit(solution)/shard_map/ppermute | solution.py:265
  15.7 1.0 %copy-start.11 = (bf16[256,1024]{1,0:T(8,128)(2,1)S(1)}, bf16[256,1024]{1,0:T(8,128)(2,1)}, u32[]{:S(2)}) copy-start(bf16[256,1024]{1,0:T(8,128)(2,1)} %copy-done.10) | copy-start | bytes 1572868
  16.8 9.3 %copy-start.13 = (f32[1,4,1024]{2,1,0:T(4,128)S(1)}, f32[1,4,1024]{2,1,0:T(4,128)}, u32[]{:S(2)}) copy-start(f32[1,4,1024]{2,1,0:T(4,128)} %param.9) | copy-start | bytes 49156
  16.8 9.4 %copy-start.14 = (s32[1,1024]{1,0:T(1,128)S(1)}, s32[1,1024]{1,0:T(1,128)}, u32[]{:S(2)}) copy-start(s32[1,1024]{1,0:T(1,128)} %param.8) | copy-start | bytes 12292
  22.3 10.9 %collective-permute-start.7 = (bf16[256,1024]{1,0:T(8,128)(2,1)S(1)}, bf16[256,1024]{1,0:T(8,128)(2,1)S(1)}, u32[]{:S(2)}, u32[]{:S(2)}) collective-permute-start(bf16[256,1024]{1,0:T(8,128)(2,1)S(1)} %get-tuple-element.43), channel_id=1, source_target_pairs={{5,0},{7,2},{13,8},{15,10},{21,16},{23,18},{29,24},{31,26},{0,3},{... | collective-permute-start | bytes 1572872 | tf_op jit(solution)/shard_map/ppermute | solution.py:265
  26.1 1.2 %collective-permute-start = (f32[4,1024]{1,0:T(4,128)S(1)}, f32[4,1024]{1,0:T(4,128)S(1)}, u32[]{:S(2)}, u32[]{:S(2)}) collective-permute-start(f32[4,1024]{1,0:T(4,128)S(1)} %bitcast.19), channel_id=1, source_target_pairs={{0,1},{1,0},{2,3},{3,2},{4,5},{5,4},{6,7},{7,6},{8,9},{9,8},{10,11... | collective-permute-start | bytes 49160 | tf_op jit(solution)/shard_map/ppermute | solution.py:265
  27.4 5.8 %collective-permute-start.4 = (f32[9,1024]{1,0:T(8,128)S(1)}, f32[9,1024]{1,0:T(8,128)S(1)}, u32[]{:S(2)}, u32[]{:S(2)}) collective-permute-start(f32[9,1024]{1,0:T(8,128)S(1)} %pad_maximum_fusion.refs_1_), channel_id=1, source_target_pairs={{12,8},{14,10},{20,16},{22,18},{28,24},{30,26},{1,5},{3,7}} | collective-permute-start | bytes 110600 | tf_op jit(solution)/shard_map/ppermute | solution.py:265
  28.5 11.3 %collective-permute-start.6 = (bf16[256,1024]{1,0:T(8,128)(2,1)S(1)}, bf16[256,1024]{1,0:T(8,128)(2,1)S(1)}, u32[]{:S(2)}, u32[]{:S(2)}) collective-permute-start(bf16[256,1024]{1,0:T(8,128)(2,1)S(1)} %get-tuple-element.49), channel_id=1, source_target_pairs={{5,0},{7,2},{13,8},{15,10},{21,16},{23,18},{29,24},{31,26},{0,3},{... | collective-permute-start | bytes 1572872 | tf_op jit(solution)/shard_map/ppermute | solution.py:265
  33.6 11.2 %collective-permute-start.8 = (bf16[256,1024]{1,0:T(8,128)(2,1)S(1)}, bf16[256,1024]{1,0:T(8,128)(2,1)S(1)}, u32[]{:S(2)}, u32[]{:S(2)}) collective-permute-start(bf16[256,1024]{1,0:T(8,128)(2,1)S(1)} %get-tuple-element.52), channel_id=1, source_target_pairs={{5,0},{7,2},{13,8},{15,10},{21,16},{23,18},{29,24},{31,26}} | collective-permute-start | bytes 1572872 | tf_op jit(solution)/shard_map/ppermute | solution.py:265
  44.8 13.0 %copy-start.2 = (bf16[256,1024]{1,0:T(8,128)(2,1)}, bf16[256,1024]{1,0:T(8,128)(2,1)S(1)}, u32[]{:S(2)}) copy-start(bf16[256,1024]{1,0:T(8,128)(2,1)S(1)} %collective-permute-done.8.refs_6_.refs_4_.refs_3_) | copy-start | bytes 1572868
  45.2 13.8 %copy-start = (bf16[1024,1024]{1,0:T(8,128)(2,1)}, bf16[1024,1024]{1,0:T(8,128)(2,1)S(1)}, u32[]{:S(2)}) copy-start(bf16[1024,1024]{1,0:T(8,128)(2,1)S(1)} %get-tuple-element.57.refs_2_) | copy-start | bytes 6291460
  45.9 11.8 %collective-permute-start.10 = (bf16[1024,1024]{1,0:T(8,128)(2,1)S(1)}, bf16[1024,1024]{1,0:T(8,128)(2,1)S(1)}, u32[]{:S(2)}, u32[]{:S(2)}) collective-permute-start(bf16[1024,1024]{1,0:T(8,128)(2,1)S(1)} %get-tuple-element.57.refs_2_), channel_id=1, source_target_pairs={{1,0},{3,2},{5,4},{7,6},{9,8},{11,10},{13,12},{15,14},{17,16},{19,... | collective-permute-start | bytes 6291464 | tf_op jit(solution)/shard_map/ppermute | solution.py:265
  47.2 10.5 %collective-permute-start.11 = (bf16[256,1024]{1,0:T(8,128)(2,1)S(1)}, bf16[256,1024]{1,0:T(8,128)(2,1)S(1)}, u32[]{:S(2)}, u32[]{:S(2)}) collective-permute-start(bf16[256,1024]{1,0:T(8,128)(2,1)S(1)} %get-tuple-element.58), channel_id=1, source_target_pairs={{5,0},{7,2},{13,8},{15,10},{21,16},{23,18},{29,24},{31,26}} | collective-permute-start | bytes 1572872 | tf_op jit(solution)/shard_map/ppermute | solution.py:265
  48.5 0.7 collective-permute-start.9
  57.7 1.4 %copy-start.5 = (bf16[256,1024]{1,0:T(8,128)(2,1)}, bf16[256,1024]{1,0:T(8,128)(2,1)S(1)}, u32[]{:S(2)}) copy-start(bf16[256,1024]{1,0:T(8,128)(2,1)S(1)} %collective-permute-done.11.refs_7_.refs_5_.refs_4_) | copy-start | bytes 1572868
  59.1 0.7 collective-permute-start.12
  59.8 1.0 %copy-start.3 = (bf16[256,1024]{1,0:T(8,128)(2,1)S(1)}, bf16[256,1024]{1,0:T(8,128)(2,1)}, u32[]{:S(2)}) copy-start(bf16[256,1024]{1,0:T(8,128)(2,1)} %copy-done.2) | copy-start | bytes 1572868
  60.9 1.0 %copy-start.6 = (bf16[256,1024]{1,0:T(8,128)(2,1)S(1)}, bf16[256,1024]{1,0:T(8,128)(2,1)}, u32[]{:S(2)}) copy-start(bf16[256,1024]{1,0:T(8,128)(2,1)} %copy-done.5) | copy-start | bytes 1572868
  63.2 2.1 %collective-permute-start.13 = (bf16[8,1024]{1,0:T(8,128)(2,1)S(1)}, bf16[8,1024]{1,0:T(8,128)(2,1)S(1)}, u32[]{:S(2)}, u32[]{:S(2)}) collective-permute-start(bf16[8,1024]{1,0:T(8,128)(2,1)S(1)} %get-tuple-element.60), channel_id=1, source_target_pairs={{16,24},{18,26}} | collective-permute-start | bytes 49160 | tf_op jit(solution)/shard_map/ppermute | solution.py:265
  63.9 4.4 %copy-start.1 = (bf16[1024,1024]{1,0:T(8,128)(2,1)S(1)}, bf16[1024,1024]{1,0:T(8,128)(2,1)}, u32[]{:S(2)}) copy-start(bf16[1024,1024]{1,0:T(8,128)(2,1)} %copy-done) | copy-start | bytes 6291460
  63.9 6.1 %collective-permute-start.18 = (f32[8,1024]{1,0:T(8,128)S(1)}, f32[8,1024]{1,0:T(8,128)S(1)}, u32[]{:S(2)}, u32[]{:S(2)}) collective-permute-start(f32[8,1024]{1,0:T(8,128)S(1)} %get-tuple-element.71), channel_id=1, source_target_pairs={{5,0},{7,2}} | collective-permute-start | bytes 98312 | tf_op jit(solution)/shard_map/ppermute | solution.py:265
  67.5 1.1 %copy-start.4 = (bf16[256,1024]{1,0:T(8,128)(2,1)S(1)}, bf16[256,1024]{1,0:T(8,128)(2,1)}, u32[]{:S(2)}) copy-start(bf16[256,1024]{1,0:T(8,128)(2,1)} %copy-done.2) | copy-start | bytes 1572868
  67.5 1.2 %copy-start.7 = (bf16[256,1024]{1,0:T(8,128)(2,1)S(1)}, bf16[256,1024]{1,0:T(8,128)(2,1)}, u32[]{:S(2)}) copy-start(bf16[256,1024]{1,0:T(8,128)(2,1)} %copy-done.5) | copy-start | bytes 1572868
  67.5 1.0 %collective-permute-start.14 = (bf16[8,1024]{1,0:T(8,128)(2,1)S(1)}, bf16[8,1024]{1,0:T(8,128)(2,1)S(1)}, u32[]{:S(2)}, u32[]{:S(2)}) collective-permute-start(bf16[8,1024]{1,0:T(8,128)(2,1)S(1)} %get-tuple-element.61), channel_id=1, source_target_pairs={{24,16},{26,18}} | collective-permute-start | bytes 49160 | tf_op jit(solution)/shard_map/ppermute | solution.py:265
  68.5 21.3 %copy-start.8 = (bf16[1024,1024]{1,0:T(8,128)(2,1)}, bf16[1024,1024]{1,0:T(8,128)(2,1)S(1)}, u32[]{:S(2)}) copy-start(bf16[1024,1024]{1,0:T(8,128)(2,1)S(1)} %broadcast_select_fusion.refs_0_) | copy-start | bytes 6291460
  69.4 0.7 collective-permute-start.15
  70.8 19.0 %collective-permute-start.16 = (bf16[8,1024]{1,0:T(8,128)(2,1)S(1)}, bf16[8,1024]{1,0:T(8,128)(2,1)S(1)}, u32[]{:S(2)}, u32[]{:S(2)}) collective-permute-start(bf16[8,1024]{1,0:T(8,128)(2,1)S(1)} %get-tuple-element.69), channel_id=1, source_target_pairs={{8,0},{10,2}} | collective-permute-start | bytes 49160 | tf_op jit(solution)/shard_map/ppermute | solution.py:265
  72.1 17.7 %collective-permute-start.17 = (bf16[8,1024]{1,0:T(8,128)(2,1)S(1)}, bf16[8,1024]{1,0:T(8,128)(2,1)S(1)}, u32[]{:S(2)}, u32[]{:S(2)}) collective-permute-start(bf16[8,1024]{1,0:T(8,128)(2,1)S(1)} %get-tuple-element.69), channel_id=1, source_target_pairs={{8,5},{10,7}} | collective-permute-start | bytes 49160 | tf_op jit(solution)/shard_map/ppermute | solution.py:265
  72.8 17.9 %collective-permute-start.19 = (f32[8,1024]{1,0:T(8,128)S(1)}, f32[8,1024]{1,0:T(8,128)S(1)}, u32[]{:S(2)}, u32[]{:S(2)}) collective-permute-start(f32[8,1024]{1,0:T(8,128)S(1)} %select_select_fusion), channel_id=1, source_target_pairs={{8,12},{10,14},{16,20},{18,22},{24,28},{26,30}} | collective-permute-start | bytes 98312 | tf_op jit(solution)/shard_map/ppermute | solution.py:265
  90.8 2.1 %collective-permute-start.20 = (f32[4,1024]{1,0:T(4,128)S(1)}, f32[4,1024]{1,0:T(4,128)S(1)}, u32[]{:S(2)}, u32[]{:S(2)}) collective-permute-start(f32[4,1024]{1,0:T(4,128)S(1)} %slice_select_fusion), channel_id=1, source_target_pairs={{5,4},{7,6},{0,1},{2,3},{8,9},{10,11},{12,13},{14,15},{16,17},{18,... | collective-permute-start | bytes 49160 | tf_op jit(solution)/shard_map/ppermute | solution.py:265

commit v6 on v5

v6 whole, which is shorter than its diff:
```python
import functools

import jax
import jax.numpy as jnp
from jax import lax
from jax.experimental import pallas as pl
from jax.experimental.pallas import tpu as pltpu
from jax.sharding import PartitionSpec as P

AXES = ("layer", "box")
AHEAD = 2
SMALL_AT = 0
VMEM = pl.BlockSpec(memory_space=pltpu.VMEM)
SMEM = pl.BlockSpec(memory_space=pltpu.SMEM)
PARAMS = pltpu.CompilerParams(vmem_limit_bytes=24 * 1024 * 1024)
SWEEP_PARAMS = pltpu.CompilerParams(vmem_limit_bytes=10 * 1024 * 1024)
OWN, PAIR = 0, 1


def cost(flops, moved):
    return pl.CostEstimate(flops=flops, bytes_accessed=moved, transcendentals=0)


def dot32(a, b):
    return jnp.dot(a, b, preferred_element_type=jnp.float32)


def dot32_t(a, b):
    return lax.dot_general(a, b, (((1,), (1,)), ((), ())), preferred_element_type=jnp.float32)


def minus_face(joined, face_at, inverse, right):
    face = inverse.shape[0]
    left = joined[:, face_at : face_at + face].astype(jnp.bfloat16)
    product = dot32(left, inverse).astype(jnp.bfloat16)
    return (joined - dot32(product, right)).astype(jnp.bfloat16)


def masked(values, pattern, row_at, row_count, block_at):
    width = values.shape[1]
    block = width // pattern.shape[1]
    strips = []
    for r in range(row_count // block):
        at = slice(row_at + r * block, row_at + (r + 1) * block)
        strips.append(
            jnp.concatenate(
                [
                    values[at, c * block : (c + 1) * block].astype(jnp.float32)
                    * (0.5 * pattern[block_at + r, c].astype(jnp.float32))
                    for c in range(width // block)
                ],
                axis=1,
            )
        )
    return jnp.concatenate(strips, axis=0)


def mask_kernel(pattern, values, out):
    block = values.shape[1] // pattern.shape[1]
    for r in range(values.shape[0] // block):
        out[r * block : (r + 1) * block] = masked(values, pattern, r * block, block, r).astype(
            jnp.bfloat16
        )


def leaf_kernel(other_pattern, own, other_there, inverse, *refs):
    *outs, other, sems = refs
    count, face, width = other.shape
    block = width // other_pattern.shape[1]
    copies = [
        pltpu.make_async_copy(other_there.at[pl.ds(i * face, face)], other.at[i], sems.at[i])
        for i in range(count)
    ]
    for copy in copies:
        copy.start()
    right = None
    for i in range(count):
        copies[i].wait()
        joined = own[i * face : (i + 1) * face].astype(jnp.float32) + masked(
            other.at[i], other_pattern, 0, face, i * face // block
        )
        if right is None:
            right = joined.astype(jnp.bfloat16)
        outs[i][...] = minus_face(joined, 0, inverse[...], right)


def leaf_combine(other_pattern, own, other, inverse):
    width = own.shape[1]
    face = inverse.shape[0]
    count = width // face
    return pl.pallas_call(
        leaf_kernel,
        out_shape=[jax.ShapeDtypeStruct((face, width), jnp.bfloat16)] * count,
        in_specs=[SMEM, VMEM, pl.BlockSpec(memory_space=pl.ANY), VMEM],
        out_specs=[VMEM] * count,
        scratch_shapes=[
            pltpu.VMEM((count, face, width), jnp.bfloat16),
            pltpu.SemaphoreType.DMA((count,)),
        ],
        compiler_params=PARAMS,
        cost_estimate=cost(2 * width * face * (width + face), 6 * width * width),
    )(other_pattern, own, other, inverse)


def combine_kernel(face_at, is_face, with_next, with_rest, is_second, own, other, inverse, *refs):
    refs = list(refs)
    following = refs.pop(0) if with_next else None
    right = None if is_face else refs.pop(0)[...]
    before = refs.pop(0) if with_rest else None
    out = refs.pop(0)
    joined = 0.5 * (own[...].astype(jnp.float32) + other[...].astype(jnp.float32))
    if is_face:
        right = joined.astype(jnp.bfloat16)
        refs.pop(0)[...] = right
    at = 0
    if with_rest:
        at = before.shape[0]
        out[:at] = before[...]
    out[at:] = minus_face(joined, face_at, inverse[...], right)
    if with_next:

        @pl.when(is_second[0] == 0)
        def _():
            out[...] = following[...]


def combine(is_second, own, other, inverse, following, right, face_at, before=None):
    is_face = right is None
    rows, width = own.shape
    extra = [value for value in (following, right, before) if value is not None]
    out_rows = rows if before is None else rows + before.shape[0]
    outs = [jax.ShapeDtypeStruct((out_rows, width), jnp.bfloat16)]
    if is_face:
        outs.append(jax.ShapeDtypeStruct((rows, width), jnp.bfloat16))
    result = pl.pallas_call(
        functools.partial(
            combine_kernel, face_at, is_face, following is not None, before is not None
        ),
        out_shape=outs,
        in_specs=[SMEM] + [VMEM] * (3 + len(extra)),
        out_specs=[VMEM] * len(outs),
        compiler_params=PARAMS,
        cost_estimate=cost(0, 0),
    )(is_second, own, other, inverse, *extra)
    return result[0], (result[1] if is_face else right)


def assemble_kernel(*refs):
    *parts, out = refs
    at = 0
    for part in parts:
        out[at : at + part.shape[0]] = part[...]
        at += part.shape[0]


def assemble(parts):
    rows, width = sum(part.shape[0] for part in parts), parts[0].shape[1]
    return pl.pallas_call(
        assemble_kernel,
        out_shape=jax.ShapeDtypeStruct((rows, width), jnp.bfloat16),
        in_specs=[VMEM] * len(parts),
        out_specs=VMEM,
        compiler_params=PARAMS,
        cost_estimate=cost(0, 4 * rows * width),
    )(*parts)


def spread(pieces, rows):
    return jnp.concatenate([dot32_t(rows, piece[...]) for piece in pieces], axis=1)


def gather_sum(pieces, rows):
    at, total = 0, None
    for piece in pieces:
        size = piece.shape[0]
        term = dot32(rows[:, at : at + size], piece[...])
        total = term if total is None else total + term
        at += size
    return total


def lanes_at(rows, index_row):
    lanes = 128
    count, width = rows.shape
    parts = [rows[:, at : at + lanes] for at in range(0, width, lanes)]
    outs = []
    for at in range(0, width, lanes):
        index = jnp.broadcast_to(index_row[:, at : at + lanes].astype(jnp.int32), (count, lanes))
        lane, part = index % lanes, index // lanes
        total = jnp.zeros((count, lanes), rows.dtype)
        for k, values in enumerate(parts):
            total = jnp.where(part == k, jnp.take_along_axis(values, lane, axis=1), total)
        outs.append(total)
    return jnp.concatenate(outs, axis=1)


def segment_kernel(coupling, pieces_of, down_steps, up_steps, active, *refs):
    @pl.when(active[0] == 1)
    def _():
        run_segment(coupling, pieces_of, down_steps, up_steps, *refs)


def run_segment(coupling, pieces_of, down_steps, up_steps, *refs):
    refs = list(refs)
    state = refs.pop(0)[...]
    maps, downs = {}, {}
    operands = []
    for slot in down_steps:
        operands.append(refs.pop(0))
        maps[slot] = [refs.pop(0) for _ in range(pieces_of[slot])]
    for slot in up_steps:
        if slot not in down_steps:
            downs[slot] = refs.pop(0)[...]
            maps[slot] = [refs.pop(0) for _ in range(pieces_of[slot])]
    for slot, packed in zip(down_steps, operands):
        count = state.shape[0]
        moved = lanes_at(state.astype(jnp.float32), packed[count:]).astype(jnp.bfloat16)
        downs[slot] = packed[:count] + coupling * spread(maps[slot], moved)
        state = downs[slot].astype(jnp.bfloat16)
        refs.pop(0)[...] = downs[slot]
    for slot in up_steps:
        value = downs[slot] + coupling * gather_sum(maps[slot], state)
        state = value.astype(jnp.bfloat16)
        refs.pop(0)[...] = value
    refs.pop(0)[...] = state


def segment(coupling, active, arrived, packed, downs, maps, down_steps, up_steps):
    operands = [active.astype(jnp.int32)[None], arrived]
    for slot in down_steps:
        operands += [packed[slot], *maps[slot]]
    for slot in up_steps:
        if slot not in down_steps:
            operands += [downs[slot], *maps[slot]]
    rows = jax.ShapeDtypeStruct(arrived.shape, jnp.float32)
    steps = len(down_steps) + len(up_steps)
    results = pl.pallas_call(
        functools.partial(
            segment_kernel, coupling, [len(entry) for entry in maps], down_steps, up_steps
        ),
        out_shape=[rows] * steps + [jax.ShapeDtypeStruct(arrived.shape, jnp.bfloat16)],
        in_specs=[SMEM] + [VMEM] * (len(operands) - 1),
        out_specs=[VMEM] * (steps + 1),
        compiler_params=SWEEP_PARAMS,
        cost_estimate=cost(steps * 2 * 256 * 1024 * 1024, steps * 2 * 1024 * 1024),
    )(*operands)
    return results[:-1], results[-1]


def last_kernel(coupling, count, odd, from_pair, from_own, source, down_odd, *refs):
    own, pair, out = refs[:count], refs[count : 2 * count], refs[2 * count]
    total = gather_sum(pair, from_pair[...]) + gather_sum(own, from_own[...])
    up_odd = down_odd[...] + coupling * total
    up_even = source[...] + coupling * gather_sum(own, up_odd.astype(jnp.bfloat16))
    out[...] = jnp.where(odd[0] == 1, up_odd, up_even)


def on_device(box_maps, block_pattern, face_inverses, index_map, sources):
    boxes = lax.axis_size("box")
    layers = lax.axis_size("layer")
    coupling = float(boxes) ** 0.5
    levels = boxes.bit_length() - 1
    face = face_inverses.shape[2]
    width = box_maps.shape[2]
    rows_here = sources.shape[1]
    position = lax.axis_index("box")
    layer = lax.axis_index("layer")
    is_second = position % 2 == 1
    second_flag = is_second.astype(jnp.int32)[None]

    chain = [(layer_at, (OWN, PAIR)) for layer_at in range(2, layers, 2)]
    pair_moves = [(layer_at + 1, layer_at) for layer_at in range(0, layers, 2)]

    def route(moves, source_core=1, target_core=1):
        return [
            (a * boxes + b + source_core, z * boxes + b + target_core)
            for a, z in moves
            for b in range(0, boxes, 2)
        ]

    def over_box(change, starts):
        return [(i * boxes + b, i * boxes + (b ^ change)) for i in range(layers) for b in starts]

    def send(value, pairs_of_devices):
        return lax.ppermute(value, AXES, pairs_of_devices)

    def after(value, *others):
        return lax.optimization_barrier((value, *others))[0]

    every = [(i, i) for i in range(layers)]

    raw = box_maps[0]
    pattern = block_pattern[0]
    raw_other = send(raw, over_box(1, range(boxes)))
    pattern_other = send(pattern, over_box(1, range(boxes)))
    first_sources = send(sources[0], route(every, 0, 1))
    own_half = pl.pallas_call(
        mask_kernel,
        out_shape=jax.ShapeDtypeStruct(raw.shape, jnp.bfloat16),
        in_specs=[SMEM, VMEM],
        out_specs=VMEM,
        compiler_params=PARAMS,
        cost_estimate=cost(width * width, 4 * width * width),
    )(pattern, raw)

    def inverse_of(level):
        node = (boxes >> (level + 1)) - 1 + (position >> (level + 1))
        return lax.dynamic_index_in_dim(face_inverses[0], node, 0, keepdims=False).astype(
            jnp.bfloat16
        )

    rows = -(-2 * rows_here // 8) * 8
    packed = jnp.concatenate(
        [
            first_sources,
            sources[0],
            jnp.zeros((rows - 2 * rows_here, width), jnp.float32),
            index_map.astype(jnp.float32),
        ],
        axis=0,
    )

    pieces = tuple((at, face) for at in range(0, width, face))
    current = dict(
        zip(pieces, leaf_combine(pattern_other, own_half, raw_other, inverse_of(0)))
    )

    for level in range(1, levels):
        final = level == levels - 1
        change = 1 << level
        inverse = inverse_of(level)
        near = (level * face, (level ^ 1) * face)
        order = [(at, face) for at in near] + [piece for piece in pieces if piece[0] not in near]
        received = {}
        right = None
        if not final:
            for piece in order:
                received[piece] = send(current[piece], over_box(change, range(boxes)))
            renewed = {}
            for piece in order:
                renewed[piece], right = combine(
                    second_flag,
                    current[piece],
                    received[piece],
                    inverse,
                    None,
                    right,
                    level * face,
                )
            current = renewed
            continue
        over = over_box(change ^ 1, range(0, boxes, 2))
        evens = [(target, target) for _, target in pair_moves]
        for piece in order[:AHEAD]:
            received[piece] = send(current[piece], over)
        pair_pieces = []
        own_pieces = []
        rest = None
        for k, piece in enumerate(order):
            following = order[k + AHEAD] if k + AHEAD < len(order) else None
            other = received[piece]
            if k == SMALL_AT + 2:
                other = after(other, pair_packed)
            if k == len(order) - 1:
                other = after(other, pair_pieces[0][1])
            payload, right = combine(
                second_flag,
                current[piece],
                other,
                inverse,
                None if following is None else current[following],
                right,
                level * face,
                rest,
            )
            if following is None:
                rest = payload
            else:
                received[following] = send(payload, route(pair_moves, 1, 0) + over)
                pair_pieces.append((piece[0], send(received[following], route(evens, 0, 1))))
                own_pieces.append((piece[0], payload))
            if k == SMALL_AT:
                sendable = after(packed, payload)
                pair_packed = send(sendable, route(pair_moves[1:] + [(0, 1)]))
    rest_at = order[AHEAD][0]
    own_pieces.append((rest_at, rest))
    pair_pieces.append((rest_at, send(rest, route(pair_moves))))
    own_maps, pair_maps = [
        [value for _, value in sorted(entries, key=lambda entry: entry[0])]
        for entries in (own_pieces, pair_pieces)
    ]
    merged = assemble(own_maps)
    small = [packed, pair_packed]

    maps = [own_maps, pair_maps]
    first = after(pair_packed[:rows].astype(jnp.bfloat16), merged)
    (down_odd,), state = segment(
        coupling, is_second & (layer == 1), first, small, {}, maps, (OWN,), ()
    )
    at = 1
    kept = []
    ups = {}
    for k, (target, slots) in enumerate(chain):
        arrived = send(state, route([(at, target)]))
        at = target
        turn = k == len(chain) - 1
        back = tuple(reversed(slots))
        results, state = segment(
            coupling,
            is_second & (layer == at),
            arrived,
            small,
            {},
            maps,
            slots,
            back[1:] if turn else (),
        )
        kept.append(dict(zip(slots, results)))
        if k == 0:
            down_odd_pair = send(after(down_odd, state), route([(1, 0)]))
            merged_first = send(after(merged, state), route(every, 1, 0))
        if turn:
            ups[at] = dict(zip(back[1:], results[len(slots) :]))
            ups[at][back[0]] = results[len(slots) - 1]
    result = jnp.where(is_second, merged, after(merged_first, state))
    down_odd = jnp.where(layer == 0, down_odd_pair, down_odd)

    for k in reversed(range(len(chain) - 1)):
        target, slots = chain[k]
        arrived = send(state, route([(at, target)]))
        at = target
        back = tuple(reversed(slots))
        results, state = segment(
            coupling, is_second & (layer == at), arrived, small, kept[k], maps, (), back
        )
        ups[at] = dict(zip(back, results))
    from_own = send(state, route([(at, 1)]))
    from_pair = send(state, route([(at, 0)]))

    mine = [jnp.zeros((rows, width), jnp.float32)] * 2
    for target, values in ups.items():
        for slot in (OWN, PAIR):
            mine[slot] = jnp.where(layer == target, values[slot], mine[slot])
    settled = mine[OWN] + send(mine[PAIR], route([(z, a) for a, z in pair_moves[1:]]))

    odd = (layer % 2).astype(jnp.int32)[None]
    last = pl.pallas_call(
        functools.partial(last_kernel, coupling, len(pair_maps)),
        out_shape=jax.ShapeDtypeStruct((rows, width), jnp.float32),
        in_specs=[SMEM] + [VMEM] * (4 + 2 * len(pair_maps)),
        out_specs=VMEM,
        compiler_params=SWEEP_PARAMS,
        cost_estimate=cost(6 * 256 * 1024 * 1024, 6 * 1024 * 1024),
    )(odd, from_pair, from_own, packed[:rows], down_odd, *own_maps, *pair_maps)
    upward = jnp.where(layer < 2, last, settled)
    first_rows = send(upward[:rows_here], route(every, 1, 0))
    upward = jnp.where(is_second, upward[rows_here : 2 * rows_here], first_rows)
    return (result[None], upward[None])


def solution(mesh):
    return jax.shard_map(
        on_device,
        mesh=mesh,
        in_specs=(
            P("layer", "box", None),
            P("layer", "box", None),
            P("layer", None, None, None),
            P("layer", None),
            P("layer", "box", None),
        ),
        out_specs=(P("layer", None, None), P("layer", "box", None)),
        check_vma=False,
    )
```

time: 94.2 us -> 106 us (1.13)
  starting transfers between devices: 29 us -> 34.5 us
  other arithmetic: 0.91 us -> 3.81 us
  waiting for transfers between devices: 38.5 us -> 40.3 us
    ppermute x21 -> x22, starting transfers between devices: 29 us -> 34.5 us  [send(): return lax.ppermute(value, AXES, pairs_of_devices)]
    broadcast_in_dim x1 -> x2, other arithmetic: 0.61 us -> 3.74 us  [on_device(): return (result[None], upward[None])]
    ppermute x21 -> x22, waiting for transfers between devices: 38.5 us -> 40.3 us  [send(): return lax.ppermute(value, AXES, pairs_of_devices)]
    unnamed x30 -> x20, local copies, waits for them, and re-layouts: 6.36 us -> 6.98 us
  transfers between devices with their start and end apart: 21 -> 22, of which waited for: 7 -> 6; matrix products, arithmetic and copies ran while one was open for 1% -> 2% of each run, Pallas kernels for 10% -> 11%
where the time goes in v6:
time: 106 us; the launch traced here: 105 us
  waiting for transfers between devices  40.3 us (38%)
  starting transfers between devices  34.5 us (33%)
  Pallas kernels  17.4 us (16%)
  local copies, waits for them, and re-layouts  8.04 us (8%)
  other arithmetic  3.81 us (4%)
  between operations  1.11 us (1%)
    ppermute x22, waiting for transfers between devices, send(): return lax.ppermute(value, AXES, pairs_of_devices)  40.3 us
    ppermute x22, starting transfers between devices, send(): return lax.ppermute(value, AXES, pairs_of_devices)  34.5 us
    unnamed x20, local copies, waits for them, and re-layouts  6.98 us
    pallas_call x6, Pallas kernels, segment(): pl.pallas_call(functools.partial(segment_kernel, coupling, [len(entry) fo...  5.83 us
    pallas_call x4, Pallas kernels, combine(): pl.pallas_call(functools.partial(combine_kernel, face_at, is_face, follow...  3.94 us
    broadcast_in_dim x2, other arithmetic, on_device(): return (result[None], upward[None])  3.74 us
    pallas_call x1, Pallas kernels, leaf_combine(): pl.pallas_call(leaf_kernel, out_shape=[jax.ShapeDtypeStruct((face, width)...  3.21 us
  transfers between devices with their start and end apart: 22, of which 6 were waited for; matrix products, arithmetic and copies ran while one was open for 2% of the time, Pallas kernels for 11%

profile of v6, /device:TPU:0, one launch (start us, length us, event | category | flops | bytes accessed | tf_op | source)
XLA Modules:
  0.0 105.1 jit_solution(6850302926698382607)
XLA Ops:
  0.6 0.5 collective-permute-start.1
  1.1 0.1 collective-permute-start
  1.2 1.1 %fusion.1 = (bf16[256,256]{1,0:T(8,128)(2,1)S(1)}, bf16[256,256]{1,0:T(8,128)(2,1)S(1)}) fusion(f32[1,3,256,256]{3,2,1,0:T(8,128)} %param.7, s32[]{:T(128)S(6)} %select_n.81, s32[]{:T(128)S(6)} %select_n.80), kind=kLoop, calls=%fused_computation.4 | loop fusion | bytes 524296 | tf_op jit(solution)/shard_map/convert_element_type | solution.py:308
  2.3 0.0 copy-start.4
  2.3 1.6 %copy-done.4 = bf16[1,1024,1024]{2,1,0:T(8,128)(2,1)S(1)} copy-done((bf16[1,1024,1024]{2,1,0:T(8,128)(2,1)S(1)}, bf16[1,1024,1024]{2,1,0:T(8,128)(2,1)}, u32[]{:S(2)}) %copy-start.4) | copy-done | bytes 2097176
  3.9 0.7 copy-done.7
  4.6 0.9 shard_map.68.own
  5.5 0.0 collective-permute-done.other_pattern
  5.5 0.0 collective-permute-done.1.other_there
  5.5 3.2 %shard_map.69 = (bf16[256,1024]{1,0:T(8,128)(2,1)S(1)}, bf16[256,1024]{1,0:T(8,128)(2,1)}, bf16[256,1024]{1,0:T(8,128)(2,1)S(1)}, bf16[256,1024]{1,0:T(8,128)(2,1)S(1)}) custom-call(s32[8,8]{1,0:T(8,128)S(1)} %collective-permute-done.other_pattern, bf16[1024,1024]{1,0:T(8,128)(2,1)S(1)} %shard_map.68.own, ...), custom_call_target="tpu_custom_call" | custom-call | flops 671088640 | bytes 6291456 | tf_op jit(solution)/shard_map/pallas_call | solution.py:91
  8.8 0.8 copy-done.5
  9.6 4.7 %collective-permute-start.3 = (bf16[256,1024]{1,0:T(8,128)(2,1)}, bf16[256,1024]{1,0:T(8,128)(2,1)S(1)}, u32[]{:S(2)}, u32[]{:S(2)}) collective-permute-start(bf16[256,1024]{1,0:T(8,128)(2,1)} %get-tuple-element.34.own), channel_id=1, source_target_pairs={{0,3},{2,1},{4,7},{6,5},{8,11},{10,9},{12,15},{14,13},{16,19},{18,... | collective-permute-start | bytes 1572872 | tf_op jit(solution)/shard_map/ppermute | solution.py:285
  14.3 1.3 %collective-permute-start.2 = (bf16[256,1024]{1,0:T(8,128)(2,1)}, bf16[256,1024]{1,0:T(8,128)(2,1)S(1)}, u32[]{:S(2)}, u32[]{:S(2)}) collective-permute-start(bf16[256,1024]{1,0:T(8,128)(2,1)} %copy-done.5), channel_id=1, source_target_pairs={{0,3},{2,1},{4,7},{6,5},{8,11},{10,9},{12,15},{14,13},{16,19},{18,... | collective-permute-start | bytes 1572872 | tf_op jit(solution)/shard_map/ppermute | solution.py:285
  15.6 5.6 %collective-permute-done.3.other = bf16[256,1024]{1,0:T(8,128)(2,1)S(1)} collective-permute-done((bf16[256,1024]{1,0:T(8,128)(2,1)}, bf16[256,1024]{1,0:T(8,128)(2,1)S(1)}, u32[]{:S(2)}, u32[]{:S(2)}) %collective-permute-start.3) | collective-permute-done | bytes 524320 | tf_op jit(solution)/shard_map/ppermute | solution.py:285
  21.2 1.5 %shard_map.70 = (bf16[256,1024]{1,0:T(8,128)(2,1)S(1)}, bf16[256,1024]{1,0:T(8,128)(2,1)S(1)}) custom-call(s32[1]{0:T(128)} %bitcast.is_second, bf16[256,1024]{1,0:T(8,128)(2,1)} %get-tuple-element.34.own, bf16[256,1024]{1,0:T(8,128)(2,1)S(1)} %collective-permute-done.3.other, bf16[256,256]{1,0:T(8,128)(2,1)S(1)} %get-tuple-element.62.inverse, ...), custom_call_target="tpu_custom_call" | custom-call | tf_op jit(solution)/shard_map/pallas_call | solution.py:135
  22.8 3.7 %collective-permute-start.5 = (bf16[256,1024]{1,0:T(8,128)(2,1)S(1)}, bf16[256,1024]{1,0:T(8,128)(2,1)S(1)}, u32[]{:S(2)}, u32[]{:S(2)}) collective-permute-start(bf16[256,1024]{1,0:T(8,128)(2,1)S(1)} %get-tuple-element.37.refs_1_.refs_3_.refs_7_), channel_id=1, source_target_pairs={{5,0},{7,2},{13,8},{15,10},{21,16},{23,18},{29,24},{31,26},{0,3},{... | collective-permute-start | bytes 1572872 | tf_op jit(solution)/shard_map/ppermute | solution.py:285
  26.5 0.4 collective-permute-done.2.other
  26.8 0.5 shard_map.71.refs_0_.refs_2_.refs_6_
  27.3 4.0 %collective-permute-start.4 = (bf16[256,1024]{1,0:T(8,128)(2,1)S(1)}, bf16[256,1024]{1,0:T(8,128)(2,1)}, u32[]{:S(2)}, u32[]{:S(2)}) collective-permute-start(bf16[256,1024]{1,0:T(8,128)(2,1)S(1)} %shard_map.71.refs_0_.refs_2_.refs_6_), channel_id=1, source_target_pairs={{5,0},{7,2},{13,8},{15,10},{21,16},{23,18},{29,24},{31,26},{0,3},{... | collective-permute-start | bytes 1572872 | tf_op jit(solution)/shard_map/ppermute | solution.py:285
  31.3 2.0 %collective-permute-done.5.other = bf16[256,1024]{1,0:T(8,128)(2,1)S(1)} collective-permute-done((bf16[256,1024]{1,0:T(8,128)(2,1)S(1)}, bf16[256,1024]{1,0:T(8,128)(2,1)S(1)}, u32[]{:S(2)}, u32[]{:S(2)}) %collective-permute-start.5) | collective-permute-done | bytes 524320 | tf_op jit(solution)/shard_map/ppermute | solution.py:285
  33.3 2.2 %collective-permute-start.6 = (bf16[256,1024]{1,0:T(8,128)(2,1)S(1)}, bf16[256,1024]{1,0:T(8,128)(2,1)S(1)}, u32[]{:S(2)}, u32[]{:S(2)}) collective-permute-start(bf16[256,1024]{1,0:T(8,128)(2,1)S(1)} %collective-permute-done.5.other), channel_id=1, source_target_pairs={{0,1},{2,3},{8,9},{10,11},{16,17},{18,19},{24,25},{26,27}} | collective-permute-start | bytes 1572872 | tf_op jit(solution)/shard_map/ppermute | solution.py:285
  35.5 1.3 %collective-permute-start.7 = (f32[4,1024]{1,0:T(4,128)S(1)}, f32[4,1024]{1,0:T(4,128)S(1)}, u32[]{:S(2)}, u32[]{:S(2)}) collective-permute-start(f32[4,1024]{1,0:T(4,128)S(1)} %bitcast.21), channel_id=1, source_target_pairs={{0,1},{2,3},{4,5},{6,7},{8,9},{10,11},{12,13},{14,15},{16,17},{18,... | collective-permute-start | bytes 49160 | tf_op jit(solution)/shard_map/ppermute | solution.py:285
  36.8 0.8 collective-permute-done.7
  37.6 0.7 collective-permute-start.8
  38.3 0.0 collective-permute-done.8.refs_5_
  38.3 0.4 shard_map.72.refs_1_
  38.7 0.3 collective-permute-done.4.other
  39.0 0.0 collective-permute-done.6.refs_7_.refs_3_.refs_4_
  39.0 0.8 copy-done
  39.8 1.5 %shard_map.73.refs_2_.refs_4_.refs_8_ = bf16[512,1024]{1,0:T(8,128)(2,1)S(1)} custom-call(s32[1]{0:T(128)} %bitcast.is_second, bf16[256,1024]{1,0:T(8,128)(2,1)S(1)} %get-tuple-element.33.refs_0_.own, bf16[256,1024]{1,0:T(8,128)(2,1)} %collective-permute-done.4.other, bf16[256,256]{1,0:T(8,128)(2,1)S(1)} %get-tuple-element.62.inverse, ...), custom_call_target="tpu_custom_call" | custom-call | tf_op jit(solution)/shard_map/pallas_call | solution.py:135
  41.3 0.7 collective-permute-start.11
  42.0 6.9 %collective-permute-start.10 = (bf16[256,1024]{1,0:T(8,128)(2,1)}, bf16[256,1024]{1,0:T(8,128)(2,1)}, u32[]{:S(2)}, u32[]{:S(2)}) collective-permute-start(bf16[256,1024]{1,0:T(8,128)(2,1)} %collective-permute-done.4.other), channel_id=1, source_target_pairs={{0,1},{2,3},{8,9},{10,11},{16,17},{18,19},{24,25},{26,27}} | collective-permute-start | bytes 1572872 | tf_op jit(solution)/shard_map/ppermute | solution.py:285
  48.9 1.5 %shard_map.74 = bf16[1024,1024]{1,0:T(8,128)(2,1)} custom-call(bf16[256,1024]{1,0:T(8,128)(2,1)S(1)} %shard_map.71.refs_0_.refs_2_.refs_6_, bf16[256,1024]{1,0:T(8,128)(2,1)S(1)} %get-tuple-element.37.refs_1_.refs_3_.refs_7_, bf16[512,1024]{1,0:T(8,128)(2,1)S(1)} %shard_map.73.refs_2_.refs_4_.refs_8_), custom_call_target="tpu_custom_call" | custom-call | bytes 4194304 | tf_op jit(solution)/shard_map/pallas_call | solution.py:158
  50.4 0.7 collective-permute-start.9
  51.1 0.0 collective-permute-done.10.refs_6_.refs_2_.refs_3_
  51.1 0.0 collective-permute-done.9.refs_0_
  51.1 0.0 collective-permute-done.11.refs_8_.refs_4_.refs_5_
  51.1 1.0 copy-done.1
  52.1 1.0 shard_map.76
  53.2 1.3 %collective-permute-start.12 = (bf16[1024,1024]{1,0:T(8,128)(2,1)}, bf16[1024,1024]{1,0:T(8,128)(2,1)}, u32[]{:S(2)}, u32[]{:S(2)}) collective-permute-start(bf16[1024,1024]{1,0:T(8,128)(2,1)} %shard_map.74), channel_id=1, source_target_pairs={{1,0},{3,2},{5,4},{7,6},{9,8},{11,10},{13,12},{15,14},{17,16},{19,... | collective-permute-start | bytes 6291464 | tf_op jit(solution)/shard_map/ppermute | solution.py:285
  54.5 0.7 collective-permute-start.13
  55.2 0.0 collective-permute-done.13.refs_0_
  55.2 1.0 copy-done.2
  56.2 1.0 shard_map.77
  57.2 0.7 collective-permute-start.14
  57.9 1.0 copy-done.3
  59.0 1.7 %shard_map.78 = (f32[8,1024]{1,0:T(8,128)}, f32[8,1024]{1,0:T(8,128)S(1)}, f32[8,1024]{1,0:T(8,128)S(1)}, bf16[8,1024]{1,0:T(8,128)(2,1)S(1)}) custom-call(s32[1]{0:T(128)} %bitcast.8.active, bf16[8,1024]{1,0:T(8,128)(2,1)S(1)} %collective-permute-done.14.refs_0_, f32[9,1024]{1,0:T(8,128)S(1)} %pad_maximum_fusion.refs_1_, ...), custom_call_target="tpu_custom_call" | custom-call | flops 1610612736 | bytes 6291456 | tf_op jit(solution)/shard_map/pallas_call | solution.py:237
  60.6 0.7 collective-permute-start.15
  61.3 0.7 collective-permute-start.19
  62.0 0.0 collective-permute-done.15.refs_0_
  62.0 1.0 shard_map.79
  63.0 0.7 collective-permute-start.16
  63.7 1.0 shard_map.80
  64.8 0.7 collective-permute-start.18
  65.4 0.7 collective-permute-start.17
  66.1 0.7 collective-permute-start.20
  66.8 0.0 collective-permute-done.18.from_own
  66.8 2.0 %shard_map.81 = f32[8,1024]{1,0:T(8,128)S(1)} custom-call(s32[1]{0:T(128)} %bitcast.11.odd, bf16[8,1024]{1,0:T(8,128)(2,1)S(1)} %collective-permute-done.17.from_pair, bf16[8,1024]{1,0:T(8,128)(2,1)S(1)} %collective-permute-done.18.from_own, f32[8,1024]{1,0:T(8,128)S(1)} %pad_maximum_fusion.1.source, f32[8,1024]{1,0:T(8,128)S(1)} %broadcast_select_fusion.down_odd, ...), custom_call_target="tpu_custom_call" | custom-call | flops 1610612736 | bytes 6291456 | tf_op jit(solution)/shard_map/pallas_call | solution.py:447
  68.8 0.0 collective-permute-done.20
  68.8 1.3 %collective-permute-start.21 = (f32[4,1024]{1,0:T(4,128)S(1)}, f32[4,1024]{1,0:T(4,128)S(1)}, u32[]{:S(2)}, u32[]{:S(2)}) collective-permute-start(f32[4,1024]{1,0:T(4,128)S(1)} %slice.17), channel_id=1, source_target_pairs={{1,0},{3,2},{5,4},{7,6},{9,8},{11,10},{13,12},{15,14},{17,16},{19,... | collective-permute-start | bytes 49160 | tf_op jit(solution)/shard_map/ppermute | solution.py:285
  70.1 31.2 %collective-permute-done.21 = f32[4,1024]{1,0:T(4,128)S(1)} collective-permute-done((f32[4,1024]{1,0:T(4,128)S(1)}, f32[4,1024]{1,0:T(4,128)S(1)}, u32[]{:S(2)}, u32[]{:S(2)}) %collective-permute-start.21) | collective-permute-done | bytes 16416 | tf_op jit(solution)/shard_map/ppermute | solution.py:285
  101.4 0.6 fusion.2
  102.0 0.0 collective-permute-done.12
  102.0 3.1 %select_bitcast_fusion = bf16[1,1024,1024]{2,1,0:T(8,128)(2,1)} fusion(bf16[1024,1024]{1,0:T(8,128)(2,1)} %shard_map.74, bf16[1024,1024]{1,0:T(8,128)(2,1)} %collective-permute-done.12, pred[]{:T(512)S(6)} %eq.15), kind=kLoop, calls=%fused_computation | loop fusion | flops 1048576 | bytes 6291457 | tf_op jit(solution)/shard_map/broadcast_in_dim | solution.py:458
  (25 shorter events, 0.1 us)
Async XLA Ops:
  0.6 4.9 %collective-permute-start.1 = (bf16[1024,1024]{1,0:T(8,128)(2,1)}, bf16[1024,1024]{1,0:T(8,128)(2,1)S(1)}, u32[]{:S(2)}, u32[]{:S(2)}) collective-permute-start(bf16[1024,1024]{1,0:T(8,128)(2,1)} %bitcast.17), channel_id=1, source_target_pairs={{0,1},{1,0},{2,3},{3,2},{4,5},{5,4},{6,7},{7,6},{8,9},{9,8},{10,11... | collective-permute-start | bytes 6291464 | tf_op jit(solution)/shard_map/ppermute | solution.py:285
  1.1 4.4 %collective-permute-start = (s32[8,8]{1,0:T(8,128)}, s32[8,8]{1,0:T(8,128)S(1)}, u32[]{:S(2)}, u32[]{:S(2)}) collective-permute-start(s32[8,8]{1,0:T(8,128)} %bitcast.19), channel_id=1, source_target_pairs={{0,1},{1,0},{2,3},{3,2},{4,5},{5,4},{6,7},{7,6},{8,9},{9,8},{10,11... | collective-permute-start | bytes 776 | tf_op jit(solution)/shard_map/ppermute | solution.py:285
  2.3 1.6 %copy-start.4 = (bf16[1,1024,1024]{2,1,0:T(8,128)(2,1)S(1)}, bf16[1,1024,1024]{2,1,0:T(8,128)(2,1)}, u32[]{:S(2)}) copy-start(bf16[1,1024,1024]{2,1,0:T(8,128)(2,1)} %param.5) | copy-start | bytes 6291460
  3.9 0.7 copy-start.7
  8.8 0.8 copy-start.5
  9.6 17.3 %copy-start.6 = (bf16[256,1024]{1,0:T(8,128)(2,1)S(1)}, bf16[256,1024]{1,0:T(8,128)(2,1)}, u32[]{:S(2)}) copy-start(bf16[256,1024]{1,0:T(8,128)(2,1)} %copy-done.5) | copy-start | bytes 1572868
  9.6 11.7 %collective-permute-start.3 = (bf16[256,1024]{1,0:T(8,128)(2,1)}, bf16[256,1024]{1,0:T(8,128)(2,1)S(1)}, u32[]{:S(2)}, u32[]{:S(2)}) collective-permute-start(bf16[256,1024]{1,0:T(8,128)(2,1)} %get-tuple-element.34.own), channel_id=1, source_target_pairs={{0,3},{2,1},{4,7},{6,5},{8,11},{10,9},{12,15},{14,13},{16,19},{18,... | collective-permute-start | bytes 1572872 | tf_op jit(solution)/shard_map/ppermute | solution.py:285
  14.3 12.6 %collective-permute-start.2 = (bf16[256,1024]{1,0:T(8,128)(2,1)}, bf16[256,1024]{1,0:T(8,128)(2,1)S(1)}, u32[]{:S(2)}, u32[]{:S(2)}) collective-permute-start(bf16[256,1024]{1,0:T(8,128)(2,1)} %copy-done.5), channel_id=1, source_target_pairs={{0,3},{2,1},{4,7},{6,5},{8,11},{10,9},{12,15},{14,13},{16,19},{18,... | collective-permute-start | bytes 1572872 | tf_op jit(solution)/shard_map/ppermute | solution.py:285
  21.2 14.2 %copy-start.8 = (f32[1,4,1024]{2,1,0:T(4,128)S(1)}, f32[1,4,1024]{2,1,0:T(4,128)}, u32[]{:S(2)}) copy-start(f32[1,4,1024]{2,1,0:T(4,128)} %param.9) | copy-start | bytes 49156
  21.2 15.5 %copy-start.9 = (s32[1,1024]{1,0:T(1,128)S(1)}, s32[1,1024]{1,0:T(1,128)}, u32[]{:S(2)}) copy-start(s32[1,1024]{1,0:T(1,128)} %param.8) | copy-start | bytes 12292
  22.8 10.5 %collective-permute-start.5 = (bf16[256,1024]{1,0:T(8,128)(2,1)S(1)}, bf16[256,1024]{1,0:T(8,128)(2,1)S(1)}, u32[]{:S(2)}, u32[]{:S(2)}) collective-permute-start(bf16[256,1024]{1,0:T(8,128)(2,1)S(1)} %get-tuple-element.37.refs_1_.refs_3_.refs_7_), channel_id=1, source_target_pairs={{5,0},{7,2},{13,8},{15,10},{21,16},{23,18},{29,24},{31,26},{0,3},{... | collective-permute-start | bytes 1572872 | tf_op jit(solution)/shard_map/ppermute | solution.py:285
  27.3 11.7 %collective-permute-start.4 = (bf16[256,1024]{1,0:T(8,128)(2,1)S(1)}, bf16[256,1024]{1,0:T(8,128)(2,1)}, u32[]{:S(2)}, u32[]{:S(2)}) collective-permute-start(bf16[256,1024]{1,0:T(8,128)(2,1)S(1)} %shard_map.71.refs_0_.refs_2_.refs_6_), channel_id=1, source_target_pairs={{5,0},{7,2},{13,8},{15,10},{21,16},{23,18},{29,24},{31,26},{0,3},{... | collective-permute-start | bytes 1572872 | tf_op jit(solution)/shard_map/ppermute | solution.py:285
  33.3 5.7 %collective-permute-start.6 = (bf16[256,1024]{1,0:T(8,128)(2,1)S(1)}, bf16[256,1024]{1,0:T(8,128)(2,1)S(1)}, u32[]{:S(2)}, u32[]{:S(2)}) collective-permute-start(bf16[256,1024]{1,0:T(8,128)(2,1)S(1)} %collective-permute-done.5.other), channel_id=1, source_target_pairs={{0,1},{2,3},{8,9},{10,11},{16,17},{18,19},{24,25},{26,27}} | collective-permute-start | bytes 1572872 | tf_op jit(solution)/shard_map/ppermute | solution.py:285
  35.5 2.1 %collective-permute-start.7 = (f32[4,1024]{1,0:T(4,128)S(1)}, f32[4,1024]{1,0:T(4,128)S(1)}, u32[]{:S(2)}, u32[]{:S(2)}) collective-permute-start(f32[4,1024]{1,0:T(4,128)S(1)} %bitcast.21), channel_id=1, source_target_pairs={{0,1},{2,3},{4,5},{6,7},{8,9},{10,11},{12,13},{14,15},{16,17},{18,... | collective-permute-start | bytes 49160 | tf_op jit(solution)/shard_map/ppermute | solution.py:285
  37.6 0.7 collective-permute-start.8
  39.0 0.8 copy-start
  41.3 9.8 %collective-permute-start.11 = (bf16[512,1024]{1,0:T(8,128)(2,1)S(1)}, bf16[512,1024]{1,0:T(8,128)(2,1)S(1)}, u32[]{:S(2)}, u32[]{:S(2)}) collective-permute-start(bf16[512,1024]{1,0:T(8,128)(2,1)S(1)} %shard_map.73.refs_2_.refs_4_.refs_8_), channel_id=1, source_target_pairs={{5,1},{7,3},{13,9},{15,11},{21,17},{23,19},{29,25},{31,27}} | collective-permute-start | bytes 3145736 | tf_op jit(solution)/shard_map/ppermute | solution.py:285
  42.0 9.0 %collective-permute-start.10 = (bf16[256,1024]{1,0:T(8,128)(2,1)}, bf16[256,1024]{1,0:T(8,128)(2,1)}, u32[]{:S(2)}, u32[]{:S(2)}) collective-permute-start(bf16[256,1024]{1,0:T(8,128)(2,1)} %collective-permute-done.4.other), channel_id=1, source_target_pairs={{0,1},{2,3},{8,9},{10,11},{16,17},{18,19},{24,25},{26,27}} | collective-permute-start | bytes 1572872 | tf_op jit(solution)/shard_map/ppermute | solution.py:285
  50.4 0.7 collective-permute-start.9
  51.1 1.0 copy-start.1
  53.2 48.8 %collective-permute-start.12 = (bf16[1024,1024]{1,0:T(8,128)(2,1)}, bf16[1024,1024]{1,0:T(8,128)(2,1)}, u32[]{:S(2)}, u32[]{:S(2)}) collective-permute-start(bf16[1024,1024]{1,0:T(8,128)(2,1)} %shard_map.74), channel_id=1, source_target_pairs={{1,0},{3,2},{5,4},{7,6},{9,8},{11,10},{13,12},{15,14},{17,16},{19,... | collective-permute-start | bytes 6291464 | tf_op jit(solution)/shard_map/ppermute | solution.py:285
  54.5 0.7 collective-permute-start.13
  55.2 1.0 copy-start.2
  57.2 0.7 collective-permute-start.14
  57.9 1.0 copy-start.3
  60.6 1.4 %collective-permute-start.15 = (bf16[8,1024]{1,0:T(8,128)(2,1)S(1)}, bf16[8,1024]{1,0:T(8,128)(2,1)S(1)}, u32[]{:S(2)}, u32[]{:S(2)}) collective-permute-start(bf16[8,1024]{1,0:T(8,128)(2,1)S(1)} %get-tuple-element.46), channel_id=1, source_target_pairs={{25,17},{27,19}} | collective-permute-start | bytes 49160 | tf_op jit(solution)/shard_map/ppermute | solution.py:285
  61.3 2.4 %collective-permute-start.19 = (f32[8,1024]{1,0:T(8,128)S(1)}, f32[8,1024]{1,0:T(8,128)S(1)}, u32[]{:S(2)}, u32[]{:S(2)}) collective-permute-start(f32[8,1024]{1,0:T(8,128)S(1)} %get-tuple-element.55), channel_id=1, source_target_pairs={{5,1},{7,3}} | collective-permute-start | bytes 98312 | tf_op jit(solution)/shard_map/ppermute | solution.py:285
  63.0 0.7 collective-permute-start.16
  64.8 2.0 %collective-permute-start.18 = (bf16[8,1024]{1,0:T(8,128)(2,1)S(1)}, bf16[8,1024]{1,0:T(8,128)(2,1)S(1)}, u32[]{:S(2)}, u32[]{:S(2)}) collective-permute-start(bf16[8,1024]{1,0:T(8,128)(2,1)S(1)} %get-tuple-element.53), channel_id=1, source_target_pairs={{9,5},{11,7}} | collective-permute-start | bytes 49160 | tf_op jit(solution)/shard_map/ppermute | solution.py:285
  65.4 1.4 %collective-permute-start.17 = (bf16[8,1024]{1,0:T(8,128)(2,1)S(1)}, bf16[8,1024]{1,0:T(8,128)(2,1)S(1)}, u32[]{:S(2)}, u32[]{:S(2)}) collective-permute-start(bf16[8,1024]{1,0:T(8,128)(2,1)S(1)} %get-tuple-element.53), channel_id=1, source_target_pairs={{9,1},{11,3}} | collective-permute-start | bytes 49160 | tf_op jit(solution)/shard_map/ppermute | solution.py:285
  66.1 2.7 %collective-permute-start.20 = (f32[8,1024]{1,0:T(8,128)S(1)}, f32[8,1024]{1,0:T(8,128)S(1)}, u32[]{:S(2)}, u32[]{:S(2)}) collective-permute-start(f32[8,1024]{1,0:T(8,128)S(1)} %select_select_fusion), channel_id=1, source_target_pairs={{9,13},{11,15},{17,21},{19,23},{25,29},{27,31}} | collective-permute-start | bytes 98312 | tf_op jit(solution)/shard_map/ppermute | solution.py:285
  68.8 32.5 %collective-permute-start.21 = (f32[4,1024]{1,0:T(4,128)S(1)}, f32[4,1024]{1,0:T(4,128)S(1)}, u32[]{:S(2)}, u32[]{:S(2)}) collective-permute-start(f32[4,1024]{1,0:T(4,128)S(1)} %slice.17), channel_id=1, source_target_pairs={{1,0},{3,2},{5,4},{7,6},{9,8},{11,10},{13,12},{15,14},{17,16},{19,... | collective-permute-start | bytes 49160 | tf_op jit(solution)/shard_map/ppermute | solution.py:285

commit v7 on v5

--- a/solution.py
+++ b/solution.py
@@ -100,7 +100,7 @@
         in_specs=[SMEM, map_spec, map_spec, VMEM] + [VMEM] * len(extra),
         out_specs=[VMEM] * len(shapes),
         compiler_params=PARAMS,
-        cost_estimate=cost(2 * rows * face * (width + face), 6 * rows * width),
+        cost_estimate=cost(0, 8 * rows * width),
     )(other_pattern, own, other, inverse, *extra)
 
 
@@ -146,7 +146,7 @@
         out_specs=[VMEM] * (3 if is_face else 2),
         input_output_aliases=aliases,
         compiler_params=PARAMS,
-        cost_estimate=cost(0, 0),
+        cost_estimate=cost(0, 8 * rows * width),
     )(is_second, own, other, inverse, *extra)
     return result[0], ((result[2] if is_face else state[0]), result[1])
 
@@ -180,7 +180,13 @@
     return jnp.concatenate(outs, axis=1)
 
 
-def segment_kernel(coupling, pieces_of, down_steps, up_steps, *refs):
+def segment_kernel(coupling, pieces_of, down_steps, up_steps, active, *refs):
+    @pl.when(active[0] == 1)
+    def _():
+        run_segment(coupling, pieces_of, down_steps, up_steps, *refs)
+
+
+def run_segment(coupling, pieces_of, down_steps, up_steps, *refs):
     refs = list(refs)
     state = refs.pop(0)[...]
     maps, downs = {}, {}
@@ -205,8 +211,8 @@
     refs.pop(0)[...] = state
 
 
-def segment(coupling, arrived, packed, downs, maps, down_steps, up_steps):
-    operands = [arrived]
+def segment(coupling, active, arrived, packed, downs, maps, down_steps, up_steps):
+    operands = [active.astype(jnp.int32)[None], arrived]
     for slot in down_steps:
         operands += [packed[slot], *maps[slot]]
     for slot in up_steps:
@@ -219,10 +225,10 @@
             segment_kernel, coupling, [len(entry) for entry in maps], down_steps, up_steps
         ),
         out_shape=[rows] * steps + [jax.ShapeDtypeStruct(arrived.shape, jnp.bfloat16)],
-        in_specs=[VMEM] * len(operands),
+        in_specs=[SMEM] + [VMEM] * (len(operands) - 1),
         out_specs=[VMEM] * (steps + 1),
         compiler_params=SWEEP_PARAMS,
-        cost_estimate=cost(steps * 2 * 256 * 1024 * 1024, steps * 2 * 1024 * 1024),
+        cost_estimate=cost(0, steps * 4 * 1024 * 1024),
     )(*operands)
     return results[:-1], results[-1]
 
@@ -280,7 +286,7 @@
         in_specs=[SMEM, VMEM],
         out_specs=VMEM,
         compiler_params=PARAMS,
-        cost_estimate=cost(width * width, 4 * width * width),
+        cost_estimate=cost(0, 4 * width * width),
     )(pattern, raw)
 
     def inverse_of(level):
@@ -366,7 +372,7 @@
 
     first = pair_packed[:rows].astype(jnp.bfloat16)
     (down_odd,), state = segment(
-        coupling, first, small, {}, [[merged], pair_maps], (OWN,), ()
+        coupling, is_second & (layer == 1), first, small, {}, [[merged], pair_maps], (OWN,), ()
     )
     merged_first = send(after(merged, state), route(every, 1, 0))
     maps = [[merged_first], pair_maps]
@@ -379,7 +385,7 @@
         turn = k == len(chain) - 1
         back = tuple(reversed(slots))
         results, state = segment(
-            coupling, arrived, small, {}, maps, slots, back[1:] if turn else ()
+            coupling, layer == at, arrived, small, {}, maps, slots, back[1:] if turn else ()
         )
         kept.append(dict(zip(slots, results)))
         if k == 0:
@@ -397,7 +403,7 @@
             arrived, merged = lax.optimization_barrier((arrived, merged))
         at = target
         back = tuple(reversed(slots))
-        results, state = segment(coupling, arrived, small, kept[k], maps, (), back)
+        results, state = segment(coupling, layer == at, arrived, small, kept[k], maps, (), back)
         ups[at] = dict(zip(back, results))
     from_own = send(state, route([(at, 1)], 0, 1))
     from_pair = send(state, route([(at, 0)]))
@@ -415,7 +421,7 @@
         in_specs=[SMEM] + [VMEM] * (5 + len(pair_maps)),
         out_specs=VMEM,
         compiler_params=SWEEP_PARAMS,
-        cost_estimate=cost(6 * 256 * 1024 * 1024, 6 * 1024 * 1024),
+        cost_estimate=cost(0, 8 * 1024 * 1024),
     )(odd, from_pair, from_own, packed[:rows], down_odd, merged, *pair_maps)
     upward = jnp.where(layer < 2, last, settled)
     ends = upward[:rows_here], upward[rows_here : 2 * rows_here]

time: 94.2 us -> 103 us (1.093)
  Pallas kernels: 16.5 us -> 20.7 us
  waiting for transfers between devices: 38.5 us -> 41.9 us
  local copies, waits for them, and re-layouts: 7.43 us -> 8.6 us
    ppermute x21, waiting for transfers between devices: 38.5 us -> 41.9 us  [send(): return lax.ppermute(value, AXES, pairs_of_devices)]
    pallas_call x4, Pallas kernels: 3.02 us -> 5.43 us  [combine(): pl.pallas_call(functools.partial(combine_kernel, face_at, is_face, follow...]
    pallas_call x1, Pallas kernels: 0.94 us -> 2.14 us  [on_device(): pl.pallas_call(functools.partial(last_kernel, coupling, len(pair_maps)),...]
    unnamed x30 -> x26, local copies, waits for them, and re-layouts: 6.36 us -> 7.54 us
  transfers between devices with their start and end apart: 21 -> 21, of which waited for: 7 -> 8; matrix products, arithmetic and copies ran while one was open for 1% -> 1% of each run, Pallas kernels for 10% -> 10%
where the time goes in v7:
time: 103 us; the launch traced here: 102 us
  waiting for transfers between devices  41.9 us (41%)
  starting transfers between devices  28.7 us (28%)
  Pallas kernels  20.7 us (20%)
  local copies, waits for them, and re-layouts  8.6 us (8%)
  between operations  1.09 us (1%)
    ppermute x21, waiting for transfers between devices, send(): return lax.ppermute(value, AXES, pairs_of_devices)  41.9 us
    ppermute x21, starting transfers between devices, send(): return lax.ppermute(value, AXES, pairs_of_devices)  28.7 us
    unnamed x26, local copies, waits for them, and re-layouts  7.54 us
    pallas_call x6, Pallas kernels, segment(): pl.pallas_call(functools.partial(segment_kernel, coupling, [len(entry) fo...  7.52 us
    pallas_call x4, Pallas kernels, combine(): pl.pallas_call(functools.partial(combine_kernel, face_at, is_face, follow...  5.43 us
    pallas_call x2, Pallas kernels, leaf_combine(): pl.pallas_call(functools.partial(leaf_kernel, half * rows, is_face, piece...  4.7 us
    pallas_call x1, Pallas kernels, on_device(): pl.pallas_call(functools.partial(last_kernel, coupling, len(pair_maps)),...  2.14 us
  transfers between devices with their start and end apart: 21, of which 8 were waited for; matrix products, arithmetic and copies ran while one was open for 1% of the time, Pallas kernels for 10%

profile of v7, /device:TPU:0, one launch (start us, length us, event | category | flops | bytes accessed | tf_op | source)
XLA Modules:
  0.0 102.0 jit_solution(2060993844061777426)
XLA Ops:
  0.6 0.5 collective-permute-start.2
  1.1 0.1 collective-permute-start.1
  1.2 1.1 %fusion.1 = (bf16[256,256]{1,0:T(8,128)(2,1)S(1)}, bf16[256,256]{1,0:T(8,128)(2,1)S(1)}) fusion(f32[1,3,256,256]{3,2,1,0:T(8,128)} %param.7, s32[]{:T(128)S(6)} %select_n.101, s32[]{:T(128)S(6)} %select_n.100), kind=kLoop, calls=%fused_computation.4 | loop fusion | bytes 524296 | tf_op jit(solution)/shard_map/convert_element_type | solution.py:294
  2.3 0.0 copy-start.5
  2.3 1.6 %copy-done.5 = bf16[1,1024,1024]{2,1,0:T(8,128)(2,1)S(1)} copy-done((bf16[1,1024,1024]{2,1,0:T(8,128)(2,1)S(1)}, bf16[1,1024,1024]{2,1,0:T(8,128)(2,1)}, u32[]{:S(2)}) %copy-start.5) | copy-done | bytes 2097176
  3.9 0.7 copy-done.10
  4.6 0.9 shard_map.68.own
  5.5 0.0 collective-permute-done.1.other_pattern
  5.5 0.0 collective-permute-done.2.other
  5.5 2.7 %shard_map.69 = (bf16[256,1024]{1,0:T(8,128)(2,1)S(1)}, bf16[256,1024]{1,0:T(8,128)(2,1)}, bf16[256,1024]{1,0:T(8,128)(2,1)S(1)}) custom-call(s32[8,8]{1,0:T(8,128)S(1)} %collective-permute-done.1.other_pattern, bf16[1024,1024]{1,0:T(8,128)(2,1)S(1)} %shard_map.68.own, bf16[1024,1024]{1,0:T(8,128)(2,1)} %collective-permute-done.2.other, ...), custom_call_target="tpu_custom_call" | custom-call | bytes 4194304 | tf_op jit(solution)/shard_map/pallas_call | solution.py:96
  8.3 0.8 copy-done.8
  9.1 5.3 %collective-permute-start.3 = (bf16[256,1024]{1,0:T(8,128)(2,1)}, bf16[256,1024]{1,0:T(8,128)(2,1)}, u32[]{:S(2)}, u32[]{:S(2)}) collective-permute-start(bf16[256,1024]{1,0:T(8,128)(2,1)} %get-tuple-element.40.own), channel_id=1, source_target_pairs={{0,3},{2,1},{4,7},{6,5},{8,11},{10,9},{12,15},{14,13},{16,19},{18,... | collective-permute-start | bytes 1572872 | tf_op jit(solution)/shard_map/ppermute | solution.py:271
  14.4 1.3 %collective-permute-start.5 = (bf16[256,1024]{1,0:T(8,128)(2,1)S(1)}, bf16[256,1024]{1,0:T(8,128)(2,1)S(1)}, u32[]{:S(2)}, u32[]{:S(2)}) collective-permute-start(bf16[256,1024]{1,0:T(8,128)(2,1)S(1)} %get-tuple-element.46.own), channel_id=1, source_target_pairs={{0,3},{2,1},{4,7},{6,5},{8,11},{10,9},{12,15},{14,13},{16,19},{18,... | collective-permute-start | bytes 1572872 | tf_op jit(solution)/shard_map/ppermute | solution.py:271
  15.8 1.0 %copy-done.9 = bf16[256,1024]{1,0:T(8,128)(2,1)S(1)} copy-done((bf16[256,1024]{1,0:T(8,128)(2,1)S(1)}, bf16[256,1024]{1,0:T(8,128)(2,1)}, u32[]{:S(2)}) %copy-start.9) | copy-done | bytes 524312
  16.8 2.0 %shard_map.70 = (bf16[256,1024]{1,0:T(8,128)(2,1)S(1)}, bf16[256,1024]{1,0:T(8,128)(2,1)S(1)}) custom-call(s32[8,8]{1,0:T(8,128)S(1)} %collective-permute-done.1.other_pattern, bf16[1024,1024]{1,0:T(8,128)(2,1)S(1)} %shard_map.68.own, bf16[1024,1024]{1,0:T(8,128)(2,1)} %collective-permute-done.2.other, bf16[256,256]{1,0:T(8,128)(2,1)S(1)} %get-tuple-element.79.inverse, ...), custom_call_target="tpu_custom_call" | custom-call | bytes 4194304 | tf_op jit(solution)/shard_map/pallas_call | solution.py:96
  18.8 1.8 %collective-permute-done.3.other = bf16[256,1024]{1,0:T(8,128)(2,1)} collective-permute-done((bf16[256,1024]{1,0:T(8,128)(2,1)}, bf16[256,1024]{1,0:T(8,128)(2,1)}, u32[]{:S(2)}, u32[]{:S(2)}) %collective-permute-start.3) | collective-permute-done | bytes 524320 | tf_op jit(solution)/shard_map/ppermute | solution.py:271
  20.6 1.7 %shard_map.71 = (bf16[256,1024]{1,0:T(8,128)(2,1)S(1)}, bf16[1024,1024]{1,0:T(8,128)(2,1)S(1)}, bf16[256,1024]{1,0:T(8,128)(2,1)S(1)}) custom-call(s32[1]{0:T(128)} %bitcast.5.is_second, bf16[256,1024]{1,0:T(8,128)(2,1)} %get-tuple-element.40.own, bf16[256,1024]{1,0:T(8,128)(2,1)} %collective-permute-done.3.other, ...), custom_call_target="tpu_custom_call" | custom-call | bytes 2097152 | tf_op jit(solution)/shard_map/pallas_call | solution.py:136
  22.3 3.8 %collective-permute-start.7 = (bf16[256,1024]{1,0:T(8,128)(2,1)S(1)}, bf16[256,1024]{1,0:T(8,128)(2,1)S(1)}, u32[]{:S(2)}, u32[]{:S(2)}) collective-permute-start(bf16[256,1024]{1,0:T(8,128)(2,1)S(1)} %get-tuple-element.43), channel_id=1, source_target_pairs={{5,0},{7,2},{13,8},{15,10},{21,16},{23,18},{29,24},{31,26},{0,3},{... | collective-permute-start | bytes 1572872 | tf_op jit(solution)/shard_map/ppermute | solution.py:271
  26.1 0.1 collective-permute-start
  26.2 1.1 %collective-permute-done = f32[4,1024]{1,0:T(4,128)S(1)} collective-permute-done((f32[4,1024]{1,0:T(4,128)S(1)}, f32[4,1024]{1,0:T(4,128)S(1)}, u32[]{:S(2)}, u32[]{:S(2)}) %collective-permute-start) | collective-permute-done | bytes 16416 | tf_op jit(solution)/shard_map/ppermute | solution.py:271
  27.4 0.7 collective-permute-start.4
  28.1 0.0 collective-permute-done.5.other
  28.1 1.3 %shard_map.72 = (bf16[256,1024]{1,0:T(8,128)(2,1)}, bf16[1024,1024]{1,0:T(8,128)(2,1)S(1)}) custom-call(s32[1]{0:T(128)} %bitcast.5.is_second, bf16[256,1024]{1,0:T(8,128)(2,1)S(1)} %get-tuple-element.46.own, bf16[256,1024]{1,0:T(8,128)(2,1)S(1)} %collective-permute-done.5.other, ...), custom_call_target="tpu_custom_call", output_to_operand_aliasing={{1}: (6, {})} | custom-call | bytes 2097152 | tf_op jit(solution)/shard_map/pallas_call | solution.py:136
  29.3 4.6 %collective-permute-start.6 = (bf16[256,1024]{1,0:T(8,128)(2,1)}, bf16[256,1024]{1,0:T(8,128)(2,1)S(1)}, u32[]{:S(2)}, u32[]{:S(2)}) collective-permute-start(bf16[256,1024]{1,0:T(8,128)(2,1)} %get-tuple-element.49), channel_id=1, source_target_pairs={{5,0},{7,2},{13,8},{15,10},{21,16},{23,18},{29,24},{31,26},{0,3},{... | collective-permute-start | bytes 1572872 | tf_op jit(solution)/shard_map/ppermute | solution.py:271
  34.0 0.0 collective-permute-done.4.refs_3_
  34.0 0.0 collective-permute-done.7.other.refs_5_.refs_3_.refs_2_
  34.0 1.3 %shard_map.73 = (bf16[256,1024]{1,0:T(8,128)(2,1)}, bf16[1024,1024]{1,0:T(8,128)(2,1)S(1)}) custom-call(s32[1]{0:T(128)} %bitcast.5.is_second, bf16[256,1024]{1,0:T(8,128)(2,1)S(1)} %get-tuple-element.42.refs_0_.own, bf16[256,1024]{1,0:T(8,128)(2,1)S(1)} %collective-permute-done.7.other.refs_5_.refs_3_.refs_2_, ...), custom_call_target="tpu_custom_call", output_to_operand_aliasing={{1}: (5, {})} | custom-call | bytes 2097152 | tf_op jit(solution)/shard_map/pallas_call | solution.py:136
  35.2 1.3 %collective-permute-start.8 = (bf16[256,1024]{1,0:T(8,128)(2,1)}, bf16[256,1024]{1,0:T(8,128)(2,1)}, u32[]{:S(2)}, u32[]{:S(2)}) collective-permute-start(bf16[256,1024]{1,0:T(8,128)(2,1)} %get-tuple-element.52), channel_id=1, source_target_pairs={{5,0},{7,2},{13,8},{15,10},{21,16},{23,18},{29,24},{31,26}} | collective-permute-start | bytes 1572872 | tf_op jit(solution)/shard_map/ppermute | solution.py:271
  36.6 4.4 %collective-permute-done.6.other.refs_4_.refs_2_.refs_1_ = bf16[256,1024]{1,0:T(8,128)(2,1)S(1)} collective-permute-done((bf16[256,1024]{1,0:T(8,128)(2,1)}, bf16[256,1024]{1,0:T(8,128)(2,1)S(1)}, u32[]{:S(2)}, u32[]{:S(2)}) %collective-permute-start.6) | collective-permute-done | bytes 524320 | tf_op jit(solution)/shard_map/ppermute | solution.py:271
  41.0 5.1 %collective-permute-done.8.refs_6_.refs_4_.refs_3_ = bf16[256,1024]{1,0:T(8,128)(2,1)} collective-permute-done((bf16[256,1024]{1,0:T(8,128)(2,1)}, bf16[256,1024]{1,0:T(8,128)(2,1)}, u32[]{:S(2)}, u32[]{:S(2)}) %collective-permute-start.8) | collective-permute-done | bytes 524320 | tf_op jit(solution)/shard_map/ppermute | solution.py:271
  46.1 1.0 %copy-done.4 = bf16[256,1024]{1,0:T(8,128)(2,1)S(1)} copy-done((bf16[256,1024]{1,0:T(8,128)(2,1)S(1)}, bf16[256,1024]{1,0:T(8,128)(2,1)}, u32[]{:S(2)}) %copy-start.4) | copy-done | bytes 524312
  47.1 1.0 %copy-done.7 = bf16[256,1024]{1,0:T(8,128)(2,1)S(1)} copy-done((bf16[256,1024]{1,0:T(8,128)(2,1)S(1)}, bf16[256,1024]{1,0:T(8,128)(2,1)}, u32[]{:S(2)}) %copy-start.7) | copy-done | bytes 524312
  48.1 1.2 %shard_map.74 = (bf16[256,1024]{1,0:T(8,128)(2,1)}, bf16[1024,1024]{1,0:T(8,128)(2,1)S(1)}) custom-call(s32[1]{0:T(128)} %bitcast.5.is_second, bf16[256,1024]{1,0:T(8,128)(2,1)S(1)} %copy-done.7, bf16[256,1024]{1,0:T(8,128)(2,1)S(1)} %collective-permute-done.6.other.refs_4_.refs_2_.refs_1_, ...), custom_call_target="tpu_custom_call", output_to_operand_aliasing={{1}: (5, {})} | custom-call | bytes 2097152 | tf_op jit(solution)/shard_map/pallas_call | solution.py:136
  49.4 1.3 %copy-done = bf16[1024,1024]{1,0:T(8,128)(2,1)} copy-done((bf16[1024,1024]{1,0:T(8,128)(2,1)}, bf16[1024,1024]{1,0:T(8,128)(2,1)S(1)}, u32[]{:S(2)}) %copy-start) | copy-done | bytes 2097176
  50.7 1.3 %collective-permute-start.10 = (bf16[1024,1024]{1,0:T(8,128)(2,1)}, bf16[1024,1024]{1,0:T(8,128)(2,1)S(1)}, u32[]{:S(2)}, u32[]{:S(2)}) collective-permute-start(bf16[1024,1024]{1,0:T(8,128)(2,1)} %copy-done), channel_id=1, source_target_pairs={{1,0},{3,2},{5,4},{7,6},{9,8},{11,10},{13,12},{15,14},{17,16},{19,... | collective-permute-start | bytes 6291464 | tf_op jit(solution)/shard_map/ppermute | solution.py:271
  52.0 1.3 %collective-permute-start.11 = (bf16[256,1024]{1,0:T(8,128)(2,1)}, bf16[256,1024]{1,0:T(8,128)(2,1)}, u32[]{:S(2)}, u32[]{:S(2)}) collective-permute-start(bf16[256,1024]{1,0:T(8,128)(2,1)} %get-tuple-element.58), channel_id=1, source_target_pairs={{5,0},{7,2},{13,8},{15,10},{21,16},{23,18},{29,24},{31,26}} | collective-permute-start | bytes 1572872 | tf_op jit(solution)/shard_map/ppermute | solution.py:271
  53.3 0.7 collective-permute-start.9
  54.0 0.0 collective-permute-done.9.refs_0_
  54.0 8.8 %collective-permute-done.11.refs_7_.refs_5_.refs_4_ = bf16[256,1024]{1,0:T(8,128)(2,1)} collective-permute-done((bf16[256,1024]{1,0:T(8,128)(2,1)}, bf16[256,1024]{1,0:T(8,128)(2,1)}, u32[]{:S(2)}, u32[]{:S(2)}) %collective-permute-start.11) | collective-permute-done | bytes 524320 | tf_op jit(solution)/shard_map/ppermute | solution.py:271
  62.8 0.0 collective-permute-done.10.refs_2_.refs_7_
  62.8 1.2 %shard_map.76 = (f32[8,1024]{1,0:T(8,128)S(1)}, f32[8,1024]{1,0:T(8,128)S(1)}, bf16[8,1024]{1,0:T(8,128)(2,1)S(1)}) custom-call(s32[1]{0:T(128)} %bitcast.2.active, bf16[8,1024]{1,0:T(8,128)(2,1)S(1)} %collective-permute-done.9.refs_0_, f32[9,1024]{1,0:T(8,128)S(1)} %pad_maximum_fusion.refs_1_, ...), custom_call_target="tpu_custom_call" | custom-call | bytes 8388608 | tf_op jit(solution)/shard_map/pallas_call | solution.py:223
  64.0 0.7 collective-permute-start.12
  64.7 1.2 %shard_map.77 = (f32[8,1024]{1,0:T(8,128)S(1)}, f32[8,1024]{1,0:T(8,128)S(1)}, bf16[8,1024]{1,0:T(8,128)(2,1)S(1)}) custom-call(s32[1]{0:T(128)} %bitcast.1.active, bf16[8,1024]{1,0:T(8,128)(2,1)S(1)} %collective-permute-done.12.refs_0_, f32[9,1024]{1,0:T(8,128)S(1)} %pad_maximum_fusion.refs_1_, ...), custom_call_target="tpu_custom_call" | custom-call | bytes 8388608 | tf_op jit(solution)/shard_map/pallas_call | solution.py:223
  65.9 0.7 collective-permute-start.13
  66.6 0.0 copy-start.1
  66.6 1.9 %shard_map.78 = (f32[8,1024]{1,0:T(8,128)}, f32[8,1024]{1,0:T(8,128)S(1)}, f32[8,1024]{1,0:T(8,128)S(1)}, bf16[8,1024]{1,0:T(8,128)(2,1)S(1)}) custom-call(s32[1]{0:T(128)} %bitcast.active, bf16[8,1024]{1,0:T(8,128)(2,1)S(1)} %collective-permute-done.13.refs_0_, f32[9,1024]{1,0:T(8,128)S(1)} %pad_maximum_fusion.refs_1_, ...), custom_call_target="tpu_custom_call" | custom-call | bytes 12582912 | tf_op jit(solution)/shard_map/pallas_call | solution.py:223
  68.5 0.7 collective-permute-start.14
  69.2 0.2 broadcast_select_fusion.refs_0_
  69.4 0.0 copy-start.2
  69.5 2.0 %shard_map.79 = (f32[8,1024]{1,0:T(8,128)S(1)}, f32[8,1024]{1,0:T(8,128)S(1)}, bf16[8,1024]{1,0:T(8,128)(2,1)S(1)}) custom-call(s32[1]{0:T(128)} %bitcast.1.active, bf16[8,1024]{1,0:T(8,128)(2,1)S(1)} %collective-permute-done.14.refs_0_, f32[8,1024]{1,0:T(8,128)S(1)} %get-tuple-element.64.refs_1_, ...), custom_call_target="tpu_custom_call" | custom-call | bytes 8388608 | tf_op jit(solution)/shard_map/pallas_call | solution.py:223
  71.4 0.7 collective-permute-start.15
  72.1 1.3 %collective-permute-start.18 = (f32[8,1024]{1,0:T(8,128)S(1)}, f32[8,1024]{1,0:T(8,128)S(1)}, u32[]{:S(2)}, u32[]{:S(2)}) collective-permute-start(f32[8,1024]{1,0:T(8,128)S(1)} %get-tuple-element.71), channel_id=1, source_target_pairs={{5,0},{7,2}} | collective-permute-start | bytes 98312 | tf_op jit(solution)/shard_map/ppermute | solution.py:271
  73.4 0.0 collective-permute-done.15.refs_0_
  73.4 1.2 %shard_map.80 = (f32[8,1024]{1,0:T(8,128)S(1)}, f32[8,1024]{1,0:T(8,128)S(1)}, bf16[8,1024]{1,0:T(8,128)(2,1)S(1)}) custom-call(s32[1]{0:T(128)} %bitcast.2.active, bf16[8,1024]{1,0:T(8,128)(2,1)S(1)} %collective-permute-done.15.refs_0_, f32[8,1024]{1,0:T(8,128)S(1)} %get-tuple-element.67.refs_1_, ...), custom_call_target="tpu_custom_call" | custom-call | bytes 8388608 | tf_op jit(solution)/shard_map/pallas_call | solution.py:223
  74.6 1.3 %collective-permute-start.16 = (bf16[8,1024]{1,0:T(8,128)(2,1)S(1)}, bf16[8,1024]{1,0:T(8,128)(2,1)S(1)}, u32[]{:S(2)}, u32[]{:S(2)}) collective-permute-start(bf16[8,1024]{1,0:T(8,128)(2,1)S(1)} %get-tuple-element.69), channel_id=1, source_target_pairs={{8,0},{10,2}} | collective-permute-start | bytes 49160 | tf_op jit(solution)/shard_map/ppermute | solution.py:271
  75.9 0.7 collective-permute-start.17
  76.6 0.7 collective-permute-start.19
  77.3 0.1 collective-permute-done.18
  77.3 19.7 %collective-permute-done.16.from_pair = bf16[8,1024]{1,0:T(8,128)(2,1)S(1)} collective-permute-done((bf16[8,1024]{1,0:T(8,128)(2,1)S(1)}, bf16[8,1024]{1,0:T(8,128)(2,1)S(1)}, u32[]{:S(2)}, u32[]{:S(2)}) %collective-permute-start.16) | collective-permute-done | bytes 16416 | tf_op jit(solution)/shard_map/ppermute | solution.py:271
  97.0 2.1 %shard_map.81 = f32[8,1024]{1,0:T(8,128)S(1)} custom-call(s32[1]{0:T(128)} %bitcast.11.odd, bf16[8,1024]{1,0:T(8,128)(2,1)S(1)} %collective-permute-done.16.from_pair, bf16[8,1024]{1,0:T(8,128)(2,1)S(1)} %collective-permute-done.17.from_own, f32[8,1024]{1,0:T(8,128)S(1)} %pad_maximum_fusion.1.source, f32[8,1024]{1,0:T(8,128)S(1)} %broadcast_select_fusion.1.down_odd, ...), custom_call_target="tpu_custom_call" | custom-call | bytes 8388608 | tf_op jit(solution)/shard_map/pallas_call | solution.py:418
  99.2 0.0 collective-permute-done.19
  99.2 1.3 %collective-permute-start.20 = (f32[4,1024]{1,0:T(4,128)S(1)}, f32[4,1024]{1,0:T(4,128)S(1)}, u32[]{:S(2)}, u32[]{:S(2)}) collective-permute-start(f32[4,1024]{1,0:T(4,128)S(1)} %slice_select_fusion), channel_id=1, source_target_pairs={{5,4},{7,6},{0,1},{2,3},{8,9},{10,11},{12,13},{14,15},{16,17},{18,... | collective-permute-start | bytes 49160 | tf_op jit(solution)/shard_map/ppermute | solution.py:271
  100.5 0.8 collective-permute-done.20
  101.3 0.6 select_bitcast_fusion
  (30 shorter events, 0.1 us)
Async XLA Ops:
  0.6 4.9 %collective-permute-start.2 = (bf16[1024,1024]{1,0:T(8,128)(2,1)}, bf16[1024,1024]{1,0:T(8,128)(2,1)}, u32[]{:S(2)}, u32[]{:S(2)}) collective-permute-start(bf16[1024,1024]{1,0:T(8,128)(2,1)} %bitcast.19), channel_id=1, source_target_pairs={{0,1},{1,0},{2,3},{3,2},{4,5},{5,4},{6,7},{7,6},{8,9},{9,8},{10,11... | collective-permute-start | bytes 6291464 | tf_op jit(solution)/shard_map/ppermute | solution.py:271
  1.1 4.4 %collective-permute-start.1 = (s32[8,8]{1,0:T(8,128)}, s32[8,8]{1,0:T(8,128)S(1)}, u32[]{:S(2)}, u32[]{:S(2)}) collective-permute-start(s32[8,8]{1,0:T(8,128)} %bitcast.21), channel_id=1, source_target_pairs={{0,1},{1,0},{2,3},{3,2},{4,5},{5,4},{6,7},{7,6},{8,9},{9,8},{10,11... | collective-permute-start | bytes 776 | tf_op jit(solution)/shard_map/ppermute | solution.py:271
  2.3 1.6 %copy-start.5 = (bf16[1,1024,1024]{2,1,0:T(8,128)(2,1)S(1)}, bf16[1,1024,1024]{2,1,0:T(8,128)(2,1)}, u32[]{:S(2)}) copy-start(bf16[1,1024,1024]{2,1,0:T(8,128)(2,1)} %param.5) | copy-start | bytes 6291460
  3.9 0.7 copy-start.10
  8.3 0.8 copy-start.8
  9.1 11.5 %collective-permute-start.3 = (bf16[256,1024]{1,0:T(8,128)(2,1)}, bf16[256,1024]{1,0:T(8,128)(2,1)}, u32[]{:S(2)}, u32[]{:S(2)}) collective-permute-start(bf16[256,1024]{1,0:T(8,128)(2,1)} %get-tuple-element.40.own), channel_id=1, source_target_pairs={{0,3},{2,1},{4,7},{6,5},{8,11},{10,9},{12,15},{14,13},{16,19},{18,... | collective-permute-start | bytes 1572872 | tf_op jit(solution)/shard_map/ppermute | solution.py:271
  14.4 13.6 %collective-permute-start.5 = (bf16[256,1024]{1,0:T(8,128)(2,1)S(1)}, bf16[256,1024]{1,0:T(8,128)(2,1)S(1)}, u32[]{:S(2)}, u32[]{:S(2)}) collective-permute-start(bf16[256,1024]{1,0:T(8,128)(2,1)S(1)} %get-tuple-element.46.own), channel_id=1, source_target_pairs={{0,3},{2,1},{4,7},{6,5},{8,11},{10,9},{12,15},{14,13},{16,19},{18,... | collective-permute-start | bytes 1572872 | tf_op jit(solution)/shard_map/ppermute | solution.py:271
  15.7 1.0 %copy-start.9 = (bf16[256,1024]{1,0:T(8,128)(2,1)S(1)}, bf16[256,1024]{1,0:T(8,128)(2,1)}, u32[]{:S(2)}) copy-start(bf16[256,1024]{1,0:T(8,128)(2,1)} %copy-done.8) | copy-start | bytes 1572868
  16.8 9.3 %copy-start.11 = (f32[1,4,1024]{2,1,0:T(4,128)S(1)}, f32[1,4,1024]{2,1,0:T(4,128)}, u32[]{:S(2)}) copy-start(f32[1,4,1024]{2,1,0:T(4,128)} %param.9) | copy-start | bytes 49156
  16.8 9.4 %copy-start.12 = (s32[1,1024]{1,0:T(1,128)S(1)}, s32[1,1024]{1,0:T(1,128)}, u32[]{:S(2)}) copy-start(s32[1,1024]{1,0:T(1,128)} %param.8) | copy-start | bytes 12292
  18.8 10.6 %copy-start.6 = (bf16[256,1024]{1,0:T(8,128)(2,1)}, bf16[256,1024]{1,0:T(8,128)(2,1)S(1)}, u32[]{:S(2)}) copy-start(bf16[256,1024]{1,0:T(8,128)(2,1)S(1)} %get-tuple-element.45.refs_0_.own) | copy-start | bytes 1572868
  22.3 11.7 %copy-start.3 = (bf16[256,1024]{1,0:T(8,128)(2,1)}, bf16[256,1024]{1,0:T(8,128)(2,1)S(1)}, u32[]{:S(2)}) copy-start(bf16[256,1024]{1,0:T(8,128)(2,1)S(1)} %get-tuple-element.47.refs_1_.refs_0_) | copy-start | bytes 1572868
  22.3 11.7 %collective-permute-start.7 = (bf16[256,1024]{1,0:T(8,128)(2,1)S(1)}, bf16[256,1024]{1,0:T(8,128)(2,1)S(1)}, u32[]{:S(2)}, u32[]{:S(2)}) collective-permute-start(bf16[256,1024]{1,0:T(8,128)(2,1)S(1)} %get-tuple-element.43), channel_id=1, source_target_pairs={{5,0},{7,2},{13,8},{15,10},{21,16},{23,18},{29,24},{31,26},{0,3},{... | collective-permute-start | bytes 1572872 | tf_op jit(solution)/shard_map/ppermute | solution.py:271
  26.1 1.2 %collective-permute-start = (f32[4,1024]{1,0:T(4,128)S(1)}, f32[4,1024]{1,0:T(4,128)S(1)}, u32[]{:S(2)}, u32[]{:S(2)}) collective-permute-start(f32[4,1024]{1,0:T(4,128)S(1)} %bitcast.23), channel_id=1, source_target_pairs={{0,1},{1,0},{2,3},{3,2},{4,5},{5,4},{6,7},{7,6},{8,9},{9,8},{10,11... | collective-permute-start | bytes 49160 | tf_op jit(solution)/shard_map/ppermute | solution.py:271
  27.4 6.6 %collective-permute-start.4 = (f32[9,1024]{1,0:T(8,128)S(1)}, f32[9,1024]{1,0:T(8,128)S(1)}, u32[]{:S(2)}, u32[]{:S(2)}) collective-permute-start(f32[9,1024]{1,0:T(8,128)S(1)} %pad_maximum_fusion.refs_1_), channel_id=1, source_target_pairs={{12,8},{14,10},{20,16},{22,18},{28,24},{30,26},{1,5},{3,7}} | collective-permute-start | bytes 110600 | tf_op jit(solution)/shard_map/ppermute | solution.py:271
  29.3 11.6 %collective-permute-start.6 = (bf16[256,1024]{1,0:T(8,128)(2,1)}, bf16[256,1024]{1,0:T(8,128)(2,1)S(1)}, u32[]{:S(2)}, u32[]{:S(2)}) collective-permute-start(bf16[256,1024]{1,0:T(8,128)(2,1)} %get-tuple-element.49), channel_id=1, source_target_pairs={{5,0},{7,2},{13,8},{15,10},{21,16},{23,18},{29,24},{31,26},{0,3},{... | collective-permute-start | bytes 1572872 | tf_op jit(solution)/shard_map/ppermute | solution.py:271
  35.2 10.8 %collective-permute-start.8 = (bf16[256,1024]{1,0:T(8,128)(2,1)}, bf16[256,1024]{1,0:T(8,128)(2,1)}, u32[]{:S(2)}, u32[]{:S(2)}) collective-permute-start(bf16[256,1024]{1,0:T(8,128)(2,1)} %get-tuple-element.52), channel_id=1, source_target_pairs={{5,0},{7,2},{13,8},{15,10},{21,16},{23,18},{29,24},{31,26}} | collective-permute-start | bytes 1572872 | tf_op jit(solution)/shard_map/ppermute | solution.py:271
  46.1 1.0 %copy-start.4 = (bf16[256,1024]{1,0:T(8,128)(2,1)S(1)}, bf16[256,1024]{1,0:T(8,128)(2,1)}, u32[]{:S(2)}) copy-start(bf16[256,1024]{1,0:T(8,128)(2,1)} %copy-done.3) | copy-start | bytes 1572868
  47.1 1.0 %copy-start.7 = (bf16[256,1024]{1,0:T(8,128)(2,1)S(1)}, bf16[256,1024]{1,0:T(8,128)(2,1)}, u32[]{:S(2)}) copy-start(bf16[256,1024]{1,0:T(8,128)(2,1)} %copy-done.6) | copy-start | bytes 1572868
  49.4 1.3 %copy-start = (bf16[1024,1024]{1,0:T(8,128)(2,1)}, bf16[1024,1024]{1,0:T(8,128)(2,1)S(1)}, u32[]{:S(2)}) copy-start(bf16[1024,1024]{1,0:T(8,128)(2,1)S(1)} %get-tuple-element.57.refs_2_) | copy-start | bytes 6291460
  50.7 12.1 %collective-permute-start.10 = (bf16[1024,1024]{1,0:T(8,128)(2,1)}, bf16[1024,1024]{1,0:T(8,128)(2,1)S(1)}, u32[]{:S(2)}, u32[]{:S(2)}) collective-permute-start(bf16[1024,1024]{1,0:T(8,128)(2,1)} %copy-done), channel_id=1, source_target_pairs={{1,0},{3,2},{5,4},{7,6},{9,8},{11,10},{13,12},{15,14},{17,16},{19,... | collective-permute-start | bytes 6291464 | tf_op jit(solution)/shard_map/ppermute | solution.py:271
  52.0 10.8 %collective-permute-start.11 = (bf16[256,1024]{1,0:T(8,128)(2,1)}, bf16[256,1024]{1,0:T(8,128)(2,1)}, u32[]{:S(2)}, u32[]{:S(2)}) collective-permute-start(bf16[256,1024]{1,0:T(8,128)(2,1)} %get-tuple-element.58), channel_id=1, source_target_pairs={{5,0},{7,2},{13,8},{15,10},{21,16},{23,18},{29,24},{31,26}} | collective-permute-start | bytes 1572872 | tf_op jit(solution)/shard_map/ppermute | solution.py:271
  53.3 0.7 collective-permute-start.9
  64.0 0.7 collective-permute-start.12
  65.9 0.7 collective-permute-start.13
  66.6 2.6 %copy-start.1 = (bf16[1024,1024]{1,0:T(8,128)(2,1)S(1)}, bf16[1024,1024]{1,0:T(8,128)(2,1)}, u32[]{:S(2)}) copy-start(bf16[1024,1024]{1,0:T(8,128)(2,1)} %copy-done) | copy-start | bytes 6291460
  68.5 0.9 collective-permute-start.14
  69.4 27.6 %copy-start.2 = (bf16[1024,1024]{1,0:T(8,128)(2,1)}, bf16[1024,1024]{1,0:T(8,128)(2,1)S(1)}, u32[]{:S(2)}) copy-start(bf16[1024,1024]{1,0:T(8,128)(2,1)S(1)} %broadcast_select_fusion.refs_0_) | copy-start | bytes 6291460
  71.4 2.0 %collective-permute-start.15 = (bf16[8,1024]{1,0:T(8,128)(2,1)S(1)}, bf16[8,1024]{1,0:T(8,128)(2,1)S(1)}, u32[]{:S(2)}, u32[]{:S(2)}) collective-permute-start(bf16[8,1024]{1,0:T(8,128)(2,1)S(1)} %get-tuple-element.66), channel_id=1, source_target_pairs={{16,8},{18,10}} | collective-permute-start | bytes 49160 | tf_op jit(solution)/shard_map/ppermute | solution.py:271
  72.1 5.2 %collective-permute-start.18 = (f32[8,1024]{1,0:T(8,128)S(1)}, f32[8,1024]{1,0:T(8,128)S(1)}, u32[]{:S(2)}, u32[]{:S(2)}) collective-permute-start(f32[8,1024]{1,0:T(8,128)S(1)} %get-tuple-element.71), channel_id=1, source_target_pairs={{5,0},{7,2}} | collective-permute-start | bytes 98312 | tf_op jit(solution)/shard_map/ppermute | solution.py:271
  74.6 22.4 %collective-permute-start.16 = (bf16[8,1024]{1,0:T(8,128)(2,1)S(1)}, bf16[8,1024]{1,0:T(8,128)(2,1)S(1)}, u32[]{:S(2)}, u32[]{:S(2)}) collective-permute-start(bf16[8,1024]{1,0:T(8,128)(2,1)S(1)} %get-tuple-element.69), channel_id=1, source_target_pairs={{8,0},{10,2}} | collective-permute-start | bytes 49160 | tf_op jit(solution)/shard_map/ppermute | solution.py:271
  75.9 21.1 %collective-permute-start.17 = (bf16[8,1024]{1,0:T(8,128)(2,1)S(1)}, bf16[8,1024]{1,0:T(8,128)(2,1)S(1)}, u32[]{:S(2)}, u32[]{:S(2)}) collective-permute-start(bf16[8,1024]{1,0:T(8,128)(2,1)S(1)} %get-tuple-element.69), channel_id=1, source_target_pairs={{8,5},{10,7}} | collective-permute-start | bytes 49160 | tf_op jit(solution)/shard_map/ppermute | solution.py:271
  76.6 22.6 %collective-permute-start.19 = (f32[8,1024]{1,0:T(8,128)S(1)}, f32[8,1024]{1,0:T(8,128)S(1)}, u32[]{:S(2)}, u32[]{:S(2)}) collective-permute-start(f32[8,1024]{1,0:T(8,128)S(1)} %select_select_fusion), channel_id=1, source_target_pairs={{8,12},{10,14},{16,20},{18,22},{24,28},{26,30}} | collective-permute-start | bytes 98312 | tf_op jit(solution)/shard_map/ppermute | solution.py:271
  99.2 2.1 %collective-permute-start.20 = (f32[4,1024]{1,0:T(4,128)S(1)}, f32[4,1024]{1,0:T(4,128)S(1)}, u32[]{:S(2)}, u32[]{:S(2)}) collective-permute-start(f32[4,1024]{1,0:T(4,128)S(1)} %slice_select_fusion), channel_id=1, source_target_pairs={{5,4},{7,6},{0,1},{2,3},{8,9},{10,11},{12,13},{14,15},{16,17},{18,... | collective-permute-start | bytes 49160 | tf_op jit(solution)/shard_map/ppermute | solution.py:271

commit v8 on v7

--- a/solution.py
+++ b/solution.py
@@ -100,7 +100,7 @@
         in_specs=[SMEM, map_spec, map_spec, VMEM] + [VMEM] * len(extra),
         out_specs=[VMEM] * len(shapes),
         compiler_params=PARAMS,
-        cost_estimate=cost(0, 8 * rows * width),
+        cost_estimate=cost(2 * rows * face * (width + face), 6 * rows * width),
     )(other_pattern, own, other, inverse, *extra)
 
 
@@ -146,7 +146,9 @@
         out_specs=[VMEM] * (3 if is_face else 2),
         input_output_aliases=aliases,
         compiler_params=PARAMS,
-        cost_estimate=cost(0, 8 * rows * width),
+        cost_estimate=cost(
+            2 * rows * inverse.shape[0] * (width + inverse.shape[0]), 6 * rows * width
+        ),
     )(is_second, own, other, inverse, *extra)
     return result[0], ((result[2] if is_face else state[0]), result[1])
 
@@ -228,7 +230,7 @@
         in_specs=[SMEM] + [VMEM] * (len(operands) - 1),
         out_specs=[VMEM] * (steps + 1),
         compiler_params=SWEEP_PARAMS,
-        cost_estimate=cost(0, steps * 4 * 1024 * 1024),
+        cost_estimate=cost(steps * 2 * 256 * 1024 * 1024, steps * 2 * 1024 * 1024),
     )(*operands)
     return results[:-1], results[-1]
 
@@ -286,7 +288,7 @@
         in_specs=[SMEM, VMEM],
         out_specs=VMEM,
         compiler_params=PARAMS,
-        cost_estimate=cost(0, 4 * width * width),
+        cost_estimate=cost(width * width, 4 * width * width),
     )(pattern, raw)
 
     def inverse_of(level):
@@ -421,7 +423,7 @@
         in_specs=[SMEM] + [VMEM] * (5 + len(pair_maps)),
         out_specs=VMEM,
         compiler_params=SWEEP_PARAMS,
-        cost_estimate=cost(0, 8 * 1024 * 1024),
+        cost_estimate=cost(6 * 256 * 1024 * 1024, 6 * 1024 * 1024),
     )(odd, from_pair, from_own, packed[:rows], down_odd, merged, *pair_maps)
     upward = jnp.where(layer < 2, last, settled)
     ends = upward[:rows_here], upward[rows_here : 2 * rows_here]

time: 103 us -> 103 us (level)
  transfers between devices with their start and end apart: 21 -> 21, of which waited for: 8 -> 7; matrix products, arithmetic and copies ran while one was open for 1% -> 1% of each run, Pallas kernels for 10% -> 13%
where the time goes in v8:
time: 103 us; the launch traced here: 102 us
  waiting for transfers between devices  41.9 us (41%)
  starting transfers between devices  28.7 us (28%)
  Pallas kernels  20.7 us (20%)
  local copies, waits for them, and re-layouts  8.6 us (8%)
  between operations  1.1 us (1%)
    ppermute x21, waiting for transfers between devices, send(): return lax.ppermute(value, AXES, pairs_of_devices)  41.9 us
    ppermute x21, starting transfers between devices, send(): return lax.ppermute(value, AXES, pairs_of_devices)  28.7 us
    unnamed x26, local copies, waits for them, and re-layouts  7.54 us
    pallas_call x6, Pallas kernels, segment(): pl.pallas_call(functools.partial(segment_kernel, coupling, [len(entry) fo...  7.52 us
    pallas_call x4, Pallas kernels, combine(): pl.pallas_call(functools.partial(combine_kernel, face_at, is_face, follow...  5.43 us
    pallas_call x2, Pallas kernels, leaf_combine(): pl.pallas_call(functools.partial(leaf_kernel, half * rows, is_face, piece...  4.7 us
    pallas_call x1, Pallas kernels, on_device(): pl.pallas_call(functools.partial(last_kernel, coupling, len(pair_maps)),...  2.14 us
  transfers between devices with their start and end apart: 21, of which 7 were waited for; matrix products, arithmetic and copies ran while one was open for 1% of the time, Pallas kernels for 13%

profile of v8, /device:TPU:0, one launch (start us, length us, event | category | flops | bytes accessed | tf_op | source)
XLA Modules:
  0.0 102.0 jit_solution(17277865911160255948)
XLA Ops:
  0.6 0.5 collective-permute-start.2
  1.1 0.1 collective-permute-start.1
  1.2 1.1 %fusion.1 = (bf16[256,256]{1,0:T(8,128)(2,1)S(1)}, bf16[256,256]{1,0:T(8,128)(2,1)S(1)}) fusion(f32[1,3,256,256]{3,2,1,0:T(8,128)} %param.7, s32[]{:T(128)S(6)} %select_n.101, s32[]{:T(128)S(6)} %select_n.100), kind=kLoop, calls=%fused_computation.4 | loop fusion | bytes 524296 | tf_op jit(solution)/shard_map/convert_element_type | solution.py:296
  2.3 0.0 copy-start.5
  2.3 1.6 %copy-done.5 = bf16[1,1024,1024]{2,1,0:T(8,128)(2,1)S(1)} copy-done((bf16[1,1024,1024]{2,1,0:T(8,128)(2,1)S(1)}, bf16[1,1024,1024]{2,1,0:T(8,128)(2,1)}, u32[]{:S(2)}) %copy-start.5) | copy-done | bytes 2097176
  3.9 0.7 copy-done.10
  4.6 0.9 shard_map.68.own
  5.5 0.0 collective-permute-done.1.other_pattern
  5.5 0.0 collective-permute-done.2.other
  5.5 2.7 %shard_map.69 = (bf16[256,1024]{1,0:T(8,128)(2,1)S(1)}, bf16[256,1024]{1,0:T(8,128)(2,1)}, bf16[256,1024]{1,0:T(8,128)(2,1)S(1)}) custom-call(s32[8,8]{1,0:T(8,128)S(1)} %collective-permute-done.1.other_pattern, bf16[1024,1024]{1,0:T(8,128)(2,1)S(1)} %shard_map.68.own, bf16[1024,1024]{1,0:T(8,128)(2,1)} %collective-permute-done.2.other, ...), custom_call_target="tpu_custom_call" | custom-call | flops 335544320 | bytes 3145728 | tf_op jit(solution)/shard_map/pallas_call | solution.py:96
  8.3 0.8 copy-done.8
  9.1 5.3 %collective-permute-start.3 = (bf16[256,1024]{1,0:T(8,128)(2,1)}, bf16[256,1024]{1,0:T(8,128)(2,1)}, u32[]{:S(2)}, u32[]{:S(2)}) collective-permute-start(bf16[256,1024]{1,0:T(8,128)(2,1)} %get-tuple-element.40.own), channel_id=1, source_target_pairs={{0,3},{2,1},{4,7},{6,5},{8,11},{10,9},{12,15},{14,13},{16,19},{18,... | collective-permute-start | bytes 1572872 | tf_op jit(solution)/shard_map/ppermute | solution.py:273
  14.4 1.3 %collective-permute-start.5 = (bf16[256,1024]{1,0:T(8,128)(2,1)S(1)}, bf16[256,1024]{1,0:T(8,128)(2,1)S(1)}, u32[]{:S(2)}, u32[]{:S(2)}) collective-permute-start(bf16[256,1024]{1,0:T(8,128)(2,1)S(1)} %get-tuple-element.46.own), channel_id=1, source_target_pairs={{0,3},{2,1},{4,7},{6,5},{8,11},{10,9},{12,15},{14,13},{16,19},{18,... | collective-permute-start | bytes 1572872 | tf_op jit(solution)/shard_map/ppermute | solution.py:273
  15.8 1.0 %copy-done.9 = bf16[256,1024]{1,0:T(8,128)(2,1)S(1)} copy-done((bf16[256,1024]{1,0:T(8,128)(2,1)S(1)}, bf16[256,1024]{1,0:T(8,128)(2,1)}, u32[]{:S(2)}) %copy-start.9) | copy-done | bytes 524312
  16.8 2.0 %shard_map.70 = (bf16[256,1024]{1,0:T(8,128)(2,1)S(1)}, bf16[256,1024]{1,0:T(8,128)(2,1)S(1)}) custom-call(s32[8,8]{1,0:T(8,128)S(1)} %collective-permute-done.1.other_pattern, bf16[1024,1024]{1,0:T(8,128)(2,1)S(1)} %shard_map.68.own, bf16[1024,1024]{1,0:T(8,128)(2,1)} %collective-permute-done.2.other, bf16[256,256]{1,0:T(8,128)(2,1)S(1)} %get-tuple-element.79.inverse, ...), custom_call_target="tpu_custom_call" | custom-call | flops 335544320 | bytes 3145728 | tf_op jit(solution)/shard_map/pallas_call | solution.py:96
  18.8 1.8 %collective-permute-done.3.other = bf16[256,1024]{1,0:T(8,128)(2,1)} collective-permute-done((bf16[256,1024]{1,0:T(8,128)(2,1)}, bf16[256,1024]{1,0:T(8,128)(2,1)}, u32[]{:S(2)}, u32[]{:S(2)}) %collective-permute-start.3) | collective-permute-done | bytes 524320 | tf_op jit(solution)/shard_map/ppermute | solution.py:273
  20.6 1.7 %shard_map.71 = (bf16[256,1024]{1,0:T(8,128)(2,1)S(1)}, bf16[1024,1024]{1,0:T(8,128)(2,1)S(1)}, bf16[256,1024]{1,0:T(8,128)(2,1)S(1)}) custom-call(s32[1]{0:T(128)} %bitcast.5.is_second, bf16[256,1024]{1,0:T(8,128)(2,1)} %get-tuple-element.40.own, bf16[256,1024]{1,0:T(8,128)(2,1)} %collective-permute-done.3.other, ...), custom_call_target="tpu_custom_call" | custom-call | flops 167772160 | bytes 1572864 | tf_op jit(solution)/shard_map/pallas_call | solution.py:136
  22.3 3.8 %collective-permute-start.7 = (bf16[256,1024]{1,0:T(8,128)(2,1)S(1)}, bf16[256,1024]{1,0:T(8,128)(2,1)S(1)}, u32[]{:S(2)}, u32[]{:S(2)}) collective-permute-start(bf16[256,1024]{1,0:T(8,128)(2,1)S(1)} %get-tuple-element.43), channel_id=1, source_target_pairs={{5,0},{7,2},{13,8},{15,10},{21,16},{23,18},{29,24},{31,26},{0,3},{... | collective-permute-start | bytes 1572872 | tf_op jit(solution)/shard_map/ppermute | solution.py:273
  26.1 0.1 collective-permute-start
  26.2 1.1 %collective-permute-done = f32[4,1024]{1,0:T(4,128)S(1)} collective-permute-done((f32[4,1024]{1,0:T(4,128)S(1)}, f32[4,1024]{1,0:T(4,128)S(1)}, u32[]{:S(2)}, u32[]{:S(2)}) %collective-permute-start) | collective-permute-done | bytes 16416 | tf_op jit(solution)/shard_map/ppermute | solution.py:273
  27.4 0.7 collective-permute-start.4
  28.1 0.0 collective-permute-done.5.other
  28.1 1.3 %shard_map.72 = (bf16[256,1024]{1,0:T(8,128)(2,1)}, bf16[1024,1024]{1,0:T(8,128)(2,1)S(1)}) custom-call(s32[1]{0:T(128)} %bitcast.5.is_second, bf16[256,1024]{1,0:T(8,128)(2,1)S(1)} %get-tuple-element.46.own, bf16[256,1024]{1,0:T(8,128)(2,1)S(1)} %collective-permute-done.5.other, ...), custom_call_target="tpu_custom_call", output_to_operand_aliasing={{1}: (6, {})} | custom-call | flops 167772160 | bytes 1572864 | tf_op jit(solution)/shard_map/pallas_call | solution.py:136
  29.3 4.6 %collective-permute-start.6 = (bf16[256,1024]{1,0:T(8,128)(2,1)}, bf16[256,1024]{1,0:T(8,128)(2,1)S(1)}, u32[]{:S(2)}, u32[]{:S(2)}) collective-permute-start(bf16[256,1024]{1,0:T(8,128)(2,1)} %get-tuple-element.49), channel_id=1, source_target_pairs={{5,0},{7,2},{13,8},{15,10},{21,16},{23,18},{29,24},{31,26},{0,3},{... | collective-permute-start | bytes 1572872 | tf_op jit(solution)/shard_map/ppermute | solution.py:273
  34.0 0.0 collective-permute-done.4.refs_3_
  34.0 0.0 collective-permute-done.7.other.refs_5_.refs_3_.refs_2_
  34.0 1.3 %shard_map.73 = (bf16[256,1024]{1,0:T(8,128)(2,1)}, bf16[1024,1024]{1,0:T(8,128)(2,1)S(1)}) custom-call(s32[1]{0:T(128)} %bitcast.5.is_second, bf16[256,1024]{1,0:T(8,128)(2,1)S(1)} %get-tuple-element.42.refs_0_.own, bf16[256,1024]{1,0:T(8,128)(2,1)S(1)} %collective-permute-done.7.other.refs_5_.refs_3_.refs_2_, ...), custom_call_target="tpu_custom_call", output_to_operand_aliasing={{1}: (5, {})} | custom-call | flops 167772160 | bytes 1572864 | tf_op jit(solution)/shard_map/pallas_call | solution.py:136
  35.2 1.3 %collective-permute-start.8 = (bf16[256,1024]{1,0:T(8,128)(2,1)}, bf16[256,1024]{1,0:T(8,128)(2,1)}, u32[]{:S(2)}, u32[]{:S(2)}) collective-permute-start(bf16[256,1024]{1,0:T(8,128)(2,1)} %get-tuple-element.52), channel_id=1, source_target_pairs={{5,0},{7,2},{13,8},{15,10},{21,16},{23,18},{29,24},{31,26}} | collective-permute-start | bytes 1572872 | tf_op jit(solution)/shard_map/ppermute | solution.py:273
  36.6 4.4 %collective-permute-done.6.other.refs_4_.refs_2_.refs_1_ = bf16[256,1024]{1,0:T(8,128)(2,1)S(1)} collective-permute-done((bf16[256,1024]{1,0:T(8,128)(2,1)}, bf16[256,1024]{1,0:T(8,128)(2,1)S(1)}, u32[]{:S(2)}, u32[]{:S(2)}) %collective-permute-start.6) | collective-permute-done | bytes 524320 | tf_op jit(solution)/shard_map/ppermute | solution.py:273
  41.0 5.1 %collective-permute-done.8.refs_6_.refs_4_.refs_3_ = bf16[256,1024]{1,0:T(8,128)(2,1)} collective-permute-done((bf16[256,1024]{1,0:T(8,128)(2,1)}, bf16[256,1024]{1,0:T(8,128)(2,1)}, u32[]{:S(2)}, u32[]{:S(2)}) %collective-permute-start.8) | collective-permute-done | bytes 524320 | tf_op jit(solution)/shard_map/ppermute | solution.py:273
  46.1 1.0 %copy-done.3 = bf16[256,1024]{1,0:T(8,128)(2,1)S(1)} copy-done((bf16[256,1024]{1,0:T(8,128)(2,1)S(1)}, bf16[256,1024]{1,0:T(8,128)(2,1)}, u32[]{:S(2)}) %copy-start.3) | copy-done | bytes 524312
  47.1 1.0 %copy-done.7 = bf16[256,1024]{1,0:T(8,128)(2,1)S(1)} copy-done((bf16[256,1024]{1,0:T(8,128)(2,1)S(1)}, bf16[256,1024]{1,0:T(8,128)(2,1)}, u32[]{:S(2)}) %copy-start.7) | copy-done | bytes 524312
  48.1 1.2 %shard_map.74 = (bf16[256,1024]{1,0:T(8,128)(2,1)}, bf16[1024,1024]{1,0:T(8,128)(2,1)S(1)}) custom-call(s32[1]{0:T(128)} %bitcast.5.is_second, bf16[256,1024]{1,0:T(8,128)(2,1)S(1)} %copy-done.7, bf16[256,1024]{1,0:T(8,128)(2,1)S(1)} %collective-permute-done.6.other.refs_4_.refs_2_.refs_1_, ...), custom_call_target="tpu_custom_call", output_to_operand_aliasing={{1}: (5, {})} | custom-call | flops 167772160 | bytes 1572864 | tf_op jit(solution)/shard_map/pallas_call | solution.py:136
  49.4 1.3 %copy-done = bf16[1024,1024]{1,0:T(8,128)(2,1)} copy-done((bf16[1024,1024]{1,0:T(8,128)(2,1)}, bf16[1024,1024]{1,0:T(8,128)(2,1)S(1)}, u32[]{:S(2)}) %copy-start) | copy-done | bytes 2097176
  50.7 1.3 %collective-permute-start.10 = (bf16[1024,1024]{1,0:T(8,128)(2,1)}, bf16[1024,1024]{1,0:T(8,128)(2,1)S(1)}, u32[]{:S(2)}, u32[]{:S(2)}) collective-permute-start(bf16[1024,1024]{1,0:T(8,128)(2,1)} %copy-done), channel_id=1, source_target_pairs={{1,0},{3,2},{5,4},{7,6},{9,8},{11,10},{13,12},{15,14},{17,16},{19,... | collective-permute-start | bytes 6291464 | tf_op jit(solution)/shard_map/ppermute | solution.py:273
  52.0 1.3 %collective-permute-start.11 = (bf16[256,1024]{1,0:T(8,128)(2,1)}, bf16[256,1024]{1,0:T(8,128)(2,1)}, u32[]{:S(2)}, u32[]{:S(2)}) collective-permute-start(bf16[256,1024]{1,0:T(8,128)(2,1)} %get-tuple-element.58), channel_id=1, source_target_pairs={{5,0},{7,2},{13,8},{15,10},{21,16},{23,18},{29,24},{31,26}} | collective-permute-start | bytes 1572872 | tf_op jit(solution)/shard_map/ppermute | solution.py:273
  53.3 0.7 collective-permute-start.9
  54.0 0.0 collective-permute-done.9.refs_0_
  54.0 8.8 %collective-permute-done.11.refs_7_.refs_5_.refs_4_ = bf16[256,1024]{1,0:T(8,128)(2,1)} collective-permute-done((bf16[256,1024]{1,0:T(8,128)(2,1)}, bf16[256,1024]{1,0:T(8,128)(2,1)}, u32[]{:S(2)}, u32[]{:S(2)}) %collective-permute-start.11) | collective-permute-done | bytes 524320 | tf_op jit(solution)/shard_map/ppermute | solution.py:273
  62.8 0.0 collective-permute-done.10.refs_2_.refs_7_
  62.8 1.2 %shard_map.76 = (f32[8,1024]{1,0:T(8,128)S(1)}, f32[8,1024]{1,0:T(8,128)S(1)}, bf16[8,1024]{1,0:T(8,128)(2,1)S(1)}) custom-call(s32[1]{0:T(128)} %bitcast.2.active, bf16[8,1024]{1,0:T(8,128)(2,1)S(1)} %collective-permute-done.9.refs_0_, f32[9,1024]{1,0:T(8,128)S(1)} %pad_maximum_fusion.refs_1_, ...), custom_call_target="tpu_custom_call" | custom-call | flops 1073741824 | bytes 4194304 | tf_op jit(solution)/shard_map/pallas_call | solution.py:225
  64.0 0.7 collective-permute-start.12
  64.7 0.0 collective-permute-done.12.refs_0_
  64.7 1.2 %shard_map.77 = (f32[8,1024]{1,0:T(8,128)S(1)}, f32[8,1024]{1,0:T(8,128)S(1)}, bf16[8,1024]{1,0:T(8,128)(2,1)S(1)}) custom-call(s32[1]{0:T(128)} %bitcast.1.active, bf16[8,1024]{1,0:T(8,128)(2,1)S(1)} %collective-permute-done.12.refs_0_, f32[9,1024]{1,0:T(8,128)S(1)} %pad_maximum_fusion.refs_1_, ...), custom_call_target="tpu_custom_call" | custom-call | flops 1073741824 | bytes 4194304 | tf_op jit(solution)/shard_map/pallas_call | solution.py:225
  65.9 0.7 collective-permute-start.13
  66.6 1.3 %collective-permute-start.18 = (f32[8,1024]{1,0:T(8,128)S(1)}, f32[8,1024]{1,0:T(8,128)S(1)}, u32[]{:S(2)}, u32[]{:S(2)}) collective-permute-start(f32[8,1024]{1,0:T(8,128)S(1)} %get-tuple-element.71), channel_id=1, source_target_pairs={{5,0},{7,2}} | collective-permute-start | bytes 98312 | tf_op jit(solution)/shard_map/ppermute | solution.py:273
  67.9 0.0 collective-permute-done.13.refs_0_
  67.9 0.0 copy-start.1
  67.9 2.0 %shard_map.78 = (f32[8,1024]{1,0:T(8,128)}, f32[8,1024]{1,0:T(8,128)S(1)}, f32[8,1024]{1,0:T(8,128)S(1)}, bf16[8,1024]{1,0:T(8,128)(2,1)S(1)}) custom-call(s32[1]{0:T(128)} %bitcast.active, bf16[8,1024]{1,0:T(8,128)(2,1)S(1)} %collective-permute-done.13.refs_0_, f32[9,1024]{1,0:T(8,128)S(1)} %pad_maximum_fusion.refs_1_, ...), custom_call_target="tpu_custom_call" | custom-call | flops 1610612736 | bytes 6291456 | tf_op jit(solution)/shard_map/pallas_call | solution.py:225
  69.9 0.7 collective-permute-start.14
  70.5 0.2 broadcast_select_fusion.refs_0_
  70.8 0.0 copy-start.4
  70.8 0.0 collective-permute-done.14.refs_0_
  70.8 2.0 %shard_map.79 = (f32[8,1024]{1,0:T(8,128)S(1)}, f32[8,1024]{1,0:T(8,128)S(1)}, bf16[8,1024]{1,0:T(8,128)(2,1)S(1)}) custom-call(s32[1]{0:T(128)} %bitcast.1.active, bf16[8,1024]{1,0:T(8,128)(2,1)S(1)} %collective-permute-done.14.refs_0_, f32[8,1024]{1,0:T(8,128)S(1)} %get-tuple-element.64.refs_1_, ...), custom_call_target="tpu_custom_call" | custom-call | flops 1073741824 | bytes 4194304 | tf_op jit(solution)/shard_map/pallas_call | solution.py:225
  72.7 0.7 collective-permute-start.15
  73.4 1.2 %shard_map.80 = (f32[8,1024]{1,0:T(8,128)S(1)}, f32[8,1024]{1,0:T(8,128)S(1)}, bf16[8,1024]{1,0:T(8,128)(2,1)S(1)}) custom-call(s32[1]{0:T(128)} %bitcast.2.active, bf16[8,1024]{1,0:T(8,128)(2,1)S(1)} %collective-permute-done.15.refs_0_, f32[8,1024]{1,0:T(8,128)S(1)} %get-tuple-element.67.refs_1_, ...), custom_call_target="tpu_custom_call" | custom-call | flops 1073741824 | bytes 4194304 | tf_op jit(solution)/shard_map/pallas_call | solution.py:225
  74.6 1.3 %collective-permute-start.16 = (bf16[8,1024]{1,0:T(8,128)(2,1)S(1)}, bf16[8,1024]{1,0:T(8,128)(2,1)S(1)}, u32[]{:S(2)}, u32[]{:S(2)}) collective-permute-start(bf16[8,1024]{1,0:T(8,128)(2,1)S(1)} %get-tuple-element.69), channel_id=1, source_target_pairs={{8,0},{10,2}} | collective-permute-start | bytes 49160 | tf_op jit(solution)/shard_map/ppermute | solution.py:273
  75.9 0.7 collective-permute-start.17
  76.6 0.7 collective-permute-start.19
  77.3 19.8 %collective-permute-done.16.from_pair = bf16[8,1024]{1,0:T(8,128)(2,1)S(1)} collective-permute-done((bf16[8,1024]{1,0:T(8,128)(2,1)S(1)}, bf16[8,1024]{1,0:T(8,128)(2,1)S(1)}, u32[]{:S(2)}, u32[]{:S(2)}) %collective-permute-start.16) | collective-permute-done | bytes 16416 | tf_op jit(solution)/shard_map/ppermute | solution.py:273
  97.0 2.1 %shard_map.81 = f32[8,1024]{1,0:T(8,128)S(1)} custom-call(s32[1]{0:T(128)} %bitcast.11.odd, bf16[8,1024]{1,0:T(8,128)(2,1)S(1)} %collective-permute-done.16.from_pair, bf16[8,1024]{1,0:T(8,128)(2,1)S(1)} %collective-permute-done.17.from_own, f32[8,1024]{1,0:T(8,128)S(1)} %pad_maximum_fusion.1.source, f32[8,1024]{1,0:T(8,128)S(1)} %broadcast_select_fusion.1.down_odd, ...), custom_call_target="tpu_custom_call" | custom-call | flops 1610612736 | bytes 6291456 | tf_op jit(solution)/shard_map/pallas_call | solution.py:420
  99.2 1.3 %collective-permute-start.20 = (f32[4,1024]{1,0:T(4,128)S(1)}, f32[4,1024]{1,0:T(4,128)S(1)}, u32[]{:S(2)}, u32[]{:S(2)}) collective-permute-start(f32[4,1024]{1,0:T(4,128)S(1)} %slice_select_fusion), channel_id=1, source_target_pairs={{5,4},{7,6},{0,1},{2,3},{8,9},{10,11},{12,13},{14,15},{16,17},{18,... | collective-permute-start | bytes 49160 | tf_op jit(solution)/shard_map/ppermute | solution.py:273
  100.5 0.8 collective-permute-done.20
  101.3 0.6 select_bitcast_fusion
  (30 shorter events, 0.1 us)
Async XLA Ops:
  0.6 4.9 %collective-permute-start.2 = (bf16[1024,1024]{1,0:T(8,128)(2,1)}, bf16[1024,1024]{1,0:T(8,128)(2,1)}, u32[]{:S(2)}, u32[]{:S(2)}) collective-permute-start(bf16[1024,1024]{1,0:T(8,128)(2,1)} %bitcast.19), channel_id=1, source_target_pairs={{0,1},{1,0},{2,3},{3,2},{4,5},{5,4},{6,7},{7,6},{8,9},{9,8},{10,11... | collective-permute-start | bytes 6291464 | tf_op jit(solution)/shard_map/ppermute | solution.py:273
  1.1 4.4 %collective-permute-start.1 = (s32[8,8]{1,0:T(8,128)}, s32[8,8]{1,0:T(8,128)S(1)}, u32[]{:S(2)}, u32[]{:S(2)}) collective-permute-start(s32[8,8]{1,0:T(8,128)} %bitcast.21), channel_id=1, source_target_pairs={{0,1},{1,0},{2,3},{3,2},{4,5},{5,4},{6,7},{7,6},{8,9},{9,8},{10,11... | collective-permute-start | bytes 776 | tf_op jit(solution)/shard_map/ppermute | solution.py:273
  2.3 1.6 %copy-start.5 = (bf16[1,1024,1024]{2,1,0:T(8,128)(2,1)S(1)}, bf16[1,1024,1024]{2,1,0:T(8,128)(2,1)}, u32[]{:S(2)}) copy-start(bf16[1,1024,1024]{2,1,0:T(8,128)(2,1)} %param.5) | copy-start | bytes 6291460
  3.9 0.7 copy-start.10
  8.3 0.8 copy-start.8
  9.1 11.5 %collective-permute-start.3 = (bf16[256,1024]{1,0:T(8,128)(2,1)}, bf16[256,1024]{1,0:T(8,128)(2,1)}, u32[]{:S(2)}, u32[]{:S(2)}) collective-permute-start(bf16[256,1024]{1,0:T(8,128)(2,1)} %get-tuple-element.40.own), channel_id=1, source_target_pairs={{0,3},{2,1},{4,7},{6,5},{8,11},{10,9},{12,15},{14,13},{16,19},{18,... | collective-permute-start | bytes 1572872 | tf_op jit(solution)/shard_map/ppermute | solution.py:273
  14.4 13.6 %collective-permute-start.5 = (bf16[256,1024]{1,0:T(8,128)(2,1)S(1)}, bf16[256,1024]{1,0:T(8,128)(2,1)S(1)}, u32[]{:S(2)}, u32[]{:S(2)}) collective-permute-start(bf16[256,1024]{1,0:T(8,128)(2,1)S(1)} %get-tuple-element.46.own), channel_id=1, source_target_pairs={{0,3},{2,1},{4,7},{6,5},{8,11},{10,9},{12,15},{14,13},{16,19},{18,... | collective-permute-start | bytes 1572872 | tf_op jit(solution)/shard_map/ppermute | solution.py:273
  15.7 1.0 %copy-start.9 = (bf16[256,1024]{1,0:T(8,128)(2,1)S(1)}, bf16[256,1024]{1,0:T(8,128)(2,1)}, u32[]{:S(2)}) copy-start(bf16[256,1024]{1,0:T(8,128)(2,1)} %copy-done.8) | copy-start | bytes 1572868
  16.8 9.3 %copy-start.11 = (f32[1,4,1024]{2,1,0:T(4,128)S(1)}, f32[1,4,1024]{2,1,0:T(4,128)}, u32[]{:S(2)}) copy-start(f32[1,4,1024]{2,1,0:T(4,128)} %param.9) | copy-start | bytes 49156
  16.8 9.4 %copy-start.12 = (s32[1,1024]{1,0:T(1,128)S(1)}, s32[1,1024]{1,0:T(1,128)}, u32[]{:S(2)}) copy-start(s32[1,1024]{1,0:T(1,128)} %param.8) | copy-start | bytes 12292
  18.8 10.6 %copy-start.6 = (bf16[256,1024]{1,0:T(8,128)(2,1)}, bf16[256,1024]{1,0:T(8,128)(2,1)S(1)}, u32[]{:S(2)}) copy-start(bf16[256,1024]{1,0:T(8,128)(2,1)S(1)} %get-tuple-element.45.refs_0_.own) | copy-start | bytes 1572868
  22.3 11.7 %copy-start.2 = (bf16[256,1024]{1,0:T(8,128)(2,1)}, bf16[256,1024]{1,0:T(8,128)(2,1)S(1)}, u32[]{:S(2)}) copy-start(bf16[256,1024]{1,0:T(8,128)(2,1)S(1)} %get-tuple-element.47.refs_1_.refs_0_) | copy-start | bytes 1572868
  22.3 11.7 %collective-permute-start.7 = (bf16[256,1024]{1,0:T(8,128)(2,1)S(1)}, bf16[256,1024]{1,0:T(8,128)(2,1)S(1)}, u32[]{:S(2)}, u32[]{:S(2)}) collective-permute-start(bf16[256,1024]{1,0:T(8,128)(2,1)S(1)} %get-tuple-element.43), channel_id=1, source_target_pairs={{5,0},{7,2},{13,8},{15,10},{21,16},{23,18},{29,24},{31,26},{0,3},{... | collective-permute-start | bytes 1572872 | tf_op jit(solution)/shard_map/ppermute | solution.py:273
  26.1 1.2 %collective-permute-start = (f32[4,1024]{1,0:T(4,128)S(1)}, f32[4,1024]{1,0:T(4,128)S(1)}, u32[]{:S(2)}, u32[]{:S(2)}) collective-permute-start(f32[4,1024]{1,0:T(4,128)S(1)} %bitcast.23), channel_id=1, source_target_pairs={{0,1},{1,0},{2,3},{3,2},{4,5},{5,4},{6,7},{7,6},{8,9},{9,8},{10,11... | collective-permute-start | bytes 49160 | tf_op jit(solution)/shard_map/ppermute | solution.py:273
  27.4 6.6 %collective-permute-start.4 = (f32[9,1024]{1,0:T(8,128)S(1)}, f32[9,1024]{1,0:T(8,128)S(1)}, u32[]{:S(2)}, u32[]{:S(2)}) collective-permute-start(f32[9,1024]{1,0:T(8,128)S(1)} %pad_maximum_fusion.refs_1_), channel_id=1, source_target_pairs={{12,8},{14,10},{20,16},{22,18},{28,24},{30,26},{1,5},{3,7}} | collective-permute-start | bytes 110600 | tf_op jit(solution)/shard_map/ppermute | solution.py:273
  29.3 11.6 %collective-permute-start.6 = (bf16[256,1024]{1,0:T(8,128)(2,1)}, bf16[256,1024]{1,0:T(8,128)(2,1)S(1)}, u32[]{:S(2)}, u32[]{:S(2)}) collective-permute-start(bf16[256,1024]{1,0:T(8,128)(2,1)} %get-tuple-element.49), channel_id=1, source_target_pairs={{5,0},{7,2},{13,8},{15,10},{21,16},{23,18},{29,24},{31,26},{0,3},{... | collective-permute-start | bytes 1572872 | tf_op jit(solution)/shard_map/ppermute | solution.py:273
  35.2 10.8 %collective-permute-start.8 = (bf16[256,1024]{1,0:T(8,128)(2,1)}, bf16[256,1024]{1,0:T(8,128)(2,1)}, u32[]{:S(2)}, u32[]{:S(2)}) collective-permute-start(bf16[256,1024]{1,0:T(8,128)(2,1)} %get-tuple-element.52), channel_id=1, source_target_pairs={{5,0},{7,2},{13,8},{15,10},{21,16},{23,18},{29,24},{31,26}} | collective-permute-start | bytes 1572872 | tf_op jit(solution)/shard_map/ppermute | solution.py:273
  46.1 1.0 %copy-start.3 = (bf16[256,1024]{1,0:T(8,128)(2,1)S(1)}, bf16[256,1024]{1,0:T(8,128)(2,1)}, u32[]{:S(2)}) copy-start(bf16[256,1024]{1,0:T(8,128)(2,1)} %copy-done.2) | copy-start | bytes 1572868
  47.1 1.0 %copy-start.7 = (bf16[256,1024]{1,0:T(8,128)(2,1)S(1)}, bf16[256,1024]{1,0:T(8,128)(2,1)}, u32[]{:S(2)}) copy-start(bf16[256,1024]{1,0:T(8,128)(2,1)} %copy-done.6) | copy-start | bytes 1572868
  49.4 1.3 %copy-start = (bf16[1024,1024]{1,0:T(8,128)(2,1)}, bf16[1024,1024]{1,0:T(8,128)(2,1)S(1)}, u32[]{:S(2)}) copy-start(bf16[1024,1024]{1,0:T(8,128)(2,1)S(1)} %get-tuple-element.57.refs_2_) | copy-start | bytes 6291460
  50.7 12.1 %collective-permute-start.10 = (bf16[1024,1024]{1,0:T(8,128)(2,1)}, bf16[1024,1024]{1,0:T(8,128)(2,1)S(1)}, u32[]{:S(2)}, u32[]{:S(2)}) collective-permute-start(bf16[1024,1024]{1,0:T(8,128)(2,1)} %copy-done), channel_id=1, source_target_pairs={{1,0},{3,2},{5,4},{7,6},{9,8},{11,10},{13,12},{15,14},{17,16},{19,... | collective-permute-start | bytes 6291464 | tf_op jit(solution)/shard_map/ppermute | solution.py:273
  52.0 10.8 %collective-permute-start.11 = (bf16[256,1024]{1,0:T(8,128)(2,1)}, bf16[256,1024]{1,0:T(8,128)(2,1)}, u32[]{:S(2)}, u32[]{:S(2)}) collective-permute-start(bf16[256,1024]{1,0:T(8,128)(2,1)} %get-tuple-element.58), channel_id=1, source_target_pairs={{5,0},{7,2},{13,8},{15,10},{21,16},{23,18},{29,24},{31,26}} | collective-permute-start | bytes 1572872 | tf_op jit(solution)/shard_map/ppermute | solution.py:273
  53.3 0.7 collective-permute-start.9
  64.0 0.7 collective-permute-start.12
  65.9 2.0 %collective-permute-start.13 = (bf16[8,1024]{1,0:T(8,128)(2,1)S(1)}, bf16[8,1024]{1,0:T(8,128)(2,1)S(1)}, u32[]{:S(2)}, u32[]{:S(2)}) collective-permute-start(bf16[8,1024]{1,0:T(8,128)(2,1)S(1)} %get-tuple-element.60), channel_id=1, source_target_pairs={{16,24},{18,26}} | collective-permute-start | bytes 49160 | tf_op jit(solution)/shard_map/ppermute | solution.py:273
  66.6 6.8 %collective-permute-start.18 = (f32[8,1024]{1,0:T(8,128)S(1)}, f32[8,1024]{1,0:T(8,128)S(1)}, u32[]{:S(2)}, u32[]{:S(2)}) collective-permute-start(f32[8,1024]{1,0:T(8,128)S(1)} %get-tuple-element.71), channel_id=1, source_target_pairs={{5,0},{7,2}} | collective-permute-start | bytes 98312 | tf_op jit(solution)/shard_map/ppermute | solution.py:273
  67.9 2.6 %copy-start.1 = (bf16[1024,1024]{1,0:T(8,128)(2,1)S(1)}, bf16[1024,1024]{1,0:T(8,128)(2,1)}, u32[]{:S(2)}) copy-start(bf16[1024,1024]{1,0:T(8,128)(2,1)} %copy-done) | copy-start | bytes 6291460
  69.9 0.9 collective-permute-start.14
  70.8 26.3 %copy-start.4 = (bf16[1024,1024]{1,0:T(8,128)(2,1)}, bf16[1024,1024]{1,0:T(8,128)(2,1)S(1)}, u32[]{:S(2)}) copy-start(bf16[1024,1024]{1,0:T(8,128)(2,1)S(1)} %broadcast_select_fusion.refs_0_) | copy-start | bytes 6291460
  72.7 0.7 collective-permute-start.15
  74.6 22.4 %collective-permute-start.16 = (bf16[8,1024]{1,0:T(8,128)(2,1)S(1)}, bf16[8,1024]{1,0:T(8,128)(2,1)S(1)}, u32[]{:S(2)}, u32[]{:S(2)}) collective-permute-start(bf16[8,1024]{1,0:T(8,128)(2,1)S(1)} %get-tuple-element.69), channel_id=1, source_target_pairs={{8,0},{10,2}} | collective-permute-start | bytes 49160 | tf_op jit(solution)/shard_map/ppermute | solution.py:273
  75.9 21.1 %collective-permute-start.17 = (bf16[8,1024]{1,0:T(8,128)(2,1)S(1)}, bf16[8,1024]{1,0:T(8,128)(2,1)S(1)}, u32[]{:S(2)}, u32[]{:S(2)}) collective-permute-start(bf16[8,1024]{1,0:T(8,128)(2,1)S(1)} %get-tuple-element.69), channel_id=1, source_target_pairs={{8,5},{10,7}} | collective-permute-start | bytes 49160 | tf_op jit(solution)/shard_map/ppermute | solution.py:273
  76.6 22.6 %collective-permute-start.19 = (f32[8,1024]{1,0:T(8,128)S(1)}, f32[8,1024]{1,0:T(8,128)S(1)}, u32[]{:S(2)}, u32[]{:S(2)}) collective-permute-start(f32[8,1024]{1,0:T(8,128)S(1)} %select_select_fusion), channel_id=1, source_target_pairs={{8,12},{10,14},{16,20},{18,22},{24,28},{26,30}} | collective-permute-start | bytes 98312 | tf_op jit(solution)/shard_map/ppermute | solution.py:273
  99.2 2.1 %collective-permute-start.20 = (f32[4,1024]{1,0:T(4,128)S(1)}, f32[4,1024]{1,0:T(4,128)S(1)}, u32[]{:S(2)}, u32[]{:S(2)}) collective-permute-start(f32[4,1024]{1,0:T(4,128)S(1)} %slice_select_fusion), channel_id=1, source_target_pairs={{5,4},{7,6},{0,1},{2,3},{8,9},{10,11},{12,13},{14,15},{16,17},{18,... | collective-permute-start | bytes 49160 | tf_op jit(solution)/shard_map/ppermute | solution.py:273

commit v9 on v5

--- a/solution.py
+++ b/solution.py
@@ -55,56 +55,43 @@
     return jnp.concatenate(strips, axis=0)
 
 
-def mask_kernel(pattern, values, out):
-    block = values.shape[1] // pattern.shape[1]
-    for r in range(values.shape[0] // block):
-        out[r * block : (r + 1) * block] = masked(values, pattern, r * block, block, r).astype(
-            jnp.bfloat16
-        )
-
-
-def leaf_kernel(first_row, is_face, pieces, other_pattern, own, other, inverse, *refs):
+def leaf_kernel(first_row, is_face, own_pattern, other_pattern, own, other, inverse, *refs):
     refs = list(refs)
     face = inverse.shape[0]
     right = None if is_face else refs.pop(0)[...]
-    block = own.shape[1] // other_pattern.shape[1]
+    block = own.shape[1] // own_pattern.shape[1]
     for i in range(own.shape[0] // face):
-        at = first_row + i * face
-        joined = own[i * face : (i + 1) * face].astype(jnp.float32) + masked(
-            other, other_pattern, i * face, face, at // block
+        block_at = (first_row + i * face) // block
+        joined = masked(own, own_pattern, i * face, face, block_at) + masked(
+            other, other_pattern, i * face, face, block_at
         )
         if right is None:
             right = joined.astype(jnp.bfloat16)
             refs[-1][...] = right
-        result = minus_face(joined, 0, inverse[...], right)
-        for ref, (start, size) in zip(refs, pieces):
-            low, high = max(start, at), min(start + size, at + face)
-            if low < high:
-                ref[low - start : high - start] = result[low - at : high - at]
-
-
-def leaf_combine(other_pattern, own, other, inverse, face_rows, half, pieces):
+        refs[i][...] = minus_face(joined, 0, inverse[...], right)
+
+
+def leaf_combine(own_pattern, other_pattern, own, other, inverse, face_rows, half):
     is_face = face_rows is None
     width = own.shape[1]
     rows = own.shape[0] // 2
     face = inverse.shape[0]
-    shapes = [jax.ShapeDtypeStruct((size, width), jnp.bfloat16) for _, size in pieces]
-    if is_face:
-        shapes.append(jax.ShapeDtypeStruct((face, width), jnp.bfloat16))
+    count = rows // face
+    piece = jax.ShapeDtypeStruct((face, width), jnp.bfloat16)
     map_spec = pl.BlockSpec((rows, width), lambda i: (half, 0))
     extra = [] if is_face else [face_rows]
     return pl.pallas_call(
-        functools.partial(leaf_kernel, half * rows, is_face, pieces),
+        functools.partial(leaf_kernel, half * rows, is_face),
         grid=(1,),
-        out_shape=shapes,
-        in_specs=[SMEM, map_spec, map_spec, VMEM] + [VMEM] * len(extra),
-        out_specs=[VMEM] * len(shapes),
+        out_shape=[piece] * (count + (1 if is_face else 0)),
+        in_specs=[SMEM, SMEM, map_spec, map_spec, VMEM] + [VMEM] * len(extra),
+        out_specs=[VMEM] * (count + (1 if is_face else 0)),
         compiler_params=PARAMS,
         cost_estimate=cost(2 * rows * face * (width + face), 6 * rows * width),
-    )(other_pattern, own, other, inverse, *extra)
-
-
-def combine_kernel(face_at, is_face, with_next, whole_rows, is_second, own, other, inverse, *refs):
+    )(own_pattern, other_pattern, own, other, inverse, *extra)
+
+
+def combine_kernel(face_at, is_face, with_next, whole_rows, own, other, inverse, *refs):
     refs = list(refs)
     following = refs.pop(0) if with_next else None
     joined = 0.5 * (own[...].astype(jnp.float32) + other[...].astype(jnp.float32))
@@ -120,16 +107,16 @@
     refs[0][...] = piece
     if with_next:
 
-        @pl.when(is_second[0] == 0)
+        @pl.when(lax.axis_index("box") % 2 == 0)
         def _():
             refs[0][...] = following[...]
 
 
-def combine(is_second, own, other, inverse, following, state, face_at, row_at):
+def combine(own, other, inverse, following, state, face_at, row_at):
     is_face = state is None
     rows, width = own.shape
     extra = [] if following is None else [following]
-    aliases = {} if is_face else {4 + len(extra) + 1: 1}
+    aliases = {} if is_face else {3 + len(extra) + 1: 1}
     extra += [] if is_face else list(state)
     piece = jax.ShapeDtypeStruct((rows, width), jnp.bfloat16)
     whole = jax.ShapeDtypeStruct((width, width), jnp.bfloat16)
@@ -142,12 +129,12 @@
             slice(row_at, row_at + rows),
         ),
         out_shape=[piece, whole] + ([piece] if is_face else []),
-        in_specs=[SMEM] + [VMEM] * (3 + len(extra)),
+        in_specs=[VMEM] * (3 + len(extra)),
         out_specs=[VMEM] * (3 if is_face else 2),
         input_output_aliases=aliases,
         compiler_params=PARAMS,
         cost_estimate=cost(0, 0),
-    )(is_second, own, other, inverse, *extra)
+    )(own, other, inverse, *extra)
     return result[0], ((result[2] if is_face else state[0]), result[1])
 
 
@@ -180,7 +167,13 @@
     return jnp.concatenate(outs, axis=1)
 
 
-def segment_kernel(coupling, pieces_of, down_steps, up_steps, *refs):
+def segment_kernel(coupling, at, pieces_of, down_steps, up_steps, *refs):
+    @pl.when(lax.axis_index("layer") == at)
+    def _():
+        run_segment(coupling, pieces_of, down_steps, up_steps, *refs)
+
+
+def run_segment(coupling, pieces_of, down_steps, up_steps, *refs):
     refs = list(refs)
     state = refs.pop(0)[...]
     maps, downs = {}, {}
@@ -205,7 +198,7 @@
     refs.pop(0)[...] = state
 
 
-def segment(coupling, arrived, packed, downs, maps, down_steps, up_steps):
+def segment(coupling, at, arrived, packed, downs, maps, down_steps, up_steps):
     operands = [arrived]
     for slot in down_steps:
         operands += [packed[slot], *maps[slot]]
@@ -216,7 +209,7 @@
     steps = len(down_steps) + len(up_steps)
     results = pl.pallas_call(
         functools.partial(
-            segment_kernel, coupling, [len(entry) for entry in maps], down_steps, up_steps
+            segment_kernel, coupling, at, [len(entry) for entry in maps], down_steps, up_steps
         ),
         out_shape=[rows] * steps + [jax.ShapeDtypeStruct(arrived.shape, jnp.bfloat16)],
         in_specs=[VMEM] * len(operands),
@@ -246,7 +239,6 @@
     position = lax.axis_index("box")
     layer = lax.axis_index("layer")
     is_second = position % 2 == 1
-    second_flag = is_second.astype(jnp.int32)[None]
 
     chain = [(layer_at, (OWN, PAIR)) for layer_at in range(2, layers, 2)]
     pair_moves = [(layer_at + 1, layer_at) for layer_at in range(0, layers, 2)]
@@ -274,15 +266,6 @@
     raw_other = send(raw, over_box(1, range(boxes)))
     pattern_other = send(pattern, over_box(1, range(boxes)))
     other_sources = send(sources[0], over_box(1, range(boxes)))
-    own_half = pl.pallas_call(
-        mask_kernel,
-        out_shape=jax.ShapeDtypeStruct(raw.shape, jnp.bfloat16),
-        in_specs=[SMEM, VMEM],
-        out_specs=VMEM,
-        compiler_params=PARAMS,
-        cost_estimate=cost(width * width, 4 * width * width),
-    )(pattern, raw)
-
     def inverse_of(level):
         node = (boxes >> (level + 1)) - 1 + (position >> (level + 1))
         return lax.dynamic_index_in_dim(face_inverses[0], node, 0, keepdims=False).astype(
@@ -304,8 +287,8 @@
     upper = tuple(piece for piece in pieces if piece[0] < width // 2)
     lower = tuple(piece for piece in pieces if piece[0] >= width // 2)
     inverse = inverse_of(0)
-    top = leaf_combine(pattern_other, own_half, raw_other, inverse, None, 0, upper)
-    bottom = leaf_combine(pattern_other, own_half, raw_other, inverse, top[-1], 1, lower)
+    top = leaf_combine(pattern, pattern_other, raw, raw_other, inverse, None, 0)
+    bottom = leaf_combine(pattern, pattern_other, raw, raw_other, inverse, top[-1], 1)
     current = dict(zip(upper + lower, [*top[:-1], *bottom]))
 
     for level in range(1, levels):
@@ -321,7 +304,6 @@
             renewed = {}
             for piece in order:
                 renewed[piece], state = combine(
-                    second_flag,
                     current[piece],
                     received[piece],
                     inverse,
@@ -345,7 +327,6 @@
             if k > AHEAD:
                 other = after(other, pair_pieces[order[k - 1]])
             payload, state = combine(
-                second_flag,
                 current[piece],
                 other,
                 inverse,
@@ -366,7 +347,7 @@
 
     first = pair_packed[:rows].astype(jnp.bfloat16)
     (down_odd,), state = segment(
-        coupling, first, small, {}, [[merged], pair_maps], (OWN,), ()
+        coupling, 1, first, small, {}, [[merged], pair_maps], (OWN,), ()
     )
     merged_first = send(after(merged, state), route(every, 1, 0))
     maps = [[merged_first], pair_maps]
@@ -379,7 +360,7 @@
         turn = k == len(chain) - 1
         back = tuple(reversed(slots))
         results, state = segment(
-            coupling, arrived, small, {}, maps, slots, back[1:] if turn else ()
+            coupling, at, arrived, small, {}, maps, slots, back[1:] if turn else ()
         )
         kept.append(dict(zip(slots, results)))
         if k == 0:
@@ -397,7 +378,7 @@
             arrived, merged = lax.optimization_barrier((arrived, merged))
         at = target
         back = tuple(reversed(slots))
-        results, state = segment(coupling, arrived, small, kept[k], maps, (), back)
+        results, state = segment(coupling, at, arrived, small, kept[k], maps, (), back)
         ups[at] = dict(zip(back, results))
     from_own = send(state, route([(at, 1)], 0, 1))
     from_pair = send(state, route([(at, 0)]))

time: 94.2 us -> 96 us (1.019)
  Pallas kernels: 16.5 us -> 9.04 us
  waiting for transfers between devices: 38.5 us -> 45.6 us
  local copies, waits for them, and re-layouts: 7.43 us -> 9.59 us
    pallas_call x9 -> x8, Pallas kernels: 12.5 us -> 4.2 us  [the longest x2 3.5 us: leaf_combine(): pl.pallas_call(functools.partial(leaf_kernel, half * rows, is_face), grid...]
    ppermute x21, waiting for transfers between devices: 38.5 us -> 45.6 us  [send(): return lax.ppermute(value, AXES, pairs_of_devices)]
    unnamed x30 -> x40, local copies, waits for them, and re-layouts: 6.36 us -> 8.53 us
  transfers between devices with their start and end apart: 21 -> 21, of which waited for: 7 -> 9; matrix products, arithmetic and copies ran while one was open for 1% -> 1% of each run, Pallas kernels for 10% -> 7%
where the time goes in v9:
time: 96 us; the launch traced here: 95.3 us
  waiting for transfers between devices  45.6 us (48%)
  starting transfers between devices  29 us (30%)
  local copies, waits for them, and re-layouts  9.59 us (10%)
  Pallas kernels  9.04 us (9%)
  between operations  1.15 us (1%)
    ppermute x21, waiting for transfers between devices, send(): return lax.ppermute(value, AXES, pairs_of_devices)  45.6 us
    ppermute x21, starting transfers between devices, send(): return lax.ppermute(value, AXES, pairs_of_devices)  29 us
    unnamed x40, local copies, waits for them, and re-layouts  8.53 us
    pallas_call x4, Pallas kernels, combine(): pl.pallas_call(functools.partial(combine_kernel, face_at, is_face, follow...  3.89 us
    pallas_call x2, Pallas kernels, leaf_combine(): pl.pallas_call(functools.partial(leaf_kernel, half * rows, is_face), grid...  3.5 us
  transfers between devices with their start and end apart: 21, of which 9 were waited for; matrix products, arithmetic and copies ran while one was open for 1% of the time, Pallas kernels for 7%

profile of v9, /device:TPU:0, one launch (start us, length us, event | category | flops | bytes accessed | tf_op | source)
XLA Modules:
  0.0 95.3 jit_solution(9965339337533381526)
XLA Ops:
  0.6 0.5 collective-permute-start.2
  1.1 0.1 collective-permute-start.1
  1.2 1.1 %fusion.1 = (bf16[256,256]{1,0:T(8,128)(2,1)S(1)}, bf16[256,256]{1,0:T(8,128)(2,1)S(1)}) fusion(f32[1,3,256,256]{3,2,1,0:T(8,128)} %param.7, s32[]{:T(128)S(6)} %select_n.101, s32[]{:T(128)S(6)} %select_n.100), kind=kLoop, calls=%fused_computation.4 | loop fusion | bytes 524296 | tf_op jit(solution)/shard_map/convert_element_type | solution.py:271
  2.3 2.9 %collective-permute-done.1.other_pattern = s32[8,8]{1,0:T(8,128)S(1)} collective-permute-done((s32[8,8]{1,0:T(8,128)}, s32[8,8]{1,0:T(8,128)S(1)}, u32[]{:S(2)}, u32[]{:S(2)}) %collective-permute-start.1) | collective-permute-done | bytes 288 | tf_op jit(solution)/shard_map/ppermute | solution.py:257
  5.2 0.0 collective-permute-done.2.other
  5.2 1.6 %copy-done.2 = bf16[1,1024,1024]{2,1,0:T(8,128)(2,1)S(1)} copy-done((bf16[1,1024,1024]{2,1,0:T(8,128)(2,1)S(1)}, bf16[1,1024,1024]{2,1,0:T(8,128)(2,1)}, u32[]{:S(2)}) %copy-start.2) | copy-done | bytes 2097176
  6.7 0.7 copy-done.17
  7.4 2.1 %shard_map.68 = (bf16[256,1024]{1,0:T(8,128)(2,1)}, bf16[256,1024]{1,0:T(8,128)(2,1)S(1)}, bf16[256,1024]{1,0:T(8,128)(2,1)S(1)}) custom-call(s32[8,8]{1,0:T(8,128)S(1)} %bitcast.18, s32[8,8]{1,0:T(8,128)S(1)} %collective-permute-done.1.other_pattern, bf16[1024,1024]{1,0:T(8,128)(2,1)S(1)} %bitcast.14, bf16[1024,1024]{1,0:T(8,128)(2,1)S(1)} %collective-permute-done.2.other, ...), custom_call_target="tpu_custom_call" | custom-call | flops 335544320 | bytes 3145728 | tf_op jit(solution)/shard_map/pallas_call | solution.py:83
  9.5 4.6 %collective-permute-start.3 = (bf16[256,1024]{1,0:T(8,128)(2,1)S(1)}, bf16[256,1024]{1,0:T(8,128)(2,1)S(1)}, u32[]{:S(2)}, u32[]{:S(2)}) collective-permute-start(bf16[256,1024]{1,0:T(8,128)(2,1)S(1)} %get-tuple-element.40.own), channel_id=1, source_target_pairs={{0,3},{2,1},{4,7},{6,5},{8,11},{10,9},{12,15},{14,13},{16,19},{18,... | collective-permute-start | bytes 1572872 | tf_op jit(solution)/shard_map/ppermute | solution.py:257
  14.1 2.1 %collective-permute-start.5 = (bf16[256,1024]{1,0:T(8,128)(2,1)}, bf16[256,1024]{1,0:T(8,128)(2,1)}, u32[]{:S(2)}, u32[]{:S(2)}) collective-permute-start(bf16[256,1024]{1,0:T(8,128)(2,1)} %get-tuple-element.46.own), channel_id=1, source_target_pairs={{0,3},{2,1},{4,7},{6,5},{8,11},{10,9},{12,15},{14,13},{16,19},{18,... | collective-permute-start | bytes 1572872 | tf_op jit(solution)/shard_map/ppermute | solution.py:257
  16.2 1.4 %shard_map.69 = (bf16[256,1024]{1,0:T(8,128)(2,1)S(1)}, bf16[256,1024]{1,0:T(8,128)(2,1)S(1)}) custom-call(s32[8,8]{1,0:T(8,128)S(1)} %bitcast.19, s32[8,8]{1,0:T(8,128)S(1)} %collective-permute-done.1.other_pattern, bf16[1024,1024]{1,0:T(8,128)(2,1)S(1)} %bitcast.15, bf16[1024,1024]{1,0:T(8,128)(2,1)S(1)} %collective-permute-done.2.other, ...), custom_call_target="tpu_custom_call" | custom-call | flops 335544320 | bytes 3145728 | tf_op jit(solution)/shard_map/pallas_call | solution.py:83
  17.6 3.1 %collective-permute-done.3.other = bf16[256,1024]{1,0:T(8,128)(2,1)S(1)} collective-permute-done((bf16[256,1024]{1,0:T(8,128)(2,1)S(1)}, bf16[256,1024]{1,0:T(8,128)(2,1)S(1)}, u32[]{:S(2)}, u32[]{:S(2)}) %collective-permute-start.3) | collective-permute-done | bytes 524320 | tf_op jit(solution)/shard_map/ppermute | solution.py:257
  20.7 1.3 %shard_map.70 = (bf16[256,1024]{1,0:T(8,128)(2,1)}, bf16[1024,1024]{1,0:T(8,128)(2,1)S(1)}, bf16[256,1024]{1,0:T(8,128)(2,1)S(1)}) custom-call(bf16[256,1024]{1,0:T(8,128)(2,1)S(1)} %get-tuple-element.40.own, bf16[256,1024]{1,0:T(8,128)(2,1)S(1)} %collective-permute-done.3.other, bf16[256,256]{1,0:T(8,128)(2,1)S(1)} %get-tuple-element.78.inverse, ...), custom_call_target="tpu_custom_call" | custom-call | tf_op jit(solution)/shard_map/pallas_call | solution.py:123
  22.0 3.8 %collective-permute-start.7 = (bf16[256,1024]{1,0:T(8,128)(2,1)}, bf16[256,1024]{1,0:T(8,128)(2,1)S(1)}, u32[]{:S(2)}, u32[]{:S(2)}) collective-permute-start(bf16[256,1024]{1,0:T(8,128)(2,1)} %get-tuple-element.43), channel_id=1, source_target_pairs={{5,0},{7,2},{13,8},{15,10},{21,16},{23,18},{29,24},{31,26},{0,3},{... | collective-permute-start | bytes 1572872 | tf_op jit(solution)/shard_map/ppermute | solution.py:257
  25.8 0.1 collective-permute-start
  25.9 1.1 %collective-permute-done = f32[4,1024]{1,0:T(4,128)S(1)} collective-permute-done((f32[4,1024]{1,0:T(4,128)S(1)}, f32[4,1024]{1,0:T(4,128)S(1)}, u32[]{:S(2)}, u32[]{:S(2)}) %collective-permute-start) | collective-permute-done | bytes 16416 | tf_op jit(solution)/shard_map/ppermute | solution.py:257
  27.1 0.7 collective-permute-start.4
  27.8 0.0 collective-permute-done.5.other
  27.8 1.0 %copy-done.13 = bf16[256,1024]{1,0:T(8,128)(2,1)S(1)} copy-done((bf16[256,1024]{1,0:T(8,128)(2,1)S(1)}, bf16[256,1024]{1,0:T(8,128)(2,1)}, u32[]{:S(2)}) %copy-start.13) | copy-done | bytes 524312
  28.8 1.8 %shard_map.71 = (bf16[256,1024]{1,0:T(8,128)(2,1)S(1)}, bf16[1024,1024]{1,0:T(8,128)(2,1)S(1)}) custom-call(bf16[256,1024]{1,0:T(8,128)(2,1)} %get-tuple-element.46.own, bf16[256,1024]{1,0:T(8,128)(2,1)} %collective-permute-done.5.other, bf16[256,256]{1,0:T(8,128)(2,1)S(1)} %get-tuple-element.78.inverse, ...), custom_call_target="tpu_custom_call", output_to_operand_aliasing={{1}: (5, {})} | custom-call | tf_op jit(solution)/shard_map/pallas_call | solution.py:123
  30.6 4.6 %collective-permute-start.6 = (bf16[256,1024]{1,0:T(8,128)(2,1)S(1)}, bf16[256,1024]{1,0:T(8,128)(2,1)S(1)}, u32[]{:S(2)}, u32[]{:S(2)}) collective-permute-start(bf16[256,1024]{1,0:T(8,128)(2,1)S(1)} %get-tuple-element.49), channel_id=1, source_target_pairs={{5,0},{7,2},{13,8},{15,10},{21,16},{23,18},{29,24},{31,26},{0,3},{... | collective-permute-start | bytes 1572872 | tf_op jit(solution)/shard_map/ppermute | solution.py:257
  35.2 0.0 collective-permute-done.4.refs_3_
  35.2 0.0 collective-permute-done.7.other.refs_5_.refs_3_.refs_2_
  35.3 1.0 %copy-done.10 = bf16[256,1024]{1,0:T(8,128)(2,1)S(1)} copy-done((bf16[256,1024]{1,0:T(8,128)(2,1)S(1)}, bf16[256,1024]{1,0:T(8,128)(2,1)}, u32[]{:S(2)}) %copy-start.10) | copy-done | bytes 524312
  36.3 0.4 shard_map.72
  36.8 1.3 %collective-permute-start.8 = (bf16[256,1024]{1,0:T(8,128)(2,1)S(1)}, bf16[256,1024]{1,0:T(8,128)(2,1)S(1)}, u32[]{:S(2)}, u32[]{:S(2)}) collective-permute-start(bf16[256,1024]{1,0:T(8,128)(2,1)S(1)} %get-tuple-element.52), channel_id=1, source_target_pairs={{5,0},{7,2},{13,8},{15,10},{21,16},{23,18},{29,24},{31,26}} | collective-permute-start | bytes 1572872 | tf_op jit(solution)/shard_map/ppermute | solution.py:257
  38.1 3.8 %collective-permute-done.6.other.refs_4_.refs_2_.refs_1_ = bf16[256,1024]{1,0:T(8,128)(2,1)S(1)} collective-permute-done((bf16[256,1024]{1,0:T(8,128)(2,1)S(1)}, bf16[256,1024]{1,0:T(8,128)(2,1)S(1)}, u32[]{:S(2)}, u32[]{:S(2)}) %collective-permute-start.6) | collective-permute-done | bytes 524320 | tf_op jit(solution)/shard_map/ppermute | solution.py:257
  41.9 5.3 %collective-permute-done.8.refs_6_.refs_4_.refs_3_ = bf16[256,1024]{1,0:T(8,128)(2,1)S(1)} collective-permute-done((bf16[256,1024]{1,0:T(8,128)(2,1)S(1)}, bf16[256,1024]{1,0:T(8,128)(2,1)S(1)}, u32[]{:S(2)}, u32[]{:S(2)}) %collective-permute-start.8) | collective-permute-done | bytes 524320 | tf_op jit(solution)/shard_map/ppermute | solution.py:257
  47.3 0.4 shard_map.73
  47.7 0.0 copy-start
  47.7 1.3 %copy-done = bf16[1024,1024]{1,0:T(8,128)(2,1)} copy-done((bf16[1024,1024]{1,0:T(8,128)(2,1)}, bf16[1024,1024]{1,0:T(8,128)(2,1)S(1)}, u32[]{:S(2)}) %copy-start) | copy-done | bytes 2097176
  49.0 1.3 %collective-permute-start.10 = (bf16[1024,1024]{1,0:T(8,128)(2,1)}, bf16[1024,1024]{1,0:T(8,128)(2,1)S(1)}, u32[]{:S(2)}, u32[]{:S(2)}) collective-permute-start(bf16[1024,1024]{1,0:T(8,128)(2,1)} %copy-done), channel_id=1, source_target_pairs={{1,0},{3,2},{5,4},{7,6},{9,8},{11,10},{13,12},{15,14},{17,16},{19,... | collective-permute-start | bytes 6291464 | tf_op jit(solution)/shard_map/ppermute | solution.py:257
  50.3 1.3 %collective-permute-start.11 = (bf16[256,1024]{1,0:T(8,128)(2,1)S(1)}, bf16[256,1024]{1,0:T(8,128)(2,1)S(1)}, u32[]{:S(2)}, u32[]{:S(2)}) collective-permute-start(bf16[256,1024]{1,0:T(8,128)(2,1)S(1)} %get-tuple-element.58), channel_id=1, source_target_pairs={{5,0},{7,2},{13,8},{15,10},{21,16},{23,18},{29,24},{31,26}} | collective-permute-start | bytes 1572872 | tf_op jit(solution)/shard_map/ppermute | solution.py:257
  51.6 0.7 collective-permute-start.9
  52.3 0.0 collective-permute-done.9.refs_0_
  52.3 8.5 %collective-permute-done.11.refs_7_.refs_5_.refs_4_ = bf16[256,1024]{1,0:T(8,128)(2,1)S(1)} collective-permute-done((bf16[256,1024]{1,0:T(8,128)(2,1)S(1)}, bf16[256,1024]{1,0:T(8,128)(2,1)S(1)}, u32[]{:S(2)}, u32[]{:S(2)}) %collective-permute-start.11) | collective-permute-done | bytes 524320 | tf_op jit(solution)/shard_map/ppermute | solution.py:257
  60.8 0.0 collective-permute-done.10.refs_2_.refs_7_
  60.8 0.8 copy-done.6
  61.6 0.7 collective-permute-start.12
  62.3 0.0 collective-permute-done.12.refs_0_
  62.3 1.0 %copy-done.4 = bf16[256,1024]{1,0:T(8,128)(2,1)S(1)} copy-done((bf16[256,1024]{1,0:T(8,128)(2,1)S(1)}, bf16[256,1024]{1,0:T(8,128)(2,1)}, u32[]{:S(2)}) %copy-start.4) | copy-done | bytes 524312
  63.3 1.0 %copy-done.7 = bf16[256,1024]{1,0:T(8,128)(2,1)S(1)} copy-done((bf16[256,1024]{1,0:T(8,128)(2,1)S(1)}, bf16[256,1024]{1,0:T(8,128)(2,1)}, u32[]{:S(2)}) %copy-start.7) | copy-done | bytes 524312
  64.4 0.8 collective-permute-start.13
  65.2 0.0 copy-start.1
  65.2 1.4 %collective-permute-start.18 = (f32[8,1024]{1,0:T(8,128)S(1)}, f32[8,1024]{1,0:T(8,128)S(1)}, u32[]{:S(2)}, u32[]{:S(2)}) collective-permute-start(f32[8,1024]{1,0:T(8,128)S(1)} %get-tuple-element.71), channel_id=1, source_target_pairs={{5,0},{7,2}} | collective-permute-start | bytes 98312 | tf_op jit(solution)/shard_map/ppermute | solution.py:257
  66.6 0.0 collective-permute-done.13.refs_0_
  66.7 0.6 shard_map.77
  67.3 0.7 collective-permute-start.14
  68.0 0.2 broadcast_select_fusion.refs_0_
  68.2 0.0 copy-start.11
  68.2 0.0 collective-permute-done.14.refs_0_
  68.2 0.7 collective-permute-start.15
  68.9 1.7 %collective-permute-done.18 = f32[8,1024]{1,0:T(8,128)S(1)} collective-permute-done((f32[8,1024]{1,0:T(8,128)S(1)}, f32[8,1024]{1,0:T(8,128)S(1)}, u32[]{:S(2)}, u32[]{:S(2)}) %collective-permute-start.18) | collective-permute-done | bytes 32800 | tf_op jit(solution)/shard_map/ppermute | solution.py:257
  70.6 0.0 collective-permute-done.15.refs_0_
  70.6 1.3 %collective-permute-start.16 = (bf16[8,1024]{1,0:T(8,128)(2,1)S(1)}, bf16[8,1024]{1,0:T(8,128)(2,1)S(1)}, u32[]{:S(2)}, u32[]{:S(2)}) collective-permute-start(bf16[8,1024]{1,0:T(8,128)(2,1)S(1)} %get-tuple-element.69), channel_id=1, source_target_pairs={{8,0},{10,2}} | collective-permute-start | bytes 49160 | tf_op jit(solution)/shard_map/ppermute | solution.py:257
  71.9 0.7 collective-permute-start.17
  72.6 0.7 collective-permute-start.19
  73.3 18.3 %collective-permute-done.16.from_pair = bf16[8,1024]{1,0:T(8,128)(2,1)S(1)} collective-permute-done((bf16[8,1024]{1,0:T(8,128)(2,1)S(1)}, bf16[8,1024]{1,0:T(8,128)(2,1)S(1)}, u32[]{:S(2)}, u32[]{:S(2)}) %collective-permute-start.16) | collective-permute-done | bytes 16416 | tf_op jit(solution)/shard_map/ppermute | solution.py:257
  91.5 0.0 collective-permute-done.17.from_own
  91.6 0.9 shard_map.80
  92.5 0.0 collective-permute-done.19
  92.5 1.3 %collective-permute-start.20 = (f32[4,1024]{1,0:T(4,128)S(1)}, f32[4,1024]{1,0:T(4,128)S(1)}, u32[]{:S(2)}, u32[]{:S(2)}) collective-permute-start(f32[4,1024]{1,0:T(4,128)S(1)} %slice_select_fusion), channel_id=1, source_target_pairs={{5,4},{7,6},{0,1},{2,3},{8,9},{10,11},{12,13},{14,15},{16,17},{18,... | collective-permute-start | bytes 49160 | tf_op jit(solution)/shard_map/ppermute | solution.py:257
  93.8 0.8 collective-permute-done.20
  94.7 0.6 select_bitcast_fusion
  (43 shorter events, 0.2 us)
Async XLA Ops:
  0.6 4.5 %collective-permute-start.2 = (bf16[1024,1024]{1,0:T(8,128)(2,1)}, bf16[1024,1024]{1,0:T(8,128)(2,1)S(1)}, u32[]{:S(2)}, u32[]{:S(2)}) collective-permute-start(bf16[1024,1024]{1,0:T(8,128)(2,1)} %bitcast.13), channel_id=1, source_target_pairs={{0,1},{1,0},{2,3},{3,2},{4,5},{5,4},{6,7},{7,6},{8,9},{9,8},{10,11... | collective-permute-start | bytes 6291464 | tf_op jit(solution)/shard_map/ppermute | solution.py:257
  1.1 4.0 %collective-permute-start.1 = (s32[8,8]{1,0:T(8,128)}, s32[8,8]{1,0:T(8,128)S(1)}, u32[]{:S(2)}, u32[]{:S(2)}) collective-permute-start(s32[8,8]{1,0:T(8,128)} %bitcast.17), channel_id=1, source_target_pairs={{0,1},{1,0},{2,3},{3,2},{4,5},{5,4},{6,7},{7,6},{8,9},{9,8},{10,11... | collective-permute-start | bytes 776 | tf_op jit(solution)/shard_map/ppermute | solution.py:257
  5.2 1.6 %copy-start.2 = (bf16[1,1024,1024]{2,1,0:T(8,128)(2,1)S(1)}, bf16[1,1024,1024]{2,1,0:T(8,128)(2,1)}, u32[]{:S(2)}) copy-start(bf16[1,1024,1024]{2,1,0:T(8,128)(2,1)} %param.5) | copy-start | bytes 6291460
  6.7 0.7 copy-start.17
  9.5 11.2 %collective-permute-start.3 = (bf16[256,1024]{1,0:T(8,128)(2,1)S(1)}, bf16[256,1024]{1,0:T(8,128)(2,1)S(1)}, u32[]{:S(2)}, u32[]{:S(2)}) collective-permute-start(bf16[256,1024]{1,0:T(8,128)(2,1)S(1)} %get-tuple-element.40.own), channel_id=1, source_target_pairs={{0,3},{2,1},{4,7},{6,5},{8,11},{10,9},{12,15},{14,13},{16,19},{18,... | collective-permute-start | bytes 1572872 | tf_op jit(solution)/shard_map/ppermute | solution.py:257
  14.1 13.7 %collective-permute-start.5 = (bf16[256,1024]{1,0:T(8,128)(2,1)}, bf16[256,1024]{1,0:T(8,128)(2,1)}, u32[]{:S(2)}, u32[]{:S(2)}) collective-permute-start(bf16[256,1024]{1,0:T(8,128)(2,1)} %get-tuple-element.46.own), channel_id=1, source_target_pairs={{0,3},{2,1},{4,7},{6,5},{8,11},{10,9},{12,15},{14,13},{16,19},{18,... | collective-permute-start | bytes 1572872 | tf_op jit(solution)/shard_map/ppermute | solution.py:257
  16.2 9.6 %copy-start.18 = (f32[1,4,1024]{2,1,0:T(4,128)S(1)}, f32[1,4,1024]{2,1,0:T(4,128)}, u32[]{:S(2)}) copy-start(f32[1,4,1024]{2,1,0:T(4,128)} %param.9) | copy-start | bytes 49156
  16.2 9.7 %copy-start.19 = (s32[1,1024]{1,0:T(1,128)S(1)}, s32[1,1024]{1,0:T(1,128)}, u32[]{:S(2)}) copy-start(s32[1,1024]{1,0:T(1,128)} %param.8) | copy-start | bytes 12292
  17.6 4.4 %copy-start.12 = (bf16[256,1024]{1,0:T(8,128)(2,1)}, bf16[256,1024]{1,0:T(8,128)(2,1)S(1)}, u32[]{:S(2)}) copy-start(bf16[256,1024]{1,0:T(8,128)(2,1)S(1)} %get-tuple-element.45.refs_0_.own) | copy-start | bytes 1572868
  17.6 4.4 %copy-start.15 = (bf16[256,1024]{1,0:T(8,128)(2,1)}, bf16[256,1024]{1,0:T(8,128)(2,1)S(1)}, u32[]{:S(2)}) copy-start(bf16[256,1024]{1,0:T(8,128)(2,1)S(1)} %get-tuple-element.42.refs_0_.own) | copy-start | bytes 1572868
  22.0 8.6 %copy-start.9 = (bf16[256,1024]{1,0:T(8,128)(2,1)}, bf16[256,1024]{1,0:T(8,128)(2,1)S(1)}, u32[]{:S(2)}) copy-start(bf16[256,1024]{1,0:T(8,128)(2,1)S(1)} %get-tuple-element.47.refs_1_.refs_0_) | copy-start | bytes 1572868
  22.0 13.2 %collective-permute-start.7 = (bf16[256,1024]{1,0:T(8,128)(2,1)}, bf16[256,1024]{1,0:T(8,128)(2,1)S(1)}, u32[]{:S(2)}, u32[]{:S(2)}) collective-permute-start(bf16[256,1024]{1,0:T(8,128)(2,1)} %get-tuple-element.43), channel_id=1, source_target_pairs={{5,0},{7,2},{13,8},{15,10},{21,16},{23,18},{29,24},{31,26},{0,3},{... | collective-permute-start | bytes 1572872 | tf_op jit(solution)/shard_map/ppermute | solution.py:257
  25.8 1.2 %collective-permute-start = (f32[4,1024]{1,0:T(4,128)S(1)}, f32[4,1024]{1,0:T(4,128)S(1)}, u32[]{:S(2)}, u32[]{:S(2)}) collective-permute-start(f32[4,1024]{1,0:T(4,128)S(1)} %bitcast.20), channel_id=1, source_target_pairs={{0,1},{1,0},{2,3},{3,2},{4,5},{5,4},{6,7},{7,6},{8,9},{9,8},{10,11... | collective-permute-start | bytes 49160 | tf_op jit(solution)/shard_map/ppermute | solution.py:257
  27.1 8.1 %collective-permute-start.4 = (f32[9,1024]{1,0:T(8,128)S(1)}, f32[9,1024]{1,0:T(8,128)S(1)}, u32[]{:S(2)}, u32[]{:S(2)}) collective-permute-start(f32[9,1024]{1,0:T(8,128)S(1)} %pad_maximum_fusion.refs_1_), channel_id=1, source_target_pairs={{12,8},{14,10},{20,16},{22,18},{28,24},{30,26},{1,5},{3,7}} | collective-permute-start | bytes 110600 | tf_op jit(solution)/shard_map/ppermute | solution.py:257
  27.8 1.0 %copy-start.13 = (bf16[256,1024]{1,0:T(8,128)(2,1)S(1)}, bf16[256,1024]{1,0:T(8,128)(2,1)}, u32[]{:S(2)}) copy-start(bf16[256,1024]{1,0:T(8,128)(2,1)} %copy-done.12) | copy-start | bytes 1572868
  28.8 6.4 %copy-start.16 = (bf16[256,1024]{1,0:T(8,128)(2,1)S(1)}, bf16[256,1024]{1,0:T(8,128)(2,1)}, u32[]{:S(2)}) copy-start(bf16[256,1024]{1,0:T(8,128)(2,1)} %copy-done.15) | copy-start | bytes 1572868
  28.8 18.4 %copy-start.14 = (bf16[256,1024]{1,0:T(8,128)(2,1)S(1)}, bf16[256,1024]{1,0:T(8,128)(2,1)}, u32[]{:S(2)}) copy-start(bf16[256,1024]{1,0:T(8,128)(2,1)} %copy-done.12) | copy-start | bytes 1572868
  30.6 11.3 %collective-permute-start.6 = (bf16[256,1024]{1,0:T(8,128)(2,1)S(1)}, bf16[256,1024]{1,0:T(8,128)(2,1)S(1)}, u32[]{:S(2)}, u32[]{:S(2)}) collective-permute-start(bf16[256,1024]{1,0:T(8,128)(2,1)S(1)} %get-tuple-element.49), channel_id=1, source_target_pairs={{5,0},{7,2},{13,8},{15,10},{21,16},{23,18},{29,24},{31,26},{0,3},{... | collective-permute-start | bytes 1572872 | tf_op jit(solution)/shard_map/ppermute | solution.py:257
  35.3 1.0 %copy-start.10 = (bf16[256,1024]{1,0:T(8,128)(2,1)S(1)}, bf16[256,1024]{1,0:T(8,128)(2,1)}, u32[]{:S(2)}) copy-start(bf16[256,1024]{1,0:T(8,128)(2,1)} %copy-done.9) | copy-start | bytes 1572868
  36.8 10.5 %collective-permute-start.8 = (bf16[256,1024]{1,0:T(8,128)(2,1)S(1)}, bf16[256,1024]{1,0:T(8,128)(2,1)S(1)}, u32[]{:S(2)}, u32[]{:S(2)}) collective-permute-start(bf16[256,1024]{1,0:T(8,128)(2,1)S(1)} %get-tuple-element.52), channel_id=1, source_target_pairs={{5,0},{7,2},{13,8},{15,10},{21,16},{23,18},{29,24},{31,26}} | collective-permute-start | bytes 1572872 | tf_op jit(solution)/shard_map/ppermute | solution.py:257
  47.3 13.6 %copy-start.3 = (bf16[256,1024]{1,0:T(8,128)(2,1)}, bf16[256,1024]{1,0:T(8,128)(2,1)S(1)}, u32[]{:S(2)}) copy-start(bf16[256,1024]{1,0:T(8,128)(2,1)S(1)} %collective-permute-done.8.refs_6_.refs_4_.refs_3_) | copy-start | bytes 1572868
  47.7 1.3 %copy-start = (bf16[1024,1024]{1,0:T(8,128)(2,1)}, bf16[1024,1024]{1,0:T(8,128)(2,1)S(1)}, u32[]{:S(2)}) copy-start(bf16[1024,1024]{1,0:T(8,128)(2,1)S(1)} %get-tuple-element.57.refs_2_) | copy-start | bytes 6291460
  49.0 11.8 %collective-permute-start.10 = (bf16[1024,1024]{1,0:T(8,128)(2,1)}, bf16[1024,1024]{1,0:T(8,128)(2,1)S(1)}, u32[]{:S(2)}, u32[]{:S(2)}) collective-permute-start(bf16[1024,1024]{1,0:T(8,128)(2,1)} %copy-done), channel_id=1, source_target_pairs={{1,0},{3,2},{5,4},{7,6},{9,8},{11,10},{13,12},{15,14},{17,16},{19,... | collective-permute-start | bytes 6291464 | tf_op jit(solution)/shard_map/ppermute | solution.py:257
  50.3 10.5 %collective-permute-start.11 = (bf16[256,1024]{1,0:T(8,128)(2,1)S(1)}, bf16[256,1024]{1,0:T(8,128)(2,1)S(1)}, u32[]{:S(2)}, u32[]{:S(2)}) collective-permute-start(bf16[256,1024]{1,0:T(8,128)(2,1)S(1)} %get-tuple-element.58), channel_id=1, source_target_pairs={{5,0},{7,2},{13,8},{15,10},{21,16},{23,18},{29,24},{31,26}} | collective-permute-start | bytes 1572872 | tf_op jit(solution)/shard_map/ppermute | solution.py:257
  51.6 0.7 collective-permute-start.9
  60.8 0.8 copy-start.6
  61.6 0.7 collective-permute-start.12
  62.3 1.0 %copy-start.4 = (bf16[256,1024]{1,0:T(8,128)(2,1)S(1)}, bf16[256,1024]{1,0:T(8,128)(2,1)}, u32[]{:S(2)}) copy-start(bf16[256,1024]{1,0:T(8,128)(2,1)} %copy-done.3) | copy-start | bytes 1572868
  63.3 1.0 %copy-start.7 = (bf16[256,1024]{1,0:T(8,128)(2,1)S(1)}, bf16[256,1024]{1,0:T(8,128)(2,1)}, u32[]{:S(2)}) copy-start(bf16[256,1024]{1,0:T(8,128)(2,1)} %copy-done.6) | copy-start | bytes 1572868
  64.4 2.3 %copy-start.5 = (bf16[256,1024]{1,0:T(8,128)(2,1)S(1)}, bf16[256,1024]{1,0:T(8,128)(2,1)}, u32[]{:S(2)}) copy-start(bf16[256,1024]{1,0:T(8,128)(2,1)} %copy-done.3) | copy-start | bytes 1572868
  64.4 2.3 %copy-start.8 = (bf16[256,1024]{1,0:T(8,128)(2,1)S(1)}, bf16[256,1024]{1,0:T(8,128)(2,1)}, u32[]{:S(2)}) copy-start(bf16[256,1024]{1,0:T(8,128)(2,1)} %copy-done.6) | copy-start | bytes 1572868
  64.4 2.3 %collective-permute-start.13 = (bf16[8,1024]{1,0:T(8,128)(2,1)S(1)}, bf16[8,1024]{1,0:T(8,128)(2,1)S(1)}, u32[]{:S(2)}, u32[]{:S(2)}) collective-permute-start(bf16[8,1024]{1,0:T(8,128)(2,1)S(1)} %get-tuple-element.60), channel_id=1, source_target_pairs={{16,24},{18,26}} | collective-permute-start | bytes 49160 | tf_op jit(solution)/shard_map/ppermute | solution.py:257
  65.2 2.8 %copy-start.1 = (bf16[1024,1024]{1,0:T(8,128)(2,1)S(1)}, bf16[1024,1024]{1,0:T(8,128)(2,1)}, u32[]{:S(2)}) copy-start(bf16[1024,1024]{1,0:T(8,128)(2,1)} %copy-done) | copy-start | bytes 6291460
  65.2 5.4 %collective-permute-start.18 = (f32[8,1024]{1,0:T(8,128)S(1)}, f32[8,1024]{1,0:T(8,128)S(1)}, u32[]{:S(2)}, u32[]{:S(2)}) collective-permute-start(f32[8,1024]{1,0:T(8,128)S(1)} %get-tuple-element.71), channel_id=1, source_target_pairs={{5,0},{7,2}} | collective-permute-start | bytes 98312 | tf_op jit(solution)/shard_map/ppermute | solution.py:257
  67.3 0.9 collective-permute-start.14
  68.2 23.4 %copy-start.11 = (bf16[1024,1024]{1,0:T(8,128)(2,1)}, bf16[1024,1024]{1,0:T(8,128)(2,1)S(1)}, u32[]{:S(2)}) copy-start(bf16[1024,1024]{1,0:T(8,128)(2,1)S(1)} %broadcast_select_fusion.refs_0_) | copy-start | bytes 6291460
  68.2 2.3 %collective-permute-start.15 = (bf16[8,1024]{1,0:T(8,128)(2,1)S(1)}, bf16[8,1024]{1,0:T(8,128)(2,1)S(1)}, u32[]{:S(2)}, u32[]{:S(2)}) collective-permute-start(bf16[8,1024]{1,0:T(8,128)(2,1)S(1)} %get-tuple-element.66), channel_id=1, source_target_pairs={{16,8},{18,10}} | collective-permute-start | bytes 49160 | tf_op jit(solution)/shard_map/ppermute | solution.py:257
  70.6 20.9 %collective-permute-start.16 = (bf16[8,1024]{1,0:T(8,128)(2,1)S(1)}, bf16[8,1024]{1,0:T(8,128)(2,1)S(1)}, u32[]{:S(2)}, u32[]{:S(2)}) collective-permute-start(bf16[8,1024]{1,0:T(8,128)(2,1)S(1)} %get-tuple-element.69), channel_id=1, source_target_pairs={{8,0},{10,2}} | collective-permute-start | bytes 49160 | tf_op jit(solution)/shard_map/ppermute | solution.py:257
  71.9 19.6 %collective-permute-start.17 = (bf16[8,1024]{1,0:T(8,128)(2,1)S(1)}, bf16[8,1024]{1,0:T(8,128)(2,1)S(1)}, u32[]{:S(2)}, u32[]{:S(2)}) collective-permute-start(bf16[8,1024]{1,0:T(8,128)(2,1)S(1)} %get-tuple-element.69), channel_id=1, source_target_pairs={{8,5},{10,7}} | collective-permute-start | bytes 49160 | tf_op jit(solution)/shard_map/ppermute | solution.py:257
  72.6 19.9 %collective-permute-start.19 = (f32[8,1024]{1,0:T(8,128)S(1)}, f32[8,1024]{1,0:T(8,128)S(1)}, u32[]{:S(2)}, u32[]{:S(2)}) collective-permute-start(f32[8,1024]{1,0:T(8,128)S(1)} %select_select_fusion), channel_id=1, source_target_pairs={{8,12},{10,14},{16,20},{18,22},{24,28},{26,30}} | collective-permute-start | bytes 98312 | tf_op jit(solution)/shard_map/ppermute | solution.py:257
  92.5 2.1 %collective-permute-start.20 = (f32[4,1024]{1,0:T(4,128)S(1)}, f32[4,1024]{1,0:T(4,128)S(1)}, u32[]{:S(2)}, u32[]{:S(2)}) collective-permute-start(f32[4,1024]{1,0:T(4,128)S(1)} %slice_select_fusion), channel_id=1, source_target_pairs={{5,4},{7,6},{0,1},{2,3},{8,9},{10,11},{12,13},{14,15},{16,17},{18,... | collective-permute-start | bytes 49160 | tf_op jit(solution)/shard_map/ppermute | solution.py:257

commit v10 on v5

--- a/solution.py
+++ b/solution.py
@@ -104,7 +104,7 @@
     )(other_pattern, own, other, inverse, *extra)
 
 
-def combine_kernel(face_at, is_face, with_next, whole_rows, is_second, own, other, inverse, *refs):
+def combine_kernel(face_at, is_face, with_next, whole_rows, own, other, inverse, *refs):
     refs = list(refs)
     following = refs.pop(0) if with_next else None
     joined = 0.5 * (own[...].astype(jnp.float32) + other[...].astype(jnp.float32))
@@ -120,16 +120,16 @@
     refs[0][...] = piece
     if with_next:
 
-        @pl.when(is_second[0] == 0)
+        @pl.when(lax.axis_index("box") % 2 == 0)
         def _():
             refs[0][...] = following[...]
 
 
-def combine(is_second, own, other, inverse, following, state, face_at, row_at):
+def combine(own, other, inverse, following, state, face_at, row_at):
     is_face = state is None
     rows, width = own.shape
     extra = [] if following is None else [following]
-    aliases = {} if is_face else {4 + len(extra) + 1: 1}
+    aliases = {} if is_face else {3 + len(extra) + 1: 1}
     extra += [] if is_face else list(state)
     piece = jax.ShapeDtypeStruct((rows, width), jnp.bfloat16)
     whole = jax.ShapeDtypeStruct((width, width), jnp.bfloat16)
@@ -142,12 +142,12 @@
             slice(row_at, row_at + rows),
         ),
         out_shape=[piece, whole] + ([piece] if is_face else []),
-        in_specs=[SMEM] + [VMEM] * (3 + len(extra)),
+        in_specs=[VMEM] * (3 + len(extra)),
         out_specs=[VMEM] * (3 if is_face else 2),
         input_output_aliases=aliases,
         compiler_params=PARAMS,
         cost_estimate=cost(0, 0),
-    )(is_second, own, other, inverse, *extra)
+    )(own, other, inverse, *extra)
     return result[0], ((result[2] if is_face else state[0]), result[1])
 
 
@@ -180,7 +180,13 @@
     return jnp.concatenate(outs, axis=1)
 
 
-def segment_kernel(coupling, pieces_of, down_steps, up_steps, *refs):
+def segment_kernel(coupling, at, pieces_of, down_steps, up_steps, *refs):
+    @pl.when(lax.axis_index("layer") == at)
+    def _():
+        run_segment(coupling, pieces_of, down_steps, up_steps, *refs)
+
+
+def run_segment(coupling, pieces_of, down_steps, up_steps, *refs):
     refs = list(refs)
     state = refs.pop(0)[...]
     maps, downs = {}, {}
@@ -205,7 +211,7 @@
     refs.pop(0)[...] = state
 
 
-def segment(coupling, arrived, packed, downs, maps, down_steps, up_steps):
+def segment(coupling, at, arrived, packed, downs, maps, down_steps, up_steps):
     operands = [arrived]
     for slot in down_steps:
         operands += [packed[slot], *maps[slot]]
@@ -216,7 +222,7 @@
     steps = len(down_steps) + len(up_steps)
     results = pl.pallas_call(
         functools.partial(
-            segment_kernel, coupling, [len(entry) for entry in maps], down_steps, up_steps
+            segment_kernel, coupling, at, [len(entry) for entry in maps], down_steps, up_steps
         ),
         out_shape=[rows] * steps + [jax.ShapeDtypeStruct(arrived.shape, jnp.bfloat16)],
         in_specs=[VMEM] * len(operands),
@@ -246,7 +252,6 @@
     position = lax.axis_index("box")
     layer = lax.axis_index("layer")
     is_second = position % 2 == 1
-    second_flag = is_second.astype(jnp.int32)[None]
 
     chain = [(layer_at, (OWN, PAIR)) for layer_at in range(2, layers, 2)]
     pair_moves = [(layer_at + 1, layer_at) for layer_at in range(0, layers, 2)]
@@ -321,7 +326,6 @@
             renewed = {}
             for piece in order:
                 renewed[piece], state = combine(
-                    second_flag,
                     current[piece],
                     received[piece],
                     inverse,
@@ -345,7 +349,6 @@
             if k > AHEAD:
                 other = after(other, pair_pieces[order[k - 1]])
             payload, state = combine(
-                second_flag,
                 current[piece],
                 other,
                 inverse,
@@ -366,7 +369,7 @@
 
     first = pair_packed[:rows].astype(jnp.bfloat16)
     (down_odd,), state = segment(
-        coupling, first, small, {}, [[merged], pair_maps], (OWN,), ()
+        coupling, 1, first, small, {}, [[merged], pair_maps], (OWN,), ()
     )
     merged_first = send(after(merged, state), route(every, 1, 0))
     maps = [[merged_first], pair_maps]
@@ -379,16 +382,17 @@
         turn = k == len(chain) - 1
         back = tuple(reversed(slots))
         results, state = segment(
-            coupling, arrived, small, {}, maps, slots, back[1:] if turn else ()
+            coupling, at, arrived, small, {}, maps, slots, back[1:] if turn else ()
         )
         kept.append(dict(zip(slots, results)))
         if k == 0:
-            down_odd_first = send(after(down_odd, state), route([(1, 0)], 1, 0))
+            down_odd_pair = send(after(down_odd, state), route([(1, 0)], 1, 0))
+            down_odd_first = send(after(down_odd, state), route([(1, 1)], 1, 0))
         if turn:
             ups[at] = dict(zip(back[1:], results[len(slots) :]))
             ups[at][back[0]] = results[len(slots) - 1]
     merged = jnp.where(is_second, merged, merged_first)
-    down_odd = jnp.where(layer == 0, down_odd_first, down_odd)
+    down_odd = down_odd_pair + down_odd_first
 
     for k in reversed(range(len(chain) - 1)):
         target, slots = chain[k]
@@ -397,9 +401,9 @@
             arrived, merged = lax.optimization_barrier((arrived, merged))
         at = target
         back = tuple(reversed(slots))
-        results, state = segment(coupling, arrived, small, kept[k], maps, (), back)
+        results, state = segment(coupling, at, arrived, small, kept[k], maps, (), back)
         ups[at] = dict(zip(back, results))
-    from_own = send(state, route([(at, 1)], 0, 1))
+    from_own = send(state, route([(at, 1)]))
     from_pair = send(state, route([(at, 0)]))
 
     mine = [jnp.zeros((rows, width), jnp.float32)] * 2
@@ -416,16 +420,11 @@
         out_specs=VMEM,
         compiler_params=SWEEP_PARAMS,
         cost_estimate=cost(6 * 256 * 1024 * 1024, 6 * 1024 * 1024),
-    )(odd, from_pair, from_own, packed[:rows], down_odd, merged, *pair_maps)
+    )(odd, from_pair, from_own, packed[:rows], down_odd, merged_first, *pair_maps)
     upward = jnp.where(layer < 2, last, settled)
-    ends = upward[:rows_here], upward[rows_here : 2 * rows_here]
-    there = send(
-        jnp.where(is_second, ends[0], ends[1]),
-        route([(1, 1)], 1, 0) + route([move for move in every if move[0] != 1], 0, 1),
-    )
-    here = jnp.where(is_second, ends[1], ends[0])
-    runs = jnp.logical_xor(is_second, layer != 1)
-    return (merged[None], jnp.where(runs, here, there)[None])
+    second_rows = send(upward[rows_here : 2 * rows_here], route(every, 0, 1))
+    upward = jnp.where(is_second, second_rows, upward[:rows_here])
+    return (merged[None], upward[None])
 
 
 def solution(mesh):

time: 94.2 us -> 93.5 us (level)
  Pallas kernels: 16.5 us -> 9.63 us
  waiting for transfers between devices: 38.5 us -> 40.9 us
  local copies, waits for them, and re-layouts: 7.43 us -> 8.93 us
  other arithmetic: 0.91 us -> 2.22 us
    pallas_call x6, Pallas kernels: 6.86 us -> 0.67 us  [segment(): pl.pallas_call(functools.partial(segment_kernel, coupling, at, [len(entry...]
    ppermute x21 -> x22, waiting for transfers between devices: 38.5 us -> 40.9 us  [send(): return lax.ppermute(value, AXES, pairs_of_devices)]
    pallas_call x2, Pallas kernels: 4.71 us -> 3.17 us  [leaf_combine(): pl.pallas_call(functools.partial(leaf_kernel, half * rows, is_face, piece...]
    unnamed x30 -> x38, local copies, waits for them, and re-layouts: 6.36 us -> 7.86 us
    select_n x1, other arithmetic: 0.22 us -> 1.54 us  [on_device(): merged = jnp.where(is_second, merged, merged_first)]
    ppermute x21 -> x22, starting transfers between devices: 29 us -> 29.6 us  [send(): return lax.ppermute(value, AXES, pairs_of_devices)]
  transfers between devices with their start and end apart: 21 -> 22, of which waited for: 7 -> 7; matrix products, arithmetic and copies ran while one was open for 1% -> 3% of each run, Pallas kernels for 10% -> 8%
where the time goes in v10:
time: 93.5 us; the launch traced here: 92.5 us
  waiting for transfers between devices  40.9 us (44%)
  starting transfers between devices  29.6 us (32%)
  Pallas kernels  9.63 us (10%)
  local copies, waits for them, and re-layouts  8.93 us (10%)
  other arithmetic  2.22 us (2%)
  between operations  1.16 us (1%)
    ppermute x22, waiting for transfers between devices, send(): return lax.ppermute(value, AXES, pairs_of_devices)  40.9 us
    ppermute x22, starting transfers between devices, send(): return lax.ppermute(value, AXES, pairs_of_devices)  29.6 us
    unnamed x38, local copies, waits for them, and re-layouts  7.86 us
    pallas_call x4, Pallas kernels, combine(): pl.pallas_call(functools.partial(combine_kernel, face_at, is_face, follow...  3.9 us
    pallas_call x2, Pallas kernels, leaf_combine(): pl.pallas_call(functools.partial(leaf_kernel, half * rows, is_face, piece...  3.17 us
  transfers between devices with their start and end apart: 22, of which 7 were waited for; matrix products, arithmetic and copies ran while one was open for 3% of the time, Pallas kernels for 8%

profile of v10, /device:TPU:0, one launch (start us, length us, event | category | flops | bytes accessed | tf_op | source)
XLA Modules:
  0.0 92.5 jit_solution(5345463413652894925)
XLA Ops:
  0.6 0.5 collective-permute-start.2
  1.1 0.1 collective-permute-start.1
  1.2 1.1 %fusion.1 = (bf16[256,256]{1,0:T(8,128)(2,1)S(1)}, bf16[256,256]{1,0:T(8,128)(2,1)S(1)}) fusion(f32[1,3,256,256]{3,2,1,0:T(8,128)} %param.7, s32[]{:T(128)S(6)} %select_n.85, s32[]{:T(128)S(6)} %select_n.84), kind=kLoop, calls=%fused_computation.4 | loop fusion | bytes 524296 | tf_op jit(solution)/shard_map/convert_element_type | solution.py:293
  2.3 0.0 copy-start.10
  2.3 1.6 %copy-done.10 = bf16[1,1024,1024]{2,1,0:T(8,128)(2,1)S(1)} copy-done((bf16[1,1024,1024]{2,1,0:T(8,128)(2,1)S(1)}, bf16[1,1024,1024]{2,1,0:T(8,128)(2,1)}, u32[]{:S(2)}) %copy-start.10) | copy-done | bytes 2097176
  3.9 0.7 copy-done.16
  4.6 0.9 %shard_map.68.own = bf16[1024,1024]{1,0:T(8,128)(2,1)S(1)} custom-call(s32[8,8]{1,0:T(8,128)S(1)} %bitcast.16, bf16[1024,1024]{1,0:T(8,128)(2,1)S(1)} %bitcast.14), custom_call_target="tpu_custom_call" | custom-call | flops 1048576 | bytes 4194304 | tf_op jit(solution)/shard_map/pallas_call | solution.py:282
  5.5 0.0 collective-permute-done.1.other_pattern
  5.5 0.0 collective-permute-done.2.other
  5.5 1.8 %shard_map.69 = (bf16[256,1024]{1,0:T(8,128)(2,1)}, bf16[256,1024]{1,0:T(8,128)(2,1)S(1)}, bf16[256,1024]{1,0:T(8,128)(2,1)S(1)}) custom-call(s32[8,8]{1,0:T(8,128)S(1)} %collective-permute-done.1.other_pattern, bf16[1024,1024]{1,0:T(8,128)(2,1)S(1)} %shard_map.68.own, bf16[1024,1024]{1,0:T(8,128)(2,1)S(1)} %collective-permute-done.2.other, ...), custom_call_target="tpu_custom_call" | custom-call | flops 335544320 | bytes 3145728 | tf_op jit(solution)/shard_map/pallas_call | solution.py:96
  7.4 4.6 %collective-permute-start.3 = (bf16[256,1024]{1,0:T(8,128)(2,1)S(1)}, bf16[256,1024]{1,0:T(8,128)(2,1)S(1)}, u32[]{:S(2)}, u32[]{:S(2)}) collective-permute-start(bf16[256,1024]{1,0:T(8,128)(2,1)S(1)} %get-tuple-element.40.own), channel_id=1, source_target_pairs={{0,3},{2,1},{4,7},{6,5},{8,11},{10,9},{12,15},{14,13},{16,19},{18,... | collective-permute-start | bytes 1572872 | tf_op jit(solution)/shard_map/ppermute | solution.py:270
  11.9 2.1 %collective-permute-start.5 = (bf16[256,1024]{1,0:T(8,128)(2,1)}, bf16[256,1024]{1,0:T(8,128)(2,1)}, u32[]{:S(2)}, u32[]{:S(2)}) collective-permute-start(bf16[256,1024]{1,0:T(8,128)(2,1)} %get-tuple-element.46.own), channel_id=1, source_target_pairs={{0,3},{2,1},{4,7},{6,5},{8,11},{10,9},{12,15},{14,13},{16,19},{18,... | collective-permute-start | bytes 1572872 | tf_op jit(solution)/shard_map/ppermute | solution.py:270
  14.0 1.3 %shard_map.70 = (bf16[256,1024]{1,0:T(8,128)(2,1)S(1)}, bf16[256,1024]{1,0:T(8,128)(2,1)S(1)}) custom-call(s32[8,8]{1,0:T(8,128)S(1)} %collective-permute-done.1.other_pattern, bf16[1024,1024]{1,0:T(8,128)(2,1)S(1)} %shard_map.68.own, bf16[1024,1024]{1,0:T(8,128)(2,1)S(1)} %collective-permute-done.2.other, bf16[256,256]{1,0:T(8,128)(2,1)S(1)} %get-tuple-element.79.inverse, ...), custom_call_target="tpu_custom_call" | custom-call | flops 335544320 | bytes 3145728 | tf_op jit(solution)/shard_map/pallas_call | solution.py:96
  15.4 3.2 %collective-permute-done.3.other = bf16[256,1024]{1,0:T(8,128)(2,1)S(1)} collective-permute-done((bf16[256,1024]{1,0:T(8,128)(2,1)S(1)}, bf16[256,1024]{1,0:T(8,128)(2,1)S(1)}, u32[]{:S(2)}, u32[]{:S(2)}) %collective-permute-start.3) | collective-permute-done | bytes 524320 | tf_op jit(solution)/shard_map/ppermute | solution.py:270
  18.6 1.3 %shard_map.71 = (bf16[256,1024]{1,0:T(8,128)(2,1)}, bf16[1024,1024]{1,0:T(8,128)(2,1)S(1)}, bf16[256,1024]{1,0:T(8,128)(2,1)S(1)}) custom-call(bf16[256,1024]{1,0:T(8,128)(2,1)S(1)} %get-tuple-element.40.own, bf16[256,1024]{1,0:T(8,128)(2,1)S(1)} %collective-permute-done.3.other, bf16[256,256]{1,0:T(8,128)(2,1)S(1)} %get-tuple-element.78.inverse, ...), custom_call_target="tpu_custom_call" | custom-call | tf_op jit(solution)/shard_map/pallas_call | solution.py:136
  19.9 3.8 %collective-permute-start.7 = (bf16[256,1024]{1,0:T(8,128)(2,1)}, bf16[256,1024]{1,0:T(8,128)(2,1)S(1)}, u32[]{:S(2)}, u32[]{:S(2)}) collective-permute-start(bf16[256,1024]{1,0:T(8,128)(2,1)} %get-tuple-element.43), channel_id=1, source_target_pairs={{5,0},{7,2},{13,8},{15,10},{21,16},{23,18},{29,24},{31,26},{0,3},{... | collective-permute-start | bytes 1572872 | tf_op jit(solution)/shard_map/ppermute | solution.py:270
  23.7 0.1 collective-permute-start
  23.8 1.1 %collective-permute-done = f32[4,1024]{1,0:T(4,128)S(1)} collective-permute-done((f32[4,1024]{1,0:T(4,128)S(1)}, f32[4,1024]{1,0:T(4,128)S(1)}, u32[]{:S(2)}, u32[]{:S(2)}) %collective-permute-start) | collective-permute-done | bytes 16416 | tf_op jit(solution)/shard_map/ppermute | solution.py:270
  25.0 0.7 collective-permute-start.4
  25.6 0.0 collective-permute-done.5.other
  25.6 1.0 %copy-done.12 = bf16[256,1024]{1,0:T(8,128)(2,1)S(1)} copy-done((bf16[256,1024]{1,0:T(8,128)(2,1)S(1)}, bf16[256,1024]{1,0:T(8,128)(2,1)}, u32[]{:S(2)}) %copy-start.12) | copy-done | bytes 524312
  26.7 1.8 %shard_map.72 = (bf16[256,1024]{1,0:T(8,128)(2,1)S(1)}, bf16[1024,1024]{1,0:T(8,128)(2,1)S(1)}) custom-call(bf16[256,1024]{1,0:T(8,128)(2,1)} %get-tuple-element.46.own, bf16[256,1024]{1,0:T(8,128)(2,1)} %collective-permute-done.5.other, bf16[256,256]{1,0:T(8,128)(2,1)S(1)} %get-tuple-element.78.inverse, ...), custom_call_target="tpu_custom_call", output_to_operand_aliasing={{1}: (5, {})} | custom-call | tf_op jit(solution)/shard_map/pallas_call | solution.py:136
  28.5 4.6 %collective-permute-start.6 = (bf16[256,1024]{1,0:T(8,128)(2,1)S(1)}, bf16[256,1024]{1,0:T(8,128)(2,1)S(1)}, u32[]{:S(2)}, u32[]{:S(2)}) collective-permute-start(bf16[256,1024]{1,0:T(8,128)(2,1)S(1)} %get-tuple-element.49), channel_id=1, source_target_pairs={{5,0},{7,2},{13,8},{15,10},{21,16},{23,18},{29,24},{31,26},{0,3},{... | collective-permute-start | bytes 1572872 | tf_op jit(solution)/shard_map/ppermute | solution.py:270
  33.1 0.0 collective-permute-done.4.refs_3_
  33.1 0.0 collective-permute-done.7.other.refs_5_.refs_3_.refs_2_
  33.1 1.0 %copy-done.9 = bf16[256,1024]{1,0:T(8,128)(2,1)S(1)} copy-done((bf16[256,1024]{1,0:T(8,128)(2,1)S(1)}, bf16[256,1024]{1,0:T(8,128)(2,1)}, u32[]{:S(2)}) %copy-start.9) | copy-done | bytes 524312
  34.1 0.4 shard_map.73
  34.6 1.3 %collective-permute-start.8 = (bf16[256,1024]{1,0:T(8,128)(2,1)S(1)}, bf16[256,1024]{1,0:T(8,128)(2,1)S(1)}, u32[]{:S(2)}, u32[]{:S(2)}) collective-permute-start(bf16[256,1024]{1,0:T(8,128)(2,1)S(1)} %get-tuple-element.52), channel_id=1, source_target_pairs={{5,0},{7,2},{13,8},{15,10},{21,16},{23,18},{29,24},{31,26}} | collective-permute-start | bytes 1572872 | tf_op jit(solution)/shard_map/ppermute | solution.py:270
  35.9 3.8 %collective-permute-done.6.other.refs_4_.refs_2_.refs_1_ = bf16[256,1024]{1,0:T(8,128)(2,1)S(1)} collective-permute-done((bf16[256,1024]{1,0:T(8,128)(2,1)S(1)}, bf16[256,1024]{1,0:T(8,128)(2,1)S(1)}, u32[]{:S(2)}, u32[]{:S(2)}) %collective-permute-start.6) | collective-permute-done | bytes 524320 | tf_op jit(solution)/shard_map/ppermute | solution.py:270
  39.8 5.3 %collective-permute-done.8.refs_6_.refs_4_.refs_3_ = bf16[256,1024]{1,0:T(8,128)(2,1)S(1)} collective-permute-done((bf16[256,1024]{1,0:T(8,128)(2,1)S(1)}, bf16[256,1024]{1,0:T(8,128)(2,1)S(1)}, u32[]{:S(2)}, u32[]{:S(2)}) %collective-permute-start.8) | collective-permute-done | bytes 524320 | tf_op jit(solution)/shard_map/ppermute | solution.py:270
  45.1 0.4 shard_map.74
  45.5 0.0 copy-start
  45.6 1.3 %copy-done = bf16[1024,1024]{1,0:T(8,128)(2,1)} copy-done((bf16[1024,1024]{1,0:T(8,128)(2,1)}, bf16[1024,1024]{1,0:T(8,128)(2,1)S(1)}, u32[]{:S(2)}) %copy-start) | copy-done | bytes 2097176
  46.9 1.3 %collective-permute-start.10 = (bf16[1024,1024]{1,0:T(8,128)(2,1)}, bf16[1024,1024]{1,0:T(8,128)(2,1)S(1)}, u32[]{:S(2)}, u32[]{:S(2)}) collective-permute-start(bf16[1024,1024]{1,0:T(8,128)(2,1)} %copy-done), channel_id=1, source_target_pairs={{1,0},{3,2},{5,4},{7,6},{9,8},{11,10},{13,12},{15,14},{17,16},{19,... | collective-permute-start | bytes 6291464 | tf_op jit(solution)/shard_map/ppermute | solution.py:270
  48.2 1.3 %collective-permute-start.11 = (bf16[256,1024]{1,0:T(8,128)(2,1)S(1)}, bf16[256,1024]{1,0:T(8,128)(2,1)S(1)}, u32[]{:S(2)}, u32[]{:S(2)}) collective-permute-start(bf16[256,1024]{1,0:T(8,128)(2,1)S(1)} %get-tuple-element.58), channel_id=1, source_target_pairs={{5,0},{7,2},{13,8},{15,10},{21,16},{23,18},{29,24},{31,26}} | collective-permute-start | bytes 1572872 | tf_op jit(solution)/shard_map/ppermute | solution.py:270
  49.5 0.7 collective-permute-start.9
  50.1 0.0 collective-permute-done.9.refs_0_
  50.1 8.5 %collective-permute-done.11.refs_7_.refs_5_.refs_4_ = bf16[256,1024]{1,0:T(8,128)(2,1)S(1)} collective-permute-done((bf16[256,1024]{1,0:T(8,128)(2,1)S(1)}, bf16[256,1024]{1,0:T(8,128)(2,1)S(1)}, u32[]{:S(2)}, u32[]{:S(2)}) %collective-permute-start.11) | collective-permute-done | bytes 524320 | tf_op jit(solution)/shard_map/ppermute | solution.py:270
  58.7 0.0 collective-permute-done.10.refs_2_.refs_7_.refs_0_
  58.7 0.7 collective-permute-start.12
  59.3 0.0 collective-permute-done.12.refs_0_
  59.3 0.1 copy-done.5
  59.5 0.7 collective-permute-start.13
  60.1 0.0 copy-start.1
  60.1 1.4 %collective-permute-start.18 = (f32[8,1024]{1,0:T(8,128)S(1)}, f32[8,1024]{1,0:T(8,128)S(1)}, u32[]{:S(2)}, u32[]{:S(2)}) collective-permute-start(f32[8,1024]{1,0:T(8,128)S(1)} %get-tuple-element.71), channel_id=1, source_target_pairs={{5,0},{7,2}} | collective-permute-start | bytes 98312 | tf_op jit(solution)/shard_map/ppermute | solution.py:270
  61.6 0.7 collective-permute-start.19
  62.2 0.0 collective-permute-done.13.refs_0_
  62.3 1.0 %copy-done.3 = bf16[256,1024]{1,0:T(8,128)(2,1)S(1)} copy-done((bf16[256,1024]{1,0:T(8,128)(2,1)S(1)}, bf16[256,1024]{1,0:T(8,128)(2,1)}, u32[]{:S(2)}) %copy-start.3) | copy-done | bytes 524312
  63.3 1.0 %copy-done.6 = bf16[256,1024]{1,0:T(8,128)(2,1)S(1)} copy-done((bf16[256,1024]{1,0:T(8,128)(2,1)S(1)}, bf16[256,1024]{1,0:T(8,128)(2,1)}, u32[]{:S(2)}) %copy-start.6) | copy-done | bytes 524312
  64.3 0.6 shard_map.78
  65.0 0.8 collective-permute-start.14
  65.8 1.5 %broadcast_select_fusion = bf16[1024,1024]{1,0:T(8,128)(2,1)} fusion(bf16[1024,1024]{1,0:T(8,128)(2,1)S(1)} %copy-done.1, bf16[1024,1024]{1,0:T(8,128)(2,1)S(1)} %collective-permute-done.10.refs_2_.refs_7_.refs_0_, pred[]{:T(512)S(6)} %eq.18), kind=kLoop, calls=%fused_computation | loop fusion | flops 1048576 | bytes 6291457 | tf_op jit(solution)/shard_map/jit(_where)/select_n | solution.py:394
  67.3 0.0 collective-permute-done.14.refs_0_
  67.3 0.7 collective-permute-start.15
  68.0 0.0 collective-permute-done.18
  68.1 1.3 %collective-permute-start.16 = (bf16[8,1024]{1,0:T(8,128)(2,1)S(1)}, bf16[8,1024]{1,0:T(8,128)(2,1)S(1)}, u32[]{:S(2)}, u32[]{:S(2)}) collective-permute-start(bf16[8,1024]{1,0:T(8,128)(2,1)S(1)} %get-tuple-element.69), channel_id=1, source_target_pairs={{8,0},{10,2}} | collective-permute-start | bytes 49160 | tf_op jit(solution)/shard_map/ppermute | solution.py:270
  69.4 0.7 collective-permute-start.17
  70.1 0.7 collective-permute-start.20
  70.8 18.0 %collective-permute-done.16.from_pair = bf16[8,1024]{1,0:T(8,128)(2,1)S(1)} collective-permute-done((bf16[8,1024]{1,0:T(8,128)(2,1)S(1)}, bf16[8,1024]{1,0:T(8,128)(2,1)S(1)}, u32[]{:S(2)}, u32[]{:S(2)}) %collective-permute-start.16) | collective-permute-done | bytes 16416 | tf_op jit(solution)/shard_map/ppermute | solution.py:270
  88.8 0.0 collective-permute-done.17.from_own
  88.8 0.9 %shard_map.81 = f32[8,1024]{1,0:T(8,128)S(1)} custom-call(s32[1]{0:T(128)} %bitcast.6.odd, bf16[8,1024]{1,0:T(8,128)(2,1)S(1)} %collective-permute-done.16.from_pair, bf16[8,1024]{1,0:T(8,128)(2,1)S(1)} %collective-permute-done.17.from_own, f32[8,1024]{1,0:T(8,128)S(1)} %pad_maximum_fusion.1.source, f32[8,1024]{1,0:T(8,128)S(1)} %add.30.down_odd, ...), custom_call_target="tpu_custom_call" | custom-call | flops 1610612736 | bytes 6291456 | tf_op jit(solution)/shard_map/pallas_call | solution.py:416
  89.7 1.3 %collective-permute-start.21 = (f32[4,1024]{1,0:T(4,128)S(1)}, f32[4,1024]{1,0:T(4,128)S(1)}, u32[]{:S(2)}, u32[]{:S(2)}) collective-permute-start(f32[4,1024]{1,0:T(4,128)S(1)} %slice.16), channel_id=1, source_target_pairs={{0,1},{2,3},{4,5},{6,7},{8,9},{10,11},{12,13},{14,15},{16,17},{18,... | collective-permute-start | bytes 49160 | tf_op jit(solution)/shard_map/ppermute | solution.py:270
  91.0 0.8 collective-permute-done.21
  91.9 0.6 fusion.2
  (44 shorter events, 0.2 us)
Async XLA Ops:
  0.6 4.9 %collective-permute-start.2 = (bf16[1024,1024]{1,0:T(8,128)(2,1)}, bf16[1024,1024]{1,0:T(8,128)(2,1)S(1)}, u32[]{:S(2)}, u32[]{:S(2)}) collective-permute-start(bf16[1024,1024]{1,0:T(8,128)(2,1)} %bitcast.13), channel_id=1, source_target_pairs={{0,1},{1,0},{2,3},{3,2},{4,5},{5,4},{6,7},{7,6},{8,9},{9,8},{10,11... | collective-permute-start | bytes 6291464 | tf_op jit(solution)/shard_map/ppermute | solution.py:270
  1.1 4.4 %collective-permute-start.1 = (s32[8,8]{1,0:T(8,128)}, s32[8,8]{1,0:T(8,128)S(1)}, u32[]{:S(2)}, u32[]{:S(2)}) collective-permute-start(s32[8,8]{1,0:T(8,128)} %bitcast.15), channel_id=1, source_target_pairs={{0,1},{1,0},{2,3},{3,2},{4,5},{5,4},{6,7},{7,6},{8,9},{9,8},{10,11... | collective-permute-start | bytes 776 | tf_op jit(solution)/shard_map/ppermute | solution.py:270
  2.3 1.6 %copy-start.10 = (bf16[1,1024,1024]{2,1,0:T(8,128)(2,1)S(1)}, bf16[1,1024,1024]{2,1,0:T(8,128)(2,1)}, u32[]{:S(2)}) copy-start(bf16[1,1024,1024]{2,1,0:T(8,128)(2,1)} %param.5) | copy-start | bytes 6291460
  3.9 0.7 copy-start.16
  7.4 11.2 %collective-permute-start.3 = (bf16[256,1024]{1,0:T(8,128)(2,1)S(1)}, bf16[256,1024]{1,0:T(8,128)(2,1)S(1)}, u32[]{:S(2)}, u32[]{:S(2)}) collective-permute-start(bf16[256,1024]{1,0:T(8,128)(2,1)S(1)} %get-tuple-element.40.own), channel_id=1, source_target_pairs={{0,3},{2,1},{4,7},{6,5},{8,11},{10,9},{12,15},{14,13},{16,19},{18,... | collective-permute-start | bytes 1572872 | tf_op jit(solution)/shard_map/ppermute | solution.py:270
  11.9 13.7 %collective-permute-start.5 = (bf16[256,1024]{1,0:T(8,128)(2,1)}, bf16[256,1024]{1,0:T(8,128)(2,1)}, u32[]{:S(2)}, u32[]{:S(2)}) collective-permute-start(bf16[256,1024]{1,0:T(8,128)(2,1)} %get-tuple-element.46.own), channel_id=1, source_target_pairs={{0,3},{2,1},{4,7},{6,5},{8,11},{10,9},{12,15},{14,13},{16,19},{18,... | collective-permute-start | bytes 1572872 | tf_op jit(solution)/shard_map/ppermute | solution.py:270
  14.0 9.6 %copy-start.17 = (f32[1,4,1024]{2,1,0:T(4,128)S(1)}, f32[1,4,1024]{2,1,0:T(4,128)}, u32[]{:S(2)}) copy-start(f32[1,4,1024]{2,1,0:T(4,128)} %param.9) | copy-start | bytes 49156
  14.0 9.7 %copy-start.18 = (s32[1,1024]{1,0:T(1,128)S(1)}, s32[1,1024]{1,0:T(1,128)}, u32[]{:S(2)}) copy-start(s32[1,1024]{1,0:T(1,128)} %param.8) | copy-start | bytes 12292
  15.4 4.5 %copy-start.11 = (bf16[256,1024]{1,0:T(8,128)(2,1)}, bf16[256,1024]{1,0:T(8,128)(2,1)S(1)}, u32[]{:S(2)}) copy-start(bf16[256,1024]{1,0:T(8,128)(2,1)S(1)} %get-tuple-element.45.refs_0_.own) | copy-start | bytes 1572868
  15.4 4.5 %copy-start.14 = (bf16[256,1024]{1,0:T(8,128)(2,1)}, bf16[256,1024]{1,0:T(8,128)(2,1)S(1)}, u32[]{:S(2)}) copy-start(bf16[256,1024]{1,0:T(8,128)(2,1)S(1)} %get-tuple-element.42.refs_0_.own) | copy-start | bytes 1572868
  19.9 8.6 %copy-start.8 = (bf16[256,1024]{1,0:T(8,128)(2,1)}, bf16[256,1024]{1,0:T(8,128)(2,1)S(1)}, u32[]{:S(2)}) copy-start(bf16[256,1024]{1,0:T(8,128)(2,1)S(1)} %get-tuple-element.47.refs_1_.refs_0_) | copy-start | bytes 1572868
  19.9 13.2 %collective-permute-start.7 = (bf16[256,1024]{1,0:T(8,128)(2,1)}, bf16[256,1024]{1,0:T(8,128)(2,1)S(1)}, u32[]{:S(2)}, u32[]{:S(2)}) collective-permute-start(bf16[256,1024]{1,0:T(8,128)(2,1)} %get-tuple-element.43), channel_id=1, source_target_pairs={{5,0},{7,2},{13,8},{15,10},{21,16},{23,18},{29,24},{31,26},{0,3},{... | collective-permute-start | bytes 1572872 | tf_op jit(solution)/shard_map/ppermute | solution.py:270
  23.7 1.2 %collective-permute-start = (f32[4,1024]{1,0:T(4,128)S(1)}, f32[4,1024]{1,0:T(4,128)S(1)}, u32[]{:S(2)}, u32[]{:S(2)}) collective-permute-start(f32[4,1024]{1,0:T(4,128)S(1)} %bitcast.18), channel_id=1, source_target_pairs={{0,1},{1,0},{2,3},{3,2},{4,5},{5,4},{6,7},{7,6},{8,9},{9,8},{10,11... | collective-permute-start | bytes 49160 | tf_op jit(solution)/shard_map/ppermute | solution.py:270
  25.0 8.1 %collective-permute-start.4 = (f32[9,1024]{1,0:T(8,128)S(1)}, f32[9,1024]{1,0:T(8,128)S(1)}, u32[]{:S(2)}, u32[]{:S(2)}) collective-permute-start(f32[9,1024]{1,0:T(8,128)S(1)} %pad_maximum_fusion.refs_1_), channel_id=1, source_target_pairs={{12,8},{14,10},{20,16},{22,18},{28,24},{30,26},{1,5},{3,7}} | collective-permute-start | bytes 110600 | tf_op jit(solution)/shard_map/ppermute | solution.py:270
  25.6 1.0 %copy-start.12 = (bf16[256,1024]{1,0:T(8,128)(2,1)S(1)}, bf16[256,1024]{1,0:T(8,128)(2,1)}, u32[]{:S(2)}) copy-start(bf16[256,1024]{1,0:T(8,128)(2,1)} %copy-done.11) | copy-start | bytes 1572868
  26.7 6.4 %copy-start.15 = (bf16[256,1024]{1,0:T(8,128)(2,1)S(1)}, bf16[256,1024]{1,0:T(8,128)(2,1)}, u32[]{:S(2)}) copy-start(bf16[256,1024]{1,0:T(8,128)(2,1)} %copy-done.14) | copy-start | bytes 1572868
  26.7 18.4 %copy-start.13 = (bf16[256,1024]{1,0:T(8,128)(2,1)S(1)}, bf16[256,1024]{1,0:T(8,128)(2,1)}, u32[]{:S(2)}) copy-start(bf16[256,1024]{1,0:T(8,128)(2,1)} %copy-done.11) | copy-start | bytes 1572868
  28.5 11.3 %collective-permute-start.6 = (bf16[256,1024]{1,0:T(8,128)(2,1)S(1)}, bf16[256,1024]{1,0:T(8,128)(2,1)S(1)}, u32[]{:S(2)}, u32[]{:S(2)}) collective-permute-start(bf16[256,1024]{1,0:T(8,128)(2,1)S(1)} %get-tuple-element.49), channel_id=1, source_target_pairs={{5,0},{7,2},{13,8},{15,10},{21,16},{23,18},{29,24},{31,26},{0,3},{... | collective-permute-start | bytes 1572872 | tf_op jit(solution)/shard_map/ppermute | solution.py:270
  33.1 1.0 %copy-start.9 = (bf16[256,1024]{1,0:T(8,128)(2,1)S(1)}, bf16[256,1024]{1,0:T(8,128)(2,1)}, u32[]{:S(2)}) copy-start(bf16[256,1024]{1,0:T(8,128)(2,1)} %copy-done.8) | copy-start | bytes 1572868
  34.6 10.5 %collective-permute-start.8 = (bf16[256,1024]{1,0:T(8,128)(2,1)S(1)}, bf16[256,1024]{1,0:T(8,128)(2,1)S(1)}, u32[]{:S(2)}, u32[]{:S(2)}) collective-permute-start(bf16[256,1024]{1,0:T(8,128)(2,1)S(1)} %get-tuple-element.52), channel_id=1, source_target_pairs={{5,0},{7,2},{13,8},{15,10},{21,16},{23,18},{29,24},{31,26}} | collective-permute-start | bytes 1572872 | tf_op jit(solution)/shard_map/ppermute | solution.py:270
  45.1 14.2 %copy-start.2 = (bf16[256,1024]{1,0:T(8,128)(2,1)}, bf16[256,1024]{1,0:T(8,128)(2,1)S(1)}, u32[]{:S(2)}) copy-start(bf16[256,1024]{1,0:T(8,128)(2,1)S(1)} %collective-permute-done.8.refs_6_.refs_4_.refs_3_) | copy-start | bytes 1572868
  45.5 1.3 %copy-start = (bf16[1024,1024]{1,0:T(8,128)(2,1)}, bf16[1024,1024]{1,0:T(8,128)(2,1)S(1)}, u32[]{:S(2)}) copy-start(bf16[1024,1024]{1,0:T(8,128)(2,1)S(1)} %get-tuple-element.57.refs_2_) | copy-start | bytes 6291460
  46.9 11.8 %collective-permute-start.10 = (bf16[1024,1024]{1,0:T(8,128)(2,1)}, bf16[1024,1024]{1,0:T(8,128)(2,1)S(1)}, u32[]{:S(2)}, u32[]{:S(2)}) collective-permute-start(bf16[1024,1024]{1,0:T(8,128)(2,1)} %copy-done), channel_id=1, source_target_pairs={{1,0},{3,2},{5,4},{7,6},{9,8},{11,10},{13,12},{15,14},{17,16},{19,... | collective-permute-start | bytes 6291464 | tf_op jit(solution)/shard_map/ppermute | solution.py:270
  48.2 10.5 %collective-permute-start.11 = (bf16[256,1024]{1,0:T(8,128)(2,1)S(1)}, bf16[256,1024]{1,0:T(8,128)(2,1)S(1)}, u32[]{:S(2)}, u32[]{:S(2)}) collective-permute-start(bf16[256,1024]{1,0:T(8,128)(2,1)S(1)} %get-tuple-element.58), channel_id=1, source_target_pairs={{5,0},{7,2},{13,8},{15,10},{21,16},{23,18},{29,24},{31,26}} | collective-permute-start | bytes 1572872 | tf_op jit(solution)/shard_map/ppermute | solution.py:270
  49.5 0.7 collective-permute-start.9
  58.7 0.8 copy-start.5
  58.7 0.7 collective-permute-start.12
  59.5 2.8 %collective-permute-start.13 = (bf16[8,1024]{1,0:T(8,128)(2,1)S(1)}, bf16[8,1024]{1,0:T(8,128)(2,1)S(1)}, u32[]{:S(2)}, u32[]{:S(2)}) collective-permute-start(bf16[8,1024]{1,0:T(8,128)(2,1)S(1)} %get-tuple-element.60), channel_id=1, source_target_pairs={{16,24},{18,26}} | collective-permute-start | bytes 49160 | tf_op jit(solution)/shard_map/ppermute | solution.py:270
  60.1 5.6 %copy-start.1 = (bf16[1024,1024]{1,0:T(8,128)(2,1)S(1)}, bf16[1024,1024]{1,0:T(8,128)(2,1)}, u32[]{:S(2)}) copy-start(bf16[1024,1024]{1,0:T(8,128)(2,1)} %copy-done) | copy-start | bytes 6291460
  60.1 7.9 %collective-permute-start.18 = (f32[8,1024]{1,0:T(8,128)S(1)}, f32[8,1024]{1,0:T(8,128)S(1)}, u32[]{:S(2)}, u32[]{:S(2)}) collective-permute-start(f32[8,1024]{1,0:T(8,128)S(1)} %get-tuple-element.71), channel_id=1, source_target_pairs={{5,0},{7,2}} | collective-permute-start | bytes 98312 | tf_op jit(solution)/shard_map/ppermute | solution.py:270
  61.6 6.5 %collective-permute-start.19 = (f32[8,1024]{1,0:T(8,128)S(1)}, f32[8,1024]{1,0:T(8,128)S(1)}, u32[]{:S(2)}, u32[]{:S(2)}) collective-permute-start(f32[8,1024]{1,0:T(8,128)S(1)} %get-tuple-element.71), channel_id=1, source_target_pairs={{5,4},{7,6}} | collective-permute-start | bytes 98312 | tf_op jit(solution)/shard_map/ppermute | solution.py:270
  62.3 1.0 %copy-start.3 = (bf16[256,1024]{1,0:T(8,128)(2,1)S(1)}, bf16[256,1024]{1,0:T(8,128)(2,1)}, u32[]{:S(2)}) copy-start(bf16[256,1024]{1,0:T(8,128)(2,1)} %copy-done.2) | copy-start | bytes 1572868
  63.3 1.0 %copy-start.6 = (bf16[256,1024]{1,0:T(8,128)(2,1)S(1)}, bf16[256,1024]{1,0:T(8,128)(2,1)}, u32[]{:S(2)}) copy-start(bf16[256,1024]{1,0:T(8,128)(2,1)} %copy-done.5) | copy-start | bytes 1572868
  65.0 2.3 %copy-start.4 = (bf16[256,1024]{1,0:T(8,128)(2,1)S(1)}, bf16[256,1024]{1,0:T(8,128)(2,1)}, u32[]{:S(2)}) copy-start(bf16[256,1024]{1,0:T(8,128)(2,1)} %copy-done.2) | copy-start | bytes 1572868
  65.0 2.3 %copy-start.7 = (bf16[256,1024]{1,0:T(8,128)(2,1)S(1)}, bf16[256,1024]{1,0:T(8,128)(2,1)}, u32[]{:S(2)}) copy-start(bf16[256,1024]{1,0:T(8,128)(2,1)} %copy-done.5) | copy-start | bytes 1572868
  65.0 2.3 %collective-permute-start.14 = (bf16[8,1024]{1,0:T(8,128)(2,1)S(1)}, bf16[8,1024]{1,0:T(8,128)(2,1)S(1)}, u32[]{:S(2)}, u32[]{:S(2)}) collective-permute-start(bf16[8,1024]{1,0:T(8,128)(2,1)S(1)} %get-tuple-element.61), channel_id=1, source_target_pairs={{24,16},{26,18}} | collective-permute-start | bytes 49160 | tf_op jit(solution)/shard_map/ppermute | solution.py:270
  67.3 0.7 collective-permute-start.15
  68.1 20.7 %collective-permute-start.16 = (bf16[8,1024]{1,0:T(8,128)(2,1)S(1)}, bf16[8,1024]{1,0:T(8,128)(2,1)S(1)}, u32[]{:S(2)}, u32[]{:S(2)}) collective-permute-start(bf16[8,1024]{1,0:T(8,128)(2,1)S(1)} %get-tuple-element.69), channel_id=1, source_target_pairs={{8,0},{10,2}} | collective-permute-start | bytes 49160 | tf_op jit(solution)/shard_map/ppermute | solution.py:270
  69.4 19.4 %collective-permute-start.17 = (bf16[8,1024]{1,0:T(8,128)(2,1)S(1)}, bf16[8,1024]{1,0:T(8,128)(2,1)S(1)}, u32[]{:S(2)}, u32[]{:S(2)}) collective-permute-start(bf16[8,1024]{1,0:T(8,128)(2,1)S(1)} %get-tuple-element.69), channel_id=1, source_target_pairs={{8,4},{10,6}} | collective-permute-start | bytes 49160 | tf_op jit(solution)/shard_map/ppermute | solution.py:270
  70.1 19.6 %collective-permute-start.20 = (f32[8,1024]{1,0:T(8,128)S(1)}, f32[8,1024]{1,0:T(8,128)S(1)}, u32[]{:S(2)}, u32[]{:S(2)}) collective-permute-start(f32[8,1024]{1,0:T(8,128)S(1)} %select_select_fusion), channel_id=1, source_target_pairs={{8,12},{10,14},{16,20},{18,22},{24,28},{26,30}} | collective-permute-start | bytes 98312 | tf_op jit(solution)/shard_map/ppermute | solution.py:270
  89.7 2.1 %collective-permute-start.21 = (f32[4,1024]{1,0:T(4,128)S(1)}, f32[4,1024]{1,0:T(4,128)S(1)}, u32[]{:S(2)}, u32[]{:S(2)}) collective-permute-start(f32[4,1024]{1,0:T(4,128)S(1)} %slice.16), channel_id=1, source_target_pairs={{0,1},{2,3},{4,5},{6,7},{8,9},{10,11},{12,13},{14,15},{16,17},{18,... | collective-permute-start | bytes 49160 | tf_op jit(solution)/shard_map/ppermute | solution.py:270

commit v11 on v10

--- a/solution.py
+++ b/solution.py
@@ -12,8 +12,9 @@
 SMALL_AT = 0
 VMEM = pl.BlockSpec(memory_space=pltpu.VMEM)
 SMEM = pl.BlockSpec(memory_space=pltpu.SMEM)
-PARAMS = pltpu.CompilerParams(vmem_limit_bytes=24 * 1024 * 1024)
-SWEEP_PARAMS = pltpu.CompilerParams(vmem_limit_bytes=10 * 1024 * 1024)
+PARAMS = pltpu.CompilerParams(vmem_limit_bytes=16 * 1024 * 1024)
+SWEEP_PARAMS = pltpu.CompilerParams(vmem_limit_bytes=6 * 1024 * 1024)
+COMBINE_PARAMS = pltpu.CompilerParams(vmem_limit_bytes=12 * 1024 * 1024)
 OWN, PAIR = 0, 1
 
 
@@ -145,7 +146,7 @@
         in_specs=[VMEM] * (3 + len(extra)),
         out_specs=[VMEM] * (3 if is_face else 2),
         input_output_aliases=aliases,
-        compiler_params=PARAMS,
+        compiler_params=COMBINE_PARAMS,
         cost_estimate=cost(0, 0),
     )(own, other, inverse, *extra)
     return result[0], ((result[2] if is_face else state[0]), result[1])

time: 93.5 us -> 93.5 us (level)
  no operation moved by 1% of the time
where the time goes in v11:
time: 93.5 us; the launch traced here: 92.5 us
  waiting for transfers between devices  40.9 us (44%)
  starting transfers between devices  29.6 us (32%)
  Pallas kernels  9.63 us (10%)
  local copies, waits for them, and re-layouts  8.93 us (10%)
  other arithmetic  2.22 us (2%)
  between operations  1.16 us (1%)
    ppermute x22, waiting for transfers between devices, send(): return lax.ppermute(value, AXES, pairs_of_devices)  40.9 us
    ppermute x22, starting transfers between devices, send(): return lax.ppermute(value, AXES, pairs_of_devices)  29.6 us
    unnamed x38, local copies, waits for them, and re-layouts  7.86 us
    pallas_call x4, Pallas kernels, combine(): pl.pallas_call(functools.partial(combine_kernel, face_at, is_face, follow...  3.9 us
    pallas_call x2, Pallas kernels, leaf_combine(): pl.pallas_call(functools.partial(leaf_kernel, half * rows, is_face, piece...  3.17 us
  transfers between devices with their start and end apart: 22, of which 7 were waited for; matrix products, arithmetic and copies ran while one was open for 3% of the time, Pallas kernels for 8%

profile of v11, /device:TPU:0, one launch (start us, length us, event | category | flops | bytes accessed | tf_op | source)
XLA Modules:
  0.0 92.5 jit_solution(6598116760572751186)
XLA Ops:
  0.6 0.5 collective-permute-start.2
  1.1 0.1 collective-permute-start.1
  1.2 1.1 %fusion.1 = (bf16[256,256]{1,0:T(8,128)(2,1)S(1)}, bf16[256,256]{1,0:T(8,128)(2,1)S(1)}) fusion(f32[1,3,256,256]{3,2,1,0:T(8,128)} %param.7, s32[]{:T(128)S(6)} %select_n.85, s32[]{:T(128)S(6)} %select_n.84), kind=kLoop, calls=%fused_computation.4 | loop fusion | bytes 524296 | tf_op jit(solution)/shard_map/convert_element_type | solution.py:294
  2.3 0.0 copy-start.10
  2.3 1.6 %copy-done.10 = bf16[1,1024,1024]{2,1,0:T(8,128)(2,1)S(1)} copy-done((bf16[1,1024,1024]{2,1,0:T(8,128)(2,1)S(1)}, bf16[1,1024,1024]{2,1,0:T(8,128)(2,1)}, u32[]{:S(2)}) %copy-start.10) | copy-done | bytes 2097176
  3.9 0.7 copy-done.16
  4.6 0.9 %shard_map.68.own = bf16[1024,1024]{1,0:T(8,128)(2,1)S(1)} custom-call(s32[8,8]{1,0:T(8,128)S(1)} %bitcast.16, bf16[1024,1024]{1,0:T(8,128)(2,1)S(1)} %bitcast.14), custom_call_target="tpu_custom_call" | custom-call | flops 1048576 | bytes 4194304 | tf_op jit(solution)/shard_map/pallas_call | solution.py:283
  5.5 0.0 collective-permute-done.1.other_pattern
  5.5 0.0 collective-permute-done.2.other
  5.5 1.8 %shard_map.69 = (bf16[256,1024]{1,0:T(8,128)(2,1)}, bf16[256,1024]{1,0:T(8,128)(2,1)S(1)}, bf16[256,1024]{1,0:T(8,128)(2,1)S(1)}) custom-call(s32[8,8]{1,0:T(8,128)S(1)} %collective-permute-done.1.other_pattern, bf16[1024,1024]{1,0:T(8,128)(2,1)S(1)} %shard_map.68.own, bf16[1024,1024]{1,0:T(8,128)(2,1)S(1)} %collective-permute-done.2.other, ...), custom_call_target="tpu_custom_call" | custom-call | flops 335544320 | bytes 3145728 | tf_op jit(solution)/shard_map/pallas_call | solution.py:97
  7.4 4.6 %collective-permute-start.3 = (bf16[256,1024]{1,0:T(8,128)(2,1)S(1)}, bf16[256,1024]{1,0:T(8,128)(2,1)S(1)}, u32[]{:S(2)}, u32[]{:S(2)}) collective-permute-start(bf16[256,1024]{1,0:T(8,128)(2,1)S(1)} %get-tuple-element.40.own), channel_id=1, source_target_pairs={{0,3},{2,1},{4,7},{6,5},{8,11},{10,9},{12,15},{14,13},{16,19},{18,... | collective-permute-start | bytes 1572872 | tf_op jit(solution)/shard_map/ppermute | solution.py:271
  11.9 2.1 %collective-permute-start.5 = (bf16[256,1024]{1,0:T(8,128)(2,1)}, bf16[256,1024]{1,0:T(8,128)(2,1)}, u32[]{:S(2)}, u32[]{:S(2)}) collective-permute-start(bf16[256,1024]{1,0:T(8,128)(2,1)} %get-tuple-element.46.own), channel_id=1, source_target_pairs={{0,3},{2,1},{4,7},{6,5},{8,11},{10,9},{12,15},{14,13},{16,19},{18,... | collective-permute-start | bytes 1572872 | tf_op jit(solution)/shard_map/ppermute | solution.py:271
  14.0 1.3 %shard_map.70 = (bf16[256,1024]{1,0:T(8,128)(2,1)S(1)}, bf16[256,1024]{1,0:T(8,128)(2,1)S(1)}) custom-call(s32[8,8]{1,0:T(8,128)S(1)} %collective-permute-done.1.other_pattern, bf16[1024,1024]{1,0:T(8,128)(2,1)S(1)} %shard_map.68.own, bf16[1024,1024]{1,0:T(8,128)(2,1)S(1)} %collective-permute-done.2.other, bf16[256,256]{1,0:T(8,128)(2,1)S(1)} %get-tuple-element.79.inverse, ...), custom_call_target="tpu_custom_call" | custom-call | flops 335544320 | bytes 3145728 | tf_op jit(solution)/shard_map/pallas_call | solution.py:97
  15.4 3.2 %collective-permute-done.3.other = bf16[256,1024]{1,0:T(8,128)(2,1)S(1)} collective-permute-done((bf16[256,1024]{1,0:T(8,128)(2,1)S(1)}, bf16[256,1024]{1,0:T(8,128)(2,1)S(1)}, u32[]{:S(2)}, u32[]{:S(2)}) %collective-permute-start.3) | collective-permute-done | bytes 524320 | tf_op jit(solution)/shard_map/ppermute | solution.py:271
  18.6 1.3 %shard_map.71 = (bf16[256,1024]{1,0:T(8,128)(2,1)}, bf16[1024,1024]{1,0:T(8,128)(2,1)S(1)}, bf16[256,1024]{1,0:T(8,128)(2,1)S(1)}) custom-call(bf16[256,1024]{1,0:T(8,128)(2,1)S(1)} %get-tuple-element.40.own, bf16[256,1024]{1,0:T(8,128)(2,1)S(1)} %collective-permute-done.3.other, bf16[256,256]{1,0:T(8,128)(2,1)S(1)} %get-tuple-element.78.inverse, ...), custom_call_target="tpu_custom_call" | custom-call | tf_op jit(solution)/shard_map/pallas_call | solution.py:137
  19.9 3.8 %collective-permute-start.7 = (bf16[256,1024]{1,0:T(8,128)(2,1)}, bf16[256,1024]{1,0:T(8,128)(2,1)S(1)}, u32[]{:S(2)}, u32[]{:S(2)}) collective-permute-start(bf16[256,1024]{1,0:T(8,128)(2,1)} %get-tuple-element.43), channel_id=1, source_target_pairs={{5,0},{7,2},{13,8},{15,10},{21,16},{23,18},{29,24},{31,26},{0,3},{... | collective-permute-start | bytes 1572872 | tf_op jit(solution)/shard_map/ppermute | solution.py:271
  23.7 0.1 collective-permute-start
  23.8 1.1 %collective-permute-done = f32[4,1024]{1,0:T(4,128)S(1)} collective-permute-done((f32[4,1024]{1,0:T(4,128)S(1)}, f32[4,1024]{1,0:T(4,128)S(1)}, u32[]{:S(2)}, u32[]{:S(2)}) %collective-permute-start) | collective-permute-done | bytes 16416 | tf_op jit(solution)/shard_map/ppermute | solution.py:271
  25.0 0.7 collective-permute-start.4
  25.6 0.0 collective-permute-done.5.other
  25.6 1.0 %copy-done.12 = bf16[256,1024]{1,0:T(8,128)(2,1)S(1)} copy-done((bf16[256,1024]{1,0:T(8,128)(2,1)S(1)}, bf16[256,1024]{1,0:T(8,128)(2,1)}, u32[]{:S(2)}) %copy-start.12) | copy-done | bytes 524312
  26.7 1.8 %shard_map.72 = (bf16[256,1024]{1,0:T(8,128)(2,1)S(1)}, bf16[1024,1024]{1,0:T(8,128)(2,1)S(1)}) custom-call(bf16[256,1024]{1,0:T(8,128)(2,1)} %get-tuple-element.46.own, bf16[256,1024]{1,0:T(8,128)(2,1)} %collective-permute-done.5.other, bf16[256,256]{1,0:T(8,128)(2,1)S(1)} %get-tuple-element.78.inverse, ...), custom_call_target="tpu_custom_call", output_to_operand_aliasing={{1}: (5, {})} | custom-call | tf_op jit(solution)/shard_map/pallas_call | solution.py:137
  28.5 4.6 %collective-permute-start.6 = (bf16[256,1024]{1,0:T(8,128)(2,1)S(1)}, bf16[256,1024]{1,0:T(8,128)(2,1)S(1)}, u32[]{:S(2)}, u32[]{:S(2)}) collective-permute-start(bf16[256,1024]{1,0:T(8,128)(2,1)S(1)} %get-tuple-element.49), channel_id=1, source_target_pairs={{5,0},{7,2},{13,8},{15,10},{21,16},{23,18},{29,24},{31,26},{0,3},{... | collective-permute-start | bytes 1572872 | tf_op jit(solution)/shard_map/ppermute | solution.py:271
  33.1 0.0 collective-permute-done.4.refs_3_
  33.1 0.0 collective-permute-done.7.other.refs_5_.refs_3_.refs_2_
  33.1 1.0 %copy-done.9 = bf16[256,1024]{1,0:T(8,128)(2,1)S(1)} copy-done((bf16[256,1024]{1,0:T(8,128)(2,1)S(1)}, bf16[256,1024]{1,0:T(8,128)(2,1)}, u32[]{:S(2)}) %copy-start.9) | copy-done | bytes 524312
  34.1 0.4 shard_map.73
  34.6 1.3 %collective-permute-start.8 = (bf16[256,1024]{1,0:T(8,128)(2,1)S(1)}, bf16[256,1024]{1,0:T(8,128)(2,1)S(1)}, u32[]{:S(2)}, u32[]{:S(2)}) collective-permute-start(bf16[256,1024]{1,0:T(8,128)(2,1)S(1)} %get-tuple-element.52), channel_id=1, source_target_pairs={{5,0},{7,2},{13,8},{15,10},{21,16},{23,18},{29,24},{31,26}} | collective-permute-start | bytes 1572872 | tf_op jit(solution)/shard_map/ppermute | solution.py:271
  35.9 3.8 %collective-permute-done.6.other.refs_4_.refs_2_.refs_1_ = bf16[256,1024]{1,0:T(8,128)(2,1)S(1)} collective-permute-done((bf16[256,1024]{1,0:T(8,128)(2,1)S(1)}, bf16[256,1024]{1,0:T(8,128)(2,1)S(1)}, u32[]{:S(2)}, u32[]{:S(2)}) %collective-permute-start.6) | collective-permute-done | bytes 524320 | tf_op jit(solution)/shard_map/ppermute | solution.py:271
  39.8 5.3 %collective-permute-done.8.refs_6_.refs_4_.refs_3_ = bf16[256,1024]{1,0:T(8,128)(2,1)S(1)} collective-permute-done((bf16[256,1024]{1,0:T(8,128)(2,1)S(1)}, bf16[256,1024]{1,0:T(8,128)(2,1)S(1)}, u32[]{:S(2)}, u32[]{:S(2)}) %collective-permute-start.8) | collective-permute-done | bytes 524320 | tf_op jit(solution)/shard_map/ppermute | solution.py:271
  45.1 0.4 shard_map.74
  45.5 0.0 copy-start
  45.6 1.3 %copy-done = bf16[1024,1024]{1,0:T(8,128)(2,1)} copy-done((bf16[1024,1024]{1,0:T(8,128)(2,1)}, bf16[1024,1024]{1,0:T(8,128)(2,1)S(1)}, u32[]{:S(2)}) %copy-start) | copy-done | bytes 2097176
  46.9 1.3 %collective-permute-start.10 = (bf16[1024,1024]{1,0:T(8,128)(2,1)}, bf16[1024,1024]{1,0:T(8,128)(2,1)S(1)}, u32[]{:S(2)}, u32[]{:S(2)}) collective-permute-start(bf16[1024,1024]{1,0:T(8,128)(2,1)} %copy-done), channel_id=1, source_target_pairs={{1,0},{3,2},{5,4},{7,6},{9,8},{11,10},{13,12},{15,14},{17,16},{19,... | collective-permute-start | bytes 6291464 | tf_op jit(solution)/shard_map/ppermute | solution.py:271
  48.2 1.3 %collective-permute-start.11 = (bf16[256,1024]{1,0:T(8,128)(2,1)S(1)}, bf16[256,1024]{1,0:T(8,128)(2,1)S(1)}, u32[]{:S(2)}, u32[]{:S(2)}) collective-permute-start(bf16[256,1024]{1,0:T(8,128)(2,1)S(1)} %get-tuple-element.58), channel_id=1, source_target_pairs={{5,0},{7,2},{13,8},{15,10},{21,16},{23,18},{29,24},{31,26}} | collective-permute-start | bytes 1572872 | tf_op jit(solution)/shard_map/ppermute | solution.py:271
  49.5 0.7 collective-permute-start.9
  50.1 0.0 collective-permute-done.9.refs_0_
  50.1 8.5 %collective-permute-done.11.refs_7_.refs_5_.refs_4_ = bf16[256,1024]{1,0:T(8,128)(2,1)S(1)} collective-permute-done((bf16[256,1024]{1,0:T(8,128)(2,1)S(1)}, bf16[256,1024]{1,0:T(8,128)(2,1)S(1)}, u32[]{:S(2)}, u32[]{:S(2)}) %collective-permute-start.11) | collective-permute-done | bytes 524320 | tf_op jit(solution)/shard_map/ppermute | solution.py:271
  58.7 0.0 collective-permute-done.10.refs_2_.refs_7_.refs_0_
  58.7 0.7 collective-permute-start.12
  59.3 0.0 collective-permute-done.12.refs_0_
  59.3 0.1 copy-done.5
  59.5 0.7 collective-permute-start.13
  60.1 0.0 copy-start.1
  60.1 1.4 %collective-permute-start.18 = (f32[8,1024]{1,0:T(8,128)S(1)}, f32[8,1024]{1,0:T(8,128)S(1)}, u32[]{:S(2)}, u32[]{:S(2)}) collective-permute-start(f32[8,1024]{1,0:T(8,128)S(1)} %get-tuple-element.71), channel_id=1, source_target_pairs={{5,0},{7,2}} | collective-permute-start | bytes 98312 | tf_op jit(solution)/shard_map/ppermute | solution.py:271
  61.6 0.7 collective-permute-start.19
  62.2 0.0 collective-permute-done.13.refs_0_
  62.3 1.0 %copy-done.3 = bf16[256,1024]{1,0:T(8,128)(2,1)S(1)} copy-done((bf16[256,1024]{1,0:T(8,128)(2,1)S(1)}, bf16[256,1024]{1,0:T(8,128)(2,1)}, u32[]{:S(2)}) %copy-start.3) | copy-done | bytes 524312
  63.3 1.0 %copy-done.6 = bf16[256,1024]{1,0:T(8,128)(2,1)S(1)} copy-done((bf16[256,1024]{1,0:T(8,128)(2,1)S(1)}, bf16[256,1024]{1,0:T(8,128)(2,1)}, u32[]{:S(2)}) %copy-start.6) | copy-done | bytes 524312
  64.3 0.6 shard_map.78
  65.0 0.8 collective-permute-start.14
  65.8 1.5 %broadcast_select_fusion = bf16[1024,1024]{1,0:T(8,128)(2,1)} fusion(bf16[1024,1024]{1,0:T(8,128)(2,1)S(1)} %copy-done.1, bf16[1024,1024]{1,0:T(8,128)(2,1)S(1)} %collective-permute-done.10.refs_2_.refs_7_.refs_0_, pred[]{:T(512)S(6)} %eq.18), kind=kLoop, calls=%fused_computation | loop fusion | flops 1048576 | bytes 6291457 | tf_op jit(solution)/shard_map/jit(_where)/select_n | solution.py:395
  67.3 0.0 collective-permute-done.14.refs_0_
  67.3 0.7 collective-permute-start.15
  68.0 0.0 collective-permute-done.18
  68.1 1.3 %collective-permute-start.16 = (bf16[8,1024]{1,0:T(8,128)(2,1)S(1)}, bf16[8,1024]{1,0:T(8,128)(2,1)S(1)}, u32[]{:S(2)}, u32[]{:S(2)}) collective-permute-start(bf16[8,1024]{1,0:T(8,128)(2,1)S(1)} %get-tuple-element.69), channel_id=1, source_target_pairs={{8,0},{10,2}} | collective-permute-start | bytes 49160 | tf_op jit(solution)/shard_map/ppermute | solution.py:271
  69.4 0.7 collective-permute-start.17
  70.1 0.7 collective-permute-start.20
  70.8 18.0 %collective-permute-done.16.from_pair = bf16[8,1024]{1,0:T(8,128)(2,1)S(1)} collective-permute-done((bf16[8,1024]{1,0:T(8,128)(2,1)S(1)}, bf16[8,1024]{1,0:T(8,128)(2,1)S(1)}, u32[]{:S(2)}, u32[]{:S(2)}) %collective-permute-start.16) | collective-permute-done | bytes 16416 | tf_op jit(solution)/shard_map/ppermute | solution.py:271
  88.8 0.0 collective-permute-done.17.from_own
  88.8 0.9 %shard_map.81 = f32[8,1024]{1,0:T(8,128)S(1)} custom-call(s32[1]{0:T(128)} %bitcast.6.odd, bf16[8,1024]{1,0:T(8,128)(2,1)S(1)} %collective-permute-done.16.from_pair, bf16[8,1024]{1,0:T(8,128)(2,1)S(1)} %collective-permute-done.17.from_own, f32[8,1024]{1,0:T(8,128)S(1)} %pad_maximum_fusion.1.source, f32[8,1024]{1,0:T(8,128)S(1)} %add.30.down_odd, ...), custom_call_target="tpu_custom_call" | custom-call | flops 1610612736 | bytes 6291456 | tf_op jit(solution)/shard_map/pallas_call | solution.py:417
  89.7 1.3 %collective-permute-start.21 = (f32[4,1024]{1,0:T(4,128)S(1)}, f32[4,1024]{1,0:T(4,128)S(1)}, u32[]{:S(2)}, u32[]{:S(2)}) collective-permute-start(f32[4,1024]{1,0:T(4,128)S(1)} %slice.16), channel_id=1, source_target_pairs={{0,1},{2,3},{4,5},{6,7},{8,9},{10,11},{12,13},{14,15},{16,17},{18,... | collective-permute-start | bytes 49160 | tf_op jit(solution)/shard_map/ppermute | solution.py:271
  91.0 0.8 collective-permute-done.21
  91.9 0.6 fusion.2
  (44 shorter events, 0.2 us)
Async XLA Ops:
  0.6 4.9 %collective-permute-start.2 = (bf16[1024,1024]{1,0:T(8,128)(2,1)}, bf16[1024,1024]{1,0:T(8,128)(2,1)S(1)}, u32[]{:S(2)}, u32[]{:S(2)}) collective-permute-start(bf16[1024,1024]{1,0:T(8,128)(2,1)} %bitcast.13), channel_id=1, source_target_pairs={{0,1},{1,0},{2,3},{3,2},{4,5},{5,4},{6,7},{7,6},{8,9},{9,8},{10,11... | collective-permute-start | bytes 6291464 | tf_op jit(solution)/shard_map/ppermute | solution.py:271
  1.1 4.4 %collective-permute-start.1 = (s32[8,8]{1,0:T(8,128)}, s32[8,8]{1,0:T(8,128)S(1)}, u32[]{:S(2)}, u32[]{:S(2)}) collective-permute-start(s32[8,8]{1,0:T(8,128)} %bitcast.15), channel_id=1, source_target_pairs={{0,1},{1,0},{2,3},{3,2},{4,5},{5,4},{6,7},{7,6},{8,9},{9,8},{10,11... | collective-permute-start | bytes 776 | tf_op jit(solution)/shard_map/ppermute | solution.py:271
  2.3 1.6 %copy-start.10 = (bf16[1,1024,1024]{2,1,0:T(8,128)(2,1)S(1)}, bf16[1,1024,1024]{2,1,0:T(8,128)(2,1)}, u32[]{:S(2)}) copy-start(bf16[1,1024,1024]{2,1,0:T(8,128)(2,1)} %param.5) | copy-start | bytes 6291460
  3.9 0.7 copy-start.16
  7.4 11.2 %collective-permute-start.3 = (bf16[256,1024]{1,0:T(8,128)(2,1)S(1)}, bf16[256,1024]{1,0:T(8,128)(2,1)S(1)}, u32[]{:S(2)}, u32[]{:S(2)}) collective-permute-start(bf16[256,1024]{1,0:T(8,128)(2,1)S(1)} %get-tuple-element.40.own), channel_id=1, source_target_pairs={{0,3},{2,1},{4,7},{6,5},{8,11},{10,9},{12,15},{14,13},{16,19},{18,... | collective-permute-start | bytes 1572872 | tf_op jit(solution)/shard_map/ppermute | solution.py:271
  11.9 13.7 %collective-permute-start.5 = (bf16[256,1024]{1,0:T(8,128)(2,1)}, bf16[256,1024]{1,0:T(8,128)(2,1)}, u32[]{:S(2)}, u32[]{:S(2)}) collective-permute-start(bf16[256,1024]{1,0:T(8,128)(2,1)} %get-tuple-element.46.own), channel_id=1, source_target_pairs={{0,3},{2,1},{4,7},{6,5},{8,11},{10,9},{12,15},{14,13},{16,19},{18,... | collective-permute-start | bytes 1572872 | tf_op jit(solution)/shard_map/ppermute | solution.py:271
  14.0 9.6 %copy-start.17 = (f32[1,4,1024]{2,1,0:T(4,128)S(1)}, f32[1,4,1024]{2,1,0:T(4,128)}, u32[]{:S(2)}) copy-start(f32[1,4,1024]{2,1,0:T(4,128)} %param.9) | copy-start | bytes 49156
  14.0 9.7 %copy-start.18 = (s32[1,1024]{1,0:T(1,128)S(1)}, s32[1,1024]{1,0:T(1,128)}, u32[]{:S(2)}) copy-start(s32[1,1024]{1,0:T(1,128)} %param.8) | copy-start | bytes 12292
  15.4 4.5 %copy-start.11 = (bf16[256,1024]{1,0:T(8,128)(2,1)}, bf16[256,1024]{1,0:T(8,128)(2,1)S(1)}, u32[]{:S(2)}) copy-start(bf16[256,1024]{1,0:T(8,128)(2,1)S(1)} %get-tuple-element.45.refs_0_.own) | copy-start | bytes 1572868
  15.4 4.5 %copy-start.14 = (bf16[256,1024]{1,0:T(8,128)(2,1)}, bf16[256,1024]{1,0:T(8,128)(2,1)S(1)}, u32[]{:S(2)}) copy-start(bf16[256,1024]{1,0:T(8,128)(2,1)S(1)} %get-tuple-element.42.refs_0_.own) | copy-start | bytes 1572868
  19.9 8.6 %copy-start.8 = (bf16[256,1024]{1,0:T(8,128)(2,1)}, bf16[256,1024]{1,0:T(8,128)(2,1)S(1)}, u32[]{:S(2)}) copy-start(bf16[256,1024]{1,0:T(8,128)(2,1)S(1)} %get-tuple-element.47.refs_1_.refs_0_) | copy-start | bytes 1572868
  19.9 13.2 %collective-permute-start.7 = (bf16[256,1024]{1,0:T(8,128)(2,1)}, bf16[256,1024]{1,0:T(8,128)(2,1)S(1)}, u32[]{:S(2)}, u32[]{:S(2)}) collective-permute-start(bf16[256,1024]{1,0:T(8,128)(2,1)} %get-tuple-element.43), channel_id=1, source_target_pairs={{5,0},{7,2},{13,8},{15,10},{21,16},{23,18},{29,24},{31,26},{0,3},{... | collective-permute-start | bytes 1572872 | tf_op jit(solution)/shard_map/ppermute | solution.py:271
  23.7 1.2 %collective-permute-start = (f32[4,1024]{1,0:T(4,128)S(1)}, f32[4,1024]{1,0:T(4,128)S(1)}, u32[]{:S(2)}, u32[]{:S(2)}) collective-permute-start(f32[4,1024]{1,0:T(4,128)S(1)} %bitcast.18), channel_id=1, source_target_pairs={{0,1},{1,0},{2,3},{3,2},{4,5},{5,4},{6,7},{7,6},{8,9},{9,8},{10,11... | collective-permute-start | bytes 49160 | tf_op jit(solution)/shard_map/ppermute | solution.py:271
  25.0 8.1 %collective-permute-start.4 = (f32[9,1024]{1,0:T(8,128)S(1)}, f32[9,1024]{1,0:T(8,128)S(1)}, u32[]{:S(2)}, u32[]{:S(2)}) collective-permute-start(f32[9,1024]{1,0:T(8,128)S(1)} %pad_maximum_fusion.refs_1_), channel_id=1, source_target_pairs={{12,8},{14,10},{20,16},{22,18},{28,24},{30,26},{1,5},{3,7}} | collective-permute-start | bytes 110600 | tf_op jit(solution)/shard_map/ppermute | solution.py:271
  25.6 1.0 %copy-start.12 = (bf16[256,1024]{1,0:T(8,128)(2,1)S(1)}, bf16[256,1024]{1,0:T(8,128)(2,1)}, u32[]{:S(2)}) copy-start(bf16[256,1024]{1,0:T(8,128)(2,1)} %copy-done.11) | copy-start | bytes 1572868
  26.7 6.4 %copy-start.15 = (bf16[256,1024]{1,0:T(8,128)(2,1)S(1)}, bf16[256,1024]{1,0:T(8,128)(2,1)}, u32[]{:S(2)}) copy-start(bf16[256,1024]{1,0:T(8,128)(2,1)} %copy-done.14) | copy-start | bytes 1572868
  26.7 18.4 %copy-start.13 = (bf16[256,1024]{1,0:T(8,128)(2,1)S(1)}, bf16[256,1024]{1,0:T(8,128)(2,1)}, u32[]{:S(2)}) copy-start(bf16[256,1024]{1,0:T(8,128)(2,1)} %copy-done.11) | copy-start | bytes 1572868
  28.5 11.3 %collective-permute-start.6 = (bf16[256,1024]{1,0:T(8,128)(2,1)S(1)}, bf16[256,1024]{1,0:T(8,128)(2,1)S(1)}, u32[]{:S(2)}, u32[]{:S(2)}) collective-permute-start(bf16[256,1024]{1,0:T(8,128)(2,1)S(1)} %get-tuple-element.49), channel_id=1, source_target_pairs={{5,0},{7,2},{13,8},{15,10},{21,16},{23,18},{29,24},{31,26},{0,3},{... | collective-permute-start | bytes 1572872 | tf_op jit(solution)/shard_map/ppermute | solution.py:271
  33.1 1.0 %copy-start.9 = (bf16[256,1024]{1,0:T(8,128)(2,1)S(1)}, bf16[256,1024]{1,0:T(8,128)(2,1)}, u32[]{:S(2)}) copy-start(bf16[256,1024]{1,0:T(8,128)(2,1)} %copy-done.8) | copy-start | bytes 1572868
  34.6 10.5 %collective-permute-start.8 = (bf16[256,1024]{1,0:T(8,128)(2,1)S(1)}, bf16[256,1024]{1,0:T(8,128)(2,1)S(1)}, u32[]{:S(2)}, u32[]{:S(2)}) collective-permute-start(bf16[256,1024]{1,0:T(8,128)(2,1)S(1)} %get-tuple-element.52), channel_id=1, source_target_pairs={{5,0},{7,2},{13,8},{15,10},{21,16},{23,18},{29,24},{31,26}} | collective-permute-start | bytes 1572872 | tf_op jit(solution)/shard_map/ppermute | solution.py:271
  45.1 14.2 %copy-start.2 = (bf16[256,1024]{1,0:T(8,128)(2,1)}, bf16[256,1024]{1,0:T(8,128)(2,1)S(1)}, u32[]{:S(2)}) copy-start(bf16[256,1024]{1,0:T(8,128)(2,1)S(1)} %collective-permute-done.8.refs_6_.refs_4_.refs_3_) | copy-start | bytes 1572868
  45.5 1.3 %copy-start = (bf16[1024,1024]{1,0:T(8,128)(2,1)}, bf16[1024,1024]{1,0:T(8,128)(2,1)S(1)}, u32[]{:S(2)}) copy-start(bf16[1024,1024]{1,0:T(8,128)(2,1)S(1)} %get-tuple-element.57.refs_2_) | copy-start | bytes 6291460
  46.9 11.8 %collective-permute-start.10 = (bf16[1024,1024]{1,0:T(8,128)(2,1)}, bf16[1024,1024]{1,0:T(8,128)(2,1)S(1)}, u32[]{:S(2)}, u32[]{:S(2)}) collective-permute-start(bf16[1024,1024]{1,0:T(8,128)(2,1)} %copy-done), channel_id=1, source_target_pairs={{1,0},{3,2},{5,4},{7,6},{9,8},{11,10},{13,12},{15,14},{17,16},{19,... | collective-permute-start | bytes 6291464 | tf_op jit(solution)/shard_map/ppermute | solution.py:271
  48.2 10.5 %collective-permute-start.11 = (bf16[256,1024]{1,0:T(8,128)(2,1)S(1)}, bf16[256,1024]{1,0:T(8,128)(2,1)S(1)}, u32[]{:S(2)}, u32[]{:S(2)}) collective-permute-start(bf16[256,1024]{1,0:T(8,128)(2,1)S(1)} %get-tuple-element.58), channel_id=1, source_target_pairs={{5,0},{7,2},{13,8},{15,10},{21,16},{23,18},{29,24},{31,26}} | collective-permute-start | bytes 1572872 | tf_op jit(solution)/shard_map/ppermute | solution.py:271
  49.5 0.7 collective-permute-start.9
  58.7 0.8 copy-start.5
  58.7 0.7 collective-permute-start.12
  59.5 2.8 %collective-permute-start.13 = (bf16[8,1024]{1,0:T(8,128)(2,1)S(1)}, bf16[8,1024]{1,0:T(8,128)(2,1)S(1)}, u32[]{:S(2)}, u32[]{:S(2)}) collective-permute-start(bf16[8,1024]{1,0:T(8,128)(2,1)S(1)} %get-tuple-element.60), channel_id=1, source_target_pairs={{16,24},{18,26}} | collective-permute-start | bytes 49160 | tf_op jit(solution)/shard_map/ppermute | solution.py:271
  60.1 5.6 %copy-start.1 = (bf16[1024,1024]{1,0:T(8,128)(2,1)S(1)}, bf16[1024,1024]{1,0:T(8,128)(2,1)}, u32[]{:S(2)}) copy-start(bf16[1024,1024]{1,0:T(8,128)(2,1)} %copy-done) | copy-start | bytes 6291460
  60.1 7.9 %collective-permute-start.18 = (f32[8,1024]{1,0:T(8,128)S(1)}, f32[8,1024]{1,0:T(8,128)S(1)}, u32[]{:S(2)}, u32[]{:S(2)}) collective-permute-start(f32[8,1024]{1,0:T(8,128)S(1)} %get-tuple-element.71), channel_id=1, source_target_pairs={{5,0},{7,2}} | collective-permute-start | bytes 98312 | tf_op jit(solution)/shard_map/ppermute | solution.py:271
  61.6 6.5 %collective-permute-start.19 = (f32[8,1024]{1,0:T(8,128)S(1)}, f32[8,1024]{1,0:T(8,128)S(1)}, u32[]{:S(2)}, u32[]{:S(2)}) collective-permute-start(f32[8,1024]{1,0:T(8,128)S(1)} %get-tuple-element.71), channel_id=1, source_target_pairs={{5,4},{7,6}} | collective-permute-start | bytes 98312 | tf_op jit(solution)/shard_map/ppermute | solution.py:271
  62.3 1.0 %copy-start.3 = (bf16[256,1024]{1,0:T(8,128)(2,1)S(1)}, bf16[256,1024]{1,0:T(8,128)(2,1)}, u32[]{:S(2)}) copy-start(bf16[256,1024]{1,0:T(8,128)(2,1)} %copy-done.2) | copy-start | bytes 1572868
  63.3 1.0 %copy-start.6 = (bf16[256,1024]{1,0:T(8,128)(2,1)S(1)}, bf16[256,1024]{1,0:T(8,128)(2,1)}, u32[]{:S(2)}) copy-start(bf16[256,1024]{1,0:T(8,128)(2,1)} %copy-done.5) | copy-start | bytes 1572868
  65.0 2.3 %copy-start.4 = (bf16[256,1024]{1,0:T(8,128)(2,1)S(1)}, bf16[256,1024]{1,0:T(8,128)(2,1)}, u32[]{:S(2)}) copy-start(bf16[256,1024]{1,0:T(8,128)(2,1)} %copy-done.2) | copy-start | bytes 1572868
  65.0 2.3 %copy-start.7 = (bf16[256,1024]{1,0:T(8,128)(2,1)S(1)}, bf16[256,1024]{1,0:T(8,128)(2,1)}, u32[]{:S(2)}) copy-start(bf16[256,1024]{1,0:T(8,128)(2,1)} %copy-done.5) | copy-start | bytes 1572868
  65.0 2.3 %collective-permute-start.14 = (bf16[8,1024]{1,0:T(8,128)(2,1)S(1)}, bf16[8,1024]{1,0:T(8,128)(2,1)S(1)}, u32[]{:S(2)}, u32[]{:S(2)}) collective-permute-start(bf16[8,1024]{1,0:T(8,128)(2,1)S(1)} %get-tuple-element.61), channel_id=1, source_target_pairs={{24,16},{26,18}} | collective-permute-start | bytes 49160 | tf_op jit(solution)/shard_map/ppermute | solution.py:271
  67.3 0.7 collective-permute-start.15
  68.1 20.7 %collective-permute-start.16 = (bf16[8,1024]{1,0:T(8,128)(2,1)S(1)}, bf16[8,1024]{1,0:T(8,128)(2,1)S(1)}, u32[]{:S(2)}, u32[]{:S(2)}) collective-permute-start(bf16[8,1024]{1,0:T(8,128)(2,1)S(1)} %get-tuple-element.69), channel_id=1, source_target_pairs={{8,0},{10,2}} | collective-permute-start | bytes 49160 | tf_op jit(solution)/shard_map/ppermute | solution.py:271
  69.4 19.4 %collective-permute-start.17 = (bf16[8,1024]{1,0:T(8,128)(2,1)S(1)}, bf16[8,1024]{1,0:T(8,128)(2,1)S(1)}, u32[]{:S(2)}, u32[]{:S(2)}) collective-permute-start(bf16[8,1024]{1,0:T(8,128)(2,1)S(1)} %get-tuple-element.69), channel_id=1, source_target_pairs={{8,4},{10,6}} | collective-permute-start | bytes 49160 | tf_op jit(solution)/shard_map/ppermute | solution.py:271
  70.1 19.6 %collective-permute-start.20 = (f32[8,1024]{1,0:T(8,128)S(1)}, f32[8,1024]{1,0:T(8,128)S(1)}, u32[]{:S(2)}, u32[]{:S(2)}) collective-permute-start(f32[8,1024]{1,0:T(8,128)S(1)} %select_select_fusion), channel_id=1, source_target_pairs={{8,12},{10,14},{16,20},{18,22},{24,28},{26,30}} | collective-permute-start | bytes 98312 | tf_op jit(solution)/shard_map/ppermute | solution.py:271
  89.7 2.1 %collective-permute-start.21 = (f32[4,1024]{1,0:T(4,128)S(1)}, f32[4,1024]{1,0:T(4,128)S(1)}, u32[]{:S(2)}, u32[]{:S(2)}) collective-permute-start(f32[4,1024]{1,0:T(4,128)S(1)} %slice.16), channel_id=1, source_target_pairs={{0,1},{2,3},{4,5},{6,7},{8,9},{10,11},{12,13},{14,15},{16,17},{18,... | collective-permute-start | bytes 49160 | tf_op jit(solution)/shard_map/ppermute | solution.py:271

commit v12 on v11

--- a/solution.py
+++ b/solution.py
@@ -347,8 +347,6 @@
             other = received[piece]
             if k == SMALL_AT + 2:
                 other = after(other, pair_packed)
-            if k > AHEAD:
-                other = after(other, pair_pieces[order[k - 1]])
             payload, state = combine(
                 current[piece],
                 other,
@@ -372,7 +370,7 @@
     (down_odd,), state = segment(
         coupling, 1, first, small, {}, [[merged], pair_maps], (OWN,), ()
     )
-    merged_first = send(after(merged, state), route(every, 1, 0))
+    merged_first = send(merged, route(every, 1, 0))
     maps = [[merged_first], pair_maps]
     at, core = 1, 1
     kept = []

time: 93.5 us -> 94.6 us (1.012)
  waiting for transfers between devices: 40.9 us -> 43 us
  local copies, waits for them, and re-layouts: 8.93 us -> 10.5 us
  starting transfers between devices: 29.6 us -> 28.3 us
  Pallas kernels: 9.63 us -> 8.62 us
    ppermute x22, waiting for transfers between devices: 40.9 us -> 43 us  [send(): return lax.ppermute(value, AXES, pairs_of_devices)]
    unnamed x38, local copies, waits for them, and re-layouts: 7.86 us -> 9.48 us
    ppermute x22, starting transfers between devices: 29.6 us -> 28.3 us  [send(): return lax.ppermute(value, AXES, pairs_of_devices)]
  transfers between devices with their start and end apart: 22 -> 22, of which waited for: 7 -> 8; matrix products, arithmetic and copies ran while one was open for 3% -> 3% of each run, Pallas kernels for 8% -> 7%
where the time goes in v12:
time: 94.6 us; the launch traced here: 93.8 us
  waiting for transfers between devices  43 us (45%)
  starting transfers between devices  28.3 us (30%)
  local copies, waits for them, and re-layouts  10.5 us (11%)
  Pallas kernels  8.62 us (9%)
  other arithmetic  2.22 us (2%)
  between operations  1.15 us (1%)
    ppermute x22, waiting for transfers between devices, send(): return lax.ppermute(value, AXES, pairs_of_devices)  43 us
    ppermute x22, starting transfers between devices, send(): return lax.ppermute(value, AXES, pairs_of_devices)  28.3 us
    unnamed x38, local copies, waits for them, and re-layouts  9.48 us
    pallas_call x4, Pallas kernels, combine(): pl.pallas_call(functools.partial(combine_kernel, face_at, is_face, follow...  3.41 us
    pallas_call x2, Pallas kernels, leaf_combine(): pl.pallas_call(functools.partial(leaf_kernel, half * rows, is_face, piece...  2.67 us
  transfers between devices with their start and end apart: 22, of which 8 were waited for; matrix products, arithmetic and copies ran while one was open for 3% of the time, Pallas kernels for 7%

profile of v12, /device:TPU:0, one launch (start us, length us, event | category | flops | bytes accessed | tf_op | source)
XLA Modules:
  0.0 93.8 jit_solution(9780398843595129617)
XLA Ops:
  0.6 0.5 collective-permute-start.2
  1.1 0.1 collective-permute-start.1
  1.2 1.1 %fusion.1 = (bf16[256,256]{1,0:T(8,128)(2,1)S(1)}, bf16[256,256]{1,0:T(8,128)(2,1)S(1)}) fusion(f32[1,3,256,256]{3,2,1,0:T(8,128)} %param.7, s32[]{:T(128)S(6)} %select_n.85, s32[]{:T(128)S(6)} %select_n.84), kind=kLoop, calls=%fused_computation.4 | loop fusion | bytes 524296 | tf_op jit(solution)/shard_map/convert_element_type | solution.py:294
  2.3 0.0 copy-start.11
  2.3 1.6 %copy-done.11 = bf16[1,1024,1024]{2,1,0:T(8,128)(2,1)S(1)} copy-done((bf16[1,1024,1024]{2,1,0:T(8,128)(2,1)S(1)}, bf16[1,1024,1024]{2,1,0:T(8,128)(2,1)}, u32[]{:S(2)}) %copy-start.11) | copy-done | bytes 2097176
  3.9 0.7 copy-done.16
  4.6 0.9 %shard_map.68.own = bf16[1024,1024]{1,0:T(8,128)(2,1)S(1)} custom-call(s32[8,8]{1,0:T(8,128)S(1)} %bitcast.16, bf16[1024,1024]{1,0:T(8,128)(2,1)S(1)} %bitcast.14), custom_call_target="tpu_custom_call" | custom-call | flops 1048576 | bytes 4194304 | tf_op jit(solution)/shard_map/pallas_call | solution.py:283
  5.5 0.0 collective-permute-done.1.other_pattern
  5.5 0.0 collective-permute-done.2.other
  5.5 1.3 %shard_map.69 = (bf16[256,1024]{1,0:T(8,128)(2,1)S(1)}, bf16[256,1024]{1,0:T(8,128)(2,1)S(1)}, bf16[256,1024]{1,0:T(8,128)(2,1)S(1)}) custom-call(s32[8,8]{1,0:T(8,128)S(1)} %collective-permute-done.1.other_pattern, bf16[1024,1024]{1,0:T(8,128)(2,1)S(1)} %shard_map.68.own, bf16[1024,1024]{1,0:T(8,128)(2,1)S(1)} %collective-permute-done.2.other, ...), custom_call_target="tpu_custom_call" | custom-call | flops 335544320 | bytes 3145728 | tf_op jit(solution)/shard_map/pallas_call | solution.py:97
  6.9 4.6 %collective-permute-start.3 = (bf16[256,1024]{1,0:T(8,128)(2,1)S(1)}, bf16[256,1024]{1,0:T(8,128)(2,1)S(1)}, u32[]{:S(2)}, u32[]{:S(2)}) collective-permute-start(bf16[256,1024]{1,0:T(8,128)(2,1)S(1)} %get-tuple-element.38.own), channel_id=1, source_target_pairs={{0,3},{2,1},{4,7},{6,5},{8,11},{10,9},{12,15},{14,13},{16,19},{18,... | collective-permute-start | bytes 1572872 | tf_op jit(solution)/shard_map/ppermute | solution.py:271
  11.5 1.3 %collective-permute-start.5 = (bf16[256,1024]{1,0:T(8,128)(2,1)S(1)}, bf16[256,1024]{1,0:T(8,128)(2,1)S(1)}, u32[]{:S(2)}, u32[]{:S(2)}) collective-permute-start(bf16[256,1024]{1,0:T(8,128)(2,1)S(1)} %get-tuple-element.44.own), channel_id=1, source_target_pairs={{0,3},{2,1},{4,7},{6,5},{8,11},{10,9},{12,15},{14,13},{16,19},{18,... | collective-permute-start | bytes 1572872 | tf_op jit(solution)/shard_map/ppermute | solution.py:271
  12.8 1.3 %shard_map.70 = (bf16[256,1024]{1,0:T(8,128)(2,1)S(1)}, bf16[256,1024]{1,0:T(8,128)(2,1)S(1)}) custom-call(s32[8,8]{1,0:T(8,128)S(1)} %collective-permute-done.1.other_pattern, bf16[1024,1024]{1,0:T(8,128)(2,1)S(1)} %shard_map.68.own, bf16[1024,1024]{1,0:T(8,128)(2,1)S(1)} %collective-permute-done.2.other, bf16[256,256]{1,0:T(8,128)(2,1)S(1)} %get-tuple-element.75.inverse, ...), custom_call_target="tpu_custom_call" | custom-call | flops 335544320 | bytes 3145728 | tf_op jit(solution)/shard_map/pallas_call | solution.py:97
  14.1 0.0 copy-start.12
  14.2 4.0 %collective-permute-done.3.other = bf16[256,1024]{1,0:T(8,128)(2,1)S(1)} collective-permute-done((bf16[256,1024]{1,0:T(8,128)(2,1)S(1)}, bf16[256,1024]{1,0:T(8,128)(2,1)S(1)}, u32[]{:S(2)}, u32[]{:S(2)}) %collective-permute-start.3) | collective-permute-done | bytes 524320 | tf_op jit(solution)/shard_map/ppermute | solution.py:271
  18.1 1.3 %shard_map.71 = (bf16[256,1024]{1,0:T(8,128)(2,1)}, bf16[1024,1024]{1,0:T(8,128)(2,1)S(1)}, bf16[256,1024]{1,0:T(8,128)(2,1)S(1)}) custom-call(bf16[256,1024]{1,0:T(8,128)(2,1)S(1)} %get-tuple-element.38.own, bf16[256,1024]{1,0:T(8,128)(2,1)S(1)} %collective-permute-done.3.other, bf16[256,256]{1,0:T(8,128)(2,1)S(1)} %get-tuple-element.74.inverse, ...), custom_call_target="tpu_custom_call" | custom-call | tf_op jit(solution)/shard_map/pallas_call | solution.py:137
  19.4 3.8 %collective-permute-start.7 = (bf16[256,1024]{1,0:T(8,128)(2,1)}, bf16[256,1024]{1,0:T(8,128)(2,1)S(1)}, u32[]{:S(2)}, u32[]{:S(2)}) collective-permute-start(bf16[256,1024]{1,0:T(8,128)(2,1)} %get-tuple-element.41), channel_id=1, source_target_pairs={{5,0},{7,2},{13,8},{15,10},{21,16},{23,18},{29,24},{31,26},{0,3},{... | collective-permute-start | bytes 1572872 | tf_op jit(solution)/shard_map/ppermute | solution.py:271
  23.2 0.5 collective-permute-done.5.other
  23.7 1.3 %shard_map.72 = (bf16[256,1024]{1,0:T(8,128)(2,1)}, bf16[1024,1024]{1,0:T(8,128)(2,1)S(1)}) custom-call(bf16[256,1024]{1,0:T(8,128)(2,1)S(1)} %get-tuple-element.44.own, bf16[256,1024]{1,0:T(8,128)(2,1)S(1)} %collective-permute-done.5.other, bf16[256,256]{1,0:T(8,128)(2,1)S(1)} %get-tuple-element.74.inverse, ...), custom_call_target="tpu_custom_call", output_to_operand_aliasing={{1}: (5, {})} | custom-call | tf_op jit(solution)/shard_map/pallas_call | solution.py:137
  25.0 4.1 %collective-permute-start.6 = (bf16[256,1024]{1,0:T(8,128)(2,1)}, bf16[256,1024]{1,0:T(8,128)(2,1)S(1)}, u32[]{:S(2)}, u32[]{:S(2)}) collective-permute-start(bf16[256,1024]{1,0:T(8,128)(2,1)} %get-tuple-element.47), channel_id=1, source_target_pairs={{5,0},{7,2},{13,8},{15,10},{21,16},{23,18},{29,24},{31,26},{0,3},{... | collective-permute-start | bytes 1572872 | tf_op jit(solution)/shard_map/ppermute | solution.py:271
  29.1 0.1 collective-permute-start
  29.2 1.1 %collective-permute-done = f32[4,1024]{1,0:T(4,128)S(1)} collective-permute-done((f32[4,1024]{1,0:T(4,128)S(1)}, f32[4,1024]{1,0:T(4,128)S(1)}, u32[]{:S(2)}, u32[]{:S(2)}) %collective-permute-start) | collective-permute-done | bytes 16416 | tf_op jit(solution)/shard_map/ppermute | solution.py:271
  30.4 0.7 collective-permute-start.4
  31.1 0.0 collective-permute-done.7.other.refs_5_.refs_3_.refs_2_
  31.1 1.0 %copy-done.10 = bf16[256,1024]{1,0:T(8,128)(2,1)S(1)} copy-done((bf16[256,1024]{1,0:T(8,128)(2,1)S(1)}, bf16[256,1024]{1,0:T(8,128)(2,1)}, u32[]{:S(2)}) %copy-start.10) | copy-done | bytes 524312
  32.1 1.0 %copy-done.15 = bf16[256,1024]{1,0:T(8,128)(2,1)S(1)} copy-done((bf16[256,1024]{1,0:T(8,128)(2,1)S(1)}, bf16[256,1024]{1,0:T(8,128)(2,1)}, u32[]{:S(2)}) %copy-start.15) | copy-done | bytes 524312
  33.2 0.4 shard_map.73
  33.6 2.5 %collective-permute-done.6.other.refs_4_.refs_2_.refs_1_ = bf16[256,1024]{1,0:T(8,128)(2,1)S(1)} collective-permute-done((bf16[256,1024]{1,0:T(8,128)(2,1)}, bf16[256,1024]{1,0:T(8,128)(2,1)S(1)}, u32[]{:S(2)}, u32[]{:S(2)}) %collective-permute-start.6) | collective-permute-done | bytes 524320 | tf_op jit(solution)/shard_map/ppermute | solution.py:271
  36.1 0.4 shard_map.74
  36.5 0.0 copy-start
  36.5 1.3 %copy-done = bf16[1024,1024]{1,0:T(8,128)(2,1)} copy-done((bf16[1024,1024]{1,0:T(8,128)(2,1)}, bf16[1024,1024]{1,0:T(8,128)(2,1)S(1)}, u32[]{:S(2)}) %copy-start) | copy-done | bytes 2097176
  37.8 1.3 %collective-permute-start.9 = (bf16[1024,1024]{1,0:T(8,128)(2,1)}, bf16[1024,1024]{1,0:T(8,128)(2,1)S(1)}, u32[]{:S(2)}, u32[]{:S(2)}) collective-permute-start(bf16[1024,1024]{1,0:T(8,128)(2,1)} %copy-done), channel_id=1, source_target_pairs={{1,0},{3,2},{5,4},{7,6},{9,8},{11,10},{13,12},{15,14},{17,16},{19,... | collective-permute-start | bytes 6291464 | tf_op jit(solution)/shard_map/ppermute | solution.py:271
  39.1 1.3 %collective-permute-start.11 = (bf16[256,1024]{1,0:T(8,128)(2,1)S(1)}, bf16[256,1024]{1,0:T(8,128)(2,1)S(1)}, u32[]{:S(2)}, u32[]{:S(2)}) collective-permute-start(bf16[256,1024]{1,0:T(8,128)(2,1)S(1)} %get-tuple-element.54), channel_id=1, source_target_pairs={{5,0},{7,2},{13,8},{15,10},{21,16},{23,18},{29,24},{31,26}} | collective-permute-start | bytes 1572872 | tf_op jit(solution)/shard_map/ppermute | solution.py:271
  40.4 1.3 %collective-permute-start.10 = (bf16[256,1024]{1,0:T(8,128)(2,1)S(1)}, bf16[256,1024]{1,0:T(8,128)(2,1)S(1)}, u32[]{:S(2)}, u32[]{:S(2)}) collective-permute-start(bf16[256,1024]{1,0:T(8,128)(2,1)S(1)} %get-tuple-element.53), channel_id=1, source_target_pairs={{5,0},{7,2},{13,8},{15,10},{21,16},{23,18},{29,24},{31,26}} | collective-permute-start | bytes 1572872 | tf_op jit(solution)/shard_map/ppermute | solution.py:271
  41.7 0.0 copy-start.1
  41.7 1.6 %copy-done.1 = bf16[1024,1024]{1,0:T(8,128)(2,1)S(1)} copy-done((bf16[1024,1024]{1,0:T(8,128)(2,1)S(1)}, bf16[1024,1024]{1,0:T(8,128)(2,1)}, u32[]{:S(2)}) %copy-start.1) | copy-done | bytes 2097176
  43.3 0.7 collective-permute-start.8
  44.0 0.0 collective-permute-done.8.refs_0_
  44.0 6.8 %collective-permute-done.11.refs_7_.refs_5_.refs_4_ = bf16[256,1024]{1,0:T(8,128)(2,1)S(1)} collective-permute-done((bf16[256,1024]{1,0:T(8,128)(2,1)S(1)}, bf16[256,1024]{1,0:T(8,128)(2,1)S(1)}, u32[]{:S(2)}, u32[]{:S(2)}) %collective-permute-start.11) | collective-permute-done | bytes 524320 | tf_op jit(solution)/shard_map/ppermute | solution.py:271
  50.8 5.6 %collective-permute-done.10.refs_6_.refs_4_.refs_3_ = bf16[256,1024]{1,0:T(8,128)(2,1)S(1)} collective-permute-done((bf16[256,1024]{1,0:T(8,128)(2,1)S(1)}, bf16[256,1024]{1,0:T(8,128)(2,1)S(1)}, u32[]{:S(2)}, u32[]{:S(2)}) %collective-permute-start.10) | collective-permute-done | bytes 524320 | tf_op jit(solution)/shard_map/ppermute | solution.py:271
  56.4 0.0 collective-permute-done.9.refs_2_.refs_7_.refs_0_
  56.4 0.7 collective-permute-start.12
  57.1 0.0 collective-permute-done.12.refs_0_
  57.1 0.1 copy-done.6
  57.2 0.7 collective-permute-start.13
  57.9 0.0 copy-start.2
  57.9 0.8 collective-permute-start.19
  58.7 1.3 %collective-permute-start.18 = (f32[8,1024]{1,0:T(8,128)S(1)}, f32[8,1024]{1,0:T(8,128)S(1)}, u32[]{:S(2)}, u32[]{:S(2)}) collective-permute-start(f32[8,1024]{1,0:T(8,128)S(1)} %get-tuple-element.67), channel_id=1, source_target_pairs={{5,0},{7,2}} | collective-permute-start | bytes 98312 | tf_op jit(solution)/shard_map/ppermute | solution.py:271
  60.0 0.0 collective-permute-done.13.refs_0_
  60.0 1.0 %copy-done.4 = bf16[256,1024]{1,0:T(8,128)(2,1)S(1)} copy-done((bf16[256,1024]{1,0:T(8,128)(2,1)S(1)}, bf16[256,1024]{1,0:T(8,128)(2,1)}, u32[]{:S(2)}) %copy-start.4) | copy-done | bytes 524312
  61.1 1.0 %copy-done.7 = bf16[256,1024]{1,0:T(8,128)(2,1)S(1)} copy-done((bf16[256,1024]{1,0:T(8,128)(2,1)S(1)}, bf16[256,1024]{1,0:T(8,128)(2,1)}, u32[]{:S(2)}) %copy-start.7) | copy-done | bytes 524312
  62.1 0.6 shard_map.78
  62.7 0.8 collective-permute-start.14
  63.5 1.5 %broadcast_select_fusion = bf16[1024,1024]{1,0:T(8,128)(2,1)} fusion(bf16[1024,1024]{1,0:T(8,128)(2,1)S(1)} %copy-done.2, bf16[1024,1024]{1,0:T(8,128)(2,1)S(1)} %collective-permute-done.9.refs_2_.refs_7_.refs_0_, pred[]{:T(512)S(6)} %eq.18), kind=kLoop, calls=%fused_computation | loop fusion | flops 1048576 | bytes 6291457 | tf_op jit(solution)/shard_map/jit(_where)/select_n | solution.py:393
  65.1 0.0 collective-permute-done.14.refs_0_
  65.1 0.7 collective-permute-start.15
  65.9 0.7 collective-permute-start.17
  66.5 1.3 %collective-permute-start.16 = (bf16[8,1024]{1,0:T(8,128)(2,1)S(1)}, bf16[8,1024]{1,0:T(8,128)(2,1)S(1)}, u32[]{:S(2)}, u32[]{:S(2)}) collective-permute-start(bf16[8,1024]{1,0:T(8,128)(2,1)S(1)} %get-tuple-element.65), channel_id=1, source_target_pairs={{8,0},{10,2}} | collective-permute-start | bytes 49160 | tf_op jit(solution)/shard_map/ppermute | solution.py:271
  67.9 0.7 collective-permute-start.20
  68.5 21.6 %collective-permute-done.16.from_pair = bf16[8,1024]{1,0:T(8,128)(2,1)S(1)} collective-permute-done((bf16[8,1024]{1,0:T(8,128)(2,1)S(1)}, bf16[8,1024]{1,0:T(8,128)(2,1)S(1)}, u32[]{:S(2)}, u32[]{:S(2)}) %collective-permute-start.16) | collective-permute-done | bytes 16416 | tf_op jit(solution)/shard_map/ppermute | solution.py:271
  90.1 0.9 %shard_map.81 = f32[8,1024]{1,0:T(8,128)S(1)} custom-call(s32[1]{0:T(128)} %bitcast.6.odd, bf16[8,1024]{1,0:T(8,128)(2,1)S(1)} %collective-permute-done.16.from_pair, bf16[8,1024]{1,0:T(8,128)(2,1)S(1)} %collective-permute-done.17.from_own, f32[8,1024]{1,0:T(8,128)S(1)} %pad_maximum_fusion.1.source, f32[8,1024]{1,0:T(8,128)S(1)} %add.30.down_odd, ...), custom_call_target="tpu_custom_call" | custom-call | flops 1610612736 | bytes 6291456 | tf_op jit(solution)/shard_map/pallas_call | solution.py:415
  91.1 1.3 %collective-permute-start.21 = (f32[4,1024]{1,0:T(4,128)S(1)}, f32[4,1024]{1,0:T(4,128)S(1)}, u32[]{:S(2)}, u32[]{:S(2)}) collective-permute-start(f32[4,1024]{1,0:T(4,128)S(1)} %slice.16), channel_id=1, source_target_pairs={{0,1},{2,3},{4,5},{6,7},{8,9},{10,11},{12,13},{14,15},{16,17},{18,... | collective-permute-start | bytes 49160 | tf_op jit(solution)/shard_map/ppermute | solution.py:271
  92.4 0.8 collective-permute-done.21
  93.2 0.6 fusion.2
  (44 shorter events, 0.2 us)
Async XLA Ops:
  0.6 4.9 %collective-permute-start.2 = (bf16[1024,1024]{1,0:T(8,128)(2,1)}, bf16[1024,1024]{1,0:T(8,128)(2,1)S(1)}, u32[]{:S(2)}, u32[]{:S(2)}) collective-permute-start(bf16[1024,1024]{1,0:T(8,128)(2,1)} %bitcast.13), channel_id=1, source_target_pairs={{0,1},{1,0},{2,3},{3,2},{4,5},{5,4},{6,7},{7,6},{8,9},{9,8},{10,11... | collective-permute-start | bytes 6291464 | tf_op jit(solution)/shard_map/ppermute | solution.py:271
  1.1 4.4 %collective-permute-start.1 = (s32[8,8]{1,0:T(8,128)}, s32[8,8]{1,0:T(8,128)S(1)}, u32[]{:S(2)}, u32[]{:S(2)}) collective-permute-start(s32[8,8]{1,0:T(8,128)} %bitcast.15), channel_id=1, source_target_pairs={{0,1},{1,0},{2,3},{3,2},{4,5},{5,4},{6,7},{7,6},{8,9},{9,8},{10,11... | collective-permute-start | bytes 776 | tf_op jit(solution)/shard_map/ppermute | solution.py:271
  2.3 1.6 %copy-start.11 = (bf16[1,1024,1024]{2,1,0:T(8,128)(2,1)S(1)}, bf16[1,1024,1024]{2,1,0:T(8,128)(2,1)}, u32[]{:S(2)}) copy-start(bf16[1,1024,1024]{2,1,0:T(8,128)(2,1)} %param.5) | copy-start | bytes 6291460
  3.9 0.7 copy-start.16
  6.9 11.2 %collective-permute-start.3 = (bf16[256,1024]{1,0:T(8,128)(2,1)S(1)}, bf16[256,1024]{1,0:T(8,128)(2,1)S(1)}, u32[]{:S(2)}, u32[]{:S(2)}) collective-permute-start(bf16[256,1024]{1,0:T(8,128)(2,1)S(1)} %get-tuple-element.38.own), channel_id=1, source_target_pairs={{0,3},{2,1},{4,7},{6,5},{8,11},{10,9},{12,15},{14,13},{16,19},{18,... | collective-permute-start | bytes 1572872 | tf_op jit(solution)/shard_map/ppermute | solution.py:271
  11.5 12.3 %collective-permute-start.5 = (bf16[256,1024]{1,0:T(8,128)(2,1)S(1)}, bf16[256,1024]{1,0:T(8,128)(2,1)S(1)}, u32[]{:S(2)}, u32[]{:S(2)}) collective-permute-start(bf16[256,1024]{1,0:T(8,128)(2,1)S(1)} %get-tuple-element.44.own), channel_id=1, source_target_pairs={{0,3},{2,1},{4,7},{6,5},{8,11},{10,9},{12,15},{14,13},{16,19},{18,... | collective-permute-start | bytes 1572872 | tf_op jit(solution)/shard_map/ppermute | solution.py:271
  14.1 10.9 %copy-start.12 = (bf16[256,1024]{1,0:T(8,128)(2,1)}, bf16[256,1024]{1,0:T(8,128)(2,1)S(1)}, u32[]{:S(2)}) copy-start(bf16[256,1024]{1,0:T(8,128)(2,1)S(1)} %get-tuple-element.43.refs_0_.own) | copy-start | bytes 1572868
  14.1 10.9 %copy-start.14 = (bf16[256,1024]{1,0:T(8,128)(2,1)}, bf16[256,1024]{1,0:T(8,128)(2,1)S(1)}, u32[]{:S(2)}) copy-start(bf16[256,1024]{1,0:T(8,128)(2,1)S(1)} %get-tuple-element.40.refs_0_.own) | copy-start | bytes 1572868
  19.4 5.6 %copy-start.9 = (bf16[256,1024]{1,0:T(8,128)(2,1)}, bf16[256,1024]{1,0:T(8,128)(2,1)S(1)}, u32[]{:S(2)}) copy-start(bf16[256,1024]{1,0:T(8,128)(2,1)S(1)} %get-tuple-element.45.refs_1_.refs_0_) | copy-start | bytes 1572868
  19.4 11.7 %collective-permute-start.7 = (bf16[256,1024]{1,0:T(8,128)(2,1)}, bf16[256,1024]{1,0:T(8,128)(2,1)S(1)}, u32[]{:S(2)}, u32[]{:S(2)}) collective-permute-start(bf16[256,1024]{1,0:T(8,128)(2,1)} %get-tuple-element.41), channel_id=1, source_target_pairs={{5,0},{7,2},{13,8},{15,10},{21,16},{23,18},{29,24},{31,26},{0,3},{... | collective-permute-start | bytes 1572872 | tf_op jit(solution)/shard_map/ppermute | solution.py:271
  23.7 5.4 %copy-start.17 = (f32[1,4,1024]{2,1,0:T(4,128)S(1)}, f32[1,4,1024]{2,1,0:T(4,128)}, u32[]{:S(2)}) copy-start(f32[1,4,1024]{2,1,0:T(4,128)} %param.9) | copy-start | bytes 49156
  23.7 5.5 %copy-start.18 = (s32[1,1024]{1,0:T(1,128)S(1)}, s32[1,1024]{1,0:T(1,128)}, u32[]{:S(2)}) copy-start(s32[1,1024]{1,0:T(1,128)} %param.8) | copy-start | bytes 12292
  25.0 11.1 %collective-permute-start.6 = (bf16[256,1024]{1,0:T(8,128)(2,1)}, bf16[256,1024]{1,0:T(8,128)(2,1)S(1)}, u32[]{:S(2)}, u32[]{:S(2)}) collective-permute-start(bf16[256,1024]{1,0:T(8,128)(2,1)} %get-tuple-element.47), channel_id=1, source_target_pairs={{5,0},{7,2},{13,8},{15,10},{21,16},{23,18},{29,24},{31,26},{0,3},{... | collective-permute-start | bytes 1572872 | tf_op jit(solution)/shard_map/ppermute | solution.py:271
  29.1 1.2 %collective-permute-start = (f32[4,1024]{1,0:T(4,128)S(1)}, f32[4,1024]{1,0:T(4,128)S(1)}, u32[]{:S(2)}, u32[]{:S(2)}) collective-permute-start(f32[4,1024]{1,0:T(4,128)S(1)} %bitcast.18), channel_id=1, source_target_pairs={{0,1},{1,0},{2,3},{3,2},{4,5},{5,4},{6,7},{7,6},{8,9},{9,8},{10,11... | collective-permute-start | bytes 49160 | tf_op jit(solution)/shard_map/ppermute | solution.py:271
  30.4 0.7 collective-permute-start.4
  31.1 1.0 %copy-start.10 = (bf16[256,1024]{1,0:T(8,128)(2,1)S(1)}, bf16[256,1024]{1,0:T(8,128)(2,1)}, u32[]{:S(2)}) copy-start(bf16[256,1024]{1,0:T(8,128)(2,1)} %copy-done.9) | copy-start | bytes 1572868
  32.1 1.0 %copy-start.15 = (bf16[256,1024]{1,0:T(8,128)(2,1)S(1)}, bf16[256,1024]{1,0:T(8,128)(2,1)}, u32[]{:S(2)}) copy-start(bf16[256,1024]{1,0:T(8,128)(2,1)} %copy-done.14) | copy-start | bytes 1572868
  33.1 2.9 %copy-start.13 = (bf16[256,1024]{1,0:T(8,128)(2,1)S(1)}, bf16[256,1024]{1,0:T(8,128)(2,1)}, u32[]{:S(2)}) copy-start(bf16[256,1024]{1,0:T(8,128)(2,1)} %copy-done.12) | copy-start | bytes 1572868
  36.5 1.3 %copy-start = (bf16[1024,1024]{1,0:T(8,128)(2,1)}, bf16[1024,1024]{1,0:T(8,128)(2,1)S(1)}, u32[]{:S(2)}) copy-start(bf16[1024,1024]{1,0:T(8,128)(2,1)S(1)} %get-tuple-element.51.refs_2_) | copy-start | bytes 6291460
  37.8 18.6 %collective-permute-start.9 = (bf16[1024,1024]{1,0:T(8,128)(2,1)}, bf16[1024,1024]{1,0:T(8,128)(2,1)S(1)}, u32[]{:S(2)}, u32[]{:S(2)}) collective-permute-start(bf16[1024,1024]{1,0:T(8,128)(2,1)} %copy-done), channel_id=1, source_target_pairs={{1,0},{3,2},{5,4},{7,6},{9,8},{11,10},{13,12},{15,14},{17,16},{19,... | collective-permute-start | bytes 6291464 | tf_op jit(solution)/shard_map/ppermute | solution.py:271
  39.1 11.7 %collective-permute-start.11 = (bf16[256,1024]{1,0:T(8,128)(2,1)S(1)}, bf16[256,1024]{1,0:T(8,128)(2,1)S(1)}, u32[]{:S(2)}, u32[]{:S(2)}) collective-permute-start(bf16[256,1024]{1,0:T(8,128)(2,1)S(1)} %get-tuple-element.54), channel_id=1, source_target_pairs={{5,0},{7,2},{13,8},{15,10},{21,16},{23,18},{29,24},{31,26}} | collective-permute-start | bytes 1572872 | tf_op jit(solution)/shard_map/ppermute | solution.py:271
  40.4 16.0 %collective-permute-start.10 = (bf16[256,1024]{1,0:T(8,128)(2,1)S(1)}, bf16[256,1024]{1,0:T(8,128)(2,1)S(1)}, u32[]{:S(2)}, u32[]{:S(2)}) collective-permute-start(bf16[256,1024]{1,0:T(8,128)(2,1)S(1)} %get-tuple-element.53), channel_id=1, source_target_pairs={{5,0},{7,2},{13,8},{15,10},{21,16},{23,18},{29,24},{31,26}} | collective-permute-start | bytes 1572872 | tf_op jit(solution)/shard_map/ppermute | solution.py:271
  41.7 1.6 %copy-start.1 = (bf16[1024,1024]{1,0:T(8,128)(2,1)S(1)}, bf16[1024,1024]{1,0:T(8,128)(2,1)}, u32[]{:S(2)}) copy-start(bf16[1024,1024]{1,0:T(8,128)(2,1)} %copy-done) | copy-start | bytes 6291460
  43.3 0.7 collective-permute-start.8
  50.8 6.3 %copy-start.3 = (bf16[256,1024]{1,0:T(8,128)(2,1)}, bf16[256,1024]{1,0:T(8,128)(2,1)S(1)}, u32[]{:S(2)}) copy-start(bf16[256,1024]{1,0:T(8,128)(2,1)S(1)} %collective-permute-done.11.refs_7_.refs_5_.refs_4_) | copy-start | bytes 1572868
  56.4 0.8 copy-start.6
  56.4 0.7 collective-permute-start.12
  57.2 2.8 %collective-permute-start.13 = (bf16[8,1024]{1,0:T(8,128)(2,1)S(1)}, bf16[8,1024]{1,0:T(8,128)(2,1)S(1)}, u32[]{:S(2)}, u32[]{:S(2)}) collective-permute-start(bf16[8,1024]{1,0:T(8,128)(2,1)S(1)} %get-tuple-element.56), channel_id=1, source_target_pairs={{16,24},{18,26}} | collective-permute-start | bytes 49160 | tf_op jit(solution)/shard_map/ppermute | solution.py:271
  57.9 5.6 %copy-start.2 = (bf16[1024,1024]{1,0:T(8,128)(2,1)S(1)}, bf16[1024,1024]{1,0:T(8,128)(2,1)}, u32[]{:S(2)}) copy-start(bf16[1024,1024]{1,0:T(8,128)(2,1)} %copy-done) | copy-start | bytes 6291460
  57.9 7.9 %collective-permute-start.19 = (f32[8,1024]{1,0:T(8,128)S(1)}, f32[8,1024]{1,0:T(8,128)S(1)}, u32[]{:S(2)}, u32[]{:S(2)}) collective-permute-start(f32[8,1024]{1,0:T(8,128)S(1)} %get-tuple-element.67), channel_id=1, source_target_pairs={{5,4},{7,6}} | collective-permute-start | bytes 98312 | tf_op jit(solution)/shard_map/ppermute | solution.py:271
  58.7 7.1 %collective-permute-start.18 = (f32[8,1024]{1,0:T(8,128)S(1)}, f32[8,1024]{1,0:T(8,128)S(1)}, u32[]{:S(2)}, u32[]{:S(2)}) collective-permute-start(f32[8,1024]{1,0:T(8,128)S(1)} %get-tuple-element.67), channel_id=1, source_target_pairs={{5,0},{7,2}} | collective-permute-start | bytes 98312 | tf_op jit(solution)/shard_map/ppermute | solution.py:271
  60.0 1.0 %copy-start.4 = (bf16[256,1024]{1,0:T(8,128)(2,1)S(1)}, bf16[256,1024]{1,0:T(8,128)(2,1)}, u32[]{:S(2)}) copy-start(bf16[256,1024]{1,0:T(8,128)(2,1)} %copy-done.3) | copy-start | bytes 1572868
  61.1 1.0 %copy-start.7 = (bf16[256,1024]{1,0:T(8,128)(2,1)S(1)}, bf16[256,1024]{1,0:T(8,128)(2,1)}, u32[]{:S(2)}) copy-start(bf16[256,1024]{1,0:T(8,128)(2,1)} %copy-done.6) | copy-start | bytes 1572868
  62.7 2.3 %copy-start.5 = (bf16[256,1024]{1,0:T(8,128)(2,1)S(1)}, bf16[256,1024]{1,0:T(8,128)(2,1)}, u32[]{:S(2)}) copy-start(bf16[256,1024]{1,0:T(8,128)(2,1)} %copy-done.3) | copy-start | bytes 1572868
  62.7 2.3 %copy-start.8 = (bf16[256,1024]{1,0:T(8,128)(2,1)S(1)}, bf16[256,1024]{1,0:T(8,128)(2,1)}, u32[]{:S(2)}) copy-start(bf16[256,1024]{1,0:T(8,128)(2,1)} %copy-done.6) | copy-start | bytes 1572868
  62.7 2.3 %collective-permute-start.14 = (bf16[8,1024]{1,0:T(8,128)(2,1)S(1)}, bf16[8,1024]{1,0:T(8,128)(2,1)S(1)}, u32[]{:S(2)}, u32[]{:S(2)}) collective-permute-start(bf16[8,1024]{1,0:T(8,128)(2,1)S(1)} %get-tuple-element.57), channel_id=1, source_target_pairs={{24,16},{26,18}} | collective-permute-start | bytes 49160 | tf_op jit(solution)/shard_map/ppermute | solution.py:271
  65.1 0.7 collective-permute-start.15
  65.9 2.7 %collective-permute-start.17 = (bf16[8,1024]{1,0:T(8,128)(2,1)S(1)}, bf16[8,1024]{1,0:T(8,128)(2,1)S(1)}, u32[]{:S(2)}, u32[]{:S(2)}) collective-permute-start(bf16[8,1024]{1,0:T(8,128)(2,1)S(1)} %get-tuple-element.65), channel_id=1, source_target_pairs={{8,4},{10,6}} | collective-permute-start | bytes 49160 | tf_op jit(solution)/shard_map/ppermute | solution.py:271
  66.5 23.6 %collective-permute-start.16 = (bf16[8,1024]{1,0:T(8,128)(2,1)S(1)}, bf16[8,1024]{1,0:T(8,128)(2,1)S(1)}, u32[]{:S(2)}, u32[]{:S(2)}) collective-permute-start(bf16[8,1024]{1,0:T(8,128)(2,1)S(1)} %get-tuple-element.65), channel_id=1, source_target_pairs={{8,0},{10,2}} | collective-permute-start | bytes 49160 | tf_op jit(solution)/shard_map/ppermute | solution.py:271
  67.9 23.2 %collective-permute-start.20 = (f32[8,1024]{1,0:T(8,128)S(1)}, f32[8,1024]{1,0:T(8,128)S(1)}, u32[]{:S(2)}, u32[]{:S(2)}) collective-permute-start(f32[8,1024]{1,0:T(8,128)S(1)} %select_select_fusion), channel_id=1, source_target_pairs={{8,12},{10,14},{16,20},{18,22},{24,28},{26,30}} | collective-permute-start | bytes 98312 | tf_op jit(solution)/shard_map/ppermute | solution.py:271
  91.1 2.1 %collective-permute-start.21 = (f32[4,1024]{1,0:T(4,128)S(1)}, f32[4,1024]{1,0:T(4,128)S(1)}, u32[]{:S(2)}, u32[]{:S(2)}) collective-permute-start(f32[4,1024]{1,0:T(4,128)S(1)} %slice.16), channel_id=1, source_target_pairs={{0,1},{2,3},{4,5},{6,7},{8,9},{10,11},{12,13},{14,15},{16,17},{18,... | collective-permute-start | bytes 49160 | tf_op jit(solution)/shard_map/ppermute | solution.py:271

commit v13 on v11

--- a/solution.py
+++ b/solution.py
@@ -234,12 +234,18 @@
     return results[:-1], results[-1]
 
 
-def last_kernel(coupling, count, odd, from_pair, from_own, source, down_odd, *refs):
+def last_kernel(coupling, count, from_pair, from_own, source, down_odd, *refs):
     own, pair, out = refs[:1], refs[1 : 1 + count], refs[1 + count]
-    total = gather_sum(pair, from_pair[...]) + gather_sum(own, from_own[...])
-    up_odd = down_odd[...] + coupling * total
-    up_even = source[...] + coupling * gather_sum(own, up_odd.astype(jnp.bfloat16))
-    out[...] = jnp.where(odd[0] == 1, up_odd, up_even)
+    layer = lax.axis_index("layer")
+
+    @pl.when(layer == 0)
+    def _():
+        up_odd = down_odd[...] + coupling * gather_sum(pair, from_pair[...])
+        out[...] = source[...] + coupling * gather_sum(own, up_odd.astype(jnp.bfloat16))
+
+    @pl.when(layer == 1)
+    def _():
+        out[...] = down_odd[...] + coupling * gather_sum(own, from_own[...])
 
 
 def on_device(box_maps, block_pattern, face_inverses, index_map, sources):
@@ -413,15 +419,14 @@
             mine[slot] = jnp.where(layer == target, values[slot], mine[slot])
     settled = mine[OWN] + send(mine[PAIR], route([(z, a) for a, z in pair_moves[1:]]))
 
-    odd = (layer % 2).astype(jnp.int32)[None]
     last = pl.pallas_call(
         functools.partial(last_kernel, coupling, len(pair_maps)),
         out_shape=jax.ShapeDtypeStruct((rows, width), jnp.float32),
-        in_specs=[SMEM] + [VMEM] * (5 + len(pair_maps)),
+        in_specs=[VMEM] * (5 + len(pair_maps)),
         out_specs=VMEM,
         compiler_params=SWEEP_PARAMS,
         cost_estimate=cost(6 * 256 * 1024 * 1024, 6 * 1024 * 1024),
-    )(odd, from_pair, from_own, packed[:rows], down_odd, merged_first, *pair_maps)
+    )(from_pair, from_own, packed[:rows], down_odd, merged_first, *pair_maps)
     upward = jnp.where(layer < 2, last, settled)
     second_rows = send(upward[rows_here : 2 * rows_here], route(every, 0, 1))
     upward = jnp.where(is_second, second_rows, upward[:rows_here])

time: 93.5 us -> 93 us (level)
  no operation moved by 1% of the time
where the time goes in v13:
time: 93 us; the launch traced here: 92.2 us
  waiting for transfers between devices  40.9 us (44%)
  starting transfers between devices  29.6 us (32%)
  Pallas kernels  9.39 us (10%)
  local copies, waits for them, and re-layouts  8.93 us (10%)
  other arithmetic  2.22 us (2%)
  between operations  1.15 us (1%)
    ppermute x22, waiting for transfers between devices, send(): return lax.ppermute(value, AXES, pairs_of_devices)  40.9 us
    ppermute x22, starting transfers between devices, send(): return lax.ppermute(value, AXES, pairs_of_devices)  29.6 us
    unnamed x38, local copies, waits for them, and re-layouts  7.86 us
    pallas_call x4, Pallas kernels, combine(): pl.pallas_call(functools.partial(combine_kernel, face_at, is_face, follow...  3.9 us
    pallas_call x2, Pallas kernels, leaf_combine(): pl.pallas_call(functools.partial(leaf_kernel, half * rows, is_face, piece...  3.17 us
  transfers between devices with their start and end apart: 22, of which 7 were waited for; matrix products, arithmetic and copies ran while one was open for 3% of the time, Pallas kernels for 8%

profile of v13, /device:TPU:0, one launch (start us, length us, event | category | flops | bytes accessed | tf_op | source)
XLA Modules:
  0.0 92.2 jit_solution(16380039330491016101)
XLA Ops:
  0.6 0.5 collective-permute-start.2
  1.1 0.1 collective-permute-start.1
  1.2 1.1 %fusion.1 = (bf16[256,256]{1,0:T(8,128)(2,1)S(1)}, bf16[256,256]{1,0:T(8,128)(2,1)S(1)}) fusion(f32[1,3,256,256]{3,2,1,0:T(8,128)} %param.7, s32[]{:T(128)S(6)} %select_n.81, s32[]{:T(128)S(6)} %select_n.80), kind=kLoop, calls=%fused_computation.4 | loop fusion | bytes 524296 | tf_op jit(solution)/shard_map/convert_element_type | solution.py:300
  2.3 0.0 copy-start.10
  2.3 1.6 %copy-done.10 = bf16[1,1024,1024]{2,1,0:T(8,128)(2,1)S(1)} copy-done((bf16[1,1024,1024]{2,1,0:T(8,128)(2,1)S(1)}, bf16[1,1024,1024]{2,1,0:T(8,128)(2,1)}, u32[]{:S(2)}) %copy-start.10) | copy-done | bytes 2097176
  3.9 0.7 copy-done.16
  4.6 0.9 %shard_map.68.own = bf16[1024,1024]{1,0:T(8,128)(2,1)S(1)} custom-call(s32[8,8]{1,0:T(8,128)S(1)} %bitcast.15, bf16[1024,1024]{1,0:T(8,128)(2,1)S(1)} %bitcast.13), custom_call_target="tpu_custom_call" | custom-call | flops 1048576 | bytes 4194304 | tf_op jit(solution)/shard_map/pallas_call | solution.py:289
  5.5 0.0 collective-permute-done.1.other_pattern
  5.5 0.0 collective-permute-done.2.other
  5.5 1.8 %shard_map.69 = (bf16[256,1024]{1,0:T(8,128)(2,1)}, bf16[256,1024]{1,0:T(8,128)(2,1)S(1)}, bf16[256,1024]{1,0:T(8,128)(2,1)S(1)}) custom-call(s32[8,8]{1,0:T(8,128)S(1)} %collective-permute-done.1.other_pattern, bf16[1024,1024]{1,0:T(8,128)(2,1)S(1)} %shard_map.68.own, bf16[1024,1024]{1,0:T(8,128)(2,1)S(1)} %collective-permute-done.2.other, ...), custom_call_target="tpu_custom_call" | custom-call | flops 335544320 | bytes 3145728 | tf_op jit(solution)/shard_map/pallas_call | solution.py:97
  7.4 4.6 %collective-permute-start.3 = (bf16[256,1024]{1,0:T(8,128)(2,1)S(1)}, bf16[256,1024]{1,0:T(8,128)(2,1)S(1)}, u32[]{:S(2)}, u32[]{:S(2)}) collective-permute-start(bf16[256,1024]{1,0:T(8,128)(2,1)S(1)} %get-tuple-element.40.own), channel_id=1, source_target_pairs={{0,3},{2,1},{4,7},{6,5},{8,11},{10,9},{12,15},{14,13},{16,19},{18,... | collective-permute-start | bytes 1572872 | tf_op jit(solution)/shard_map/ppermute | solution.py:277
  11.9 2.1 %collective-permute-start.5 = (bf16[256,1024]{1,0:T(8,128)(2,1)}, bf16[256,1024]{1,0:T(8,128)(2,1)}, u32[]{:S(2)}, u32[]{:S(2)}) collective-permute-start(bf16[256,1024]{1,0:T(8,128)(2,1)} %get-tuple-element.46.own), channel_id=1, source_target_pairs={{0,3},{2,1},{4,7},{6,5},{8,11},{10,9},{12,15},{14,13},{16,19},{18,... | collective-permute-start | bytes 1572872 | tf_op jit(solution)/shard_map/ppermute | solution.py:277
  14.0 1.3 %shard_map.70 = (bf16[256,1024]{1,0:T(8,128)(2,1)S(1)}, bf16[256,1024]{1,0:T(8,128)(2,1)S(1)}) custom-call(s32[8,8]{1,0:T(8,128)S(1)} %collective-permute-done.1.other_pattern, bf16[1024,1024]{1,0:T(8,128)(2,1)S(1)} %shard_map.68.own, bf16[1024,1024]{1,0:T(8,128)(2,1)S(1)} %collective-permute-done.2.other, bf16[256,256]{1,0:T(8,128)(2,1)S(1)} %get-tuple-element.79.inverse, ...), custom_call_target="tpu_custom_call" | custom-call | flops 335544320 | bytes 3145728 | tf_op jit(solution)/shard_map/pallas_call | solution.py:97
  15.4 3.2 %collective-permute-done.3.other = bf16[256,1024]{1,0:T(8,128)(2,1)S(1)} collective-permute-done((bf16[256,1024]{1,0:T(8,128)(2,1)S(1)}, bf16[256,1024]{1,0:T(8,128)(2,1)S(1)}, u32[]{:S(2)}, u32[]{:S(2)}) %collective-permute-start.3) | collective-permute-done | bytes 524320 | tf_op jit(solution)/shard_map/ppermute | solution.py:277
  18.6 1.3 %shard_map.71 = (bf16[256,1024]{1,0:T(8,128)(2,1)}, bf16[1024,1024]{1,0:T(8,128)(2,1)S(1)}, bf16[256,1024]{1,0:T(8,128)(2,1)S(1)}) custom-call(bf16[256,1024]{1,0:T(8,128)(2,1)S(1)} %get-tuple-element.40.own, bf16[256,1024]{1,0:T(8,128)(2,1)S(1)} %collective-permute-done.3.other, bf16[256,256]{1,0:T(8,128)(2,1)S(1)} %get-tuple-element.78.inverse, ...), custom_call_target="tpu_custom_call" | custom-call | tf_op jit(solution)/shard_map/pallas_call | solution.py:137
  19.9 3.8 %collective-permute-start.7 = (bf16[256,1024]{1,0:T(8,128)(2,1)}, bf16[256,1024]{1,0:T(8,128)(2,1)S(1)}, u32[]{:S(2)}, u32[]{:S(2)}) collective-permute-start(bf16[256,1024]{1,0:T(8,128)(2,1)} %get-tuple-element.43), channel_id=1, source_target_pairs={{5,0},{7,2},{13,8},{15,10},{21,16},{23,18},{29,24},{31,26},{0,3},{... | collective-permute-start | bytes 1572872 | tf_op jit(solution)/shard_map/ppermute | solution.py:277
  23.7 0.1 collective-permute-start
  23.8 1.1 %collective-permute-done = f32[4,1024]{1,0:T(4,128)S(1)} collective-permute-done((f32[4,1024]{1,0:T(4,128)S(1)}, f32[4,1024]{1,0:T(4,128)S(1)}, u32[]{:S(2)}, u32[]{:S(2)}) %collective-permute-start) | collective-permute-done | bytes 16416 | tf_op jit(solution)/shard_map/ppermute | solution.py:277
  25.0 0.7 collective-permute-start.4
  25.6 0.0 collective-permute-done.5.other
  25.6 1.0 %copy-done.12 = bf16[256,1024]{1,0:T(8,128)(2,1)S(1)} copy-done((bf16[256,1024]{1,0:T(8,128)(2,1)S(1)}, bf16[256,1024]{1,0:T(8,128)(2,1)}, u32[]{:S(2)}) %copy-start.12) | copy-done | bytes 524312
  26.7 1.8 %shard_map.72 = (bf16[256,1024]{1,0:T(8,128)(2,1)S(1)}, bf16[1024,1024]{1,0:T(8,128)(2,1)S(1)}) custom-call(bf16[256,1024]{1,0:T(8,128)(2,1)} %get-tuple-element.46.own, bf16[256,1024]{1,0:T(8,128)(2,1)} %collective-permute-done.5.other, bf16[256,256]{1,0:T(8,128)(2,1)S(1)} %get-tuple-element.78.inverse, ...), custom_call_target="tpu_custom_call", output_to_operand_aliasing={{1}: (5, {})} | custom-call | tf_op jit(solution)/shard_map/pallas_call | solution.py:137
  28.5 4.6 %collective-permute-start.6 = (bf16[256,1024]{1,0:T(8,128)(2,1)S(1)}, bf16[256,1024]{1,0:T(8,128)(2,1)S(1)}, u32[]{:S(2)}, u32[]{:S(2)}) collective-permute-start(bf16[256,1024]{1,0:T(8,128)(2,1)S(1)} %get-tuple-element.49), channel_id=1, source_target_pairs={{5,0},{7,2},{13,8},{15,10},{21,16},{23,18},{29,24},{31,26},{0,3},{... | collective-permute-start | bytes 1572872 | tf_op jit(solution)/shard_map/ppermute | solution.py:277
  33.1 0.0 collective-permute-done.4.refs_3_
  33.1 0.0 collective-permute-done.7.other.refs_5_.refs_3_.refs_2_
  33.1 1.0 %copy-done.9 = bf16[256,1024]{1,0:T(8,128)(2,1)S(1)} copy-done((bf16[256,1024]{1,0:T(8,128)(2,1)S(1)}, bf16[256,1024]{1,0:T(8,128)(2,1)}, u32[]{:S(2)}) %copy-start.9) | copy-done | bytes 524312
  34.1 0.4 shard_map.73
  34.6 1.3 %collective-permute-start.8 = (bf16[256,1024]{1,0:T(8,128)(2,1)S(1)}, bf16[256,1024]{1,0:T(8,128)(2,1)S(1)}, u32[]{:S(2)}, u32[]{:S(2)}) collective-permute-start(bf16[256,1024]{1,0:T(8,128)(2,1)S(1)} %get-tuple-element.52), channel_id=1, source_target_pairs={{5,0},{7,2},{13,8},{15,10},{21,16},{23,18},{29,24},{31,26}} | collective-permute-start | bytes 1572872 | tf_op jit(solution)/shard_map/ppermute | solution.py:277
  35.9 3.8 %collective-permute-done.6.other.refs_4_.refs_2_.refs_1_ = bf16[256,1024]{1,0:T(8,128)(2,1)S(1)} collective-permute-done((bf16[256,1024]{1,0:T(8,128)(2,1)S(1)}, bf16[256,1024]{1,0:T(8,128)(2,1)S(1)}, u32[]{:S(2)}, u32[]{:S(2)}) %collective-permute-start.6) | collective-permute-done | bytes 524320 | tf_op jit(solution)/shard_map/ppermute | solution.py:277
  39.8 5.3 %collective-permute-done.8.refs_6_.refs_4_.refs_3_ = bf16[256,1024]{1,0:T(8,128)(2,1)S(1)} collective-permute-done((bf16[256,1024]{1,0:T(8,128)(2,1)S(1)}, bf16[256,1024]{1,0:T(8,128)(2,1)S(1)}, u32[]{:S(2)}, u32[]{:S(2)}) %collective-permute-start.8) | collective-permute-done | bytes 524320 | tf_op jit(solution)/shard_map/ppermute | solution.py:277
  45.1 0.4 shard_map.74
  45.5 0.0 copy-start
  45.6 1.3 %copy-done = bf16[1024,1024]{1,0:T(8,128)(2,1)} copy-done((bf16[1024,1024]{1,0:T(8,128)(2,1)}, bf16[1024,1024]{1,0:T(8,128)(2,1)S(1)}, u32[]{:S(2)}) %copy-start) | copy-done | bytes 2097176
  46.9 1.3 %collective-permute-start.10 = (bf16[1024,1024]{1,0:T(8,128)(2,1)}, bf16[1024,1024]{1,0:T(8,128)(2,1)S(1)}, u32[]{:S(2)}, u32[]{:S(2)}) collective-permute-start(bf16[1024,1024]{1,0:T(8,128)(2,1)} %copy-done), channel_id=1, source_target_pairs={{1,0},{3,2},{5,4},{7,6},{9,8},{11,10},{13,12},{15,14},{17,16},{19,... | collective-permute-start | bytes 6291464 | tf_op jit(solution)/shard_map/ppermute | solution.py:277
  48.2 1.3 %collective-permute-start.11 = (bf16[256,1024]{1,0:T(8,128)(2,1)S(1)}, bf16[256,1024]{1,0:T(8,128)(2,1)S(1)}, u32[]{:S(2)}, u32[]{:S(2)}) collective-permute-start(bf16[256,1024]{1,0:T(8,128)(2,1)S(1)} %get-tuple-element.58), channel_id=1, source_target_pairs={{5,0},{7,2},{13,8},{15,10},{21,16},{23,18},{29,24},{31,26}} | collective-permute-start | bytes 1572872 | tf_op jit(solution)/shard_map/ppermute | solution.py:277
  49.5 0.7 collective-permute-start.9
  50.1 0.0 collective-permute-done.9.refs_0_
  50.1 8.5 %collective-permute-done.11.refs_7_.refs_5_.refs_4_ = bf16[256,1024]{1,0:T(8,128)(2,1)S(1)} collective-permute-done((bf16[256,1024]{1,0:T(8,128)(2,1)S(1)}, bf16[256,1024]{1,0:T(8,128)(2,1)S(1)}, u32[]{:S(2)}, u32[]{:S(2)}) %collective-permute-start.11) | collective-permute-done | bytes 524320 | tf_op jit(solution)/shard_map/ppermute | solution.py:277
  58.7 0.0 collective-permute-done.10.refs_2_.refs_7_.refs_0_
  58.7 0.7 collective-permute-start.12
  59.3 0.0 collective-permute-done.12.refs_0_
  59.3 0.1 copy-done.5
  59.5 0.7 collective-permute-start.13
  60.1 0.0 copy-start.1
  60.1 1.4 %collective-permute-start.18 = (f32[8,1024]{1,0:T(8,128)S(1)}, f32[8,1024]{1,0:T(8,128)S(1)}, u32[]{:S(2)}, u32[]{:S(2)}) collective-permute-start(f32[8,1024]{1,0:T(8,128)S(1)} %get-tuple-element.71), channel_id=1, source_target_pairs={{5,0},{7,2}} | collective-permute-start | bytes 98312 | tf_op jit(solution)/shard_map/ppermute | solution.py:277
  61.6 0.7 collective-permute-start.19
  62.2 0.0 collective-permute-done.13.refs_0_
  62.3 1.0 %copy-done.3 = bf16[256,1024]{1,0:T(8,128)(2,1)S(1)} copy-done((bf16[256,1024]{1,0:T(8,128)(2,1)S(1)}, bf16[256,1024]{1,0:T(8,128)(2,1)}, u32[]{:S(2)}) %copy-start.3) | copy-done | bytes 524312
  63.3 1.0 %copy-done.6 = bf16[256,1024]{1,0:T(8,128)(2,1)S(1)} copy-done((bf16[256,1024]{1,0:T(8,128)(2,1)S(1)}, bf16[256,1024]{1,0:T(8,128)(2,1)}, u32[]{:S(2)}) %copy-start.6) | copy-done | bytes 524312
  64.3 0.6 shard_map.78
  65.0 0.8 collective-permute-start.14
  65.8 1.5 %broadcast_select_fusion = bf16[1024,1024]{1,0:T(8,128)(2,1)} fusion(bf16[1024,1024]{1,0:T(8,128)(2,1)S(1)} %copy-done.1, bf16[1024,1024]{1,0:T(8,128)(2,1)S(1)} %collective-permute-done.10.refs_2_.refs_7_.refs_0_, pred[]{:T(512)S(6)} %eq.17), kind=kLoop, calls=%fused_computation | loop fusion | flops 1048576 | bytes 6291457 | tf_op jit(solution)/shard_map/jit(_where)/select_n | solution.py:401
  67.3 0.0 collective-permute-done.14.refs_0_
  67.3 0.7 collective-permute-start.15
  68.0 0.0 collective-permute-done.19
  68.1 0.0 collective-permute-done.15.refs_0_
  68.1 1.3 %collective-permute-start.16 = (bf16[8,1024]{1,0:T(8,128)(2,1)S(1)}, bf16[8,1024]{1,0:T(8,128)(2,1)S(1)}, u32[]{:S(2)}, u32[]{:S(2)}) collective-permute-start(bf16[8,1024]{1,0:T(8,128)(2,1)S(1)} %get-tuple-element.69), channel_id=1, source_target_pairs={{8,0},{10,2}} | collective-permute-start | bytes 49160 | tf_op jit(solution)/shard_map/ppermute | solution.py:277
  69.4 0.7 collective-permute-start.17
  70.1 0.7 collective-permute-start.20
  70.7 18.0 %collective-permute-done.16.from_pair = bf16[8,1024]{1,0:T(8,128)(2,1)S(1)} collective-permute-done((bf16[8,1024]{1,0:T(8,128)(2,1)S(1)}, bf16[8,1024]{1,0:T(8,128)(2,1)S(1)}, u32[]{:S(2)}, u32[]{:S(2)}) %collective-permute-start.16) | collective-permute-done | bytes 16416 | tf_op jit(solution)/shard_map/ppermute | solution.py:277
  88.8 0.7 shard_map.81
  89.5 1.3 %collective-permute-start.21 = (f32[4,1024]{1,0:T(4,128)S(1)}, f32[4,1024]{1,0:T(4,128)S(1)}, u32[]{:S(2)}, u32[]{:S(2)}) collective-permute-start(f32[4,1024]{1,0:T(4,128)S(1)} %slice.16), channel_id=1, source_target_pairs={{0,1},{2,3},{4,5},{6,7},{8,9},{10,11},{12,13},{14,15},{16,17},{18,... | collective-permute-start | bytes 49160 | tf_op jit(solution)/shard_map/ppermute | solution.py:277
  90.8 0.8 collective-permute-done.21
  91.6 0.6 fusion.2
  (44 shorter events, 0.2 us)
Async XLA Ops:
  0.6 4.9 %collective-permute-start.2 = (bf16[1024,1024]{1,0:T(8,128)(2,1)}, bf16[1024,1024]{1,0:T(8,128)(2,1)S(1)}, u32[]{:S(2)}, u32[]{:S(2)}) collective-permute-start(bf16[1024,1024]{1,0:T(8,128)(2,1)} %bitcast.12), channel_id=1, source_target_pairs={{0,1},{1,0},{2,3},{3,2},{4,5},{5,4},{6,7},{7,6},{8,9},{9,8},{10,11... | collective-permute-start | bytes 6291464 | tf_op jit(solution)/shard_map/ppermute | solution.py:277
  1.1 4.4 %collective-permute-start.1 = (s32[8,8]{1,0:T(8,128)}, s32[8,8]{1,0:T(8,128)S(1)}, u32[]{:S(2)}, u32[]{:S(2)}) collective-permute-start(s32[8,8]{1,0:T(8,128)} %bitcast.14), channel_id=1, source_target_pairs={{0,1},{1,0},{2,3},{3,2},{4,5},{5,4},{6,7},{7,6},{8,9},{9,8},{10,11... | collective-permute-start | bytes 776 | tf_op jit(solution)/shard_map/ppermute | solution.py:277
  2.3 1.6 %copy-start.10 = (bf16[1,1024,1024]{2,1,0:T(8,128)(2,1)S(1)}, bf16[1,1024,1024]{2,1,0:T(8,128)(2,1)}, u32[]{:S(2)}) copy-start(bf16[1,1024,1024]{2,1,0:T(8,128)(2,1)} %param.5) | copy-start | bytes 6291460
  3.9 0.7 copy-start.16
  7.4 11.2 %collective-permute-start.3 = (bf16[256,1024]{1,0:T(8,128)(2,1)S(1)}, bf16[256,1024]{1,0:T(8,128)(2,1)S(1)}, u32[]{:S(2)}, u32[]{:S(2)}) collective-permute-start(bf16[256,1024]{1,0:T(8,128)(2,1)S(1)} %get-tuple-element.40.own), channel_id=1, source_target_pairs={{0,3},{2,1},{4,7},{6,5},{8,11},{10,9},{12,15},{14,13},{16,19},{18,... | collective-permute-start | bytes 1572872 | tf_op jit(solution)/shard_map/ppermute | solution.py:277
  11.9 13.7 %collective-permute-start.5 = (bf16[256,1024]{1,0:T(8,128)(2,1)}, bf16[256,1024]{1,0:T(8,128)(2,1)}, u32[]{:S(2)}, u32[]{:S(2)}) collective-permute-start(bf16[256,1024]{1,0:T(8,128)(2,1)} %get-tuple-element.46.own), channel_id=1, source_target_pairs={{0,3},{2,1},{4,7},{6,5},{8,11},{10,9},{12,15},{14,13},{16,19},{18,... | collective-permute-start | bytes 1572872 | tf_op jit(solution)/shard_map/ppermute | solution.py:277
  14.0 9.6 %copy-start.17 = (f32[1,4,1024]{2,1,0:T(4,128)S(1)}, f32[1,4,1024]{2,1,0:T(4,128)}, u32[]{:S(2)}) copy-start(f32[1,4,1024]{2,1,0:T(4,128)} %param.9) | copy-start | bytes 49156
  14.0 9.7 %copy-start.18 = (s32[1,1024]{1,0:T(1,128)S(1)}, s32[1,1024]{1,0:T(1,128)}, u32[]{:S(2)}) copy-start(s32[1,1024]{1,0:T(1,128)} %param.8) | copy-start | bytes 12292
  15.4 4.5 %copy-start.11 = (bf16[256,1024]{1,0:T(8,128)(2,1)}, bf16[256,1024]{1,0:T(8,128)(2,1)S(1)}, u32[]{:S(2)}) copy-start(bf16[256,1024]{1,0:T(8,128)(2,1)S(1)} %get-tuple-element.45.refs_0_.own) | copy-start | bytes 1572868
  15.4 4.5 %copy-start.14 = (bf16[256,1024]{1,0:T(8,128)(2,1)}, bf16[256,1024]{1,0:T(8,128)(2,1)S(1)}, u32[]{:S(2)}) copy-start(bf16[256,1024]{1,0:T(8,128)(2,1)S(1)} %get-tuple-element.42.refs_0_.own) | copy-start | bytes 1572868
  19.9 8.6 %copy-start.8 = (bf16[256,1024]{1,0:T(8,128)(2,1)}, bf16[256,1024]{1,0:T(8,128)(2,1)S(1)}, u32[]{:S(2)}) copy-start(bf16[256,1024]{1,0:T(8,128)(2,1)S(1)} %get-tuple-element.47.refs_1_.refs_0_) | copy-start | bytes 1572868
  19.9 13.2 %collective-permute-start.7 = (bf16[256,1024]{1,0:T(8,128)(2,1)}, bf16[256,1024]{1,0:T(8,128)(2,1)S(1)}, u32[]{:S(2)}, u32[]{:S(2)}) collective-permute-start(bf16[256,1024]{1,0:T(8,128)(2,1)} %get-tuple-element.43), channel_id=1, source_target_pairs={{5,0},{7,2},{13,8},{15,10},{21,16},{23,18},{29,24},{31,26},{0,3},{... | collective-permute-start | bytes 1572872 | tf_op jit(solution)/shard_map/ppermute | solution.py:277
  23.7 1.2 %collective-permute-start = (f32[4,1024]{1,0:T(4,128)S(1)}, f32[4,1024]{1,0:T(4,128)S(1)}, u32[]{:S(2)}, u32[]{:S(2)}) collective-permute-start(f32[4,1024]{1,0:T(4,128)S(1)} %bitcast.17), channel_id=1, source_target_pairs={{0,1},{1,0},{2,3},{3,2},{4,5},{5,4},{6,7},{7,6},{8,9},{9,8},{10,11... | collective-permute-start | bytes 49160 | tf_op jit(solution)/shard_map/ppermute | solution.py:277
  25.0 8.1 %collective-permute-start.4 = (f32[9,1024]{1,0:T(8,128)S(1)}, f32[9,1024]{1,0:T(8,128)S(1)}, u32[]{:S(2)}, u32[]{:S(2)}) collective-permute-start(f32[9,1024]{1,0:T(8,128)S(1)} %pad_maximum_fusion.refs_1_), channel_id=1, source_target_pairs={{12,8},{14,10},{20,16},{22,18},{28,24},{30,26},{1,5},{3,7}} | collective-permute-start | bytes 110600 | tf_op jit(solution)/shard_map/ppermute | solution.py:277
  25.6 1.0 %copy-start.12 = (bf16[256,1024]{1,0:T(8,128)(2,1)S(1)}, bf16[256,1024]{1,0:T(8,128)(2,1)}, u32[]{:S(2)}) copy-start(bf16[256,1024]{1,0:T(8,128)(2,1)} %copy-done.11) | copy-start | bytes 1572868
  26.7 6.4 %copy-start.15 = (bf16[256,1024]{1,0:T(8,128)(2,1)S(1)}, bf16[256,1024]{1,0:T(8,128)(2,1)}, u32[]{:S(2)}) copy-start(bf16[256,1024]{1,0:T(8,128)(2,1)} %copy-done.14) | copy-start | bytes 1572868
  26.7 18.4 %copy-start.13 = (bf16[256,1024]{1,0:T(8,128)(2,1)S(1)}, bf16[256,1024]{1,0:T(8,128)(2,1)}, u32[]{:S(2)}) copy-start(bf16[256,1024]{1,0:T(8,128)(2,1)} %copy-done.11) | copy-start | bytes 1572868
  28.5 11.3 %collective-permute-start.6 = (bf16[256,1024]{1,0:T(8,128)(2,1)S(1)}, bf16[256,1024]{1,0:T(8,128)(2,1)S(1)}, u32[]{:S(2)}, u32[]{:S(2)}) collective-permute-start(bf16[256,1024]{1,0:T(8,128)(2,1)S(1)} %get-tuple-element.49), channel_id=1, source_target_pairs={{5,0},{7,2},{13,8},{15,10},{21,16},{23,18},{29,24},{31,26},{0,3},{... | collective-permute-start | bytes 1572872 | tf_op jit(solution)/shard_map/ppermute | solution.py:277
  33.1 1.0 %copy-start.9 = (bf16[256,1024]{1,0:T(8,128)(2,1)S(1)}, bf16[256,1024]{1,0:T(8,128)(2,1)}, u32[]{:S(2)}) copy-start(bf16[256,1024]{1,0:T(8,128)(2,1)} %copy-done.8) | copy-start | bytes 1572868
  34.6 10.5 %collective-permute-start.8 = (bf16[256,1024]{1,0:T(8,128)(2,1)S(1)}, bf16[256,1024]{1,0:T(8,128)(2,1)S(1)}, u32[]{:S(2)}, u32[]{:S(2)}) collective-permute-start(bf16[256,1024]{1,0:T(8,128)(2,1)S(1)} %get-tuple-element.52), channel_id=1, source_target_pairs={{5,0},{7,2},{13,8},{15,10},{21,16},{23,18},{29,24},{31,26}} | collective-permute-start | bytes 1572872 | tf_op jit(solution)/shard_map/ppermute | solution.py:277
  45.1 14.2 %copy-start.2 = (bf16[256,1024]{1,0:T(8,128)(2,1)}, bf16[256,1024]{1,0:T(8,128)(2,1)S(1)}, u32[]{:S(2)}) copy-start(bf16[256,1024]{1,0:T(8,128)(2,1)S(1)} %collective-permute-done.8.refs_6_.refs_4_.refs_3_) | copy-start | bytes 1572868
  45.5 1.3 %copy-start = (bf16[1024,1024]{1,0:T(8,128)(2,1)}, bf16[1024,1024]{1,0:T(8,128)(2,1)S(1)}, u32[]{:S(2)}) copy-start(bf16[1024,1024]{1,0:T(8,128)(2,1)S(1)} %get-tuple-element.57.refs_2_) | copy-start | bytes 6291460
  46.9 11.8 %collective-permute-start.10 = (bf16[1024,1024]{1,0:T(8,128)(2,1)}, bf16[1024,1024]{1,0:T(8,128)(2,1)S(1)}, u32[]{:S(2)}, u32[]{:S(2)}) collective-permute-start(bf16[1024,1024]{1,0:T(8,128)(2,1)} %copy-done), channel_id=1, source_target_pairs={{1,0},{3,2},{5,4},{7,6},{9,8},{11,10},{13,12},{15,14},{17,16},{19,... | collective-permute-start | bytes 6291464 | tf_op jit(solution)/shard_map/ppermute | solution.py:277
  48.2 10.5 %collective-permute-start.11 = (bf16[256,1024]{1,0:T(8,128)(2,1)S(1)}, bf16[256,1024]{1,0:T(8,128)(2,1)S(1)}, u32[]{:S(2)}, u32[]{:S(2)}) collective-permute-start(bf16[256,1024]{1,0:T(8,128)(2,1)S(1)} %get-tuple-element.58), channel_id=1, source_target_pairs={{5,0},{7,2},{13,8},{15,10},{21,16},{23,18},{29,24},{31,26}} | collective-permute-start | bytes 1572872 | tf_op jit(solution)/shard_map/ppermute | solution.py:277
  49.5 0.7 collective-permute-start.9
  58.7 0.8 copy-start.5
  58.7 0.7 collective-permute-start.12
  59.5 2.8 %collective-permute-start.13 = (bf16[8,1024]{1,0:T(8,128)(2,1)S(1)}, bf16[8,1024]{1,0:T(8,128)(2,1)S(1)}, u32[]{:S(2)}, u32[]{:S(2)}) collective-permute-start(bf16[8,1024]{1,0:T(8,128)(2,1)S(1)} %get-tuple-element.60), channel_id=1, source_target_pairs={{16,24},{18,26}} | collective-permute-start | bytes 49160 | tf_op jit(solution)/shard_map/ppermute | solution.py:277
  60.1 5.6 %copy-start.1 = (bf16[1024,1024]{1,0:T(8,128)(2,1)S(1)}, bf16[1024,1024]{1,0:T(8,128)(2,1)}, u32[]{:S(2)}) copy-start(bf16[1024,1024]{1,0:T(8,128)(2,1)} %copy-done) | copy-start | bytes 6291460
  60.1 7.9 %collective-permute-start.18 = (f32[8,1024]{1,0:T(8,128)S(1)}, f32[8,1024]{1,0:T(8,128)S(1)}, u32[]{:S(2)}, u32[]{:S(2)}) collective-permute-start(f32[8,1024]{1,0:T(8,128)S(1)} %get-tuple-element.71), channel_id=1, source_target_pairs={{5,0},{7,2}} | collective-permute-start | bytes 98312 | tf_op jit(solution)/shard_map/ppermute | solution.py:277
  61.6 6.5 %collective-permute-start.19 = (f32[8,1024]{1,0:T(8,128)S(1)}, f32[8,1024]{1,0:T(8,128)S(1)}, u32[]{:S(2)}, u32[]{:S(2)}) collective-permute-start(f32[8,1024]{1,0:T(8,128)S(1)} %get-tuple-element.71), channel_id=1, source_target_pairs={{5,4},{7,6}} | collective-permute-start | bytes 98312 | tf_op jit(solution)/shard_map/ppermute | solution.py:277
  62.2 1.0 %copy-start.3 = (bf16[256,1024]{1,0:T(8,128)(2,1)S(1)}, bf16[256,1024]{1,0:T(8,128)(2,1)}, u32[]{:S(2)}) copy-start(bf16[256,1024]{1,0:T(8,128)(2,1)} %copy-done.2) | copy-start | bytes 1572868
  63.3 1.0 %copy-start.6 = (bf16[256,1024]{1,0:T(8,128)(2,1)S(1)}, bf16[256,1024]{1,0:T(8,128)(2,1)}, u32[]{:S(2)}) copy-start(bf16[256,1024]{1,0:T(8,128)(2,1)} %copy-done.5) | copy-start | bytes 1572868
  64.9 2.3 %copy-start.4 = (bf16[256,1024]{1,0:T(8,128)(2,1)S(1)}, bf16[256,1024]{1,0:T(8,128)(2,1)}, u32[]{:S(2)}) copy-start(bf16[256,1024]{1,0:T(8,128)(2,1)} %copy-done.2) | copy-start | bytes 1572868
  64.9 2.3 %copy-start.7 = (bf16[256,1024]{1,0:T(8,128)(2,1)S(1)}, bf16[256,1024]{1,0:T(8,128)(2,1)}, u32[]{:S(2)}) copy-start(bf16[256,1024]{1,0:T(8,128)(2,1)} %copy-done.5) | copy-start | bytes 1572868
  65.0 2.3 %collective-permute-start.14 = (bf16[8,1024]{1,0:T(8,128)(2,1)S(1)}, bf16[8,1024]{1,0:T(8,128)(2,1)S(1)}, u32[]{:S(2)}, u32[]{:S(2)}) collective-permute-start(bf16[8,1024]{1,0:T(8,128)(2,1)S(1)} %get-tuple-element.61), channel_id=1, source_target_pairs={{24,16},{26,18}} | collective-permute-start | bytes 49160 | tf_op jit(solution)/shard_map/ppermute | solution.py:277
  67.3 0.7 collective-permute-start.15
  68.1 20.7 %collective-permute-start.16 = (bf16[8,1024]{1,0:T(8,128)(2,1)S(1)}, bf16[8,1024]{1,0:T(8,128)(2,1)S(1)}, u32[]{:S(2)}, u32[]{:S(2)}) collective-permute-start(bf16[8,1024]{1,0:T(8,128)(2,1)S(1)} %get-tuple-element.69), channel_id=1, source_target_pairs={{8,0},{10,2}} | collective-permute-start | bytes 49160 | tf_op jit(solution)/shard_map/ppermute | solution.py:277
  69.4 19.4 %collective-permute-start.17 = (bf16[8,1024]{1,0:T(8,128)(2,1)S(1)}, bf16[8,1024]{1,0:T(8,128)(2,1)S(1)}, u32[]{:S(2)}, u32[]{:S(2)}) collective-permute-start(bf16[8,1024]{1,0:T(8,128)(2,1)S(1)} %get-tuple-element.69), channel_id=1, source_target_pairs={{8,4},{10,6}} | collective-permute-start | bytes 49160 | tf_op jit(solution)/shard_map/ppermute | solution.py:277
  70.1 19.4 %collective-permute-start.20 = (f32[8,1024]{1,0:T(8,128)S(1)}, f32[8,1024]{1,0:T(8,128)S(1)}, u32[]{:S(2)}, u32[]{:S(2)}) collective-permute-start(f32[8,1024]{1,0:T(8,128)S(1)} %select_select_fusion), channel_id=1, source_target_pairs={{8,12},{10,14},{16,20},{18,22},{24,28},{26,30}} | collective-permute-start | bytes 98312 | tf_op jit(solution)/shard_map/ppermute | solution.py:277
  89.5 2.1 %collective-permute-start.21 = (f32[4,1024]{1,0:T(4,128)S(1)}, f32[4,1024]{1,0:T(4,128)S(1)}, u32[]{:S(2)}, u32[]{:S(2)}) collective-permute-start(f32[4,1024]{1,0:T(4,128)S(1)} %slice.16), channel_id=1, source_target_pairs={{0,1},{2,3},{4,5},{6,7},{8,9},{10,11},{12,13},{14,15},{16,17},{18,... | collective-permute-start | bytes 49160 | tf_op jit(solution)/shard_map/ppermute | solution.py:277

commit v14 on v13

--- a/solution.py
+++ b/solution.py
@@ -105,7 +105,7 @@
     )(other_pattern, own, other, inverse, *extra)
 
 
-def combine_kernel(face_at, is_face, with_next, whole_rows, own, other, inverse, *refs):
+def combine_kernel(face_at, is_face, with_next, whole_rows, done, own, other, inverse, *refs):
     refs = list(refs)
     following = refs.pop(0) if with_next else None
     joined = 0.5 * (own[...].astype(jnp.float32) + other[...].astype(jnp.float32))
@@ -113,7 +113,9 @@
         right = joined.astype(jnp.bfloat16)
     else:
         right = refs.pop(0)[...]
-        refs.pop(0)
+        before = refs.pop(0)
+        for rows in done:
+            refs[1][rows, :] = before[rows, :]
     piece = minus_face(joined, face_at, inverse[...], right)
     refs[1][whole_rows, :] = piece
     if is_face:
@@ -126,7 +128,7 @@
             refs[0][...] = following[...]
 
 
-def combine(own, other, inverse, following, state, face_at, row_at):
+def combine(own, other, inverse, following, state, face_at, row_at, done):
     is_face = state is None
     rows, width = own.shape
     extra = [] if following is None else [following]
@@ -141,6 +143,7 @@
             is_face,
             following is not None,
             slice(row_at, row_at + rows),
+            [slice(at, at + size) for at, size in done],
         ),
         out_shape=[piece, whole] + ([piece] if is_face else []),
         in_specs=[VMEM] * (3 + len(extra)),
@@ -340,6 +343,7 @@
                     state,
                     level * face,
                     piece[0],
+                    order[: order.index(piece)],
                 )
             current = renewed
             continue
@@ -363,6 +367,7 @@
                 state,
                 level * face,
                 piece[0],
+                order[:k],
             )
             pair_pieces[piece] = send(payload, forward + ([] if following is None else over))
             if following is not None:

time: 93 us -> 93.3 us (level)
  no operation moved by 1% of the time
where the time goes in v14:
time: 93.3 us; the launch traced here: 92.5 us
  waiting for transfers between devices  40.8 us (44%)
  starting transfers between devices  29.6 us (32%)
  Pallas kernels  9.76 us (10%)
  local copies, waits for them, and re-layouts  8.93 us (10%)
  other arithmetic  2.22 us (2%)
  between operations  1.15 us (1%)
    ppermute x22, waiting for transfers between devices, send(): return lax.ppermute(value, AXES, pairs_of_devices)  40.8 us
    ppermute x22, starting transfers between devices, send(): return lax.ppermute(value, AXES, pairs_of_devices)  29.6 us
    unnamed x38, local copies, waits for them, and re-layouts  7.86 us
    pallas_call x4, Pallas kernels, combine(): pl.pallas_call(functools.partial(combine_kernel, face_at, is_face, follow...  4.27 us
    pallas_call x2, Pallas kernels, leaf_combine(): pl.pallas_call(functools.partial(leaf_kernel, half * rows, is_face, piece...  3.17 us
  transfers between devices with their start and end apart: 22, of which 7 were waited for; matrix products, arithmetic and copies ran while one was open for 3% of the time, Pallas kernels for 8%

profile of v14, /device:TPU:0, one launch (start us, length us, event | category | flops | bytes accessed | tf_op | source)
XLA Modules:
  0.0 92.5 jit_solution(13037580816614155427)
XLA Ops:
  0.6 0.5 collective-permute-start.2
  1.1 0.1 collective-permute-start.1
  1.2 1.1 %fusion.1 = (bf16[256,256]{1,0:T(8,128)(2,1)S(1)}, bf16[256,256]{1,0:T(8,128)(2,1)S(1)}) fusion(f32[1,3,256,256]{3,2,1,0:T(8,128)} %param.7, s32[]{:T(128)S(6)} %select_n.81, s32[]{:T(128)S(6)} %select_n.80), kind=kLoop, calls=%fused_computation.4 | loop fusion | bytes 524296 | tf_op jit(solution)/shard_map/convert_element_type | solution.py:303
  2.3 0.0 copy-start.10
  2.3 1.6 %copy-done.10 = bf16[1,1024,1024]{2,1,0:T(8,128)(2,1)S(1)} copy-done((bf16[1,1024,1024]{2,1,0:T(8,128)(2,1)S(1)}, bf16[1,1024,1024]{2,1,0:T(8,128)(2,1)}, u32[]{:S(2)}) %copy-start.10) | copy-done | bytes 2097176
  3.9 0.7 copy-done.16
  4.6 0.9 %shard_map.68.own = bf16[1024,1024]{1,0:T(8,128)(2,1)S(1)} custom-call(s32[8,8]{1,0:T(8,128)S(1)} %bitcast.15, bf16[1024,1024]{1,0:T(8,128)(2,1)S(1)} %bitcast.13), custom_call_target="tpu_custom_call" | custom-call | flops 1048576 | bytes 4194304 | tf_op jit(solution)/shard_map/pallas_call | solution.py:292
  5.5 0.0 collective-permute-done.1.other_pattern
  5.5 0.0 collective-permute-done.2.other
  5.5 1.8 %shard_map.69 = (bf16[256,1024]{1,0:T(8,128)(2,1)}, bf16[256,1024]{1,0:T(8,128)(2,1)S(1)}, bf16[256,1024]{1,0:T(8,128)(2,1)S(1)}) custom-call(s32[8,8]{1,0:T(8,128)S(1)} %collective-permute-done.1.other_pattern, bf16[1024,1024]{1,0:T(8,128)(2,1)S(1)} %shard_map.68.own, bf16[1024,1024]{1,0:T(8,128)(2,1)S(1)} %collective-permute-done.2.other, ...), custom_call_target="tpu_custom_call" | custom-call | flops 335544320 | bytes 3145728 | tf_op jit(solution)/shard_map/pallas_call | solution.py:97
  7.4 4.6 %collective-permute-start.3 = (bf16[256,1024]{1,0:T(8,128)(2,1)S(1)}, bf16[256,1024]{1,0:T(8,128)(2,1)S(1)}, u32[]{:S(2)}, u32[]{:S(2)}) collective-permute-start(bf16[256,1024]{1,0:T(8,128)(2,1)S(1)} %get-tuple-element.40.own), channel_id=1, source_target_pairs={{0,3},{2,1},{4,7},{6,5},{8,11},{10,9},{12,15},{14,13},{16,19},{18,... | collective-permute-start | bytes 1572872 | tf_op jit(solution)/shard_map/ppermute | solution.py:280
  11.9 2.1 %collective-permute-start.5 = (bf16[256,1024]{1,0:T(8,128)(2,1)}, bf16[256,1024]{1,0:T(8,128)(2,1)}, u32[]{:S(2)}, u32[]{:S(2)}) collective-permute-start(bf16[256,1024]{1,0:T(8,128)(2,1)} %get-tuple-element.46.own), channel_id=1, source_target_pairs={{0,3},{2,1},{4,7},{6,5},{8,11},{10,9},{12,15},{14,13},{16,19},{18,... | collective-permute-start | bytes 1572872 | tf_op jit(solution)/shard_map/ppermute | solution.py:280
  14.0 1.3 %shard_map.70 = (bf16[256,1024]{1,0:T(8,128)(2,1)S(1)}, bf16[256,1024]{1,0:T(8,128)(2,1)S(1)}) custom-call(s32[8,8]{1,0:T(8,128)S(1)} %collective-permute-done.1.other_pattern, bf16[1024,1024]{1,0:T(8,128)(2,1)S(1)} %shard_map.68.own, bf16[1024,1024]{1,0:T(8,128)(2,1)S(1)} %collective-permute-done.2.other, bf16[256,256]{1,0:T(8,128)(2,1)S(1)} %get-tuple-element.79.inverse, ...), custom_call_target="tpu_custom_call" | custom-call | flops 335544320 | bytes 3145728 | tf_op jit(solution)/shard_map/pallas_call | solution.py:97
  15.4 3.2 %collective-permute-done.3.other = bf16[256,1024]{1,0:T(8,128)(2,1)S(1)} collective-permute-done((bf16[256,1024]{1,0:T(8,128)(2,1)S(1)}, bf16[256,1024]{1,0:T(8,128)(2,1)S(1)}, u32[]{:S(2)}, u32[]{:S(2)}) %collective-permute-start.3) | collective-permute-done | bytes 524320 | tf_op jit(solution)/shard_map/ppermute | solution.py:280
  18.6 1.3 %shard_map.71 = (bf16[256,1024]{1,0:T(8,128)(2,1)}, bf16[1024,1024]{1,0:T(8,128)(2,1)S(1)}, bf16[256,1024]{1,0:T(8,128)(2,1)S(1)}) custom-call(bf16[256,1024]{1,0:T(8,128)(2,1)S(1)} %get-tuple-element.40.own, bf16[256,1024]{1,0:T(8,128)(2,1)S(1)} %collective-permute-done.3.other, bf16[256,256]{1,0:T(8,128)(2,1)S(1)} %get-tuple-element.78.inverse, ...), custom_call_target="tpu_custom_call" | custom-call | tf_op jit(solution)/shard_map/pallas_call | solution.py:139
  19.9 3.8 %collective-permute-start.7 = (bf16[256,1024]{1,0:T(8,128)(2,1)}, bf16[256,1024]{1,0:T(8,128)(2,1)S(1)}, u32[]{:S(2)}, u32[]{:S(2)}) collective-permute-start(bf16[256,1024]{1,0:T(8,128)(2,1)} %get-tuple-element.43), channel_id=1, source_target_pairs={{5,0},{7,2},{13,8},{15,10},{21,16},{23,18},{29,24},{31,26},{0,3},{... | collective-permute-start | bytes 1572872 | tf_op jit(solution)/shard_map/ppermute | solution.py:280
  23.7 0.1 collective-permute-start
  23.8 1.1 %collective-permute-done = f32[4,1024]{1,0:T(4,128)S(1)} collective-permute-done((f32[4,1024]{1,0:T(4,128)S(1)}, f32[4,1024]{1,0:T(4,128)S(1)}, u32[]{:S(2)}, u32[]{:S(2)}) %collective-permute-start) | collective-permute-done | bytes 16416 | tf_op jit(solution)/shard_map/ppermute | solution.py:280
  25.0 0.7 collective-permute-start.4
  25.6 0.0 collective-permute-done.5.other
  25.6 1.0 %copy-done.12 = bf16[256,1024]{1,0:T(8,128)(2,1)S(1)} copy-done((bf16[256,1024]{1,0:T(8,128)(2,1)S(1)}, bf16[256,1024]{1,0:T(8,128)(2,1)}, u32[]{:S(2)}) %copy-start.12) | copy-done | bytes 524312
  26.7 1.8 %shard_map.72 = (bf16[256,1024]{1,0:T(8,128)(2,1)S(1)}, bf16[1024,1024]{1,0:T(8,128)(2,1)S(1)}) custom-call(bf16[256,1024]{1,0:T(8,128)(2,1)} %get-tuple-element.46.own, bf16[256,1024]{1,0:T(8,128)(2,1)} %collective-permute-done.5.other, bf16[256,256]{1,0:T(8,128)(2,1)S(1)} %get-tuple-element.78.inverse, ...), custom_call_target="tpu_custom_call", output_to_operand_aliasing={{1}: (5, {})} | custom-call | tf_op jit(solution)/shard_map/pallas_call | solution.py:139
  28.5 4.6 %collective-permute-start.6 = (bf16[256,1024]{1,0:T(8,128)(2,1)S(1)}, bf16[256,1024]{1,0:T(8,128)(2,1)S(1)}, u32[]{:S(2)}, u32[]{:S(2)}) collective-permute-start(bf16[256,1024]{1,0:T(8,128)(2,1)S(1)} %get-tuple-element.49), channel_id=1, source_target_pairs={{5,0},{7,2},{13,8},{15,10},{21,16},{23,18},{29,24},{31,26},{0,3},{... | collective-permute-start | bytes 1572872 | tf_op jit(solution)/shard_map/ppermute | solution.py:280
  33.1 0.0 collective-permute-done.4.refs_3_
  33.1 0.0 collective-permute-done.7.other.refs_5_.refs_3_.refs_2_
  33.2 1.0 %copy-done.9 = bf16[256,1024]{1,0:T(8,128)(2,1)S(1)} copy-done((bf16[256,1024]{1,0:T(8,128)(2,1)S(1)}, bf16[256,1024]{1,0:T(8,128)(2,1)}, u32[]{:S(2)}) %copy-start.9) | copy-done | bytes 524312
  34.2 0.6 shard_map.73
  34.8 1.3 %collective-permute-start.8 = (bf16[256,1024]{1,0:T(8,128)(2,1)S(1)}, bf16[256,1024]{1,0:T(8,128)(2,1)S(1)}, u32[]{:S(2)}, u32[]{:S(2)}) collective-permute-start(bf16[256,1024]{1,0:T(8,128)(2,1)S(1)} %get-tuple-element.52), channel_id=1, source_target_pairs={{5,0},{7,2},{13,8},{15,10},{21,16},{23,18},{29,24},{31,26}} | collective-permute-start | bytes 1572872 | tf_op jit(solution)/shard_map/ppermute | solution.py:280
  36.1 3.7 %collective-permute-done.6.other.refs_4_.refs_2_.refs_1_ = bf16[256,1024]{1,0:T(8,128)(2,1)S(1)} collective-permute-done((bf16[256,1024]{1,0:T(8,128)(2,1)S(1)}, bf16[256,1024]{1,0:T(8,128)(2,1)S(1)}, u32[]{:S(2)}, u32[]{:S(2)}) %collective-permute-start.6) | collective-permute-done | bytes 524320 | tf_op jit(solution)/shard_map/ppermute | solution.py:280
  39.8 5.5 %collective-permute-done.8.refs_6_.refs_4_.refs_3_ = bf16[256,1024]{1,0:T(8,128)(2,1)S(1)} collective-permute-done((bf16[256,1024]{1,0:T(8,128)(2,1)S(1)}, bf16[256,1024]{1,0:T(8,128)(2,1)S(1)}, u32[]{:S(2)}, u32[]{:S(2)}) %collective-permute-start.8) | collective-permute-done | bytes 524320 | tf_op jit(solution)/shard_map/ppermute | solution.py:280
  45.3 0.6 shard_map.74
  45.9 0.0 copy-start
  46.0 1.3 %copy-done = bf16[1024,1024]{1,0:T(8,128)(2,1)} copy-done((bf16[1024,1024]{1,0:T(8,128)(2,1)}, bf16[1024,1024]{1,0:T(8,128)(2,1)S(1)}, u32[]{:S(2)}) %copy-start) | copy-done | bytes 2097176
  47.2 1.3 %collective-permute-start.10 = (bf16[1024,1024]{1,0:T(8,128)(2,1)}, bf16[1024,1024]{1,0:T(8,128)(2,1)S(1)}, u32[]{:S(2)}, u32[]{:S(2)}) collective-permute-start(bf16[1024,1024]{1,0:T(8,128)(2,1)} %copy-done), channel_id=1, source_target_pairs={{1,0},{3,2},{5,4},{7,6},{9,8},{11,10},{13,12},{15,14},{17,16},{19,... | collective-permute-start | bytes 6291464 | tf_op jit(solution)/shard_map/ppermute | solution.py:280
  48.5 1.3 %collective-permute-start.11 = (bf16[256,1024]{1,0:T(8,128)(2,1)S(1)}, bf16[256,1024]{1,0:T(8,128)(2,1)S(1)}, u32[]{:S(2)}, u32[]{:S(2)}) collective-permute-start(bf16[256,1024]{1,0:T(8,128)(2,1)S(1)} %get-tuple-element.58), channel_id=1, source_target_pairs={{5,0},{7,2},{13,8},{15,10},{21,16},{23,18},{29,24},{31,26}} | collective-permute-start | bytes 1572872 | tf_op jit(solution)/shard_map/ppermute | solution.py:280
  49.8 0.7 collective-permute-start.9
  50.5 0.0 collective-permute-done.9.refs_0_
  50.5 8.5 %collective-permute-done.11.refs_7_.refs_5_.refs_4_ = bf16[256,1024]{1,0:T(8,128)(2,1)S(1)} collective-permute-done((bf16[256,1024]{1,0:T(8,128)(2,1)S(1)}, bf16[256,1024]{1,0:T(8,128)(2,1)S(1)}, u32[]{:S(2)}, u32[]{:S(2)}) %collective-permute-start.11) | collective-permute-done | bytes 524320 | tf_op jit(solution)/shard_map/ppermute | solution.py:280
  59.0 0.0 collective-permute-done.10.refs_2_.refs_7_.refs_0_
  59.0 0.7 collective-permute-start.12
  59.7 0.1 copy-done.5
  59.8 0.7 collective-permute-start.13
  60.5 0.0 copy-start.1
  60.5 1.4 %collective-permute-start.18 = (f32[8,1024]{1,0:T(8,128)S(1)}, f32[8,1024]{1,0:T(8,128)S(1)}, u32[]{:S(2)}, u32[]{:S(2)}) collective-permute-start(f32[8,1024]{1,0:T(8,128)S(1)} %get-tuple-element.71), channel_id=1, source_target_pairs={{5,0},{7,2}} | collective-permute-start | bytes 98312 | tf_op jit(solution)/shard_map/ppermute | solution.py:280
  61.9 0.7 collective-permute-start.19
  62.6 0.0 collective-permute-done.13.refs_0_
  62.6 1.0 %copy-done.3 = bf16[256,1024]{1,0:T(8,128)(2,1)S(1)} copy-done((bf16[256,1024]{1,0:T(8,128)(2,1)S(1)}, bf16[256,1024]{1,0:T(8,128)(2,1)}, u32[]{:S(2)}) %copy-start.3) | copy-done | bytes 524312
  63.7 1.0 %copy-done.6 = bf16[256,1024]{1,0:T(8,128)(2,1)S(1)} copy-done((bf16[256,1024]{1,0:T(8,128)(2,1)S(1)}, bf16[256,1024]{1,0:T(8,128)(2,1)}, u32[]{:S(2)}) %copy-start.6) | copy-done | bytes 524312
  64.7 0.6 shard_map.78
  65.3 0.8 collective-permute-start.14
  66.1 1.5 %broadcast_select_fusion = bf16[1024,1024]{1,0:T(8,128)(2,1)} fusion(bf16[1024,1024]{1,0:T(8,128)(2,1)S(1)} %copy-done.1, bf16[1024,1024]{1,0:T(8,128)(2,1)S(1)} %collective-permute-done.10.refs_2_.refs_7_.refs_0_, pred[]{:T(512)S(6)} %eq.17), kind=kLoop, calls=%fused_computation | loop fusion | flops 1048576 | bytes 6291457 | tf_op jit(solution)/shard_map/jit(_where)/select_n | solution.py:406
  67.7 0.0 collective-permute-done.14.refs_0_
  67.7 0.7 collective-permute-start.15
  68.4 0.0 collective-permute-done.18
  68.5 1.3 %collective-permute-start.16 = (bf16[8,1024]{1,0:T(8,128)(2,1)S(1)}, bf16[8,1024]{1,0:T(8,128)(2,1)S(1)}, u32[]{:S(2)}, u32[]{:S(2)}) collective-permute-start(bf16[8,1024]{1,0:T(8,128)(2,1)S(1)} %get-tuple-element.69), channel_id=1, source_target_pairs={{8,0},{10,2}} | collective-permute-start | bytes 49160 | tf_op jit(solution)/shard_map/ppermute | solution.py:280
  69.8 0.7 collective-permute-start.17
  70.5 0.7 collective-permute-start.20
  71.1 17.9 %collective-permute-done.16.from_pair = bf16[8,1024]{1,0:T(8,128)(2,1)S(1)} collective-permute-done((bf16[8,1024]{1,0:T(8,128)(2,1)S(1)}, bf16[8,1024]{1,0:T(8,128)(2,1)S(1)}, u32[]{:S(2)}, u32[]{:S(2)}) %collective-permute-start.16) | collective-permute-done | bytes 16416 | tf_op jit(solution)/shard_map/ppermute | solution.py:280
  89.0 0.0 collective-permute-done.17.from_own
  89.0 0.7 shard_map.81
  89.7 0.0 collective-permute-done.20
  89.7 1.3 %collective-permute-start.21 = (f32[4,1024]{1,0:T(4,128)S(1)}, f32[4,1024]{1,0:T(4,128)S(1)}, u32[]{:S(2)}, u32[]{:S(2)}) collective-permute-start(f32[4,1024]{1,0:T(4,128)S(1)} %slice.16), channel_id=1, source_target_pairs={{0,1},{2,3},{4,5},{6,7},{8,9},{10,11},{12,13},{14,15},{16,17},{18,... | collective-permute-start | bytes 49160 | tf_op jit(solution)/shard_map/ppermute | solution.py:280
  91.0 0.8 collective-permute-done.21
  91.9 0.6 fusion.2
  (44 shorter events, 0.2 us)
Async XLA Ops:
  0.6 4.9 %collective-permute-start.2 = (bf16[1024,1024]{1,0:T(8,128)(2,1)}, bf16[1024,1024]{1,0:T(8,128)(2,1)S(1)}, u32[]{:S(2)}, u32[]{:S(2)}) collective-permute-start(bf16[1024,1024]{1,0:T(8,128)(2,1)} %bitcast.12), channel_id=1, source_target_pairs={{0,1},{1,0},{2,3},{3,2},{4,5},{5,4},{6,7},{7,6},{8,9},{9,8},{10,11... | collective-permute-start | bytes 6291464 | tf_op jit(solution)/shard_map/ppermute | solution.py:280
  1.1 4.4 %collective-permute-start.1 = (s32[8,8]{1,0:T(8,128)}, s32[8,8]{1,0:T(8,128)S(1)}, u32[]{:S(2)}, u32[]{:S(2)}) collective-permute-start(s32[8,8]{1,0:T(8,128)} %bitcast.14), channel_id=1, source_target_pairs={{0,1},{1,0},{2,3},{3,2},{4,5},{5,4},{6,7},{7,6},{8,9},{9,8},{10,11... | collective-permute-start | bytes 776 | tf_op jit(solution)/shard_map/ppermute | solution.py:280
  2.3 1.6 %copy-start.10 = (bf16[1,1024,1024]{2,1,0:T(8,128)(2,1)S(1)}, bf16[1,1024,1024]{2,1,0:T(8,128)(2,1)}, u32[]{:S(2)}) copy-start(bf16[1,1024,1024]{2,1,0:T(8,128)(2,1)} %param.5) | copy-start | bytes 6291460
  3.9 0.7 copy-start.16
  7.4 11.2 %collective-permute-start.3 = (bf16[256,1024]{1,0:T(8,128)(2,1)S(1)}, bf16[256,1024]{1,0:T(8,128)(2,1)S(1)}, u32[]{:S(2)}, u32[]{:S(2)}) collective-permute-start(bf16[256,1024]{1,0:T(8,128)(2,1)S(1)} %get-tuple-element.40.own), channel_id=1, source_target_pairs={{0,3},{2,1},{4,7},{6,5},{8,11},{10,9},{12,15},{14,13},{16,19},{18,... | collective-permute-start | bytes 1572872 | tf_op jit(solution)/shard_map/ppermute | solution.py:280
  11.9 13.7 %collective-permute-start.5 = (bf16[256,1024]{1,0:T(8,128)(2,1)}, bf16[256,1024]{1,0:T(8,128)(2,1)}, u32[]{:S(2)}, u32[]{:S(2)}) collective-permute-start(bf16[256,1024]{1,0:T(8,128)(2,1)} %get-tuple-element.46.own), channel_id=1, source_target_pairs={{0,3},{2,1},{4,7},{6,5},{8,11},{10,9},{12,15},{14,13},{16,19},{18,... | collective-permute-start | bytes 1572872 | tf_op jit(solution)/shard_map/ppermute | solution.py:280
  14.0 9.6 %copy-start.17 = (f32[1,4,1024]{2,1,0:T(4,128)S(1)}, f32[1,4,1024]{2,1,0:T(4,128)}, u32[]{:S(2)}) copy-start(f32[1,4,1024]{2,1,0:T(4,128)} %param.9) | copy-start | bytes 49156
  14.0 9.7 %copy-start.18 = (s32[1,1024]{1,0:T(1,128)S(1)}, s32[1,1024]{1,0:T(1,128)}, u32[]{:S(2)}) copy-start(s32[1,1024]{1,0:T(1,128)} %param.8) | copy-start | bytes 12292
  15.4 4.5 %copy-start.11 = (bf16[256,1024]{1,0:T(8,128)(2,1)}, bf16[256,1024]{1,0:T(8,128)(2,1)S(1)}, u32[]{:S(2)}) copy-start(bf16[256,1024]{1,0:T(8,128)(2,1)S(1)} %get-tuple-element.45.refs_0_.own) | copy-start | bytes 1572868
  15.4 4.5 %copy-start.14 = (bf16[256,1024]{1,0:T(8,128)(2,1)}, bf16[256,1024]{1,0:T(8,128)(2,1)S(1)}, u32[]{:S(2)}) copy-start(bf16[256,1024]{1,0:T(8,128)(2,1)S(1)} %get-tuple-element.42.refs_0_.own) | copy-start | bytes 1572868
  19.9 8.6 %copy-start.8 = (bf16[256,1024]{1,0:T(8,128)(2,1)}, bf16[256,1024]{1,0:T(8,128)(2,1)S(1)}, u32[]{:S(2)}) copy-start(bf16[256,1024]{1,0:T(8,128)(2,1)S(1)} %get-tuple-element.47.refs_1_.refs_0_) | copy-start | bytes 1572868
  19.9 13.3 %collective-permute-start.7 = (bf16[256,1024]{1,0:T(8,128)(2,1)}, bf16[256,1024]{1,0:T(8,128)(2,1)S(1)}, u32[]{:S(2)}, u32[]{:S(2)}) collective-permute-start(bf16[256,1024]{1,0:T(8,128)(2,1)} %get-tuple-element.43), channel_id=1, source_target_pairs={{5,0},{7,2},{13,8},{15,10},{21,16},{23,18},{29,24},{31,26},{0,3},{... | collective-permute-start | bytes 1572872 | tf_op jit(solution)/shard_map/ppermute | solution.py:280
  23.7 1.2 %collective-permute-start = (f32[4,1024]{1,0:T(4,128)S(1)}, f32[4,1024]{1,0:T(4,128)S(1)}, u32[]{:S(2)}, u32[]{:S(2)}) collective-permute-start(f32[4,1024]{1,0:T(4,128)S(1)} %bitcast.17), channel_id=1, source_target_pairs={{0,1},{1,0},{2,3},{3,2},{4,5},{5,4},{6,7},{7,6},{8,9},{9,8},{10,11... | collective-permute-start | bytes 49160 | tf_op jit(solution)/shard_map/ppermute | solution.py:280
  25.0 8.2 %collective-permute-start.4 = (f32[9,1024]{1,0:T(8,128)S(1)}, f32[9,1024]{1,0:T(8,128)S(1)}, u32[]{:S(2)}, u32[]{:S(2)}) collective-permute-start(f32[9,1024]{1,0:T(8,128)S(1)} %pad_maximum_fusion.refs_1_), channel_id=1, source_target_pairs={{12,8},{14,10},{20,16},{22,18},{28,24},{30,26},{1,5},{3,7}} | collective-permute-start | bytes 110600 | tf_op jit(solution)/shard_map/ppermute | solution.py:280
  25.6 1.0 %copy-start.12 = (bf16[256,1024]{1,0:T(8,128)(2,1)S(1)}, bf16[256,1024]{1,0:T(8,128)(2,1)}, u32[]{:S(2)}) copy-start(bf16[256,1024]{1,0:T(8,128)(2,1)} %copy-done.11) | copy-start | bytes 1572868
  26.7 6.5 %copy-start.15 = (bf16[256,1024]{1,0:T(8,128)(2,1)S(1)}, bf16[256,1024]{1,0:T(8,128)(2,1)}, u32[]{:S(2)}) copy-start(bf16[256,1024]{1,0:T(8,128)(2,1)} %copy-done.14) | copy-start | bytes 1572868
  26.7 18.6 %copy-start.13 = (bf16[256,1024]{1,0:T(8,128)(2,1)S(1)}, bf16[256,1024]{1,0:T(8,128)(2,1)}, u32[]{:S(2)}) copy-start(bf16[256,1024]{1,0:T(8,128)(2,1)} %copy-done.11) | copy-start | bytes 1572868
  28.5 11.3 %collective-permute-start.6 = (bf16[256,1024]{1,0:T(8,128)(2,1)S(1)}, bf16[256,1024]{1,0:T(8,128)(2,1)S(1)}, u32[]{:S(2)}, u32[]{:S(2)}) collective-permute-start(bf16[256,1024]{1,0:T(8,128)(2,1)S(1)} %get-tuple-element.49), channel_id=1, source_target_pairs={{5,0},{7,2},{13,8},{15,10},{21,16},{23,18},{29,24},{31,26},{0,3},{... | collective-permute-start | bytes 1572872 | tf_op jit(solution)/shard_map/ppermute | solution.py:280
  33.2 1.0 %copy-start.9 = (bf16[256,1024]{1,0:T(8,128)(2,1)S(1)}, bf16[256,1024]{1,0:T(8,128)(2,1)}, u32[]{:S(2)}) copy-start(bf16[256,1024]{1,0:T(8,128)(2,1)} %copy-done.8) | copy-start | bytes 1572868
  34.8 10.5 %collective-permute-start.8 = (bf16[256,1024]{1,0:T(8,128)(2,1)S(1)}, bf16[256,1024]{1,0:T(8,128)(2,1)S(1)}, u32[]{:S(2)}, u32[]{:S(2)}) collective-permute-start(bf16[256,1024]{1,0:T(8,128)(2,1)S(1)} %get-tuple-element.52), channel_id=1, source_target_pairs={{5,0},{7,2},{13,8},{15,10},{21,16},{23,18},{29,24},{31,26}} | collective-permute-start | bytes 1572872 | tf_op jit(solution)/shard_map/ppermute | solution.py:280
  45.3 14.4 %copy-start.2 = (bf16[256,1024]{1,0:T(8,128)(2,1)}, bf16[256,1024]{1,0:T(8,128)(2,1)S(1)}, u32[]{:S(2)}) copy-start(bf16[256,1024]{1,0:T(8,128)(2,1)S(1)} %collective-permute-done.8.refs_6_.refs_4_.refs_3_) | copy-start | bytes 1572868
  45.9 1.3 %copy-start = (bf16[1024,1024]{1,0:T(8,128)(2,1)}, bf16[1024,1024]{1,0:T(8,128)(2,1)S(1)}, u32[]{:S(2)}) copy-start(bf16[1024,1024]{1,0:T(8,128)(2,1)S(1)} %get-tuple-element.57.refs_2_) | copy-start | bytes 6291460
  47.2 11.8 %collective-permute-start.10 = (bf16[1024,1024]{1,0:T(8,128)(2,1)}, bf16[1024,1024]{1,0:T(8,128)(2,1)S(1)}, u32[]{:S(2)}, u32[]{:S(2)}) collective-permute-start(bf16[1024,1024]{1,0:T(8,128)(2,1)} %copy-done), channel_id=1, source_target_pairs={{1,0},{3,2},{5,4},{7,6},{9,8},{11,10},{13,12},{15,14},{17,16},{19,... | collective-permute-start | bytes 6291464 | tf_op jit(solution)/shard_map/ppermute | solution.py:280
  48.5 10.5 %collective-permute-start.11 = (bf16[256,1024]{1,0:T(8,128)(2,1)S(1)}, bf16[256,1024]{1,0:T(8,128)(2,1)S(1)}, u32[]{:S(2)}, u32[]{:S(2)}) collective-permute-start(bf16[256,1024]{1,0:T(8,128)(2,1)S(1)} %get-tuple-element.58), channel_id=1, source_target_pairs={{5,0},{7,2},{13,8},{15,10},{21,16},{23,18},{29,24},{31,26}} | collective-permute-start | bytes 1572872 | tf_op jit(solution)/shard_map/ppermute | solution.py:280
  49.8 0.7 collective-permute-start.9
  59.0 0.8 copy-start.5
  59.0 0.7 collective-permute-start.12
  59.8 2.8 %collective-permute-start.13 = (bf16[8,1024]{1,0:T(8,128)(2,1)S(1)}, bf16[8,1024]{1,0:T(8,128)(2,1)S(1)}, u32[]{:S(2)}, u32[]{:S(2)}) collective-permute-start(bf16[8,1024]{1,0:T(8,128)(2,1)S(1)} %get-tuple-element.60), channel_id=1, source_target_pairs={{16,24},{18,26}} | collective-permute-start | bytes 49160 | tf_op jit(solution)/shard_map/ppermute | solution.py:280
  60.5 5.6 %copy-start.1 = (bf16[1024,1024]{1,0:T(8,128)(2,1)S(1)}, bf16[1024,1024]{1,0:T(8,128)(2,1)}, u32[]{:S(2)}) copy-start(bf16[1024,1024]{1,0:T(8,128)(2,1)} %copy-done) | copy-start | bytes 6291460
  60.5 7.9 %collective-permute-start.18 = (f32[8,1024]{1,0:T(8,128)S(1)}, f32[8,1024]{1,0:T(8,128)S(1)}, u32[]{:S(2)}, u32[]{:S(2)}) collective-permute-start(f32[8,1024]{1,0:T(8,128)S(1)} %get-tuple-element.71), channel_id=1, source_target_pairs={{5,0},{7,2}} | collective-permute-start | bytes 98312 | tf_op jit(solution)/shard_map/ppermute | solution.py:280
  61.9 6.5 %collective-permute-start.19 = (f32[8,1024]{1,0:T(8,128)S(1)}, f32[8,1024]{1,0:T(8,128)S(1)}, u32[]{:S(2)}, u32[]{:S(2)}) collective-permute-start(f32[8,1024]{1,0:T(8,128)S(1)} %get-tuple-element.71), channel_id=1, source_target_pairs={{5,4},{7,6}} | collective-permute-start | bytes 98312 | tf_op jit(solution)/shard_map/ppermute | solution.py:280
  62.6 1.0 %copy-start.3 = (bf16[256,1024]{1,0:T(8,128)(2,1)S(1)}, bf16[256,1024]{1,0:T(8,128)(2,1)}, u32[]{:S(2)}) copy-start(bf16[256,1024]{1,0:T(8,128)(2,1)} %copy-done.2) | copy-start | bytes 1572868
  63.7 1.0 %copy-start.6 = (bf16[256,1024]{1,0:T(8,128)(2,1)S(1)}, bf16[256,1024]{1,0:T(8,128)(2,1)}, u32[]{:S(2)}) copy-start(bf16[256,1024]{1,0:T(8,128)(2,1)} %copy-done.5) | copy-start | bytes 1572868
  65.3 2.3 %copy-start.4 = (bf16[256,1024]{1,0:T(8,128)(2,1)S(1)}, bf16[256,1024]{1,0:T(8,128)(2,1)}, u32[]{:S(2)}) copy-start(bf16[256,1024]{1,0:T(8,128)(2,1)} %copy-done.2) | copy-start | bytes 1572868
  65.3 2.3 %copy-start.7 = (bf16[256,1024]{1,0:T(8,128)(2,1)S(1)}, bf16[256,1024]{1,0:T(8,128)(2,1)}, u32[]{:S(2)}) copy-start(bf16[256,1024]{1,0:T(8,128)(2,1)} %copy-done.5) | copy-start | bytes 1572868
  65.3 2.3 %collective-permute-start.14 = (bf16[8,1024]{1,0:T(8,128)(2,1)S(1)}, bf16[8,1024]{1,0:T(8,128)(2,1)S(1)}, u32[]{:S(2)}, u32[]{:S(2)}) collective-permute-start(bf16[8,1024]{1,0:T(8,128)(2,1)S(1)} %get-tuple-element.61), channel_id=1, source_target_pairs={{24,16},{26,18}} | collective-permute-start | bytes 49160 | tf_op jit(solution)/shard_map/ppermute | solution.py:280
  67.7 0.7 collective-permute-start.15
  68.5 20.5 %collective-permute-start.16 = (bf16[8,1024]{1,0:T(8,128)(2,1)S(1)}, bf16[8,1024]{1,0:T(8,128)(2,1)S(1)}, u32[]{:S(2)}, u32[]{:S(2)}) collective-permute-start(bf16[8,1024]{1,0:T(8,128)(2,1)S(1)} %get-tuple-element.69), channel_id=1, source_target_pairs={{8,0},{10,2}} | collective-permute-start | bytes 49160 | tf_op jit(solution)/shard_map/ppermute | solution.py:280
  69.8 19.2 %collective-permute-start.17 = (bf16[8,1024]{1,0:T(8,128)(2,1)S(1)}, bf16[8,1024]{1,0:T(8,128)(2,1)S(1)}, u32[]{:S(2)}, u32[]{:S(2)}) collective-permute-start(bf16[8,1024]{1,0:T(8,128)(2,1)S(1)} %get-tuple-element.69), channel_id=1, source_target_pairs={{8,4},{10,6}} | collective-permute-start | bytes 49160 | tf_op jit(solution)/shard_map/ppermute | solution.py:280
  70.5 19.3 %collective-permute-start.20 = (f32[8,1024]{1,0:T(8,128)S(1)}, f32[8,1024]{1,0:T(8,128)S(1)}, u32[]{:S(2)}, u32[]{:S(2)}) collective-permute-start(f32[8,1024]{1,0:T(8,128)S(1)} %select_select_fusion), channel_id=1, source_target_pairs={{8,12},{10,14},{16,20},{18,22},{24,28},{26,30}} | collective-permute-start | bytes 98312 | tf_op jit(solution)/shard_map/ppermute | solution.py:280
  89.7 2.1 %collective-permute-start.21 = (f32[4,1024]{1,0:T(4,128)S(1)}, f32[4,1024]{1,0:T(4,128)S(1)}, u32[]{:S(2)}, u32[]{:S(2)}) collective-permute-start(f32[4,1024]{1,0:T(4,128)S(1)} %slice.16), channel_id=1, source_target_pairs={{0,1},{2,3},{4,5},{6,7},{8,9},{10,11},{12,13},{14,15},{16,17},{18,... | collective-permute-start | bytes 49160 | tf_op jit(solution)/shard_map/ppermute | solution.py:280
